TPU v7x, 512 devices: a whole 4x8x8 slice. The times are simulated.
512 devices in a mesh: dp: 64 (over x, y_lo, z), vocab: 8 (over y_hi, core).
Axes of the slice: x: 4, y: 8 (y_hi: 4, y_lo: 2; y = y_hi * 2 + y_lo), z: 8, core: 2. Of those that a mesh axis runs over, the one named last changes fastest.
Arguments:
- hidden: bfloat16 [32768, 4096], P(('dp', 'vocab')), may hold values from -64 to 64
- targets: int32 [32768], P('dp'), may hold values from 0 to 1535
- token_weight: float32 [32768], P('dp'), may hold values from 0.25 to 4
- head_weight: bfloat16 [1536, 4096], P('vocab')
Outputs:
- token_loss: float32 [32768], P(('dp', 'vocab'))
- grad_hidden: bfloat16 [32768, 4096], P(('dp', 'vocab'))
- grad_weight: bfloat16 [1536, 4096], P('vocab')
All inputs are finite; a program needn't handle non-finite values.
Results may differ from a plain program's by a relative error of at most 0.012.
Values may be sent and summed in bfloat16 or wider, within the bound.
No kernel may reach another device: no remote copies, remote signals or barrier semaphores. Data moves between devices by JAX's collectives and lax.ppermute only.
A program may use at most 64 MiB of HBM per device.

v0:
```python
import jax
import jax.numpy as jnp
from jax import lax
from jax.sharding import PartitionSpec as P


def per_device(hidden, targets, token_weight, head_weight):
    shard_index = lax.axis_index("vocab")
    tok_dev = hidden.shape[0]
    v_dev = head_weight.shape[0]
    dims_rows = (((1,), (1,)), ((), ()))
    dims_tokens = (((0,), (0,)), ((), ()))
    gathered = lax.all_gather(hidden, "vocab", axis=0, tiled=True)
    logits = lax.dot_general(gathered, head_weight, dims_rows, preferred_element_type=jnp.float32)
    columns = shard_index * v_dev + lax.broadcasted_iota(jnp.int32, (1, v_dev), 1)
    target_hit = columns == targets[:, None]
    local_top = jnp.max(logits, axis=1)
    local_total = jnp.sum(jnp.exp(logits - local_top[:, None]), axis=1)
    local_target = jnp.sum(jnp.where(target_hit, logits, jnp.zeros_like(logits)), axis=1)
    row_top = lax.pmax(local_top, "vocab")
    row_total, target_logit = lax.psum(
        (local_total * jnp.exp(local_top - row_top), local_target), "vocab"
    )
    log_total = row_top + jnp.log(row_total)
    token_loss = lax.dynamic_slice_in_dim(log_total - target_logit, shard_index * tok_dev, tok_dev)
    softmax_rows = jnp.exp(logits - log_total[:, None])
    score_grad = (token_weight[:, None] * (softmax_rows - target_hit.astype(jnp.float32))).astype(
        jnp.bfloat16
    )
    grad_hidden = lax.psum_scatter(
        jnp.dot(score_grad, head_weight, preferred_element_type=jnp.float32).astype(jnp.bfloat16),
        "vocab",
        scatter_dimension=0,
        tiled=True,
    )
    partial_value = lax.dot_general(
        score_grad, gathered, dims_tokens, preferred_element_type=jnp.float32
    )
    grad_weight = lax.psum(partial_value, "dp").astype(jnp.bfloat16)
    return (token_loss, grad_hidden, grad_weight)


def solution(mesh):
    placed = (P(("dp", "vocab"), None), P("dp"), P("dp"), P("vocab", None))
    return jax.shard_map(
        per_device,
        mesh=mesh,
        in_specs=placed,
        out_specs=(P(("dp", "vocab")), P(("dp", "vocab"), None), P("vocab", None)),
        check_vma=False,
    )
```

profile of v0, /device:TPU:32, one launch (start us, length us, event | category | flops | bytes accessed | tf_op | source)
XLA Modules:
  0.0 479.9 jit_solution(13257151096737758729)
XLA Ops:
  7.2 0.0 copy-start
  7.2 0.0 copy-start.1
  7.2 0.0 copy-start.2
  7.2 0.0 all-gather.2.cloned.1.call-start
  7.2 0.7 all-gather.2.cloned.1.call-update
  7.9 0.0 reduce-scatter.2.cloned.1.call-start
  8.0 59.0 %all-gather.2.cloned.1.call-done = bf16[512,4096]{1,0:T(8,128)(2,1)} async-done(((bf16[64,4096]{1,0:T(8,128)(2,1)}), bf16[512,4096]{1,0:T(8,128)(2,1)}) %all-gather.2.cloned.1.call-update) | async-done | bytes 4194320 | tf_op jit(solution)/shard_map/all_gather | solution.py:13
  67.0 0.0 copy-done
  67.0 3.7 fusion.8
  70.8 17.5 %pmax.7 = f32[512]{0:T(512)S(1)} all-reduce(f32[512]{0:T(512)S(1)} %get-tuple-element.9), channel_id=1, replica_groups=mesh['dp'=64,'vocab'=8] {'vocab'}, use_global_device_ids=true, to_apply=%region_1.0 | all-reduce | flops 512 | bytes 4096 | tf_op jit(solution)/shard_map/pmax | solution.py:20
  88.3 0.0 copy-done.1
  88.3 0.1 fusion
  88.4 14.2 %all-reduce = (f32[512]{0:T(512)S(1)}, f32[512]{0:T(512)S(1)}) all-reduce(f32[512]{0:T(512)S(1)} %exponential_multiply_fusion, f32[512]{0:T(512)S(1)} %get-tuple-element.3), channel_id=1, replica_groups=mesh['dp'=64,'vocab'=8] {'vocab'}, use_global_device_ids=true, to_apply=%region_3.4 | all-reduce | flops 1024 | bytes 8192 | tf_op jit(solution)/shard_map/psum | solution.py:21
  102.6 0.0 copy-done.2
  102.6 3.3 convolution_convert_fusion
  105.9 0.0 reduce-scatter.2.cloned.1.call-update
  106.0 5.0 %fusion.4 = f32[192,4096]{1,0:T(8,128)} fusion(bf16[512,4096]{1,0:T(8,128)(2,1)} %all-gather.2.cloned.1.call-done, f32[512,192]{0,1:T(8,128)S(1)} %get-tuple-element.10, f32[512]{0:T(512)S(1)} %get-tuple-element.8, f32[512]{0:T(512)S(1)} %copy-done.2, s32[512]{0:T(512)S(1)} %copy-done.1, s32[192]{0:T(256)S(1)} %iota_add_fusion), kind=kOutput, calls=%fused_computation.11 | convolution fusion | flops 805896192 | bytes 7740160 | tf_op jit(solution)/shard_map/dot_general | solution.py:36
  111.0 0.6 dynamic_slice.3
  111.6 361.5 %all-reduce.2 = bf16[192,4096]{1,0:T(8,128)(2,1)} all-reduce(f32[192,4096]{1,0:T(8,128)} %fusion.4), channel_id=1, replica_groups=mesh['dp'=64,'vocab'=8] {'dp'}, use_global_device_ids=true, to_apply=%region_7.8 | all-reduce | flops 786432 | bytes 4718592 | tf_op jit(solution)/shard_map/psum | solution.py:39
  473.1 0.0 reduce-scatter.2.cloned.1.call-done
  (3 shorter events, 0.0 us)
Async XLA Ops:
  7.2 59.9 %copy-start = (bf16[192,4096]{1,0:T(8,128)(2,1)S(1)}, bf16[192,4096]{1,0:T(8,128)(2,1)}, u32[]{:S(2)}) copy-start(bf16[192,4096]{1,0:T(8,128)(2,1)} %param.7) | copy-start | bytes 4718596
  7.2 81.1 %copy-start.1 = (s32[512]{0:T(512)S(1)}, s32[512]{0:T(512)}, u32[]{:S(2)}) copy-start(s32[512]{0:T(512)} %param.5) | copy-start | bytes 6148
  7.2 95.5 %copy-start.2 = (f32[512]{0:T(512)S(1)}, f32[512]{0:T(512)}, u32[]{:S(2)}) copy-start(f32[512]{0:T(512)} %param.6) | copy-start | bytes 6148
  7.2 59.8 %all-gather.2.cloned.1.call-start = ((), (), s32[]{:S(2)}) async-start(), calls=%async_computation.1 | async-start | bytes 4718592 | tf_op jit(solution)/shard_map/all_gather | solution.py:13
  7.9 465.1 %reduce-scatter.2.cloned.1.call-start = ((), (), s32[]{:S(2)}) async-start(), calls=%async_computation.2 | async-start | bytes 4718592 | tf_op jit(solution)/shard_map/reduce_scatter | solution.py:30
Sparse Core Ops, SparseCore 0:
  10.2 56.7 all-gather.1
  106.1 63.9 reduce-scatter.1
where the time goes:
time: 480 us
  blocking collectives  393 us (82%)
  waiting for transfers between devices  59.7 us (12%)
  between operations  14.1 us (3%)
  matrix products  12.1 us (3%)
    psum x1, blocking collectives, per_device(): grad_weight = lax.psum(partial_value, 'dp').astype(jnp.bfloat16)  361 us
    all_gather x1, waiting for transfers between devices, per_device(): gathered = lax.all_gather(hidden, 'vocab', axis=0, tiled=True)  59 us
    pmax x1, blocking collectives, per_device(): row_top = lax.pmax(local_top, 'vocab')  17.5 us
    psum x1, blocking collectives, per_device(): lax.psum((local_total * jnp.exp(local_top - row_top), local_target), 'voc...  14.2 us
  transfers between devices with their start and end apart: 2, of which 1 were waited for; matrix products, arithmetic and copies ran while one was open for 1% of the time, Pallas kernels for 0%

commit v1 on v0

v1 whole, which is shorter than its diff:
```python
import jax
import jax.numpy as jnp
from jax import lax
from jax.sharding import Mesh
from jax.sharding import PartitionSpec as P

F32, BF16 = jnp.float32, jnp.bfloat16
DP = ("x", "yl", "z")


def shift(value, axis, step, size):
    return lax.ppermute(value, axis, [(i, (i + step) % size) for i in range(size)])


def relative(value, yh, core):
    n_yh, n_core, _ = value.shape
    value = lax.dynamic_slice_in_dim(jnp.concatenate([value, value], 0), yh, n_yh, 0)
    value = lax.dynamic_slice_in_dim(jnp.concatenate([value, value], 1), core, n_core, 1)
    return value.transpose(1, 0, 2).reshape(-1)


def merge(a, b):
    top = jnp.maximum(a[0], b[0])
    return jnp.stack([top, a[1] * jnp.exp(a[0] - top) + b[1] * jnp.exp(b[0] - top), a[2] + b[2]])


def per_device(hidden, targets, token_weight, head_weight, *, n_yh, n_dp):
    yh, core = lax.axis_index("yh"), lax.axis_index("core")
    tok, width = hidden.shape
    v_dev = head_weight.shape[0]
    half = tok // 2
    labels = relative(targets.reshape(n_yh, 2, tok), yh, core)
    weights = relative(token_weight.reshape(n_yh, 2, tok), yh, core)

    swap = lambda v: shift(v, "core", 1, 2)
    before = shift(hidden, "yh", 1, n_yh)
    after = shift(hidden, "yh", -1, n_yh)
    far_a = shift(before[:half], "yh", 1, n_yh)
    far_b = shift(after[half:], "yh", -1, n_yh)
    mine = [hidden, after, far_a, far_b, before]
    gathered = jnp.concatenate(mine + [swap(v) for v in mine], 0)

    logits = lax.dot_general(gathered, head_weight, (((1,), (1,)), ((), ())), preferred_element_type=F32)
    columns = (yh * 2 + core) * v_dev + lax.broadcasted_iota(jnp.int32, (1, v_dev), 1)
    hit = columns == labels[:, None]
    top = jnp.max(logits, axis=1)
    total = jnp.sum(jnp.exp(logits - top[:, None]), axis=1)
    target = jnp.sum(jnp.where(hit, logits, jnp.zeros_like(logits)), axis=1)
    stats = jnp.stack([top, total, target]).reshape(3, 2, n_yh, tok)
    stats = merge(stats, swap(stats)[:, ::-1])
    others = [jnp.roll(shift(stats, "yh", s, n_yh), -s, axis=2) for s in (1, 2, 3)]
    stats = merge(merge(stats, others[0]), merge(others[1], others[2])).reshape(3, -1)
    log_total = stats[0] + jnp.log(stats[1])
    token_loss = (log_total - stats[2])[:tok]

    softmax = jnp.exp(logits - log_total[:, None])
    score = (weights[:, None] * (softmax - hit.astype(F32))).astype(BF16)

    partial = lax.dot_general(score, gathered, (((0,), (0,)), ((), ())), preferred_element_type=F32).astype(BF16)
    rows, cols = v_dev // 4, width * 4 // n_dp
    chunks = partial.reshape(4, rows, n_dp // 4, cols).transpose(0, 2, 1, 3).reshape(n_dp, rows, cols)
    chunks = lax.all_to_all(chunks, DP, 0, 0, tiled=True)

    terms = jnp.dot(score, head_weight, preferred_element_type=F32).astype(BF16)
    own = n_yh * tok
    terms = (terms[:own].astype(F32) + swap(terms[own:]).astype(F32)).astype(BF16).reshape(n_yh, tok, width)
    grad_hidden = terms[0].astype(F32)
    for s in range(1, n_yh):
        grad_hidden = grad_hidden + shift(terms[s], "yh", s, n_yh).astype(F32)
    grad_hidden = grad_hidden.astype(BF16)

    chunk = jnp.sum(chunks.astype(F32), axis=0).astype(BF16)
    chunks = lax.all_to_all(jnp.broadcast_to(chunk, (n_dp, rows, cols)), DP, 0, 0, tiled=True)
    grad_weight = chunks.reshape(4, n_dp // 4, rows, cols).transpose(0, 2, 1, 3).reshape(v_dev, width)
    return token_loss, grad_hidden, grad_weight


def fine(mesh_devices, sizes):
    mesh = Mesh(mesh_devices.reshape(sizes), ("x", "yl", "z", "yh", "core"))

    def body(*args):
        return per_device(*args, n_yh=sizes[3], n_dp=sizes[0] * sizes[1] * sizes[2])

    tokens = ("x", "yl", "z", "yh", "core")
    return jax.shard_map(
        body,
        mesh=mesh,
        in_specs=(P(tokens, None), P(DP), P(DP), P(("yh", "core"), None)),
        out_specs=(P(tokens), P(tokens, None), P(("yh", "core"), None)),
        check_vma=False,
    )


def solution(mesh):
    return fine(mesh.devices, (4, 2, 8, 4, 2))
```

time: 480 us -> 215 us (0.45)
  the two profiles are of different devices: /device:TPU:32 before, /device:TPU:16 now
where the time goes in v1:
time: 215 us; the launch traced here: 214 us
  waiting for transfers between devices  109 us (51%)
  starting transfers between devices  73.2 us (34%)
  local copies, waits for them, and re-layouts  17.8 us (8%)
  matrix products  6.97 us (3%)
  other arithmetic  6.1 us (3%)
    ppermute x17, waiting for transfers between devices, shift(): lax.ppermute(value, axis, [(i, (i + step) % size) for i in range(size)])  77.7 us
    ppermute x17, starting transfers between devices, shift(): lax.ppermute(value, axis, [(i, (i + step) % size) for i in range(size)])  52.7 us
    all_to_all x1, waiting for transfers between devices, per_device(): chunks = lax.all_to_all(chunks, DP, 0, 0, tiled=True)  30.8 us
    all_to_all x1, starting transfers between devices, per_device(): chunks = lax.all_to_all(chunks, DP, 0, 0, tiled=True)  13.7 us
    unnamed x21, local copies, waits for them, and re-layouts  8.78 us
    all_to_all x1, starting transfers between devices, per_device(): lax.all_to_all(jnp.broadcast_to(chunk, (n_dp, rows, cols)), DP, 0, 0, til...  6.78 us
  transfers between devices with their start and end apart: 19, of which 10 were waited for; matrix products, arithmetic and copies ran while one was open for 7% of the time, Pallas kernels for 0%

profile of v1, /device:TPU:16, one launch (start us, length us, event | category | flops | bytes accessed | tf_op | source)
XLA Modules:
  0.0 213.7 jit_solution(16604875666821522388)
XLA Ops:
  0.6 5.8 %collective-permute-start.1 = (bf16[64,4096]{1,0:T(8,128)(2,1)}, bf16[64,4096]{1,0:T(8,128)(2,1)S(1)}, u32[]{:S(2)}, u32[]{:S(2)}) collective-permute-start(bf16[64,4096]{1,0:T(8,128)(2,1)} %param.4), channel_id=1, source_target_pairs={{0,2},{2,4},{4,6},{6,0},{1,3},{3,5},{5,7},{7,1},{8,10},{10,12},{12... | collective-permute-start | bytes 1572872 | tf_op jit(solution)/shard_map/ppermute | solution.py:12
  6.5 3.8 %collective-permute-start = (bf16[64,4096]{1,0:T(8,128)(2,1)}, bf16[64,4096]{1,0:T(8,128)(2,1)S(1)}, u32[]{:S(2)}, u32[]{:S(2)}) collective-permute-start(bf16[64,4096]{1,0:T(8,128)(2,1)} %param.4), channel_id=1, source_target_pairs={{0,6},{2,0},{4,2},{6,4},{1,7},{3,1},{5,3},{7,5},{8,14},{10,8},{12,... | collective-permute-start | bytes 1572872 | tf_op jit(solution)/shard_map/ppermute | solution.py:12
  10.3 1.9 collective-permute-start.4
  15.0 14.1 %collective-permute-done.1 = bf16[64,4096]{1,0:T(8,128)(2,1)S(1)} collective-permute-done((bf16[64,4096]{1,0:T(8,128)(2,1)}, bf16[64,4096]{1,0:T(8,128)(2,1)S(1)}, u32[]{:S(2)}, u32[]{:S(2)}) %collective-permute-start.1) | collective-permute-done | bytes 524320 | tf_op jit(solution)/shard_map/ppermute | solution.py:12
  29.1 6.4 %collective-permute-start.2 = (bf16[32,4096]{1,0:T(8,128)(2,1)S(1)}, bf16[32,4096]{1,0:T(8,128)(2,1)S(1)}, u32[]{:S(2)}, u32[]{:S(2)}) collective-permute-start(bf16[32,4096]{1,0:T(8,128)(2,1)S(1)} %slice.147), channel_id=1, source_target_pairs={{0,2},{2,4},{4,6},{6,0},{1,3},{3,5},{5,7},{7,1},{8,10},{10,12},{12... | collective-permute-start | bytes 786440 | tf_op jit(solution)/shard_map/ppermute | solution.py:12
  35.6 1.9 collective-permute-start.3
  37.5 1.9 collective-permute-start.5
  39.4 2.4 %collective-permute-start.8 = (bf16[64,4096]{1,0:T(8,128)(2,1)S(1)}, bf16[64,4096]{1,0:T(8,128)(2,1)S(1)}, u32[]{:S(2)}, u32[]{:S(2)}) collective-permute-start(bf16[64,4096]{1,0:T(8,128)(2,1)S(1)} %collective-permute-done.1), channel_id=1, source_target_pairs={{0,1},{1,0},{2,3},{3,2},{4,5},{5,4},{6,7},{7,6},{8,9},{9,8},{10,11... | collective-permute-start | bytes 1572872 | tf_op jit(solution)/shard_map/ppermute | solution.py:12
  41.9 2.8 %collective-permute-done.2 = bf16[32,4096]{1,0:T(8,128)(2,1)S(1)} collective-permute-done((bf16[32,4096]{1,0:T(8,128)(2,1)S(1)}, bf16[32,4096]{1,0:T(8,128)(2,1)S(1)}, u32[]{:S(2)}, u32[]{:S(2)}) %collective-permute-start.2) | collective-permute-done | bytes 262176 | tf_op jit(solution)/shard_map/ppermute | solution.py:12
  44.7 1.9 collective-permute-start.6
  46.6 5.6 %collective-permute-done.3 = bf16[32,4096]{1,0:T(8,128)(2,1)S(1)} collective-permute-done((bf16[32,4096]{1,0:T(8,128)(2,1)S(1)}, bf16[32,4096]{1,0:T(8,128)(2,1)S(1)}, u32[]{:S(2)}, u32[]{:S(2)}) %collective-permute-start.3) | collective-permute-done | bytes 262176 | tf_op jit(solution)/shard_map/ppermute | solution.py:12
  52.2 1.9 collective-permute-start.7
  55.7 1.9 copy-done.3
  59.7 2.0 collective-permute-start.9
  62.8 1.9 collective-permute-start.11
  64.9 4.6 %collective-permute-start.10 = (f32[3,2,4,64]{3,2,1,0:T(4,128)S(1)}, f32[3,2,4,64]{3,2,1,0:T(4,128)S(1)}, u32[]{:S(2)}, u32[]{:S(2)}) collective-permute-start(f32[3,2,4,64]{3,2,1,0:T(4,128)S(1)} %pad_maximum_fusion.1), channel_id=1, source_target_pairs={{0,2},{2,4},{4,6},{6,0},{1,3},{3,5},{5,7},{7,1},{8,10},{10,12},{12... | collective-permute-start | bytes 18440 | tf_op jit(solution)/shard_map/ppermute | solution.py:12
  69.4 2.1 %collective-permute-start.12 = (f32[3,2,4,64]{3,2,1,0:T(4,128)S(1)}, f32[3,2,4,64]{3,2,1,0:T(4,128)S(1)}, u32[]{:S(2)}, u32[]{:S(2)}) collective-permute-start(f32[3,2,4,64]{3,2,1,0:T(4,128)S(1)} %pad_maximum_fusion.1), channel_id=1, source_target_pairs={{0,6},{2,0},{4,2},{6,4},{1,7},{3,1},{5,3},{7,5},{8,14},{10,8},{12,... | collective-permute-start | bytes 18440 | tf_op jit(solution)/shard_map/ppermute | solution.py:12
  72.3 4.8 %collective-permute-done.12 = f32[3,2,4,64]{3,2,1,0:T(4,128)S(1)} collective-permute-done((f32[3,2,4,64]{3,2,1,0:T(4,128)S(1)}, f32[3,2,4,64]{3,2,1,0:T(4,128)S(1)}, u32[]{:S(2)}, u32[]{:S(2)}) %collective-permute-start.12) | collective-permute-done | bytes 6176 | tf_op jit(solution)/shard_map/ppermute | solution.py:12
  77.3 3.3 %convolution_convert_fusion.1 = bf16[192,4096]{1,0:T(8,128)(2,1)S(1)} fusion(bf16[512,4096]{1,0:T(8,128)(2,1)} %copy-done.3, f32[512,192]{0,1:T(8,128)S(1)} %get-tuple-element.18, f32[512]{0:T(512)S(1)} %add.89, f32[512]{0:T(512)S(1)} %mul.60, s32[512]{0:T(512)S(1)} %eq.16, s32[192]{0:T(256)} %copy-done.4), kind=kOutput, calls=%fused_computation.1 | convolution fusion | flops 806682624 | bytes 6167296 | tf_op jit(solution)/shard_map/dot_general | solution.py:59
  82.7 13.7 %all-to-all-start = ((bf16[64,48,256]{2,1,0:T(8,128)(2,1)}), bf16[64,48,256]{2,1,0:T(8,128)(2,1)S(1)}, u32[]{:S(2)}, u32[]{:S(2)}) async-start(bf16[64,48,256]{2,1,0:T(8,128)(2,1)} %bitcast.22), calls=%async_computation | async-start | bytes 3145728 | tf_op jit(solution)/shard_map/all_to_all | solution.py:62
  96.5 2.1 convolution_convert_fusion
  98.6 1.9 copy-done.1
  102.1 1.9 collective-permute-start.13
  104.0 30.8 %all-to-all-done = bf16[64,48,256]{2,1,0:T(8,128)(2,1)S(1)} async-done(((bf16[64,48,256]{2,1,0:T(8,128)(2,1)}), bf16[64,48,256]{2,1,0:T(8,128)(2,1)S(1)}, u32[]{:S(2)}, u32[]{:S(2)}) %all-to-all-start) | async-done | bytes 1572896 | tf_op jit(solution)/shard_map/all_to_all | solution.py:62
  136.3 6.8 %all-to-all-start.1 = ((bf16[64,48,256]{2,1,0:T(8,128)(2,1)}), bf16[64,48,256]{2,1,0:T(8,128)(2,1)S(1)}, u32[]{:S(2)}, u32[]{:S(2)}) async-start(bf16[64,48,256]{2,1,0:T(8,128)(2,1)} %broadcast_in_dim.9), calls=%async_computation.1 | async-start | bytes 3145728 | tf_op jit(solution)/shard_map/all_to_all | solution.py:73
  143.1 3.0 %add_convert_fusion = bf16[256,4096]{1,0:T(8,128)(2,1)S(1)} fusion(bf16[256,4096]{1,0:T(8,128)(2,1)} %collective-permute-done.13, bf16[512,4096]{1,0:T(8,128)(2,1)} %copy-done.1), kind=kLoop, calls=%fused_computation.2 | loop fusion | flops 4194304 | bytes 6291456 | tf_op jit(solution)/shard_map/convert_element_type | solution.py:66
  148.6 4.6 %collective-permute-start.14 = (bf16[64,4096]{1,0:T(8,128)(2,1)}, bf16[64,4096]{1,0:T(8,128)(2,1)}, u32[]{:S(2)}, u32[]{:S(2)}) collective-permute-start(bf16[64,4096]{1,0:T(8,128)(2,1)} %get-tuple-element.5), channel_id=1, source_target_pairs={{0,2},{2,4},{4,6},{6,0},{1,3},{3,5},{5,7},{7,1},{8,10},{10,12},{12... | collective-permute-start | bytes 1572872 | tf_op jit(solution)/shard_map/ppermute | solution.py:12
  153.1 2.8 %collective-permute-start.15 = (bf16[64,4096]{1,0:T(8,128)(2,1)}, bf16[64,4096]{1,0:T(8,128)(2,1)}, u32[]{:S(2)}, u32[]{:S(2)}) collective-permute-start(bf16[64,4096]{1,0:T(8,128)(2,1)} %get-tuple-element.7), channel_id=1, source_target_pairs={{0,4},{2,6},{4,0},{6,2},{1,5},{3,7},{5,1},{7,3},{8,12},{10,14},{12... | collective-permute-start | bytes 1572872 | tf_op jit(solution)/shard_map/ppermute | solution.py:12
  156.0 4.7 %collective-permute-start.16 = (bf16[64,4096]{1,0:T(8,128)(2,1)}, bf16[64,4096]{1,0:T(8,128)(2,1)}, u32[]{:S(2)}, u32[]{:S(2)}) collective-permute-start(bf16[64,4096]{1,0:T(8,128)(2,1)} %get-tuple-element.6), channel_id=1, source_target_pairs={{0,6},{2,0},{4,2},{6,4},{1,7},{3,1},{5,3},{7,5},{8,14},{10,8},{12,... | collective-permute-start | bytes 1572872 | tf_op jit(solution)/shard_map/ppermute | solution.py:12
  161.3 26.4 %collective-permute-done.14 = bf16[64,4096]{1,0:T(8,128)(2,1)} collective-permute-done((bf16[64,4096]{1,0:T(8,128)(2,1)}, bf16[64,4096]{1,0:T(8,128)(2,1)}, u32[]{:S(2)}, u32[]{:S(2)}) %collective-permute-start.14) | collective-permute-done | bytes 524320 | tf_op jit(solution)/shard_map/ppermute | solution.py:12
  187.7 21.0 %collective-permute-done.15 = bf16[64,4096]{1,0:T(8,128)(2,1)} collective-permute-done((bf16[64,4096]{1,0:T(8,128)(2,1)}, bf16[64,4096]{1,0:T(8,128)(2,1)}, u32[]{:S(2)}, u32[]{:S(2)}) %collective-permute-start.15) | collective-permute-done | bytes 524320 | tf_op jit(solution)/shard_map/ppermute | solution.py:12
  208.7 2.6 %add_convert_fusion.1 = bf16[64,4096]{1,0:T(8,128)(2,1)} fusion(bf16[64,4096]{1,0:T(8,128)(2,1)} %collective-permute-done.16, bf16[64,4096]{1,0:T(8,128)(2,1)} %collective-permute-done.15, bf16[64,4096]{1,0:T(8,128)(2,1)} %collective-permute-done.14, bf16[256,4096]{1,0:T(8,128)(2,1)} %copy-done.2), kind=kLoop, calls=%fused_computation.3 | loop fusion | flops 2097152 | bytes 2621440 | tf_op jit(solution)/shard_map/convert_element_type | solution.py:70
  (69 shorter events, 19.1 us)
Async XLA Ops:
  0.6 57.0 %copy-start = (bf16[192,4096]{1,0:T(8,128)(2,1)S(1)}, bf16[192,4096]{1,0:T(8,128)(2,1)}, u32[]{:S(2)}) copy-start(bf16[192,4096]{1,0:T(8,128)(2,1)} %param.7) | copy-start | bytes 4718596
  0.6 28.5 %collective-permute-start.1 = (bf16[64,4096]{1,0:T(8,128)(2,1)}, bf16[64,4096]{1,0:T(8,128)(2,1)S(1)}, u32[]{:S(2)}, u32[]{:S(2)}) collective-permute-start(bf16[64,4096]{1,0:T(8,128)(2,1)} %param.4), channel_id=1, source_target_pairs={{0,2},{2,4},{4,6},{6,0},{1,3},{3,5},{5,7},{7,1},{8,10},{10,12},{12... | collective-permute-start | bytes 1572872 | tf_op jit(solution)/shard_map/ppermute | solution.py:12
  6.5 29.0 %collective-permute-start = (bf16[64,4096]{1,0:T(8,128)(2,1)}, bf16[64,4096]{1,0:T(8,128)(2,1)S(1)}, u32[]{:S(2)}, u32[]{:S(2)}) collective-permute-start(bf16[64,4096]{1,0:T(8,128)(2,1)} %param.4), channel_id=1, source_target_pairs={{0,6},{2,0},{4,2},{6,4},{1,7},{3,1},{5,3},{7,5},{8,14},{10,8},{12,... | collective-permute-start | bytes 1572872 | tf_op jit(solution)/shard_map/ppermute | solution.py:12
  10.3 43.9 %collective-permute-start.4 = (bf16[64,4096]{1,0:T(8,128)(2,1)}, bf16[64,4096]{1,0:T(8,128)(2,1)S(1)}, u32[]{:S(2)}, u32[]{:S(2)}) collective-permute-start(bf16[64,4096]{1,0:T(8,128)(2,1)} %param.4), channel_id=1, source_target_pairs={{0,1},{1,0},{2,3},{3,2},{4,5},{5,4},{6,7},{7,6},{8,9},{9,8},{10,11... | collective-permute-start | bytes 1572872 | tf_op jit(solution)/shard_map/ppermute | solution.py:12
  13.9 45.5 %copy-start.4 = (s32[192]{0:T(256)}, s32[192]{0:T(256)S(1)}, u32[]{:S(2)}) copy-start(s32[192]{0:T(256)S(1)} %iota_add_fusion) | copy-start | bytes 2308
  29.1 15.5 %collective-permute-start.2 = (bf16[32,4096]{1,0:T(8,128)(2,1)S(1)}, bf16[32,4096]{1,0:T(8,128)(2,1)S(1)}, u32[]{:S(2)}, u32[]{:S(2)}) collective-permute-start(bf16[32,4096]{1,0:T(8,128)(2,1)S(1)} %slice.147), channel_id=1, source_target_pairs={{0,2},{2,4},{4,6},{6,0},{1,3},{3,5},{5,7},{7,1},{8,10},{10,12},{12... | collective-permute-start | bytes 786440 | tf_op jit(solution)/shard_map/ppermute | solution.py:12
  35.6 16.7 %collective-permute-start.3 = (bf16[32,4096]{1,0:T(8,128)(2,1)S(1)}, bf16[32,4096]{1,0:T(8,128)(2,1)S(1)}, u32[]{:S(2)}, u32[]{:S(2)}) collective-permute-start(bf16[32,4096]{1,0:T(8,128)(2,1)S(1)} %slice.148), channel_id=1, source_target_pairs={{0,6},{2,0},{4,2},{6,4},{1,7},{3,1},{5,3},{7,5},{8,14},{10,8},{12,... | collective-permute-start | bytes 786440 | tf_op jit(solution)/shard_map/ppermute | solution.py:12
  37.5 16.8 %collective-permute-start.5 = (bf16[64,4096]{1,0:T(8,128)(2,1)S(1)}, bf16[64,4096]{1,0:T(8,128)(2,1)S(1)}, u32[]{:S(2)}, u32[]{:S(2)}) collective-permute-start(bf16[64,4096]{1,0:T(8,128)(2,1)S(1)} %collective-permute-done), channel_id=1, source_target_pairs={{0,1},{1,0},{2,3},{3,2},{4,5},{5,4},{6,7},{7,6},{8,9},{9,8},{10,11... | collective-permute-start | bytes 1572872 | tf_op jit(solution)/shard_map/ppermute | solution.py:12
  39.4 16.3 %collective-permute-start.8 = (bf16[64,4096]{1,0:T(8,128)(2,1)S(1)}, bf16[64,4096]{1,0:T(8,128)(2,1)S(1)}, u32[]{:S(2)}, u32[]{:S(2)}) collective-permute-start(bf16[64,4096]{1,0:T(8,128)(2,1)S(1)} %collective-permute-done.1), channel_id=1, source_target_pairs={{0,1},{1,0},{2,3},{3,2},{4,5},{5,4},{6,7},{7,6},{8,9},{9,8},{10,11... | collective-permute-start | bytes 1572872 | tf_op jit(solution)/shard_map/ppermute | solution.py:12
  44.7 9.7 %collective-permute-start.6 = (bf16[32,4096]{1,0:T(8,128)(2,1)S(1)}, bf16[32,4096]{1,0:T(8,128)(2,1)S(1)}, u32[]{:S(2)}, u32[]{:S(2)}) collective-permute-start(bf16[32,4096]{1,0:T(8,128)(2,1)S(1)} %collective-permute-done.2), channel_id=1, source_target_pairs={{0,1},{1,0},{2,3},{3,2},{4,5},{5,4},{6,7},{7,6},{8,9},{9,8},{10,11... | collective-permute-start | bytes 786440 | tf_op jit(solution)/shard_map/ppermute | solution.py:12
  52.2 3.4 %collective-permute-start.7 = (bf16[32,4096]{1,0:T(8,128)(2,1)S(1)}, bf16[32,4096]{1,0:T(8,128)(2,1)S(1)}, u32[]{:S(2)}, u32[]{:S(2)}) collective-permute-start(bf16[32,4096]{1,0:T(8,128)(2,1)S(1)} %collective-permute-done.3), channel_id=1, source_target_pairs={{0,1},{1,0},{2,3},{3,2},{4,5},{5,4},{6,7},{7,6},{8,9},{9,8},{10,11... | collective-permute-start | bytes 786440 | tf_op jit(solution)/shard_map/ppermute | solution.py:12
  55.7 1.9 copy-start.3
  59.7 3.1 %collective-permute-start.9 = (f32[3,2,4,64]{3,2,1,0:T(4,128)S(1)}, f32[3,2,4,64]{3,2,1,0:T(4,128)S(1)}, u32[]{:S(2)}, u32[]{:S(2)}) collective-permute-start(f32[3,2,4,64]{3,2,1,0:T(4,128)S(1)} %pad_maximum_fusion), channel_id=1, source_target_pairs={{0,1},{1,0},{2,3},{3,2},{4,5},{5,4},{6,7},{7,6},{8,9},{9,8},{10,11... | collective-permute-start | bytes 18440 | tf_op jit(solution)/shard_map/ppermute | solution.py:12
  62.8 9.5 %collective-permute-start.11 = (f32[3,2,4,64]{3,2,1,0:T(4,128)S(1)}, f32[3,2,4,64]{3,2,1,0:T(4,128)S(1)}, u32[]{:S(2)}, u32[]{:S(2)}) collective-permute-start(f32[3,2,4,64]{3,2,1,0:T(4,128)S(1)} %pad_maximum_fusion.1), channel_id=1, source_target_pairs={{0,4},{2,6},{4,0},{6,2},{1,5},{3,7},{5,1},{7,3},{8,12},{10,14},{12... | collective-permute-start | bytes 18440 | tf_op jit(solution)/shard_map/ppermute | solution.py:12
  64.9 7.5 %collective-permute-start.10 = (f32[3,2,4,64]{3,2,1,0:T(4,128)S(1)}, f32[3,2,4,64]{3,2,1,0:T(4,128)S(1)}, u32[]{:S(2)}, u32[]{:S(2)}) collective-permute-start(f32[3,2,4,64]{3,2,1,0:T(4,128)S(1)} %pad_maximum_fusion.1), channel_id=1, source_target_pairs={{0,2},{2,4},{4,6},{6,0},{1,3},{3,5},{5,7},{7,1},{8,10},{10,12},{12... | collective-permute-start | bytes 18440 | tf_op jit(solution)/shard_map/ppermute | solution.py:12
  69.4 7.7 %collective-permute-start.12 = (f32[3,2,4,64]{3,2,1,0:T(4,128)S(1)}, f32[3,2,4,64]{3,2,1,0:T(4,128)S(1)}, u32[]{:S(2)}, u32[]{:S(2)}) collective-permute-start(f32[3,2,4,64]{3,2,1,0:T(4,128)S(1)} %pad_maximum_fusion.1), channel_id=1, source_target_pairs={{0,6},{2,0},{4,2},{6,4},{1,7},{3,1},{5,3},{7,5},{8,14},{10,8},{12,... | collective-permute-start | bytes 18440 | tf_op jit(solution)/shard_map/ppermute | solution.py:12
  82.7 52.0 %all-to-all-start = ((bf16[64,48,256]{2,1,0:T(8,128)(2,1)}), bf16[64,48,256]{2,1,0:T(8,128)(2,1)S(1)}, u32[]{:S(2)}, u32[]{:S(2)}) async-start(bf16[64,48,256]{2,1,0:T(8,128)(2,1)} %bitcast.22), calls=%async_computation | async-start | bytes 3145728 | tf_op jit(solution)/shard_map/all_to_all | solution.py:62
  98.5 1.9 copy-start.1
  102.1 41.0 %collective-permute-start.13 = (bf16[256,4096]{1,0:T(8,128)(2,1)}, bf16[256,4096]{1,0:T(8,128)(2,1)}, u32[]{:S(2)}, u32[]{:S(2)}) collective-permute-start(bf16[256,4096]{1,0:T(8,128)(2,1)} %slice.171), channel_id=1, source_target_pairs={{0,1},{1,0},{2,3},{3,2},{4,5},{5,4},{6,7},{7,6},{8,9},{9,8},{10,11... | collective-permute-start | bytes 6291464 | tf_op jit(solution)/shard_map/ppermute | solution.py:12
  136.3 75.0 %all-to-all-start.1 = ((bf16[64,48,256]{2,1,0:T(8,128)(2,1)}), bf16[64,48,256]{2,1,0:T(8,128)(2,1)S(1)}, u32[]{:S(2)}, u32[]{:S(2)}) async-start(bf16[64,48,256]{2,1,0:T(8,128)(2,1)} %broadcast_in_dim.9), calls=%async_computation.1 | async-start | bytes 3145728 | tf_op jit(solution)/shard_map/all_to_all | solution.py:73
  146.1 1.3 copy-start.2
  148.6 39.1 %collective-permute-start.14 = (bf16[64,4096]{1,0:T(8,128)(2,1)}, bf16[64,4096]{1,0:T(8,128)(2,1)}, u32[]{:S(2)}, u32[]{:S(2)}) collective-permute-start(bf16[64,4096]{1,0:T(8,128)(2,1)} %get-tuple-element.5), channel_id=1, source_target_pairs={{0,2},{2,4},{4,6},{6,0},{1,3},{3,5},{5,7},{7,1},{8,10},{10,12},{12... | collective-permute-start | bytes 1572872 | tf_op jit(solution)/shard_map/ppermute | solution.py:12
  153.1 55.6 %collective-permute-start.15 = (bf16[64,4096]{1,0:T(8,128)(2,1)}, bf16[64,4096]{1,0:T(8,128)(2,1)}, u32[]{:S(2)}, u32[]{:S(2)}) collective-permute-start(bf16[64,4096]{1,0:T(8,128)(2,1)} %get-tuple-element.7), channel_id=1, source_target_pairs={{0,4},{2,6},{4,0},{6,2},{1,5},{3,7},{5,1},{7,3},{8,12},{10,14},{12... | collective-permute-start | bytes 1572872 | tf_op jit(solution)/shard_map/ppermute | solution.py:12
  156.0 52.7 %collective-permute-start.16 = (bf16[64,4096]{1,0:T(8,128)(2,1)}, bf16[64,4096]{1,0:T(8,128)(2,1)}, u32[]{:S(2)}, u32[]{:S(2)}) collective-permute-start(bf16[64,4096]{1,0:T(8,128)(2,1)} %get-tuple-element.6), channel_id=1, source_target_pairs={{0,6},{2,0},{4,2},{6,4},{1,7},{3,1},{5,3},{7,5},{8,14},{10,8},{12,... | collective-permute-start | bytes 1572872 | tf_op jit(solution)/shard_map/ppermute | solution.py:12

commit v2 on v1

v2 whole, which is shorter than its diff:
```python
import jax
import jax.numpy as jnp
from jax import lax
from jax.sharding import Mesh
from jax.sharding import PartitionSpec as P

F32, BF16 = jnp.float32, jnp.bfloat16
DP = ("x", "yl", "z")
VOCAB = ("yh", "core")


def shift(value, axis, step, size):
    return lax.ppermute(value, axis, [(i, (i + step) % size) for i in range(size)])


def swap(value):
    return shift(value, "core", 1, 2)


def by_core(value, core):
    return jnp.where(core == 0, value, value[::-1])


def gather_yh(hidden, yh, n_yh):
    half = hidden.shape[0] // 2
    low, high = hidden[:half], hidden[half:]
    up_low = shift(low, "yh", 1, n_yh)
    down_high = shift(high, "yh", -1, n_yh)
    up_high = shift(high, "yh", 1, n_yh)
    down_low = shift(low, "yh", -1, n_yh)
    far_low = shift(up_low, "yh", 1, n_yh)
    far_high = shift(down_high, "yh", -1, n_yh)
    out = jnp.zeros((n_yh, 2, half, hidden.shape[1]), hidden.dtype)
    out = lax.dynamic_update_slice(out, hidden.reshape(1, 2, half, -1), (yh, 0, 0, 0))
    before, after, far = (yh - 1) % n_yh, (yh + 1) % n_yh, (yh + 2) % n_yh
    for piece, owner, part in (
        (up_low, before, 0),
        (down_high, after, 1),
        (up_high, before, 1),
        (down_low, after, 0),
        (far_low, far, 0),
        (far_high, far, 1),
    ):
        out = lax.dynamic_update_slice(out, piece[None, None], (owner, part, 0, 0))
    return out.reshape(n_yh * 2 * half, -1)


def per_device(hidden, targets, token_weight, head_weight, *, n_yh, n_dp):
    yh, core = lax.axis_index("yh"), lax.axis_index("core")
    tok, width = hidden.shape
    v_dev = head_weight.shape[0]
    n_own = n_yh * tok
    rows_t, rows_v = (((1,), (1,)), ((), ())), (((0,), (0,)), ((), ()))
    labels = by_core(targets.reshape(n_yh, 2, tok).transpose(1, 0, 2), core).reshape(2, n_own)
    weights = by_core(token_weight.reshape(n_yh, 2, tok).transpose(1, 0, 2), core).reshape(2, n_own)

    own = gather_yh(hidden, yh, n_yh)
    gathered = (own, swap(own))

    columns = (yh * 2 + core) * v_dev + lax.broadcasted_iota(jnp.int32, (1, v_dev), 1)
    logits, hits, stats = [], [], []
    for k in range(2):
        part = lax.dot_general(gathered[k], head_weight, rows_t, preferred_element_type=F32)
        hit = columns == labels[k][:, None]
        top = jnp.max(part, axis=1)
        total = jnp.sum(jnp.exp(part - top[:, None]), axis=1)
        target = jnp.sum(jnp.where(hit, part, jnp.zeros_like(part)), axis=1)
        logits.append(part)
        hits.append(hit)
        stats.append(jnp.stack([top, total, target]))
    stats = by_core(jnp.stack(stats), core)
    stats = lax.all_to_all(jnp.broadcast_to(stats, (2 * n_yh,) + stats.shape), VOCAB, 0, 0, tiled=True)
    top = jnp.max(stats[:, :, 0], axis=0)
    log_total = top + jnp.log(jnp.sum(stats[:, :, 1] * jnp.exp(stats[:, :, 0] - top), axis=0))
    loss = by_core(log_total - jnp.sum(stats[:, :, 2], axis=0), core)[0]
    token_loss = lax.dynamic_slice_in_dim(loss, yh * tok, tok)
    log_total = by_core(log_total, core)

    score = [
        (weights[k][:, None] * (jnp.exp(logits[k] - log_total[k][:, None]) - hits[k].astype(F32))).astype(BF16)
        for k in range(2)
    ]

    away = jnp.dot(score[1], head_weight, preferred_element_type=F32).astype(BF16)
    home = jnp.dot(score[0], head_weight, preferred_element_type=F32).astype(BF16)
    terms = (home.astype(F32) + swap(away).astype(F32)).astype(BF16).reshape(n_yh, tok, width)

    partial = sum(lax.dot_general(score[k], gathered[k], rows_v, preferred_element_type=F32) for k in range(2))
    rows, cols = v_dev // 4, width * 4 // n_dp
    chunks = partial.astype(BF16).reshape(4, rows, n_dp // 4, cols).transpose(0, 2, 1, 3).reshape(n_dp, rows, cols)
    chunks, terms = lax.optimization_barrier((chunks, terms))
    chunks = lax.all_to_all(chunks, DP, 0, 0, tiled=True)

    grad_hidden = lax.dynamic_index_in_dim(terms, yh, 0, False).astype(F32)
    for s in (1, -1, 2):
        there = lax.dynamic_index_in_dim(terms, (yh + s) % n_yh, 0, False)
        grad_hidden = grad_hidden + shift(there, "yh", s, n_yh).astype(F32)
    grad_hidden = grad_hidden.astype(BF16)

    chunk = jnp.sum(chunks.astype(F32), axis=0).astype(BF16)
    chunks = lax.all_to_all(jnp.broadcast_to(chunk, (n_dp, rows, cols)), DP, 0, 0, tiled=True)
    grad_weight = chunks.reshape(4, n_dp // 4, rows, cols).transpose(0, 2, 1, 3).reshape(v_dev, width)
    return token_loss, grad_hidden, grad_weight


def fine(mesh_devices, sizes):
    mesh = Mesh(mesh_devices.reshape(sizes), ("x", "yl", "z", "yh", "core"))

    def body(*args):
        return per_device(*args, n_yh=sizes[3], n_dp=sizes[0] * sizes[1] * sizes[2])

    tokens = ("x", "yl", "z", "yh", "core")
    return jax.shard_map(
        body,
        mesh=mesh,
        in_specs=(P(tokens, None), P(DP), P(DP), P(VOCAB, None)),
        out_specs=(P(tokens), P(tokens, None), P(VOCAB, None)),
        check_vma=False,
    )


def solution(mesh):
    return fine(mesh.devices, (4, 2, 8, 4, 2))
```

time: 215 us -> 221 us (1.028)
  the two profiles are of different devices: /device:TPU:16 before, /device:TPU:126 now
where the time goes in v2:
time: 221 us; the launch traced here: 220 us
  waiting for transfers between devices  64.9 us (29%)
  starting transfers between devices  60.8 us (28%)
  blocking collectives  57.3 us (26%)
  local copies, waits for them, and re-layouts  17.4 us (8%)
  matrix products  15.3 us (7%)
  other arithmetic  3.66 us (2%)
    ppermute x11, waiting for transfers between devices, shift(): lax.ppermute(value, axis, [(i, (i + step) % size) for i in range(size)])  60.7 us
    all_to_all x1, blocking collectives, per_device(): chunks = lax.all_to_all(chunks, DP, 0, 0, tiled=True)  57.3 us
    ppermute x11, starting transfers between devices, shift(): lax.ppermute(value, axis, [(i, (i + step) % size) for i in range(size)])  38.3 us
    all_to_all x1, starting transfers between devices, per_device(): lax.all_to_all(jnp.broadcast_to(stats, (2 * n_yh,) + stats.shape), VOCAB,...  13.5 us
    all_to_all x1, starting transfers between devices, per_device(): lax.all_to_all(jnp.broadcast_to(chunk, (n_dp, rows, cols)), DP, 0, 0, til...  8.99 us
    dot_general x2, matrix products, per_device(): lax.dot_general(gathered[k], head_weight, rows_t, preferred_element_type=...  4.9 us
    dot_general x2, matrix products, per_device(): lax.dot_general(score[k], gathered[k], rows_v, preferred_element_type=F32)  4.46 us
  transfers between devices with their start and end apart: 13, of which 7 were waited for; matrix products, arithmetic and copies ran while one was open for 9% of the time, Pallas kernels for 0%

profile of v2, /device:TPU:126, one launch (start us, length us, event | category | flops | bytes accessed | tf_op | source)
XLA Modules:
  0.0 220.3 jit_solution(10645313953588744649)
XLA Ops:
  0.7 1.9 fusion.25
  2.6 2.7 %collective-permute-start.2 = (bf16[32,4096]{1,0:T(8,128)(2,1)}, bf16[32,4096]{1,0:T(8,128)(2,1)S(1)}, u32[]{:S(2)}, u32[]{:S(2)}) collective-permute-start(bf16[32,4096]{1,0:T(8,128)(2,1)} %get-tuple-element.20), channel_id=1, source_target_pairs={{0,2},{2,4},{4,6},{6,0},{1,3},{3,5},{5,7},{7,1},{8,10},{10,12},{12... | collective-permute-start | bytes 786440 | tf_op jit(solution)/shard_map/ppermute | solution.py:13
  5.3 4.1 %collective-permute-start.1 = (bf16[32,4096]{1,0:T(8,128)(2,1)}, bf16[32,4096]{1,0:T(8,128)(2,1)S(1)}, u32[]{:S(2)}, u32[]{:S(2)}) collective-permute-start(bf16[32,4096]{1,0:T(8,128)(2,1)} %get-tuple-element.20), channel_id=1, source_target_pairs={{0,6},{2,0},{4,2},{6,4},{1,7},{3,1},{5,3},{7,5},{8,14},{10,8},{12,... | collective-permute-start | bytes 786440 | tf_op jit(solution)/shard_map/ppermute | solution.py:13
  9.3 5.3 %collective-permute-start.3 = (bf16[32,4096]{1,0:T(8,128)(2,1)S(1)}, bf16[32,4096]{1,0:T(8,128)(2,1)S(1)}, u32[]{:S(2)}, u32[]{:S(2)}) collective-permute-start(bf16[32,4096]{1,0:T(8,128)(2,1)S(1)} %get-tuple-element.21), channel_id=1, source_target_pairs={{0,6},{2,0},{4,2},{6,4},{1,7},{3,1},{5,3},{7,5},{8,14},{10,8},{12,... | collective-permute-start | bytes 786440 | tf_op jit(solution)/shard_map/ppermute | solution.py:13
  14.6 2.7 %collective-permute-start = (bf16[32,4096]{1,0:T(8,128)(2,1)S(1)}, bf16[32,4096]{1,0:T(8,128)(2,1)S(1)}, u32[]{:S(2)}, u32[]{:S(2)}) collective-permute-start(bf16[32,4096]{1,0:T(8,128)(2,1)S(1)} %get-tuple-element.21), channel_id=1, source_target_pairs={{0,2},{2,4},{4,6},{6,0},{1,3},{3,5},{5,7},{7,1},{8,10},{10,12},{12... | collective-permute-start | bytes 786440 | tf_op jit(solution)/shard_map/ppermute | solution.py:13
  17.3 1.6 broadcast_in_dim.30
  19.8 4.0 %collective-permute-start.5 = (bf16[32,4096]{1,0:T(8,128)(2,1)S(1)}, bf16[32,4096]{1,0:T(8,128)(2,1)S(1)}, u32[]{:S(2)}, u32[]{:S(2)}) collective-permute-start(bf16[32,4096]{1,0:T(8,128)(2,1)S(1)} %collective-permute-done.1), channel_id=1, source_target_pairs={{0,6},{2,0},{4,2},{6,4},{1,7},{3,1},{5,3},{7,5},{8,14},{10,8},{12,... | collective-permute-start | bytes 786440 | tf_op jit(solution)/shard_map/ppermute | solution.py:13
  23.8 1.9 collective-permute-done
  25.7 3.5 %collective-permute-start.4 = (bf16[32,4096]{1,0:T(8,128)(2,1)S(1)}, bf16[32,4096]{1,0:T(8,128)(2,1)S(1)}, u32[]{:S(2)}, u32[]{:S(2)}) collective-permute-start(bf16[32,4096]{1,0:T(8,128)(2,1)S(1)} %collective-permute-done), channel_id=1, source_target_pairs={{0,2},{2,4},{4,6},{6,0},{1,3},{3,5},{5,7},{7,1},{8,10},{10,12},{12... | collective-permute-start | bytes 786440 | tf_op jit(solution)/shard_map/ppermute | solution.py:13
  32.1 5.6 %collective-permute-done.4 = bf16[32,4096]{1,0:T(8,128)(2,1)S(1)} collective-permute-done((bf16[32,4096]{1,0:T(8,128)(2,1)S(1)}, bf16[32,4096]{1,0:T(8,128)(2,1)S(1)}, u32[]{:S(2)}, u32[]{:S(2)}) %collective-permute-start.4) | collective-permute-done | bytes 262176 | tf_op jit(solution)/shard_map/ppermute | solution.py:13
  39.2 1.9 collective-permute-start.6
  41.6 2.4 %fusion.28 = (f32[256]{0:T(256)S(1)}, f32[256,192]{0,1:T(8,128)S(1)}) fusion(bf16[256,4096]{1,0:T(8,128)(2,1)} %bitcast.7, bf16[192,4096]{1,0:T(8,128)(2,1)S(1)} %copy-done), kind=kOutput, calls=%fused_computation.63 | convolution fusion | flops 402702080 | bytes 3867648 | tf_op jit(solution)/shard_map/dot_general | solution.py:63
  44.0 1.5 collective-permute-done.6
  45.6 2.4 %fusion.29 = (f32[256]{0:T(256)S(1)}, f32[256,192]{0,1:T(8,128)S(1)}) fusion(bf16[256,4096]{1,0:T(8,128)(2,1)} %collective-permute-done.6, bf16[192,4096]{1,0:T(8,128)(2,1)S(1)} %copy-done), kind=kOutput, calls=%fused_computation.64 | convolution fusion | flops 402702080 | bytes 3867648 | tf_op jit(solution)/shard_map/dot_general | solution.py:63
  49.0 13.5 %all-to-all-start = ((f32[8,2,3,256]{3,1,2,0:T(2,128)}), f32[8,2,3,256]{3,1,2,0:T(2,128)S(1)}, u32[]{:S(2)}, u32[]{:S(2)}) async-start(f32[8,2,3,256]{3,1,2,0:T(2,128)} %broadcast_in_dim.37), calls=%async_computation | async-start | bytes 98304 | tf_op jit(solution)/shard_map/all_to_all | solution.py:72
  62.6 4.3 %all-to-all-done = f32[8,2,3,256]{3,1,2,0:T(2,128)S(1)} async-done(((f32[8,2,3,256]{3,1,2,0:T(2,128)}), f32[8,2,3,256]{3,1,2,0:T(2,128)S(1)}, u32[]{:S(2)}, u32[]{:S(2)}) %all-to-all-start) | async-done | bytes 49184 | tf_op jit(solution)/shard_map/all_to_all | solution.py:72
  67.1 2.2 convolution_convert_fusion
  69.2 1.9 collective-permute-start.7
  71.2 2.2 fusion.18
  73.4 2.3 %fusion.1 = bf16[192,4096]{1,0:T(8,128)(2,1)S(1)} fusion(f32[192,4096]{1,0:T(8,128)S(1)} %fusion.18, bf16[256,4096]{1,0:T(8,128)(2,1)} %bitcast.7, f32[256,192]{0,1:T(8,128)S(1)} %get-tuple-element.29, f32[256]{0:T(256)S(1)} %bitcast.88, f32[256]{0:T(256)S(1)} %mul.36, s32[256]{0:T(256)S(1)} %eq.44, s32[192]{0:T(256)S(1)} %iota_add_fusion), kind=kOutput, calls=%fused_computation.4 | convolution fusion | flops 404520960 | bytes 7016192 | tf_op jit(solution)/shard_map/dot_general | solution.py:88
  76.8 3.8 %add_convert_fusion = bf16[256,4096]{1,0:T(8,128)(2,1)} fusion(bf16[256,4096]{1,0:T(8,128)(2,1)} %collective-permute-done.7, bf16[192,4096]{1,0:T(8,128)(2,1)S(1)} %copy-done, f32[256,192]{0,1:T(8,128)S(1)} %get-tuple-element.29, f32[256]{0:T(256)S(1)} %bitcast.89, f32[256]{0:T(256)S(1)} %mul.36, s32[256]{0:T(256)S(1)} %eq.44, s32[192]{0:T(256)S(1)} %iota_add_fusion), kind=kOutput, calls=%fused_computation.5 | convolution fusion | flops 408190976 | bytes 5967616 | tf_op jit(solution)/shard_map/dot_general | solution.py:85
  80.5 57.3 %all_to_all.15 = bf16[64,48,256]{2,1,0:T(8,128)(2,1)S(1)} all-to-all(bf16[64,48,256]{2,1,0:T(8,128)(2,1)S(1)} %bitcast.76), channel_id=1, replica_groups=mesh['x'=4,'yl'=2,'z'=8,'yh'=4,'core'=2] {'x','yl','z'}, dimensions={0} | all-to-all | bytes 3145728 | tf_op jit(solution)/shard_map/all_to_all | solution.py:92
  139.3 9.0 %all-to-all-start.2 = ((bf16[64,48,256]{2,1,0:T(8,128)(2,1)}), bf16[64,48,256]{2,1,0:T(8,128)(2,1)S(1)}, u32[]{:S(2)}, u32[]{:S(2)}) async-start(bf16[64,48,256]{2,1,0:T(8,128)(2,1)} %broadcast_in_dim.38), calls=%async_computation.2 | async-start | bytes 3145728 | tf_op jit(solution)/shard_map/all_to_all | solution.py:101
  148.3 2.5 %dynamic-slice_bitcast_fusion.2 = (bf16[64,4096]{1,0:T(8,128)(2,1)}, bf16[64,4096]{1,0:T(8,128)(2,1)}, bf16[64,4096]{1,0:T(8,128)(2,1)}) fusion(bf16[4,64,4096]{2,1,0:T(8,128)(2,1)} %bitcast.73, s32[]{:T(128)S(6)} %select_n.91, s32[]{:T(128)S(6)} %select_n.93, s32[]{:T(128)S(6)} %select_n.89), kind=kLoop, calls=%fused_computation.12 | loop fusion | bytes 3145740 | tf_op jit(solution)/shard_map/jit(dynamic_index_in_dim)/squeeze | solution.py:96
  150.8 5.6 %collective-permute-start.8 = (bf16[64,4096]{1,0:T(8,128)(2,1)}, bf16[64,4096]{1,0:T(8,128)(2,1)}, u32[]{:S(2)}, u32[]{:S(2)}) collective-permute-start(bf16[64,4096]{1,0:T(8,128)(2,1)} %get-tuple-element.17), channel_id=1, source_target_pairs={{0,2},{2,4},{4,6},{6,0},{1,3},{3,5},{5,7},{7,1},{8,10},{10,12},{12... | collective-permute-start | bytes 1572872 | tf_op jit(solution)/shard_map/ppermute | solution.py:13
  156.5 2.3 %collective-permute-start.10 = (bf16[64,4096]{1,0:T(8,128)(2,1)}, bf16[64,4096]{1,0:T(8,128)(2,1)}, u32[]{:S(2)}, u32[]{:S(2)}) collective-permute-start(bf16[64,4096]{1,0:T(8,128)(2,1)} %get-tuple-element.18), channel_id=1, source_target_pairs={{0,4},{2,6},{4,0},{6,2},{1,5},{3,7},{5,1},{7,3},{8,12},{10,14},{12... | collective-permute-start | bytes 1572872 | tf_op jit(solution)/shard_map/ppermute | solution.py:13
  158.7 4.4 %collective-permute-start.9 = (bf16[64,4096]{1,0:T(8,128)(2,1)}, bf16[64,4096]{1,0:T(8,128)(2,1)}, u32[]{:S(2)}, u32[]{:S(2)}) collective-permute-start(bf16[64,4096]{1,0:T(8,128)(2,1)} %get-tuple-element.19), channel_id=1, source_target_pairs={{0,6},{2,0},{4,2},{6,4},{1,7},{3,1},{5,3},{7,5},{8,14},{10,8},{12,... | collective-permute-start | bytes 1572872 | tf_op jit(solution)/shard_map/ppermute | solution.py:13
  163.7 3.9 %collective-permute-done.8 = bf16[64,4096]{1,0:T(8,128)(2,1)} collective-permute-done((bf16[64,4096]{1,0:T(8,128)(2,1)}, bf16[64,4096]{1,0:T(8,128)(2,1)}, u32[]{:S(2)}, u32[]{:S(2)}) %collective-permute-start.8) | collective-permute-done | bytes 524320 | tf_op jit(solution)/shard_map/ppermute | solution.py:13
  167.6 37.6 %collective-permute-done.10 = bf16[64,4096]{1,0:T(8,128)(2,1)} collective-permute-done((bf16[64,4096]{1,0:T(8,128)(2,1)}, bf16[64,4096]{1,0:T(8,128)(2,1)}, u32[]{:S(2)}, u32[]{:S(2)}) %collective-permute-start.10) | collective-permute-done | bytes 524320 | tf_op jit(solution)/shard_map/ppermute | solution.py:13
  205.3 10.0 %collective-permute-done.9 = bf16[64,4096]{1,0:T(8,128)(2,1)} collective-permute-done((bf16[64,4096]{1,0:T(8,128)(2,1)}, bf16[64,4096]{1,0:T(8,128)(2,1)}, u32[]{:S(2)}, u32[]{:S(2)}) %collective-permute-start.9) | collective-permute-done | bytes 524320 | tf_op jit(solution)/shard_map/ppermute | solution.py:13
  215.3 2.6 %fusion.4 = bf16[64,4096]{1,0:T(8,128)(2,1)} fusion(bf16[64,4096]{1,0:T(8,128)(2,1)} %collective-permute-done.10, bf16[64,4096]{1,0:T(8,128)(2,1)} %collective-permute-done.9, bf16[64,4096]{1,0:T(8,128)(2,1)} %collective-permute-done.8, bf16[4,64,4096]{2,1,0:T(8,128)(2,1)} %bitcast.74, s32[]{:T(128)S(6)} %select_n.87), kind=kLoop, calls=%fused_computation.9 | loop fusion | flops 2097152 | bytes 2621444 | tf_op jit(solution)/shard_map/convert_element_type | solution.py:98
  218.4 1.8 copy.18
  (57 shorter events, 10.6 us)
Async XLA Ops:
  0.6 40.9 %copy-start = (bf16[192,4096]{1,0:T(8,128)(2,1)S(1)}, bf16[192,4096]{1,0:T(8,128)(2,1)}, u32[]{:S(2)}) copy-start(bf16[192,4096]{1,0:T(8,128)(2,1)} %param.7) | copy-start | bytes 4718596
  0.6 18.3 %copy-start.1 = (bf16[64,4096]{1,0:T(8,128)(2,1)S(1)}, bf16[64,4096]{1,0:T(8,128)(2,1)}, u32[]{:S(2)}) copy-start(bf16[64,4096]{1,0:T(8,128)(2,1)} %param.4) | copy-start | bytes 1572868
  2.6 28.1 %collective-permute-start.2 = (bf16[32,4096]{1,0:T(8,128)(2,1)}, bf16[32,4096]{1,0:T(8,128)(2,1)S(1)}, u32[]{:S(2)}, u32[]{:S(2)}) collective-permute-start(bf16[32,4096]{1,0:T(8,128)(2,1)} %get-tuple-element.20), channel_id=1, source_target_pairs={{0,2},{2,4},{4,6},{6,0},{1,3},{3,5},{5,7},{7,1},{8,10},{10,12},{12... | collective-permute-start | bytes 786440 | tf_op jit(solution)/shard_map/ppermute | solution.py:13
  5.3 14.5 %collective-permute-start.1 = (bf16[32,4096]{1,0:T(8,128)(2,1)}, bf16[32,4096]{1,0:T(8,128)(2,1)S(1)}, u32[]{:S(2)}, u32[]{:S(2)}) collective-permute-start(bf16[32,4096]{1,0:T(8,128)(2,1)} %get-tuple-element.20), channel_id=1, source_target_pairs={{0,6},{2,0},{4,2},{6,4},{1,7},{3,1},{5,3},{7,5},{8,14},{10,8},{12,... | collective-permute-start | bytes 786440 | tf_op jit(solution)/shard_map/ppermute | solution.py:13
  9.3 22.1 %collective-permute-start.3 = (bf16[32,4096]{1,0:T(8,128)(2,1)S(1)}, bf16[32,4096]{1,0:T(8,128)(2,1)S(1)}, u32[]{:S(2)}, u32[]{:S(2)}) collective-permute-start(bf16[32,4096]{1,0:T(8,128)(2,1)S(1)} %get-tuple-element.21), channel_id=1, source_target_pairs={{0,6},{2,0},{4,2},{6,4},{1,7},{3,1},{5,3},{7,5},{8,14},{10,8},{12,... | collective-permute-start | bytes 786440 | tf_op jit(solution)/shard_map/ppermute | solution.py:13
  14.6 11.2 %collective-permute-start = (bf16[32,4096]{1,0:T(8,128)(2,1)S(1)}, bf16[32,4096]{1,0:T(8,128)(2,1)S(1)}, u32[]{:S(2)}, u32[]{:S(2)}) collective-permute-start(bf16[32,4096]{1,0:T(8,128)(2,1)S(1)} %get-tuple-element.21), channel_id=1, source_target_pairs={{0,2},{2,4},{4,6},{6,0},{1,3},{3,5},{5,7},{7,1},{8,10},{10,12},{12... | collective-permute-start | bytes 786440 | tf_op jit(solution)/shard_map/ppermute | solution.py:13
  18.9 22.2 %copy-start.2 = (s32[512]{0:T(512)S(1)}, s32[512]{0:T(512)}, u32[]{:S(2)}) copy-start(s32[512]{0:T(512)} %param.5) | copy-start | bytes 6148
  18.9 22.3 %copy-start.3 = (f32[512]{0:T(512)S(1)}, f32[512]{0:T(512)}, u32[]{:S(2)}) copy-start(f32[512]{0:T(512)} %param.6) | copy-start | bytes 6148
  19.8 18.7 %collective-permute-start.5 = (bf16[32,4096]{1,0:T(8,128)(2,1)S(1)}, bf16[32,4096]{1,0:T(8,128)(2,1)S(1)}, u32[]{:S(2)}, u32[]{:S(2)}) collective-permute-start(bf16[32,4096]{1,0:T(8,128)(2,1)S(1)} %collective-permute-done.1), channel_id=1, source_target_pairs={{0,6},{2,0},{4,2},{6,4},{1,7},{3,1},{5,3},{7,5},{8,14},{10,8},{12,... | collective-permute-start | bytes 786440 | tf_op jit(solution)/shard_map/ppermute | solution.py:13
  25.7 12.0 %collective-permute-start.4 = (bf16[32,4096]{1,0:T(8,128)(2,1)S(1)}, bf16[32,4096]{1,0:T(8,128)(2,1)S(1)}, u32[]{:S(2)}, u32[]{:S(2)}) collective-permute-start(bf16[32,4096]{1,0:T(8,128)(2,1)S(1)} %collective-permute-done), channel_id=1, source_target_pairs={{0,2},{2,4},{4,6},{6,0},{1,3},{3,5},{5,7},{7,1},{8,10},{10,12},{12... | collective-permute-start | bytes 786440 | tf_op jit(solution)/shard_map/ppermute | solution.py:13
  39.2 6.4 %collective-permute-start.6 = (bf16[256,4096]{1,0:T(8,128)(2,1)}, bf16[256,4096]{1,0:T(8,128)(2,1)}, u32[]{:S(2)}, u32[]{:S(2)}) collective-permute-start(bf16[256,4096]{1,0:T(8,128)(2,1)} %bitcast.7), channel_id=1, source_target_pairs={{0,1},{1,0},{2,3},{3,2},{4,5},{5,4},{6,7},{7,6},{8,9},{9,8},{10,11... | collective-permute-start | bytes 6291464 | tf_op jit(solution)/shard_map/ppermute | solution.py:13
  49.0 17.9 %all-to-all-start = ((f32[8,2,3,256]{3,1,2,0:T(2,128)}), f32[8,2,3,256]{3,1,2,0:T(2,128)S(1)}, u32[]{:S(2)}, u32[]{:S(2)}) async-start(f32[8,2,3,256]{3,1,2,0:T(2,128)} %broadcast_in_dim.37), calls=%async_computation | async-start | bytes 98304 | tf_op jit(solution)/shard_map/all_to_all | solution.py:72
  69.2 7.5 %collective-permute-start.7 = (bf16[256,4096]{1,0:T(8,128)(2,1)}, bf16[256,4096]{1,0:T(8,128)(2,1)}, u32[]{:S(2)}, u32[]{:S(2)}) collective-permute-start(bf16[256,4096]{1,0:T(8,128)(2,1)} %convolution_convert_fusion), channel_id=1, source_target_pairs={{0,1},{1,0},{2,3},{3,2},{4,5},{5,4},{6,7},{7,6},{8,9},{9,8},{10,11... | collective-permute-start | bytes 6291464 | tf_op jit(solution)/shard_map/ppermute | solution.py:13
  139.3 78.6 %all-to-all-start.2 = ((bf16[64,48,256]{2,1,0:T(8,128)(2,1)}), bf16[64,48,256]{2,1,0:T(8,128)(2,1)S(1)}, u32[]{:S(2)}, u32[]{:S(2)}) async-start(bf16[64,48,256]{2,1,0:T(8,128)(2,1)} %broadcast_in_dim.38), calls=%async_computation.2 | async-start | bytes 3145728 | tf_op jit(solution)/shard_map/all_to_all | solution.py:101
  150.8 16.8 %collective-permute-start.8 = (bf16[64,4096]{1,0:T(8,128)(2,1)}, bf16[64,4096]{1,0:T(8,128)(2,1)}, u32[]{:S(2)}, u32[]{:S(2)}) collective-permute-start(bf16[64,4096]{1,0:T(8,128)(2,1)} %get-tuple-element.17), channel_id=1, source_target_pairs={{0,2},{2,4},{4,6},{6,0},{1,3},{3,5},{5,7},{7,1},{8,10},{10,12},{12... | collective-permute-start | bytes 1572872 | tf_op jit(solution)/shard_map/ppermute | solution.py:13
  156.5 48.8 %collective-permute-start.10 = (bf16[64,4096]{1,0:T(8,128)(2,1)}, bf16[64,4096]{1,0:T(8,128)(2,1)}, u32[]{:S(2)}, u32[]{:S(2)}) collective-permute-start(bf16[64,4096]{1,0:T(8,128)(2,1)} %get-tuple-element.18), channel_id=1, source_target_pairs={{0,4},{2,6},{4,0},{6,2},{1,5},{3,7},{5,1},{7,3},{8,12},{10,14},{12... | collective-permute-start | bytes 1572872 | tf_op jit(solution)/shard_map/ppermute | solution.py:13
  158.7 56.6 %collective-permute-start.9 = (bf16[64,4096]{1,0:T(8,128)(2,1)}, bf16[64,4096]{1,0:T(8,128)(2,1)}, u32[]{:S(2)}, u32[]{:S(2)}) collective-permute-start(bf16[64,4096]{1,0:T(8,128)(2,1)} %get-tuple-element.19), channel_id=1, source_target_pairs={{0,6},{2,0},{4,2},{6,4},{1,7},{3,1},{5,3},{7,5},{8,14},{10,8},{12,... | collective-permute-start | bytes 1572872 | tf_op jit(solution)/shard_map/ppermute | solution.py:13

commit v3 on v2

--- a/solution.py
+++ b/solution.py
@@ -45,7 +45,7 @@
     return out.reshape(n_yh * 2 * half, -1)
 
 
-def per_device(hidden, targets, token_weight, head_weight, *, n_yh, n_dp):
+def per_device(hidden, targets, token_weight, head_weight, *, n_x, n_yl, n_z, n_yh):
     yh, core = lax.axis_index("yh"), lax.axis_index("core")
     tok, width = hidden.shape
     v_dev = head_weight.shape[0]
@@ -86,20 +86,27 @@
     terms = (home.astype(F32) + swap(away).astype(F32)).astype(BF16).reshape(n_yh, tok, width)
 
     partial = sum(lax.dot_general(score[k], gathered[k], rows_v, preferred_element_type=F32) for k in range(2))
-    rows, cols = v_dev // 4, width * 4 // n_dp
-    chunks = partial.astype(BF16).reshape(4, rows, n_dp // 4, cols).transpose(0, 2, 1, 3).reshape(n_dp, rows, cols)
-    chunks, terms = lax.optimization_barrier((chunks, terms))
-    chunks = lax.all_to_all(chunks, DP, 0, 0, tiled=True)
+    part = partial.astype(BF16).reshape(n_x, v_dev // n_x, width)
+    part = lax.all_to_all(part, "x", 0, 0, tiled=True)
+    part = jnp.sum(part.astype(F32), axis=0).astype(BF16)
+    part = part.reshape(v_dev // n_x, n_yl * n_z, -1).transpose(1, 0, 2)
+    block = lambda s: lax.dynamic_index_in_dim(terms, (yh + s) % n_yh, 0, False)
+    half, far = tok // 2, block(2)
+    from_below = shift(far[:half], "yh", 1, n_yh)
+    from_above = shift(far[half:], "yh", -1, n_yh)
+    part, from_below, from_above = lax.optimization_barrier((part, from_below, from_above))
+    zero = jnp.zeros((half, width), F32)
+    up = block(1).astype(F32) + jnp.concatenate([from_below.astype(F32), zero], 0)
+    down = block(-1).astype(F32) + jnp.concatenate([zero, from_above.astype(F32)], 0)
+    came = [shift(up.astype(BF16), "yh", 1, n_yh), shift(down.astype(BF16), "yh", -1, n_yh)]
 
-    grad_hidden = lax.dynamic_index_in_dim(terms, yh, 0, False).astype(F32)
-    for s in (1, -1, 2):
-        there = lax.dynamic_index_in_dim(terms, (yh + s) % n_yh, 0, False)
-        grad_hidden = grad_hidden + shift(there, "yh", s, n_yh).astype(F32)
-    grad_hidden = grad_hidden.astype(BF16)
-
-    chunk = jnp.sum(chunks.astype(F32), axis=0).astype(BF16)
-    chunks = lax.all_to_all(jnp.broadcast_to(chunk, (n_dp, rows, cols)), DP, 0, 0, tiled=True)
-    grad_weight = chunks.reshape(4, n_dp // 4, rows, cols).transpose(0, 2, 1, 3).reshape(v_dev, width)
+    part = lax.all_to_all(part, ("yl", "z"), 0, 0, tiled=True)
+    part = jnp.sum(part.astype(F32), axis=0).astype(BF16)
+    part = lax.all_to_all(jnp.broadcast_to(part, (n_yl * n_z,) + part.shape), ("yl", "z"), 0, 0, tiled=True)
+    part = part.transpose(1, 0, 2).reshape(v_dev // n_x, width)
+    part = lax.all_to_all(jnp.broadcast_to(part, (n_x,) + part.shape), "x", 0, 0, tiled=True)
+    grad_hidden = (block(0).astype(F32) + sum(v.astype(F32) for v in came)).astype(BF16)
+    grad_weight = part.reshape(v_dev, width)
     return token_loss, grad_hidden, grad_weight
 
 
@@ -107,7 +114,7 @@
     mesh = Mesh(mesh_devices.reshape(sizes), ("x", "yl", "z", "yh", "core"))
 
     def body(*args):
-        return per_device(*args, n_yh=sizes[3], n_dp=sizes[0] * sizes[1] * sizes[2])
+        return per_device(*args, n_x=sizes[0], n_yl=sizes[1], n_z=sizes[2], n_yh=sizes[3])
 
     tokens = ("x", "yl", "z", "yh", "core")
     return jax.shard_map(

time: 221 us -> 181 us (0.82)
  the two profiles are of different devices: /device:TPU:126 before, /device:TPU:72 now
where the time goes in v3:
time: 181 us; the launch traced here: 180 us
  starting transfers between devices  65.8 us (36%)
  waiting for transfers between devices  47.6 us (26%)
  blocking collectives  28.4 us (16%)
  local copies, waits for them, and re-layouts  15.8 us (9%)
  matrix products  15.1 us (8%)
  other arithmetic  6.01 us (3%)
    ppermute x12, starting transfers between devices, shift(): lax.ppermute(value, axis, [(i, (i + step) % size) for i in range(size)])  41.7 us
    all_to_all x1, blocking collectives, per_device(): part = lax.all_to_all(part, ('yl', 'z'), 0, 0, tiled=True)  28.4 us
    ppermute x12, waiting for transfers between devices, shift(): lax.ppermute(value, axis, [(i, (i + step) % size) for i in range(size)])  21.9 us
    all_to_all x1, starting transfers between devices, per_device(): lax.all_to_all(jnp.broadcast_to(stats, (2 * n_yh,) + stats.shape), VOCAB,...  11.6 us
    all_to_all x1, waiting for transfers between devices, per_device(): part = lax.all_to_all(part, 'x', 0, 0, tiled=True)  10 us
    all_to_all x1, waiting for transfers between devices, per_device(): lax.all_to_all(jnp.broadcast_to(stats, (2 * n_yh,) + stats.shape), VOCAB,...  7.96 us
    dot_general x2, matrix products, per_device(): lax.dot_general(score[k], gathered[k], rows_v, preferred_element_type=F32)  5.61 us
    all_to_all x1, waiting for transfers between devices, per_device(): lax.all_to_all(jnp.broadcast_to(part, (n_x,) + part.shape), 'x', 0, 0, ti...  5.17 us
  transfers between devices with their start and end apart: 16, of which 10 were waited for; matrix products, arithmetic and copies ran while one was open for 14% of the time, Pallas kernels for 0%

profile of v3, /device:TPU:72, one launch (start us, length us, event | category | flops | bytes accessed | tf_op | source)
XLA Modules:
  0.0 179.7 jit_solution(16019213206728260200)
XLA Ops:
  0.7 1.9 %fusion.25 = (bf16[32,4096]{1,0:T(8,128)(2,1)}, bf16[32,4096]{1,0:T(8,128)(2,1)S(1)}) fusion(bf16[64,4096]{1,0:T(8,128)(2,1)} %param.4), kind=kLoop, calls=%fused_computation.61 | loop fusion | bytes 1048576 | tf_op jit(solution)/shard_map/slice | solution.py:26
  2.6 4.5 %collective-permute-start.2 = (bf16[32,4096]{1,0:T(8,128)(2,1)}, bf16[32,4096]{1,0:T(8,128)(2,1)S(1)}, u32[]{:S(2)}, u32[]{:S(2)}) collective-permute-start(bf16[32,4096]{1,0:T(8,128)(2,1)} %get-tuple-element.23), channel_id=1, source_target_pairs={{0,2},{2,4},{4,6},{6,0},{1,3},{3,5},{5,7},{7,1},{8,10},{10,12},{12... | collective-permute-start | bytes 786440 | tf_op jit(solution)/shard_map/ppermute | solution.py:13
  7.1 3.5 %collective-permute-start.1 = (bf16[32,4096]{1,0:T(8,128)(2,1)}, bf16[32,4096]{1,0:T(8,128)(2,1)S(1)}, u32[]{:S(2)}, u32[]{:S(2)}) collective-permute-start(bf16[32,4096]{1,0:T(8,128)(2,1)} %get-tuple-element.23), channel_id=1, source_target_pairs={{0,6},{2,0},{4,2},{6,4},{1,7},{3,1},{5,3},{7,5},{8,14},{10,8},{12,... | collective-permute-start | bytes 786440 | tf_op jit(solution)/shard_map/ppermute | solution.py:13
  10.5 4.1 %collective-permute-start.3 = (bf16[32,4096]{1,0:T(8,128)(2,1)S(1)}, bf16[32,4096]{1,0:T(8,128)(2,1)S(1)}, u32[]{:S(2)}, u32[]{:S(2)}) collective-permute-start(bf16[32,4096]{1,0:T(8,128)(2,1)S(1)} %get-tuple-element.24), channel_id=1, source_target_pairs={{0,6},{2,0},{4,2},{6,4},{1,7},{3,1},{5,3},{7,5},{8,14},{10,8},{12,... | collective-permute-start | bytes 786440 | tf_op jit(solution)/shard_map/ppermute | solution.py:13
  14.6 2.7 %collective-permute-start = (bf16[32,4096]{1,0:T(8,128)(2,1)S(1)}, bf16[32,4096]{1,0:T(8,128)(2,1)S(1)}, u32[]{:S(2)}, u32[]{:S(2)}) collective-permute-start(bf16[32,4096]{1,0:T(8,128)(2,1)S(1)} %get-tuple-element.24), channel_id=1, source_target_pairs={{0,2},{2,4},{4,6},{6,0},{1,3},{3,5},{5,7},{7,1},{8,10},{10,12},{12... | collective-permute-start | bytes 786440 | tf_op jit(solution)/shard_map/ppermute | solution.py:13
  20.2 4.8 %collective-permute-start.5 = (bf16[32,4096]{1,0:T(8,128)(2,1)S(1)}, bf16[32,4096]{1,0:T(8,128)(2,1)S(1)}, u32[]{:S(2)}, u32[]{:S(2)}) collective-permute-start(bf16[32,4096]{1,0:T(8,128)(2,1)S(1)} %collective-permute-done.1), channel_id=1, source_target_pairs={{0,6},{2,0},{4,2},{6,4},{1,7},{3,1},{5,3},{7,5},{8,14},{10,8},{12,... | collective-permute-start | bytes 786440 | tf_op jit(solution)/shard_map/ppermute | solution.py:13
  26.6 3.6 %collective-permute-start.4 = (bf16[32,4096]{1,0:T(8,128)(2,1)S(1)}, bf16[32,4096]{1,0:T(8,128)(2,1)S(1)}, u32[]{:S(2)}, u32[]{:S(2)}) collective-permute-start(bf16[32,4096]{1,0:T(8,128)(2,1)S(1)} %collective-permute-done), channel_id=1, source_target_pairs={{0,2},{2,4},{4,6},{6,0},{1,3},{3,5},{5,7},{7,1},{8,10},{10,12},{12... | collective-permute-start | bytes 786440 | tf_op jit(solution)/shard_map/ppermute | solution.py:13
  33.1 5.7 %collective-permute-done.4 = bf16[32,4096]{1,0:T(8,128)(2,1)S(1)} collective-permute-done((bf16[32,4096]{1,0:T(8,128)(2,1)S(1)}, bf16[32,4096]{1,0:T(8,128)(2,1)S(1)}, u32[]{:S(2)}, u32[]{:S(2)}) %collective-permute-start.4) | collective-permute-done | bytes 262176 | tf_op jit(solution)/shard_map/ppermute | solution.py:13
  40.3 1.9 %collective-permute-start.6 = (bf16[256,4096]{1,0:T(8,128)(2,1)}, bf16[256,4096]{1,0:T(8,128)(2,1)}, u32[]{:S(2)}, u32[]{:S(2)}) collective-permute-start(bf16[256,4096]{1,0:T(8,128)(2,1)} %bitcast.7), channel_id=1, source_target_pairs={{0,1},{1,0},{2,3},{3,2},{4,5},{5,4},{6,7},{7,6},{8,9},{9,8},{10,11... | collective-permute-start | bytes 6291464 | tf_op jit(solution)/shard_map/ppermute | solution.py:13
  42.7 2.4 %fusion.28 = (f32[256]{0:T(256)S(1)}, f32[256,192]{0,1:T(8,128)S(1)}) fusion(bf16[256,4096]{1,0:T(8,128)(2,1)} %bitcast.7, bf16[192,4096]{1,0:T(8,128)(2,1)S(1)} %copy-done), kind=kOutput, calls=%fused_computation.64 | convolution fusion | flops 402702080 | bytes 3867648 | tf_op jit(solution)/shard_map/dot_general | solution.py:63
  46.7 2.4 %fusion.29 = (f32[256]{0:T(256)S(1)}, f32[256,192]{0,1:T(8,128)S(1)}) fusion(bf16[256,4096]{1,0:T(8,128)(2,1)} %collective-permute-done.6, bf16[192,4096]{1,0:T(8,128)(2,1)S(1)} %copy-done), kind=kOutput, calls=%fused_computation.65 | convolution fusion | flops 402702080 | bytes 3867648 | tf_op jit(solution)/shard_map/dot_general | solution.py:63
  50.1 11.6 %all-to-all-start = ((f32[8,2,3,256]{3,1,2,0:T(2,128)}), f32[8,2,3,256]{3,1,2,0:T(2,128)S(1)}, u32[]{:S(2)}, u32[]{:S(2)}) async-start(f32[8,2,3,256]{3,1,2,0:T(2,128)} %broadcast_in_dim.41), calls=%async_computation | async-start | bytes 98304 | tf_op jit(solution)/shard_map/all_to_all | solution.py:72
  61.8 8.0 %all-to-all-done = f32[8,2,3,256]{3,1,2,0:T(2,128)S(1)} async-done(((f32[8,2,3,256]{3,1,2,0:T(2,128)}), f32[8,2,3,256]{3,1,2,0:T(2,128)S(1)}, u32[]{:S(2)}, u32[]{:S(2)}) %all-to-all-start) | async-done | bytes 49184 | tf_op jit(solution)/shard_map/all_to_all | solution.py:72
  70.0 2.2 %convolution_convert_fusion = bf16[256,4096]{1,0:T(8,128)(2,1)} fusion(bf16[192,4096]{1,0:T(8,128)(2,1)S(1)} %copy-done, f32[256,192]{0,1:T(8,128)S(1)} %get-tuple-element.34, f32[256]{0:T(256)S(1)} %bitcast.86, f32[256]{0:T(256)S(1)} %mul.39, s32[256]{0:T(256)S(1)} %eq.48, s32[192]{0:T(256)S(1)} %iota_add_fusion), kind=kOutput, calls=%fused_computation.1 | convolution fusion | flops 403996672 | bytes 3870464 | tf_op jit(solution)/shard_map/dot_general | solution.py:84
  72.2 1.9 %collective-permute-start.7 = (bf16[256,4096]{1,0:T(8,128)(2,1)}, bf16[256,4096]{1,0:T(8,128)(2,1)}, u32[]{:S(2)}, u32[]{:S(2)}) collective-permute-start(bf16[256,4096]{1,0:T(8,128)(2,1)} %convolution_convert_fusion), channel_id=1, source_target_pairs={{0,1},{1,0},{2,3},{3,2},{4,5},{5,4},{6,7},{7,6},{8,9},{9,8},{10,11... | collective-permute-start | bytes 6291464 | tf_op jit(solution)/shard_map/ppermute | solution.py:13
  74.2 2.2 %fusion.17 = f32[192,4096]{1,0:T(8,128)S(1)} fusion(bf16[256,4096]{1,0:T(8,128)(2,1)} %collective-permute-done.6, f32[256,192]{0,1:T(8,128)S(1)} %get-tuple-element.34, f32[256]{0:T(256)S(1)} %bitcast.87, f32[256]{0:T(256)S(1)} %mul.39, s32[256]{0:T(256)S(1)} %eq.48, s32[192]{0:T(256)S(1)} %iota_add_fusion), kind=kOutput, calls=%fused_computation.59 | convolution fusion | flops 402948096 | bytes 5443328 | tf_op jit(solution)/shard_map/dot_general | solution.py:88
  76.4 3.4 %fusion.1 = bf16[192,4096]{1,0:T(8,128)(2,1)} fusion(f32[192,4096]{1,0:T(8,128)S(1)} %fusion.17, bf16[256,4096]{1,0:T(8,128)(2,1)} %bitcast.7, f32[256,192]{0,1:T(8,128)S(1)} %get-tuple-element.32, f32[256]{0:T(256)S(1)} %bitcast.90, f32[256]{0:T(256)S(1)} %mul.36, s32[256]{0:T(256)S(1)} %eq.45, s32[192]{0:T(256)S(1)} %iota_add_fusion), kind=kOutput, calls=%fused_computation.4 | convolution fusion | flops 404520960 | bytes 7016192 | tf_op jit(solution)/shard_map/dot_general | solution.py:88
  79.8 4.3 %all-to-all-start.1 = ((bf16[4,48,4096]{2,1,0:T(8,128)(2,1)}), bf16[4,48,4096]{2,1,0:T(8,128)(2,1)S(1)}, u32[]{:S(2)}, u32[]{:S(2)}) async-start(bf16[4,48,4096]{2,1,0:T(8,128)(2,1)} %bitcast.78), calls=%async_computation.1 | async-start | bytes 3145728 | tf_op jit(solution)/shard_map/all_to_all | solution.py:90
  84.1 2.4 %add_convert_fusion = bf16[256,4096]{1,0:T(8,128)(2,1)S(1)} fusion(bf16[256,4096]{1,0:T(8,128)(2,1)} %collective-permute-done.7, bf16[192,4096]{1,0:T(8,128)(2,1)S(1)} %copy-done, f32[256,192]{0,1:T(8,128)S(1)} %get-tuple-element.32, f32[256]{0:T(256)S(1)} %bitcast.91, f32[256]{0:T(256)S(1)} %mul.36, s32[256]{0:T(256)S(1)} %eq.45, s32[192]{0:T(256)S(1)} %iota_add_fusion), kind=kOutput, calls=%fused_computation.5 | convolution fusion | flops 408190976 | bytes 5967616 | tf_op jit(solution)/shard_map/dot_general | solution.py:85
  88.7 2.3 %collective-permute-start.9 = (bf16[32,4096]{1,0:T(8,128)(2,1)}, bf16[32,4096]{1,0:T(8,128)(2,1)}, u32[]{:S(2)}, u32[]{:S(2)}) collective-permute-start(bf16[32,4096]{1,0:T(8,128)(2,1)} %get-tuple-element.21), channel_id=1, source_target_pairs={{0,6},{2,0},{4,2},{6,4},{1,7},{3,1},{5,3},{7,5},{8,14},{10,8},{12,... | collective-permute-start | bytes 786440 | tf_op jit(solution)/shard_map/ppermute | solution.py:13
  91.0 4.4 %collective-permute-start.8 = (bf16[32,4096]{1,0:T(8,128)(2,1)}, bf16[32,4096]{1,0:T(8,128)(2,1)}, u32[]{:S(2)}, u32[]{:S(2)}) collective-permute-start(bf16[32,4096]{1,0:T(8,128)(2,1)} %get-tuple-element.22), channel_id=1, source_target_pairs={{0,2},{2,4},{4,6},{6,0},{1,3},{3,5},{5,7},{7,1},{8,10},{10,12},{12... | collective-permute-start | bytes 786440 | tf_op jit(solution)/shard_map/ppermute | solution.py:13
  95.4 10.0 %all-to-all-done.1 = bf16[4,48,4096]{2,1,0:T(8,128)(2,1)S(1)} async-done(((bf16[4,48,4096]{2,1,0:T(8,128)(2,1)}), bf16[4,48,4096]{2,1,0:T(8,128)(2,1)S(1)}, u32[]{:S(2)}, u32[]{:S(2)}) %all-to-all-start.1) | async-done | bytes 1572896 | tf_op jit(solution)/shard_map/all_to_all | solution.py:90
  106.0 28.4 %all_to_all.25 = bf16[16,48,256]{2,1,0:T(8,128)(2,1)S(1)} all-to-all(bf16[16,48,256]{2,1,0:T(8,128)(2,1)S(1)} %copy.11), channel_id=1, replica_groups=mesh['x'=4,'yl'=2,'z'=8,'yh'=4,'core'=2] {'yl','z'}, dimensions={0} | all-to-all | bytes 786432 | tf_op jit(solution)/shard_map/all_to_all | solution.py:103
  135.3 4.7 %all-to-all-start.3 = ((bf16[16,48,256]{2,1,0:T(8,128)(2,1)}), bf16[16,48,256]{2,1,0:T(8,128)(2,1)S(1)}, u32[]{:S(2)}, u32[]{:S(2)}) async-start(bf16[16,48,256]{2,1,0:T(8,128)(2,1)} %broadcast_in_dim.42), calls=%async_computation.3 | async-start | bytes 786432 | tf_op jit(solution)/shard_map/all_to_all | solution.py:105
  139.9 2.5 %fusion.3 = (bf16[64,4096]{1,0:T(8,128)(2,1)}, bf16[64,4096]{1,0:T(8,128)(2,1)}) fusion(bf16[32,4096]{1,0:T(8,128)(2,1)} %collective-permute-done.8, bf16[4,64,4096]{2,1,0:T(8,128)(2,1)} %bitcast.75, s32[]{:T(128)S(6)} %select_n.97, bf16[32,4096]{1,0:T(8,128)(2,1)} %collective-permute-done.9, s32[]{:T(128)S(6)} %select_n.95), kind=kLoop, calls=%fused_computation.9 | loop fusion | flops 2097152 | bytes 2621448 | tf_op jit(solution)/shard_map/convert_element_type | solution.py:101
  142.4 2.3 %collective-permute-start.10 = (bf16[64,4096]{1,0:T(8,128)(2,1)}, bf16[64,4096]{1,0:T(8,128)(2,1)}, u32[]{:S(2)}, u32[]{:S(2)}) collective-permute-start(bf16[64,4096]{1,0:T(8,128)(2,1)} %get-tuple-element.19), channel_id=1, source_target_pairs={{0,2},{2,4},{4,6},{6,0},{1,3},{3,5},{5,7},{7,1},{8,10},{10,12},{12... | collective-permute-start | bytes 1572872 | tf_op jit(solution)/shard_map/ppermute | solution.py:13
  144.7 5.6 %collective-permute-start.11 = (bf16[64,4096]{1,0:T(8,128)(2,1)}, bf16[64,4096]{1,0:T(8,128)(2,1)}, u32[]{:S(2)}, u32[]{:S(2)}) collective-permute-start(bf16[64,4096]{1,0:T(8,128)(2,1)} %get-tuple-element.20), channel_id=1, source_target_pairs={{0,6},{2,0},{4,2},{6,4},{1,7},{3,1},{5,3},{7,5},{8,14},{10,8},{12,... | collective-permute-start | bytes 1572872 | tf_op jit(solution)/shard_map/ppermute | solution.py:13
  150.4 2.5 %all-to-all-done.3 = bf16[16,48,256]{2,1,0:T(8,128)(2,1)S(1)} async-done(((bf16[16,48,256]{2,1,0:T(8,128)(2,1)}), bf16[16,48,256]{2,1,0:T(8,128)(2,1)S(1)}, u32[]{:S(2)}, u32[]{:S(2)}) %all-to-all-start.3) | async-done | bytes 393248 | tf_op jit(solution)/shard_map/all_to_all | solution.py:105
  154.2 3.6 %all-to-all-start.4 = ((bf16[4,48,4096]{2,1,0:T(8,128)(2,1)}), bf16[4,48,4096]{2,1,0:T(8,128)(2,1)S(1)}, u32[]{:S(2)}, u32[]{:S(2)}) async-start(bf16[4,48,4096]{2,1,0:T(8,128)(2,1)} %broadcast_in_dim.43), calls=%async_computation.4 | async-start | bytes 3145728 | tf_op jit(solution)/shard_map/all_to_all | solution.py:107
  158.4 12.4 %collective-permute-done.10 = bf16[64,4096]{1,0:T(8,128)(2,1)} collective-permute-done((bf16[64,4096]{1,0:T(8,128)(2,1)}, bf16[64,4096]{1,0:T(8,128)(2,1)}, u32[]{:S(2)}, u32[]{:S(2)}) %collective-permute-start.10) | collective-permute-done | bytes 524320 | tf_op jit(solution)/shard_map/ppermute | solution.py:13
  171.0 2.3 %fusion.4 = bf16[64,4096]{1,0:T(8,128)(2,1)} fusion(bf16[64,4096]{1,0:T(8,128)(2,1)} %collective-permute-done.11, bf16[64,4096]{1,0:T(8,128)(2,1)} %collective-permute-done.10, bf16[4,64,4096]{2,1,0:T(8,128)(2,1)} %bitcast.76, s32[]{:T(128)S(6)} %select_n.110), kind=kLoop, calls=%fused_computation.11 | loop fusion | flops 1572864 | bytes 2097156 | tf_op jit(solution)/shard_map/convert_element_type | solution.py:108
  173.4 5.2 %all-to-all-done.4 = bf16[4,48,4096]{2,1,0:T(8,128)(2,1)S(1)} async-done(((bf16[4,48,4096]{2,1,0:T(8,128)(2,1)}), bf16[4,48,4096]{2,1,0:T(8,128)(2,1)S(1)}, u32[]{:S(2)}, u32[]{:S(2)}) %all-to-all-start.4) | async-done | bytes 1572896 | tf_op jit(solution)/shard_map/all_to_all | solution.py:107
  (68 shorter events, 18.9 us)
Async XLA Ops:
  0.6 42.1 %copy-start = (bf16[192,4096]{1,0:T(8,128)(2,1)S(1)}, bf16[192,4096]{1,0:T(8,128)(2,1)}, u32[]{:S(2)}) copy-start(bf16[192,4096]{1,0:T(8,128)(2,1)} %param.7) | copy-start | bytes 4718596
  0.6 18.3 %copy-start.2 = (bf16[64,4096]{1,0:T(8,128)(2,1)S(1)}, bf16[64,4096]{1,0:T(8,128)(2,1)}, u32[]{:S(2)}) copy-start(bf16[64,4096]{1,0:T(8,128)(2,1)} %param.4) | copy-start | bytes 1572868
  2.6 29.1 %collective-permute-start.2 = (bf16[32,4096]{1,0:T(8,128)(2,1)}, bf16[32,4096]{1,0:T(8,128)(2,1)S(1)}, u32[]{:S(2)}, u32[]{:S(2)}) collective-permute-start(bf16[32,4096]{1,0:T(8,128)(2,1)} %get-tuple-element.23), channel_id=1, source_target_pairs={{0,2},{2,4},{4,6},{6,0},{1,3},{3,5},{5,7},{7,1},{8,10},{10,12},{12... | collective-permute-start | bytes 786440 | tf_op jit(solution)/shard_map/ppermute | solution.py:13
  7.1 13.1 %collective-permute-start.1 = (bf16[32,4096]{1,0:T(8,128)(2,1)}, bf16[32,4096]{1,0:T(8,128)(2,1)S(1)}, u32[]{:S(2)}, u32[]{:S(2)}) collective-permute-start(bf16[32,4096]{1,0:T(8,128)(2,1)} %get-tuple-element.23), channel_id=1, source_target_pairs={{0,6},{2,0},{4,2},{6,4},{1,7},{3,1},{5,3},{7,5},{8,14},{10,8},{12,... | collective-permute-start | bytes 786440 | tf_op jit(solution)/shard_map/ppermute | solution.py:13
  10.5 21.9 %collective-permute-start.3 = (bf16[32,4096]{1,0:T(8,128)(2,1)S(1)}, bf16[32,4096]{1,0:T(8,128)(2,1)S(1)}, u32[]{:S(2)}, u32[]{:S(2)}) collective-permute-start(bf16[32,4096]{1,0:T(8,128)(2,1)S(1)} %get-tuple-element.24), channel_id=1, source_target_pairs={{0,6},{2,0},{4,2},{6,4},{1,7},{3,1},{5,3},{7,5},{8,14},{10,8},{12,... | collective-permute-start | bytes 786440 | tf_op jit(solution)/shard_map/ppermute | solution.py:13
  14.6 12.0 %collective-permute-start = (bf16[32,4096]{1,0:T(8,128)(2,1)S(1)}, bf16[32,4096]{1,0:T(8,128)(2,1)S(1)}, u32[]{:S(2)}, u32[]{:S(2)}) collective-permute-start(bf16[32,4096]{1,0:T(8,128)(2,1)S(1)} %get-tuple-element.24), channel_id=1, source_target_pairs={{0,2},{2,4},{4,6},{6,0},{1,3},{3,5},{5,7},{7,1},{8,10},{10,12},{12... | collective-permute-start | bytes 786440 | tf_op jit(solution)/shard_map/ppermute | solution.py:13
  18.9 23.3 %copy-start.3 = (s32[512]{0:T(512)S(1)}, s32[512]{0:T(512)}, u32[]{:S(2)}) copy-start(s32[512]{0:T(512)} %param.5) | copy-start | bytes 6148
  18.9 23.4 %copy-start.4 = (f32[512]{0:T(512)S(1)}, f32[512]{0:T(512)}, u32[]{:S(2)}) copy-start(f32[512]{0:T(512)} %param.6) | copy-start | bytes 6148
  20.2 19.4 %collective-permute-start.5 = (bf16[32,4096]{1,0:T(8,128)(2,1)S(1)}, bf16[32,4096]{1,0:T(8,128)(2,1)S(1)}, u32[]{:S(2)}, u32[]{:S(2)}) collective-permute-start(bf16[32,4096]{1,0:T(8,128)(2,1)S(1)} %collective-permute-done.1), channel_id=1, source_target_pairs={{0,6},{2,0},{4,2},{6,4},{1,7},{3,1},{5,3},{7,5},{8,14},{10,8},{12,... | collective-permute-start | bytes 786440 | tf_op jit(solution)/shard_map/ppermute | solution.py:13
  26.6 12.3 %collective-permute-start.4 = (bf16[32,4096]{1,0:T(8,128)(2,1)S(1)}, bf16[32,4096]{1,0:T(8,128)(2,1)S(1)}, u32[]{:S(2)}, u32[]{:S(2)}) collective-permute-start(bf16[32,4096]{1,0:T(8,128)(2,1)S(1)} %collective-permute-done), channel_id=1, source_target_pairs={{0,2},{2,4},{4,6},{6,0},{1,3},{3,5},{5,7},{7,1},{8,10},{10,12},{12... | collective-permute-start | bytes 786440 | tf_op jit(solution)/shard_map/ppermute | solution.py:13
  40.3 6.4 %collective-permute-start.6 = (bf16[256,4096]{1,0:T(8,128)(2,1)}, bf16[256,4096]{1,0:T(8,128)(2,1)}, u32[]{:S(2)}, u32[]{:S(2)}) collective-permute-start(bf16[256,4096]{1,0:T(8,128)(2,1)} %bitcast.7), channel_id=1, source_target_pairs={{0,1},{1,0},{2,3},{3,2},{4,5},{5,4},{6,7},{7,6},{8,9},{9,8},{10,11... | collective-permute-start | bytes 6291464 | tf_op jit(solution)/shard_map/ppermute | solution.py:13
  50.1 19.7 %all-to-all-start = ((f32[8,2,3,256]{3,1,2,0:T(2,128)}), f32[8,2,3,256]{3,1,2,0:T(2,128)S(1)}, u32[]{:S(2)}, u32[]{:S(2)}) async-start(f32[8,2,3,256]{3,1,2,0:T(2,128)} %broadcast_in_dim.41), calls=%async_computation | async-start | bytes 98304 | tf_op jit(solution)/shard_map/all_to_all | solution.py:72
  72.2 11.9 %collective-permute-start.7 = (bf16[256,4096]{1,0:T(8,128)(2,1)}, bf16[256,4096]{1,0:T(8,128)(2,1)}, u32[]{:S(2)}, u32[]{:S(2)}) collective-permute-start(bf16[256,4096]{1,0:T(8,128)(2,1)} %convolution_convert_fusion), channel_id=1, source_target_pairs={{0,1},{1,0},{2,3},{3,2},{4,5},{5,4},{6,7},{7,6},{8,9},{9,8},{10,11... | collective-permute-start | bytes 6291464 | tf_op jit(solution)/shard_map/ppermute | solution.py:13
  79.8 25.7 %all-to-all-start.1 = ((bf16[4,48,4096]{2,1,0:T(8,128)(2,1)}), bf16[4,48,4096]{2,1,0:T(8,128)(2,1)S(1)}, u32[]{:S(2)}, u32[]{:S(2)}) async-start(bf16[4,48,4096]{2,1,0:T(8,128)(2,1)} %bitcast.78), calls=%async_computation.1 | async-start | bytes 3145728 | tf_op jit(solution)/shard_map/all_to_all | solution.py:90
  86.5 1.4 copy-start.1
  88.7 17.2 %collective-permute-start.9 = (bf16[32,4096]{1,0:T(8,128)(2,1)}, bf16[32,4096]{1,0:T(8,128)(2,1)}, u32[]{:S(2)}, u32[]{:S(2)}) collective-permute-start(bf16[32,4096]{1,0:T(8,128)(2,1)} %get-tuple-element.21), channel_id=1, source_target_pairs={{0,6},{2,0},{4,2},{6,4},{1,7},{3,1},{5,3},{7,5},{8,14},{10,8},{12,... | collective-permute-start | bytes 786440 | tf_op jit(solution)/shard_map/ppermute | solution.py:13
  91.0 14.8 %collective-permute-start.8 = (bf16[32,4096]{1,0:T(8,128)(2,1)}, bf16[32,4096]{1,0:T(8,128)(2,1)}, u32[]{:S(2)}, u32[]{:S(2)}) collective-permute-start(bf16[32,4096]{1,0:T(8,128)(2,1)} %get-tuple-element.22), channel_id=1, source_target_pairs={{0,2},{2,4},{4,6},{6,0},{1,3},{3,5},{5,7},{7,1},{8,10},{10,12},{12... | collective-permute-start | bytes 786440 | tf_op jit(solution)/shard_map/ppermute | solution.py:13
  135.3 17.6 %all-to-all-start.3 = ((bf16[16,48,256]{2,1,0:T(8,128)(2,1)}), bf16[16,48,256]{2,1,0:T(8,128)(2,1)S(1)}, u32[]{:S(2)}, u32[]{:S(2)}) async-start(bf16[16,48,256]{2,1,0:T(8,128)(2,1)} %broadcast_in_dim.42), calls=%async_computation.3 | async-start | bytes 786432 | tf_op jit(solution)/shard_map/all_to_all | solution.py:105
  142.4 28.4 %collective-permute-start.10 = (bf16[64,4096]{1,0:T(8,128)(2,1)}, bf16[64,4096]{1,0:T(8,128)(2,1)}, u32[]{:S(2)}, u32[]{:S(2)}) collective-permute-start(bf16[64,4096]{1,0:T(8,128)(2,1)} %get-tuple-element.19), channel_id=1, source_target_pairs={{0,2},{2,4},{4,6},{6,0},{1,3},{3,5},{5,7},{7,1},{8,10},{10,12},{12... | collective-permute-start | bytes 1572872 | tf_op jit(solution)/shard_map/ppermute | solution.py:13
  144.7 26.3 %collective-permute-start.11 = (bf16[64,4096]{1,0:T(8,128)(2,1)}, bf16[64,4096]{1,0:T(8,128)(2,1)}, u32[]{:S(2)}, u32[]{:S(2)}) collective-permute-start(bf16[64,4096]{1,0:T(8,128)(2,1)} %get-tuple-element.20), channel_id=1, source_target_pairs={{0,6},{2,0},{4,2},{6,4},{1,7},{3,1},{5,3},{7,5},{8,14},{10,8},{12,... | collective-permute-start | bytes 1572872 | tf_op jit(solution)/shard_map/ppermute | solution.py:13
  154.2 24.3 %all-to-all-start.4 = ((bf16[4,48,4096]{2,1,0:T(8,128)(2,1)}), bf16[4,48,4096]{2,1,0:T(8,128)(2,1)S(1)}, u32[]{:S(2)}, u32[]{:S(2)}) async-start(bf16[4,48,4096]{2,1,0:T(8,128)(2,1)} %broadcast_in_dim.43), calls=%async_computation.4 | async-start | bytes 3145728 | tf_op jit(solution)/shard_map/all_to_all | solution.py:107

commit v4 on v3

v4 whole, which is shorter than its diff:
```python
import jax
import jax.numpy as jnp
from jax import lax
from jax.experimental import pallas as pl
from jax.experimental.pallas import tpu as pltpu
from jax.sharding import Mesh
from jax.sharding import PartitionSpec as P

F32, BF16 = jnp.float32, jnp.bfloat16
DP = ("x", "yl", "z")
VOCAB = ("yh", "core")


def shift(value, axis, step, size):
    return lax.ppermute(value, axis, [(i, (i + step) % size) for i in range(size)])


def swap(value):
    return shift(value, "core", 1, 2)


def by_core(value, core):
    return jnp.where(core == 0, value, value[::-1])


def gather_yh(hidden, small, yh, n_yh):
    half = hidden.shape[0] // 2
    low, high = hidden[:half], hidden[half:]
    up_low = shift(low, "yh", 1, n_yh)
    down_high = shift(high, "yh", -1, n_yh)
    up_low, down_high, low, high, small = lax.optimization_barrier((up_low, down_high, low, high, small))
    far_low = shift(up_low, "yh", 1, n_yh)
    far_high = shift(down_high, "yh", -1, n_yh)
    up_high = shift(high, "yh", 1, n_yh)
    down_low = shift(low, "yh", -1, n_yh)
    out = jnp.zeros((n_yh, 2, half, hidden.shape[1]), hidden.dtype)
    out = lax.dynamic_update_slice(out, hidden.reshape(1, 2, half, -1), (yh, 0, 0, 0))
    before, after, far = (yh - 1) % n_yh, (yh + 1) % n_yh, (yh + 2) % n_yh
    for piece, owner, part in (
        (up_low, before, 0),
        (down_high, after, 1),
        (far_low, far, 0),
        (far_high, far, 1),
        (up_high, before, 1),
        (down_low, after, 0),
    ):
        out = lax.dynamic_update_slice(out, piece[None, None], (owner, part, 0, 0))
    return out.reshape(n_yh * 2 * half, -1), small


def hits(where, labels, shape):
    return lax.broadcasted_iota(jnp.int32, shape, 0) + where[1] == labels


def local_stats(where, head, block, labels, logits):
    rows_t = (((1,), (1,)), ((), ()))
    value = lax.dot_general(head[...], block[...], rows_t, preferred_element_type=F32)
    logits[...] = value
    top = jnp.max(value, axis=0, keepdims=True)
    total = jnp.sum(jnp.exp(value - top), axis=0, keepdims=True)
    target = jnp.sum(jnp.where(hits(where, labels, value.shape), value, 0.0), axis=0, keepdims=True)
    return top, total, target


def own_kernel(where, head, block, labels, logits, stats):
    top, total, target = local_stats(where, head, block, labels[0:1], logits)
    stats[...] = jnp.zeros_like(stats)
    stats[0:1], stats[1:2], stats[2:3] = top, total, target


def other_kernel(where, head, block, labels, own_stats, logits, stats):
    ours = local_stats(where, head, block, labels[1:2], logits)
    first = where[0] == 0
    rows = [own_stats[i : i + 1] for i in range(3)]
    line = [jnp.where(first, rows[i], ours[i]) for i in range(3)] + [jnp.where(first, ours[i], rows[i]) for i in range(3)]
    blank = jnp.zeros_like(rows[0])
    tile = jnp.concatenate(line + [blank, blank], axis=0)
    for shard in range(stats.shape[0]):
        stats[shard] = tile


def score_kernel(where, stats, labels, weights, own_logits, other_logits, own, other, head, grad, away, score, loss, held):
    n_own = own_logits.shape[1]

    @pl.when(pl.program_id(0) == 0)
    def _():
        merged = []
        for c in range(2):
            top = jnp.max(stats[:, 3 * c], axis=0, keepdims=True)
            total = jnp.sum(stats[:, 3 * c + 1] * jnp.exp(stats[:, 3 * c] - top), axis=0, keepdims=True)
            log_total = top + jnp.log(total)
            merged.append((log_total, log_total - jnp.sum(stats[:, 3 * c + 2], axis=0, keepdims=True)))
        first = where[0] == 0
        loss[...] = jnp.where(first, merged[0][1], merged[1][1])
        for k, logits in enumerate((own_logits, other_logits)):
            log_total = jnp.where(first, merged[k][0], merged[1 - k][0])
            hit = hits(where, labels[k : k + 1], logits.shape).astype(F32)
            value = weights[k : k + 1] * (jnp.exp(logits[...] - log_total) - hit)
            held[:, k * n_own : (k + 1) * n_own] = value.astype(BF16)
        score[...] = held[:, :n_own]

    total = jnp.dot(held[:, :n_own], own[...], preferred_element_type=F32)
    total += jnp.dot(held[:, n_own:], other[...], preferred_element_type=F32)
    grad[...] = total.astype(BF16)
    rows_v = (((0,), (0,)), ((), ()))
    away[...] = lax.dot_general(held[:, n_own:], head[...], rows_v, preferred_element_type=F32).astype(BF16)


def per_device(hidden, targets, token_weight, head_weight, *, n_x, n_yl, n_z, n_yh):
    yh, core = lax.axis_index("yh"), lax.axis_index("core")
    tok, width = hidden.shape
    v_dev = head_weight.shape[0]
    n_own, n_shards = n_yh * tok, 2 * n_yh
    labels = by_core(targets.reshape(n_yh, 2, tok).transpose(1, 0, 2), core).reshape(2, n_own)
    weights = by_core(token_weight.reshape(n_yh, 2, tok).transpose(1, 0, 2), core).reshape(2, n_own)
    where = jnp.stack([core, (yh * 2 + core) * v_dev])

    own, (labels, weights, where) = gather_yh(hidden, (labels, weights, where), yh, n_yh)
    other = swap(own)

    smem, vmem = pl.BlockSpec(memory_space=pltpu.SMEM), pl.BlockSpec(memory_space=pltpu.VMEM)
    params = pltpu.CompilerParams(vmem_limit_bytes=32 << 20)
    cost = pl.CostEstimate(flops=2 * v_dev * n_own * width, bytes_accessed=2 * (v_dev + n_own) * width, transcendentals=v_dev * n_own)
    own_logits, stats = pl.pallas_call(
        own_kernel,
        out_shape=(jax.ShapeDtypeStruct((v_dev, n_own), F32), jax.ShapeDtypeStruct((8, n_own), F32)),
        in_specs=[smem, vmem, vmem, vmem],
        out_specs=(vmem, vmem),
        compiler_params=params,
        cost_estimate=cost,
    )(where, head_weight, own, labels)
    other_logits, stats = pl.pallas_call(
        other_kernel,
        out_shape=(jax.ShapeDtypeStruct((v_dev, n_own), F32), jax.ShapeDtypeStruct((n_shards, 8, n_own), F32)),
        in_specs=[smem, vmem, vmem, vmem, vmem],
        out_specs=(vmem, vmem),
        compiler_params=params,
        cost_estimate=cost,
    )(where, head_weight, other, labels, stats)
    stats = lax.all_to_all(stats, VOCAB, 0, 0, tiled=True)

    cols = min(1024, width)
    whole = lambda *shape: pl.BlockSpec(shape, lambda i: (0,) * len(shape))
    wide = lambda rows: pl.BlockSpec((rows, cols), lambda i: (0, i))
    partial, away, score, loss = pl.pallas_call(
        score_kernel,
        out_shape=(
            jax.ShapeDtypeStruct((v_dev, width), BF16),
            jax.ShapeDtypeStruct((n_own, width), BF16),
            jax.ShapeDtypeStruct((v_dev, n_own), BF16),
            jax.ShapeDtypeStruct((1, n_own), F32),
        ),
        grid=(width // cols,),
        in_specs=[
            smem,
            whole(n_shards, 8, n_own),
            whole(2, n_own),
            whole(2, n_own),
            whole(v_dev, n_own),
            whole(v_dev, n_own),
            wide(n_own),
            wide(n_own),
            wide(v_dev),
        ],
        out_specs=(wide(v_dev), wide(n_own), whole(v_dev, n_own), whole(1, n_own)),
        scratch_shapes=[pltpu.VMEM((v_dev, 2 * n_own), BF16)],
        compiler_params=params,
        cost_estimate=pl.CostEstimate(
            flops=6 * v_dev * n_own * width,
            bytes_accessed=2 * (2 * v_dev + 3 * n_own) * width,
            transcendentals=2 * v_dev * n_own,
        ),
    )(where, stats, labels, weights, own_logits, other_logits, own, other, head_weight)
    token_loss = lax.dynamic_slice_in_dim(loss[0], yh * tok, tok)

    part = partial.reshape(n_x, v_dev // n_x, width)
    part = lax.all_to_all(part, "x", 0, 0, tiled=True)
    part = jnp.sum(part.astype(F32), axis=0).astype(BF16)
    part = part.reshape(v_dev // n_x, n_yl * n_z, -1).transpose(1, 0, 2)

    rows_v = (((0,), (0,)), ((), ()))
    home = lax.dot_general(score, head_weight, rows_v, preferred_element_type=F32).astype(BF16)
    terms = (home.astype(F32) + swap(away).astype(F32)).astype(BF16).reshape(n_yh, tok, width)

    block = lambda s: lax.dynamic_index_in_dim(terms, (yh + s) % n_yh, 0, False)
    half, far = tok // 2, block(2)
    from_below = shift(far[:half], "yh", 1, n_yh)
    from_above = shift(far[half:], "yh", -1, n_yh)
    part, from_below, from_above = lax.optimization_barrier((part, from_below, from_above))
    zero = jnp.zeros((half, width), F32)
    up = block(1).astype(F32) + jnp.concatenate([from_below.astype(F32), zero], 0)
    down = block(-1).astype(F32) + jnp.concatenate([zero, from_above.astype(F32)], 0)
    came = [shift(up.astype(BF16), "yh", 1, n_yh), shift(down.astype(BF16), "yh", -1, n_yh)]

    part = lax.all_to_all(part, ("yl", "z"), 0, 0, tiled=True)
    part = jnp.sum(part.astype(F32), axis=0).astype(BF16)
    part = lax.all_to_all(jnp.broadcast_to(part, (n_yl * n_z,) + part.shape), ("yl", "z"), 0, 0, tiled=True)
    part = part.transpose(1, 0, 2).reshape(v_dev // n_x, width)
    part = lax.all_to_all(jnp.broadcast_to(part, (n_x,) + part.shape), "x", 0, 0, tiled=True)
    grad_weight = part.reshape(v_dev, width)

    grad_hidden = (block(0).astype(F32) + sum(v.astype(F32) for v in came)).astype(BF16)
    return token_loss, grad_hidden, grad_weight


def fine(mesh_devices, sizes):
    mesh = Mesh(mesh_devices.reshape(sizes), ("x", "yl", "z", "yh", "core"))

    def body(*args):
        return per_device(*args, n_x=sizes[0], n_yl=sizes[1], n_z=sizes[2], n_yh=sizes[3])

    tokens = ("x", "yl", "z", "yh", "core")
    return jax.shard_map(
        body,
        mesh=mesh,
        in_specs=(P(tokens, None), P(DP), P(DP), P(VOCAB, None)),
        out_specs=(P(tokens), P(tokens, None), P(VOCAB, None)),
        check_vma=False,
    )


def solution(mesh):
    return fine(mesh.devices, (4, 2, 8, 4, 2))
```

time: 181 us -> 179 us (0.989)
  matrix products: 15.1 us -> 2.33 us
  Pallas kernels: 0 us -> 8.94 us
  starting transfers between devices: 65.8 us -> 59.8 us
  blocking collectives: 28.4 us -> 33.9 us
  waiting for transfers between devices: 47.6 us -> 50.8 us
    dot_general x6 -> x1, matrix products: 15.1 us -> 2.33 us  [per_device(): lax.dot_general(score, head_weight, rows_v, preferred_element_type=F32)]
    all_to_all x1 -> x0, starting transfers between devices: 11.6 us -> none  [per_device(): lax.all_to_all(jnp.broadcast_to(stats, (2 * n_yh,) + stats.shape), VOCAB,...]
    all_to_all x0 -> x1, blocking collectives: none -> 10.7 us  [per_device(): stats = lax.all_to_all(stats, VOCAB, 0, 0, tiled=True)]
    ppermute x12, waiting for transfers between devices: 21.9 us -> 32.3 us  [shift(): lax.ppermute(value, axis, [(i, (i + step) % size) for i in range(size)])]
    pallas_call x0 -> x3, Pallas kernels: none -> 8.94 us  [the longest x1 4.98 us: per_device(): pl.pallas_call(score_kernel, out_shape=(jax.ShapeDtypeStruct((v_dev, widt...]
    all_to_all x1 -> x0, waiting for transfers between devices: 7.96 us -> none  [per_device(): lax.all_to_all(jnp.broadcast_to(stats, (2 * n_yh,) + stats.shape), VOCAB,...]
    all_to_all x1, blocking collectives: 28.4 us -> 23.1 us  [per_device(): part = lax.all_to_all(part, ('yl', 'z'), 0, 0, tiled=True)]
    ppermute x12, starting transfers between devices: 41.7 us -> 46.4 us  [shift(): lax.ppermute(value, axis, [(i, (i + step) % size) for i in range(size)])]
  transfers between devices with their start and end apart: 16 -> 15, of which waited for: 10 -> 10; matrix products, arithmetic and copies ran while one was open for 14% -> 10% of each run, Pallas kernels for 0% -> 1%
where the time goes in v4:
time: 179 us; the launch traced here: 178 us
  starting transfers between devices  59.8 us (33%)
  waiting for transfers between devices  50.8 us (28%)
  blocking collectives  33.9 us (19%)
  local copies, waits for them, and re-layouts  17.3 us (10%)
  Pallas kernels  8.94 us (5%)
  other arithmetic  4.46 us (2%)
  matrix products  2.33 us (1%)
    ppermute x12, starting transfers between devices, shift(): lax.ppermute(value, axis, [(i, (i + step) % size) for i in range(size)])  46.4 us
    ppermute x12, waiting for transfers between devices, shift(): lax.ppermute(value, axis, [(i, (i + step) % size) for i in range(size)])  32.3 us
    all_to_all x1, blocking collectives, per_device(): part = lax.all_to_all(part, ('yl', 'z'), 0, 0, tiled=True)  23.1 us
    all_to_all x1, blocking collectives, per_device(): stats = lax.all_to_all(stats, VOCAB, 0, 0, tiled=True)  10.7 us
    all_to_all x1, waiting for transfers between devices, per_device(): part = lax.all_to_all(part, 'x', 0, 0, tiled=True)  8.75 us
    all_to_all x1, waiting for transfers between devices, per_device(): lax.all_to_all(jnp.broadcast_to(part, (n_x,) + part.shape), 'x', 0, 0, ti...  6.76 us
    pallas_call x1, Pallas kernels, per_device(): pl.pallas_call(score_kernel, out_shape=(jax.ShapeDtypeStruct((v_dev, widt...  4.98 us
    all_to_all x1, starting transfers between devices, per_device(): lax.all_to_all(jnp.broadcast_to(part, (n_yl * n_z,) + part.shape), ('yl',...  4.69 us
  transfers between devices with their start and end apart: 15, of which 10 were waited for; matrix products, arithmetic and copies ran while one was open for 10% of the time, Pallas kernels for 1%

profile of v4, /device:TPU:72, one launch (start us, length us, event | category | flops | bytes accessed | tf_op | source)
XLA Modules:
  0.0 178.4 jit_solution(14272150033916286755)
XLA Ops:
  1.8 4.5 %collective-permute-start = (bf16[32,4096]{1,0:T(8,128)(2,1)S(1)}, bf16[32,4096]{1,0:T(8,128)(2,1)S(1)}, u32[]{:S(2)}, u32[]{:S(2)}) collective-permute-start(bf16[32,4096]{1,0:T(8,128)(2,1)S(1)} %get-tuple-element.25), channel_id=1, source_target_pairs={{0,2},{2,4},{4,6},{6,0},{1,3},{3,5},{5,7},{7,1},{8,10},{10,12},{12... | collective-permute-start | bytes 786440 | tf_op jit(solution)/shard_map/ppermute | solution.py:15
  6.3 3.5 %collective-permute-start.1 = (bf16[32,4096]{1,0:T(8,128)(2,1)S(1)}, bf16[32,4096]{1,0:T(8,128)(2,1)S(1)}, u32[]{:S(2)}, u32[]{:S(2)}) collective-permute-start(bf16[32,4096]{1,0:T(8,128)(2,1)S(1)} %get-tuple-element.24), channel_id=1, source_target_pairs={{0,6},{2,0},{4,2},{6,4},{1,7},{3,1},{5,3},{7,5},{8,14},{10,8},{12,... | collective-permute-start | bytes 786440 | tf_op jit(solution)/shard_map/ppermute | solution.py:15
  14.0 5.4 %collective-permute-done = bf16[32,4096]{1,0:T(8,128)(2,1)S(1)} collective-permute-done((bf16[32,4096]{1,0:T(8,128)(2,1)S(1)}, bf16[32,4096]{1,0:T(8,128)(2,1)S(1)}, u32[]{:S(2)}, u32[]{:S(2)}) %collective-permute-start) | collective-permute-done | bytes 262176 | tf_op jit(solution)/shard_map/ppermute | solution.py:15
  19.4 8.9 %collective-permute-start.2 = (bf16[32,4096]{1,0:T(8,128)(2,1)S(1)}, bf16[32,4096]{1,0:T(8,128)(2,1)S(1)}, u32[]{:S(2)}, u32[]{:S(2)}) collective-permute-start(bf16[32,4096]{1,0:T(8,128)(2,1)S(1)} %collective-permute-done), channel_id=1, source_target_pairs={{0,2},{2,4},{4,6},{6,0},{1,3},{3,5},{5,7},{7,1},{8,10},{10,12},{12... | collective-permute-start | bytes 786440 | tf_op jit(solution)/shard_map/ppermute | solution.py:15
  28.3 1.9 %collective-permute-start.3 = (bf16[32,4096]{1,0:T(8,128)(2,1)S(1)}, bf16[32,4096]{1,0:T(8,128)(2,1)S(1)}, u32[]{:S(2)}, u32[]{:S(2)}) collective-permute-start(bf16[32,4096]{1,0:T(8,128)(2,1)S(1)} %collective-permute-done.1), channel_id=1, source_target_pairs={{0,6},{2,0},{4,2},{6,4},{1,7},{3,1},{5,3},{7,5},{8,14},{10,8},{12,... | collective-permute-start | bytes 786440 | tf_op jit(solution)/shard_map/ppermute | solution.py:15
  30.3 4.8 %collective-permute-start.4 = (bf16[32,4096]{1,0:T(8,128)(2,1)S(1)}, bf16[32,4096]{1,0:T(8,128)(2,1)S(1)}, u32[]{:S(2)}, u32[]{:S(2)}) collective-permute-start(bf16[32,4096]{1,0:T(8,128)(2,1)S(1)} %get-tuple-element.24), channel_id=1, source_target_pairs={{0,2},{2,4},{4,6},{6,0},{1,3},{3,5},{5,7},{7,1},{8,10},{10,12},{12... | collective-permute-start | bytes 786440 | tf_op jit(solution)/shard_map/ppermute | solution.py:15
  35.1 3.1 %collective-permute-start.5 = (bf16[32,4096]{1,0:T(8,128)(2,1)S(1)}, bf16[32,4096]{1,0:T(8,128)(2,1)S(1)}, u32[]{:S(2)}, u32[]{:S(2)}) collective-permute-start(bf16[32,4096]{1,0:T(8,128)(2,1)S(1)} %get-tuple-element.25), channel_id=1, source_target_pairs={{0,6},{2,0},{4,2},{6,4},{1,7},{3,1},{5,3},{7,5},{8,14},{10,8},{12,... | collective-permute-start | bytes 786440 | tf_op jit(solution)/shard_map/ppermute | solution.py:15
  39.7 6.4 %collective-permute-done.2 = bf16[32,4096]{1,0:T(8,128)(2,1)S(1)} collective-permute-done((bf16[32,4096]{1,0:T(8,128)(2,1)S(1)}, bf16[32,4096]{1,0:T(8,128)(2,1)S(1)}, u32[]{:S(2)}, u32[]{:S(2)}) %collective-permute-start.2) | collective-permute-done | bytes 262176 | tf_op jit(solution)/shard_map/ppermute | solution.py:15
  46.8 4.5 %collective-permute-done.3 = bf16[32,4096]{1,0:T(8,128)(2,1)S(1)} collective-permute-done((bf16[32,4096]{1,0:T(8,128)(2,1)S(1)}, bf16[32,4096]{1,0:T(8,128)(2,1)S(1)}, u32[]{:S(2)}, u32[]{:S(2)}) %collective-permute-start.3) | collective-permute-done | bytes 262176 | tf_op jit(solution)/shard_map/ppermute | solution.py:15
  52.7 2.5 %collective-permute-done.5 = bf16[32,4096]{1,0:T(8,128)(2,1)S(1)} collective-permute-done((bf16[32,4096]{1,0:T(8,128)(2,1)S(1)}, bf16[32,4096]{1,0:T(8,128)(2,1)S(1)}, u32[]{:S(2)}, u32[]{:S(2)}) %collective-permute-start.5) | collective-permute-done | bytes 262176 | tf_op jit(solution)/shard_map/ppermute | solution.py:15
  56.0 1.9 %collective-permute-start.6 = (bf16[256,4096]{1,0:T(8,128)(2,1)}, bf16[256,4096]{1,0:T(8,128)(2,1)S(1)}, u32[]{:S(2)}, u32[]{:S(2)}) collective-permute-start(bf16[256,4096]{1,0:T(8,128)(2,1)} %bitcast.11.block.own), channel_id=1, source_target_pairs={{0,1},{1,0},{2,3},{3,2},{4,5},{5,4},{6,7},{7,6},{8,9},{9,8},{10,11... | collective-permute-start | bytes 6291464 | tf_op jit(solution)/shard_map/ppermute | solution.py:15
  57.9 2.5 %shard_map.67 = (f32[192,256]{1,0:T(8,128)S(1)}, f32[8,256]{1,0:T(8,128)S(1)}) custom-call(s32[2]{0:T(128)S(1)} %pad_add_fusion.where, bf16[192,4096]{1,0:T(8,128)(2,1)S(1)} %copy-done, bf16[256,4096]{1,0:T(8,128)(2,1)} %bitcast.11.block.own, s32[2,256]{1,0:T(2,128)S(1)} %reshape.49.labels), custom_call_target="tpu_custom_call" | custom-call | flops 402653184 | bytes 3670016 | tf_op jit(solution)/shard_map/pallas_call | solution.py:124
  60.4 1.8 %collective-permute-done.6.block.other = bf16[256,4096]{1,0:T(8,128)(2,1)S(1)} collective-permute-done((bf16[256,4096]{1,0:T(8,128)(2,1)}, bf16[256,4096]{1,0:T(8,128)(2,1)S(1)}, u32[]{:S(2)}, u32[]{:S(2)}) %collective-permute-start.6) | collective-permute-done | bytes 2097184 | tf_op jit(solution)/shard_map/ppermute | solution.py:15
  63.7 10.7 %all_to_all.25.stats = f32[8,8,256]{2,1,0:T(8,128)S(1)} all-to-all(f32[8,8,256]{2,1,0:T(8,128)S(1)} %get-tuple-element.28), channel_id=1, replica_groups=mesh['x'=4,'yl'=2,'z'=8,'yh'=4,'core'=2] {'yh','core'}, dimensions={0} | all-to-all | bytes 131072 | tf_op jit(solution)/shard_map/all_to_all | solution.py:140
  74.5 5.0 %shard_map.69 = (bf16[192,4096]{1,0:T(8,128)(2,1)}, bf16[256,4096]{1,0:T(8,128)(2,1)}, bf16[192,256]{1,0:T(8,128)(2,1)S(1)}, f32[1,256]{1,0:T(1,128)S(1)}) custom-call(s32[2]{0:T(128)S(1)} %pad_add_fusion.where, f32[8,8,256]{2,1,0:T(8,128)S(1)} %all_to_all.25.stats, s32[2,256]{1,0:T(2,128)S(1)} %reshape.49.labels, f32[2,256]{1,0:T(2,128)S(1)} %reshape.51.weights, ...), custom_call_target="tpu_custom_call" | custom-call | flops 1207959552 | bytes 9437184 | tf_op jit(solution)/shard_map/pallas_call | solution.py:145
  79.4 1.9 %collective-permute-start.7 = (bf16[256,4096]{1,0:T(8,128)(2,1)}, bf16[256,4096]{1,0:T(8,128)(2,1)}, u32[]{:S(2)}, u32[]{:S(2)}) collective-permute-start(bf16[256,4096]{1,0:T(8,128)(2,1)} %get-tuple-element.34), channel_id=1, source_target_pairs={{0,1},{1,0},{2,3},{3,2},{4,5},{5,4},{6,7},{7,6},{8,9},{9,8},{10,11... | collective-permute-start | bytes 6291464 | tf_op jit(solution)/shard_map/ppermute | solution.py:15
  81.4 4.3 %all-to-all-start.1 = ((bf16[4,48,4096]{2,1,0:T(8,128)(2,1)}), bf16[4,48,4096]{2,1,0:T(8,128)(2,1)S(1)}, u32[]{:S(2)}, u32[]{:S(2)}) async-start(bf16[4,48,4096]{2,1,0:T(8,128)(2,1)} %bitcast.16), calls=%async_computation.1 | async-start | bytes 3145728 | tf_op jit(solution)/shard_map/all_to_all | solution.py:177
  85.8 2.3 %fusion.2 = bf16[256,4096]{1,0:T(8,128)(2,1)S(1)} fusion(bf16[192,256]{1,0:T(8,128)(2,1)S(1)} %get-tuple-element.33, bf16[192,4096]{1,0:T(8,128)(2,1)S(1)} %copy-done, bf16[256,4096]{1,0:T(8,128)(2,1)} %collective-permute-done.7), kind=kOutput, calls=%fused_computation.3 | convolution fusion | flops 407896064 | bytes 5865472 | tf_op jit(solution)/shard_map/dot_general | solution.py:182
  90.3 2.3 %collective-permute-start.8 = (bf16[32,4096]{1,0:T(8,128)(2,1)}, bf16[32,4096]{1,0:T(8,128)(2,1)}, u32[]{:S(2)}, u32[]{:S(2)}) collective-permute-start(bf16[32,4096]{1,0:T(8,128)(2,1)} %get-tuple-element.42), channel_id=1, source_target_pairs={{0,2},{2,4},{4,6},{6,0},{1,3},{3,5},{5,7},{7,1},{8,10},{10,12},{12... | collective-permute-start | bytes 786440 | tf_op jit(solution)/shard_map/ppermute | solution.py:15
  92.7 5.6 %collective-permute-start.9 = (bf16[32,4096]{1,0:T(8,128)(2,1)}, bf16[32,4096]{1,0:T(8,128)(2,1)}, u32[]{:S(2)}, u32[]{:S(2)}) collective-permute-start(bf16[32,4096]{1,0:T(8,128)(2,1)} %get-tuple-element.41), channel_id=1, source_target_pairs={{0,6},{2,0},{4,2},{6,4},{1,7},{3,1},{5,3},{7,5},{8,14},{10,8},{12,... | collective-permute-start | bytes 786440 | tf_op jit(solution)/shard_map/ppermute | solution.py:15
  98.3 8.7 %all-to-all-done.1 = bf16[4,48,4096]{2,1,0:T(8,128)(2,1)S(1)} async-done(((bf16[4,48,4096]{2,1,0:T(8,128)(2,1)}), bf16[4,48,4096]{2,1,0:T(8,128)(2,1)S(1)}, u32[]{:S(2)}, u32[]{:S(2)}) %all-to-all-start.1) | async-done | bytes 1572896 | tf_op jit(solution)/shard_map/all_to_all | solution.py:177
  107.6 23.1 %all_to_all.26 = bf16[16,48,256]{2,1,0:T(8,128)(2,1)S(1)} all-to-all(bf16[16,48,256]{2,1,0:T(8,128)(2,1)S(1)} %copy.13), channel_id=1, replica_groups=mesh['x'=4,'yl'=2,'z'=8,'yh'=4,'core'=2] {'yl','z'}, dimensions={0} | all-to-all | bytes 786432 | tf_op jit(solution)/shard_map/all_to_all | solution.py:195
  131.5 4.7 %all-to-all-start.3 = ((bf16[16,48,256]{2,1,0:T(8,128)(2,1)}), bf16[16,48,256]{2,1,0:T(8,128)(2,1)S(1)}, u32[]{:S(2)}, u32[]{:S(2)}) async-start(bf16[16,48,256]{2,1,0:T(8,128)(2,1)} %broadcast_in_dim.35), calls=%async_computation.3 | async-start | bytes 786432 | tf_op jit(solution)/shard_map/all_to_all | solution.py:197
  136.2 2.0 %fusion.4 = (bf16[64,4096]{1,0:T(8,128)(2,1)}, bf16[64,4096]{1,0:T(8,128)(2,1)S(1)}) fusion(bf16[32,4096]{1,0:T(8,128)(2,1)} %collective-permute-done.8, bf16[4,64,4096]{2,1,0:T(8,128)(2,1)S(1)} %bitcast.48, s32[]{:T(128)S(6)} %select_n.71, bf16[32,4096]{1,0:T(8,128)(2,1)} %collective-permute-done.9, s32[]{:T(128)S(6)} %select_n.69), kind=kLoop, calls=%fused_computation.7 | loop fusion | flops 2097152 | bytes 2621448 | tf_op jit(solution)/shard_map/convert_element_type | solution.py:193
  138.2 3.9 %collective-permute-start.10 = (bf16[64,4096]{1,0:T(8,128)(2,1)}, bf16[64,4096]{1,0:T(8,128)(2,1)S(1)}, u32[]{:S(2)}, u32[]{:S(2)}) collective-permute-start(bf16[64,4096]{1,0:T(8,128)(2,1)} %get-tuple-element.39), channel_id=1, source_target_pairs={{0,2},{2,4},{4,6},{6,0},{1,3},{3,5},{5,7},{7,1},{8,10},{10,12},{12... | collective-permute-start | bytes 1572872 | tf_op jit(solution)/shard_map/ppermute | solution.py:15
  142.1 4.0 %collective-permute-start.11 = (bf16[64,4096]{1,0:T(8,128)(2,1)S(1)}, bf16[64,4096]{1,0:T(8,128)(2,1)}, u32[]{:S(2)}, u32[]{:S(2)}) collective-permute-start(bf16[64,4096]{1,0:T(8,128)(2,1)S(1)} %get-tuple-element.40), channel_id=1, source_target_pairs={{0,6},{2,0},{4,2},{6,4},{1,7},{3,1},{5,3},{7,5},{8,14},{10,8},{12,... | collective-permute-start | bytes 1572872 | tf_op jit(solution)/shard_map/ppermute | solution.py:15
  146.2 3.0 %all-to-all-done.3 = bf16[16,48,256]{2,1,0:T(8,128)(2,1)S(1)} async-done(((bf16[16,48,256]{2,1,0:T(8,128)(2,1)}), bf16[16,48,256]{2,1,0:T(8,128)(2,1)S(1)}, u32[]{:S(2)}, u32[]{:S(2)}) %all-to-all-start.3) | async-done | bytes 393248 | tf_op jit(solution)/shard_map/all_to_all | solution.py:197
  150.5 4.4 %all-to-all-start.4 = ((bf16[4,48,4096]{2,1,0:T(8,128)(2,1)}), bf16[4,48,4096]{2,1,0:T(8,128)(2,1)}, u32[]{:S(2)}, u32[]{:S(2)}) async-start(bf16[4,48,4096]{2,1,0:T(8,128)(2,1)} %broadcast_in_dim.36), calls=%async_computation.4 | async-start | bytes 3145728 | tf_op jit(solution)/shard_map/all_to_all | solution.py:199
  155.5 11.5 %collective-permute-done.10 = bf16[64,4096]{1,0:T(8,128)(2,1)S(1)} collective-permute-done((bf16[64,4096]{1,0:T(8,128)(2,1)}, bf16[64,4096]{1,0:T(8,128)(2,1)S(1)}, u32[]{:S(2)}, u32[]{:S(2)}) %collective-permute-start.10) | collective-permute-done | bytes 524320 | tf_op jit(solution)/shard_map/ppermute | solution.py:15
  166.9 2.0 %fusion.5 = bf16[64,4096]{1,0:T(8,128)(2,1)} fusion(bf16[64,4096]{1,0:T(8,128)(2,1)} %collective-permute-done.11, bf16[64,4096]{1,0:T(8,128)(2,1)S(1)} %collective-permute-done.10, bf16[4,64,4096]{2,1,0:T(8,128)(2,1)S(1)} %bitcast.49, s32[]{:T(128)S(6)} %select_n.76), kind=kLoop, calls=%fused_computation.9 | loop fusion | flops 1572864 | bytes 2097156 | tf_op jit(solution)/shard_map/convert_element_type | solution.py:202
  169.0 6.8 %all-to-all-done.4 = bf16[4,48,4096]{2,1,0:T(8,128)(2,1)} async-done(((bf16[4,48,4096]{2,1,0:T(8,128)(2,1)}), bf16[4,48,4096]{2,1,0:T(8,128)(2,1)}, u32[]{:S(2)}, u32[]{:S(2)}) %all-to-all-start.4) | async-done | bytes 1572896 | tf_op jit(solution)/shard_map/all_to_all | solution.py:199
  175.7 2.7 %copy.25 = bf16[192,4096]{1,0:T(8,128)(2,1)} copy(bf16[192,4096]{1,0:T(8,128)(2,1)} %bitcast.22) | data formatting | bytes 3145728
  (44 shorter events, 16.7 us)
Async XLA Ops:
  0.6 12.4 %copy-start.3 = (bf16[64,4096]{1,0:T(8,128)(2,1)S(1)}, bf16[64,4096]{1,0:T(8,128)(2,1)}, u32[]{:S(2)}) copy-start(bf16[64,4096]{1,0:T(8,128)(2,1)} %param.4) | copy-start | bytes 1572868
  1.8 17.7 %collective-permute-start = (bf16[32,4096]{1,0:T(8,128)(2,1)S(1)}, bf16[32,4096]{1,0:T(8,128)(2,1)S(1)}, u32[]{:S(2)}, u32[]{:S(2)}) collective-permute-start(bf16[32,4096]{1,0:T(8,128)(2,1)S(1)} %get-tuple-element.25), channel_id=1, source_target_pairs={{0,2},{2,4},{4,6},{6,0},{1,3},{3,5},{5,7},{7,1},{8,10},{10,12},{12... | collective-permute-start | bytes 786440 | tf_op jit(solution)/shard_map/ppermute | solution.py:15
  6.3 13.2 %collective-permute-start.1 = (bf16[32,4096]{1,0:T(8,128)(2,1)S(1)}, bf16[32,4096]{1,0:T(8,128)(2,1)S(1)}, u32[]{:S(2)}, u32[]{:S(2)}) collective-permute-start(bf16[32,4096]{1,0:T(8,128)(2,1)S(1)} %get-tuple-element.24), channel_id=1, source_target_pairs={{0,6},{2,0},{4,2},{6,4},{1,7},{3,1},{5,3},{7,5},{8,14},{10,8},{12,... | collective-permute-start | bytes 786440 | tf_op jit(solution)/shard_map/ppermute | solution.py:15
  13.0 44.9 %copy-start = (bf16[192,4096]{1,0:T(8,128)(2,1)S(1)}, bf16[192,4096]{1,0:T(8,128)(2,1)}, u32[]{:S(2)}) copy-start(bf16[192,4096]{1,0:T(8,128)(2,1)} %head.5) | copy-start | bytes 4718596
  19.4 26.6 %collective-permute-start.2 = (bf16[32,4096]{1,0:T(8,128)(2,1)S(1)}, bf16[32,4096]{1,0:T(8,128)(2,1)S(1)}, u32[]{:S(2)}, u32[]{:S(2)}) collective-permute-start(bf16[32,4096]{1,0:T(8,128)(2,1)S(1)} %collective-permute-done), channel_id=1, source_target_pairs={{0,2},{2,4},{4,6},{6,0},{1,3},{3,5},{5,7},{7,1},{8,10},{10,12},{12... | collective-permute-start | bytes 786440 | tf_op jit(solution)/shard_map/ppermute | solution.py:15
  28.3 22.9 %collective-permute-start.3 = (bf16[32,4096]{1,0:T(8,128)(2,1)S(1)}, bf16[32,4096]{1,0:T(8,128)(2,1)S(1)}, u32[]{:S(2)}, u32[]{:S(2)}) collective-permute-start(bf16[32,4096]{1,0:T(8,128)(2,1)S(1)} %collective-permute-done.1), channel_id=1, source_target_pairs={{0,6},{2,0},{4,2},{6,4},{1,7},{3,1},{5,3},{7,5},{8,14},{10,8},{12,... | collective-permute-start | bytes 786440 | tf_op jit(solution)/shard_map/ppermute | solution.py:15
  30.3 21.7 %collective-permute-start.4 = (bf16[32,4096]{1,0:T(8,128)(2,1)S(1)}, bf16[32,4096]{1,0:T(8,128)(2,1)S(1)}, u32[]{:S(2)}, u32[]{:S(2)}) collective-permute-start(bf16[32,4096]{1,0:T(8,128)(2,1)S(1)} %get-tuple-element.24), channel_id=1, source_target_pairs={{0,2},{2,4},{4,6},{6,0},{1,3},{3,5},{5,7},{7,1},{8,10},{10,12},{12... | collective-permute-start | bytes 786440 | tf_op jit(solution)/shard_map/ppermute | solution.py:15
  35.1 20.2 %collective-permute-start.5 = (bf16[32,4096]{1,0:T(8,128)(2,1)S(1)}, bf16[32,4096]{1,0:T(8,128)(2,1)S(1)}, u32[]{:S(2)}, u32[]{:S(2)}) collective-permute-start(bf16[32,4096]{1,0:T(8,128)(2,1)S(1)} %get-tuple-element.25), channel_id=1, source_target_pairs={{0,6},{2,0},{4,2},{6,4},{1,7},{3,1},{5,3},{7,5},{8,14},{10,8},{12,... | collective-permute-start | bytes 786440 | tf_op jit(solution)/shard_map/ppermute | solution.py:15
  56.0 6.3 %collective-permute-start.6 = (bf16[256,4096]{1,0:T(8,128)(2,1)}, bf16[256,4096]{1,0:T(8,128)(2,1)S(1)}, u32[]{:S(2)}, u32[]{:S(2)}) collective-permute-start(bf16[256,4096]{1,0:T(8,128)(2,1)} %bitcast.11.block.own), channel_id=1, source_target_pairs={{0,1},{1,0},{2,3},{3,2},{4,5},{5,4},{6,7},{7,6},{8,9},{9,8},{10,11... | collective-permute-start | bytes 6291464 | tf_op jit(solution)/shard_map/ppermute | solution.py:15
  79.4 6.4 %collective-permute-start.7 = (bf16[256,4096]{1,0:T(8,128)(2,1)}, bf16[256,4096]{1,0:T(8,128)(2,1)}, u32[]{:S(2)}, u32[]{:S(2)}) collective-permute-start(bf16[256,4096]{1,0:T(8,128)(2,1)} %get-tuple-element.34), channel_id=1, source_target_pairs={{0,1},{1,0},{2,3},{3,2},{4,5},{5,4},{6,7},{7,6},{8,9},{9,8},{10,11... | collective-permute-start | bytes 6291464 | tf_op jit(solution)/shard_map/ppermute | solution.py:15
  81.4 25.7 %all-to-all-start.1 = ((bf16[4,48,4096]{2,1,0:T(8,128)(2,1)}), bf16[4,48,4096]{2,1,0:T(8,128)(2,1)S(1)}, u32[]{:S(2)}, u32[]{:S(2)}) async-start(bf16[4,48,4096]{2,1,0:T(8,128)(2,1)} %bitcast.16), calls=%async_computation.1 | async-start | bytes 3145728 | tf_op jit(solution)/shard_map/all_to_all | solution.py:177
  88.2 1.3 copy-start.1
  90.3 17.1 %collective-permute-start.8 = (bf16[32,4096]{1,0:T(8,128)(2,1)}, bf16[32,4096]{1,0:T(8,128)(2,1)}, u32[]{:S(2)}, u32[]{:S(2)}) collective-permute-start(bf16[32,4096]{1,0:T(8,128)(2,1)} %get-tuple-element.42), channel_id=1, source_target_pairs={{0,2},{2,4},{4,6},{6,0},{1,3},{3,5},{5,7},{7,1},{8,10},{10,12},{12... | collective-permute-start | bytes 786440 | tf_op jit(solution)/shard_map/ppermute | solution.py:15
  92.7 14.8 %collective-permute-start.9 = (bf16[32,4096]{1,0:T(8,128)(2,1)}, bf16[32,4096]{1,0:T(8,128)(2,1)}, u32[]{:S(2)}, u32[]{:S(2)}) collective-permute-start(bf16[32,4096]{1,0:T(8,128)(2,1)} %get-tuple-element.41), channel_id=1, source_target_pairs={{0,6},{2,0},{4,2},{6,4},{1,7},{3,1},{5,3},{7,5},{8,14},{10,8},{12,... | collective-permute-start | bytes 786440 | tf_op jit(solution)/shard_map/ppermute | solution.py:15
  107.3 28.9 %copy-start.2 = (bf16[256,4096]{1,0:T(8,128)(2,1)S(1)}, bf16[256,4096]{1,0:T(8,128)(2,1)}, u32[]{:S(2)}) copy-start(bf16[256,4096]{1,0:T(8,128)(2,1)} %copy-done.1) | copy-start | bytes 6291460
  131.5 17.6 %all-to-all-start.3 = ((bf16[16,48,256]{2,1,0:T(8,128)(2,1)}), bf16[16,48,256]{2,1,0:T(8,128)(2,1)S(1)}, u32[]{:S(2)}, u32[]{:S(2)}) async-start(bf16[16,48,256]{2,1,0:T(8,128)(2,1)} %broadcast_in_dim.35), calls=%async_computation.3 | async-start | bytes 786432 | tf_op jit(solution)/shard_map/all_to_all | solution.py:197
  138.2 28.7 %collective-permute-start.10 = (bf16[64,4096]{1,0:T(8,128)(2,1)}, bf16[64,4096]{1,0:T(8,128)(2,1)S(1)}, u32[]{:S(2)}, u32[]{:S(2)}) collective-permute-start(bf16[64,4096]{1,0:T(8,128)(2,1)} %get-tuple-element.39), channel_id=1, source_target_pairs={{0,2},{2,4},{4,6},{6,0},{1,3},{3,5},{5,7},{7,1},{8,10},{10,12},{12... | collective-permute-start | bytes 1572872 | tf_op jit(solution)/shard_map/ppermute | solution.py:15
  142.1 24.8 %collective-permute-start.11 = (bf16[64,4096]{1,0:T(8,128)(2,1)S(1)}, bf16[64,4096]{1,0:T(8,128)(2,1)}, u32[]{:S(2)}, u32[]{:S(2)}) collective-permute-start(bf16[64,4096]{1,0:T(8,128)(2,1)S(1)} %get-tuple-element.40), channel_id=1, source_target_pairs={{0,6},{2,0},{4,2},{6,4},{1,7},{3,1},{5,3},{7,5},{8,14},{10,8},{12,... | collective-permute-start | bytes 1572872 | tf_op jit(solution)/shard_map/ppermute | solution.py:15
  150.5 25.2 %all-to-all-start.4 = ((bf16[4,48,4096]{2,1,0:T(8,128)(2,1)}), bf16[4,48,4096]{2,1,0:T(8,128)(2,1)}, u32[]{:S(2)}, u32[]{:S(2)}) async-start(bf16[4,48,4096]{2,1,0:T(8,128)(2,1)} %broadcast_in_dim.36), calls=%async_computation.4 | async-start | bytes 3145728 | tf_op jit(solution)/shard_map/all_to_all | solution.py:199

commit v5 on v4

--- a/solution.py
+++ b/solution.py
@@ -28,11 +28,11 @@
     low, high = hidden[:half], hidden[half:]
     up_low = shift(low, "yh", 1, n_yh)
     down_high = shift(high, "yh", -1, n_yh)
-    up_low, down_high, low, high, small = lax.optimization_barrier((up_low, down_high, low, high, small))
+    up_high = shift(high, "yh", 1, n_yh)
+    down_low = shift(low, "yh", -1, n_yh)
+    up_low, down_high, small = lax.optimization_barrier((up_low, down_high, small))
     far_low = shift(up_low, "yh", 1, n_yh)
     far_high = shift(down_high, "yh", -1, n_yh)
-    up_high = shift(high, "yh", 1, n_yh)
-    down_low = shift(low, "yh", -1, n_yh)
     out = jnp.zeros((n_yh, 2, half, hidden.shape[1]), hidden.dtype)
     out = lax.dynamic_update_slice(out, hidden.reshape(1, 2, half, -1), (yh, 0, 0, 0))
     before, after, far = (yh - 1) % n_yh, (yh + 1) % n_yh, (yh + 2) % n_yh
@@ -104,6 +104,12 @@
     grad[...] = total.astype(BF16)
     rows_v = (((0,), (0,)), ((), ()))
     away[...] = lax.dot_general(held[:, n_own:], head[...], rows_v, preferred_element_type=F32).astype(BF16)
+
+
+def lay_kernel(pieces, out):
+    cols = pieces.shape[3]
+    for i in range(pieces.shape[1]):
+        out[:, i * cols : (i + 1) * cols] = pieces[0, i]
 
 
 def per_device(hidden, targets, token_weight, head_weight, *, n_x, n_yl, n_z, n_yh):
@@ -175,31 +181,29 @@
 
     part = partial.reshape(n_x, v_dev // n_x, width)
     part = lax.all_to_all(part, "x", 0, 0, tiled=True)
+
+    rows_v = (((0,), (0,)), ((), ()))
+    home = lax.dot_general(score, head_weight, rows_v, preferred_element_type=F32).astype(BF16)
+    terms = (home.astype(F32) + swap(away).astype(F32)).astype(BF16)
+
+    part, terms = lax.optimization_barrier((part, terms))
     part = jnp.sum(part.astype(F32), axis=0).astype(BF16)
     part = part.reshape(v_dev // n_x, n_yl * n_z, -1).transpose(1, 0, 2)
-
-    rows_v = (((0,), (0,)), ((), ()))
-    home = lax.dot_general(score, head_weight, rows_v, preferred_element_type=F32).astype(BF16)
-    terms = (home.astype(F32) + swap(away).astype(F32)).astype(BF16).reshape(n_yh, tok, width)
-
-    block = lambda s: lax.dynamic_index_in_dim(terms, (yh + s) % n_yh, 0, False)
-    half, far = tok // 2, block(2)
-    from_below = shift(far[:half], "yh", 1, n_yh)
-    from_above = shift(far[half:], "yh", -1, n_yh)
-    part, from_below, from_above = lax.optimization_barrier((part, from_below, from_above))
-    zero = jnp.zeros((half, width), F32)
-    up = block(1).astype(F32) + jnp.concatenate([from_below.astype(F32), zero], 0)
-    down = block(-1).astype(F32) + jnp.concatenate([zero, from_above.astype(F32)], 0)
-    came = [shift(up.astype(BF16), "yh", 1, n_yh), shift(down.astype(BF16), "yh", -1, n_yh)]
+    grad_hidden = lax.psum_scatter(terms, "yh", scatter_dimension=0, tiled=True)
 
     part = lax.all_to_all(part, ("yl", "z"), 0, 0, tiled=True)
     part = jnp.sum(part.astype(F32), axis=0).astype(BF16)
     part = lax.all_to_all(jnp.broadcast_to(part, (n_yl * n_z,) + part.shape), ("yl", "z"), 0, 0, tiled=True)
-    part = part.transpose(1, 0, 2).reshape(v_dev // n_x, width)
     part = lax.all_to_all(jnp.broadcast_to(part, (n_x,) + part.shape), "x", 0, 0, tiled=True)
-    grad_weight = part.reshape(v_dev, width)
-
-    grad_hidden = (block(0).astype(F32) + sum(v.astype(F32) for v in came)).astype(BF16)
+    grad_weight = pl.pallas_call(
+        lay_kernel,
+        out_shape=jax.ShapeDtypeStruct((v_dev, width), BF16),
+        grid=(n_x,),
+        in_specs=[pl.BlockSpec((1,) + part.shape[1:], lambda i: (i, 0, 0, 0))],
+        out_specs=pl.BlockSpec((v_dev // n_x, width), lambda i: (i, 0)),
+        compiler_params=params,
+        cost_estimate=pl.CostEstimate(flops=0, bytes_accessed=4 * v_dev * width, transcendentals=0),
+    )(part)
     return token_loss, grad_hidden, grad_weight
 
 

time: 179 us -> 199 us (1.11)
  the two profiles are of different devices: /device:TPU:72 before, /device:TPU:2 now
where the time goes in v5:
time: 199 us; the launch traced here: 198 us
  blocking collectives  63.7 us (32%)
  waiting for transfers between devices  51.8 us (26%)
  starting transfers between devices  41.1 us (21%)
  between operations  14.2 us (7%)
  local copies, waits for them, and re-layouts  12.4 us (6%)
  Pallas kernels  10.6 us (5%)
  matrix products  3.66 us (2%)
    ppermute x8, starting transfers between devices, shift(): lax.ppermute(value, axis, [(i, (i + step) % size) for i in range(size)])  27.9 us
    all_to_all x1, blocking collectives, per_device(): lax.all_to_all(jnp.broadcast_to(part, (n_yl * n_z,) + part.shape), ('yl',...  26.5 us
    all_to_all x1, blocking collectives, per_device(): part = lax.all_to_all(part, ('yl', 'z'), 0, 0, tiled=True)  23.8 us
    ppermute x8, waiting for transfers between devices, shift(): lax.ppermute(value, axis, [(i, (i + step) % size) for i in range(size)])  20.2 us
    all_to_all x1, waiting for transfers between devices, per_device(): part = lax.all_to_all(part, 'x', 0, 0, tiled=True)  16.3 us
    all_to_all x1, waiting for transfers between devices, per_device(): lax.all_to_all(jnp.broadcast_to(part, (n_x,) + part.shape), 'x', 0, 0, ti...  15.3 us
    all_to_all x1, blocking collectives, per_device(): stats = lax.all_to_all(stats, VOCAB, 0, 0, tiled=True)  13.4 us
    all_to_all x1, starting transfers between devices, per_device(): lax.all_to_all(jnp.broadcast_to(part, (n_x,) + part.shape), 'x', 0, 0, ti...  8.32 us
  transfers between devices with their start and end apart: 11, of which 7 were waited for; matrix products, arithmetic and copies ran while one was open for 7% of the time, Pallas kernels for 2%

profile of v5, /device:TPU:2, one launch (start us, length us, event | category | flops | bytes accessed | tf_op | source)
XLA Modules:
  0.0 197.9 jit_solution(8909858372081612529)
XLA Ops:
  7.2 1.8 fusion.4
  9.0 4.5 %collective-permute-start.4 = (bf16[32,4096]{1,0:T(8,128)(2,1)}, bf16[32,4096]{1,0:T(8,128)(2,1)S(1)}, u32[]{:S(2)}, u32[]{:S(2)}) collective-permute-start(bf16[32,4096]{1,0:T(8,128)(2,1)} %get-tuple-element.33), channel_id=1, source_target_pairs={{0,2},{2,4},{4,6},{6,0},{1,3},{3,5},{5,7},{7,1},{8,10},{10,12},{12... | collective-permute-start | bytes 786440 | tf_op jit(solution)/shard_map/ppermute | solution.py:15
  13.5 3.6 %collective-permute-start.1 = (bf16[32,4096]{1,0:T(8,128)(2,1)}, bf16[32,4096]{1,0:T(8,128)(2,1)S(1)}, u32[]{:S(2)}, u32[]{:S(2)}) collective-permute-start(bf16[32,4096]{1,0:T(8,128)(2,1)} %get-tuple-element.33), channel_id=1, source_target_pairs={{0,6},{2,0},{4,2},{6,4},{1,7},{3,1},{5,3},{7,5},{8,14},{10,8},{12,... | collective-permute-start | bytes 786440 | tf_op jit(solution)/shard_map/ppermute | solution.py:15
  17.1 4.8 %collective-permute-start.5 = (bf16[32,4096]{1,0:T(8,128)(2,1)S(1)}, bf16[32,4096]{1,0:T(8,128)(2,1)S(1)}, u32[]{:S(2)}, u32[]{:S(2)}) collective-permute-start(bf16[32,4096]{1,0:T(8,128)(2,1)S(1)} %get-tuple-element.34), channel_id=1, source_target_pairs={{0,6},{2,0},{4,2},{6,4},{1,7},{3,1},{5,3},{7,5},{8,14},{10,8},{12,... | collective-permute-start | bytes 786440 | tf_op jit(solution)/shard_map/ppermute | solution.py:15
  21.9 1.9 collective-permute-start
  23.9 0.8 reshape.31
  24.7 0.8 reshape.33
  25.6 1.6 broadcast_in_dim.27
  27.1 0.8 constant_dynamic-update-slice_fusion
  28.2 8.7 %collective-permute-done.1 = bf16[32,4096]{1,0:T(8,128)(2,1)S(1)} collective-permute-done((bf16[32,4096]{1,0:T(8,128)(2,1)}, bf16[32,4096]{1,0:T(8,128)(2,1)S(1)}, u32[]{:S(2)}, u32[]{:S(2)}) %collective-permute-start.1) | collective-permute-done | bytes 262176 | tf_op jit(solution)/shard_map/ppermute | solution.py:15
  36.9 3.0 %collective-permute-done = bf16[32,4096]{1,0:T(8,128)(2,1)S(1)} collective-permute-done((bf16[32,4096]{1,0:T(8,128)(2,1)S(1)}, bf16[32,4096]{1,0:T(8,128)(2,1)S(1)}, u32[]{:S(2)}, u32[]{:S(2)}) %collective-permute-start) | collective-permute-done | bytes 262176 | tf_op jit(solution)/shard_map/ppermute | solution.py:15
  39.9 7.4 %collective-permute-start.2 = (bf16[32,4096]{1,0:T(8,128)(2,1)S(1)}, bf16[32,4096]{1,0:T(8,128)(2,1)S(1)}, u32[]{:S(2)}, u32[]{:S(2)}) collective-permute-start(bf16[32,4096]{1,0:T(8,128)(2,1)S(1)} %collective-permute-done), channel_id=1, source_target_pairs={{0,2},{2,4},{4,6},{6,0},{1,3},{3,5},{5,7},{7,1},{8,10},{10,12},{12... | collective-permute-start | bytes 786440 | tf_op jit(solution)/shard_map/ppermute | solution.py:15
  47.3 1.9 collective-permute-start.3
  50.0 0.8 bitcast_dynamic-update-slice_fusion.4
  50.7 1.9 collective-permute-done.2
  53.4 4.7 %collective-permute-done.3 = bf16[32,4096]{1,0:T(8,128)(2,1)S(1)} collective-permute-done((bf16[32,4096]{1,0:T(8,128)(2,1)S(1)}, bf16[32,4096]{1,0:T(8,128)(2,1)S(1)}, u32[]{:S(2)}, u32[]{:S(2)}) %collective-permute-start.3) | collective-permute-done | bytes 262176 | tf_op jit(solution)/shard_map/ppermute | solution.py:15
  60.3 1.9 collective-permute-start.6
  62.2 2.5 %shard_map.67 = (f32[192,256]{1,0:T(8,128)S(1)}, f32[8,256]{1,0:T(8,128)S(1)}) custom-call(s32[2]{0:T(128)S(1)} %pad_add_fusion.where, bf16[192,4096]{1,0:T(8,128)(2,1)S(1)} %copy-done, bf16[256,4096]{1,0:T(8,128)(2,1)} %bitcast.11.block.own, s32[2,256]{1,0:T(2,128)S(1)} %reshape.32.labels), custom_call_target="tpu_custom_call" | custom-call | flops 402653184 | bytes 3670016 | tf_op jit(solution)/shard_map/pallas_call | solution.py:130
  64.7 1.8 collective-permute-done.6.block.other
  66.5 1.5 shard_map.68
  68.0 13.4 %all_to_all.25.stats = f32[8,8,256]{2,1,0:T(8,128)S(1)} all-to-all(f32[8,8,256]{2,1,0:T(8,128)S(1)} %get-tuple-element.23), channel_id=1, replica_groups=mesh['x'=4,'yl'=2,'z'=8,'yh'=4,'core'=2] {'yh','core'}, dimensions={0} | all-to-all | bytes 131072 | tf_op jit(solution)/shard_map/all_to_all | solution.py:146
  81.4 4.9 %shard_map.69 = (bf16[192,4096]{1,0:T(8,128)(2,1)}, bf16[256,4096]{1,0:T(8,128)(2,1)}, bf16[192,256]{1,0:T(8,128)(2,1)S(1)}, f32[1,256]{1,0:T(1,128)S(1)}) custom-call(s32[2]{0:T(128)S(1)} %pad_add_fusion.where, f32[8,8,256]{2,1,0:T(8,128)S(1)} %all_to_all.25.stats, s32[2,256]{1,0:T(2,128)S(1)} %reshape.32.labels, f32[2,256]{1,0:T(2,128)S(1)} %reshape.34.weights, ...), custom_call_target="tpu_custom_call" | custom-call | flops 1207959552 | bytes 9437184 | tf_op jit(solution)/shard_map/pallas_call | solution.py:151
  86.3 1.9 collective-permute-start.7
  88.2 4.8 %all-to-all-start.1 = ((bf16[4,48,4096]{2,1,0:T(8,128)(2,1)}), bf16[4,48,4096]{2,1,0:T(8,128)(2,1)S(1)}, u32[]{:S(2)}, u32[]{:S(2)}) async-start(bf16[4,48,4096]{2,1,0:T(8,128)(2,1)} %bitcast.13), calls=%async_computation.1 | async-start | bytes 3145728 | tf_op jit(solution)/shard_map/all_to_all | solution.py:183
  93.1 3.7 %fusion.2 = bf16[256,4096]{1,0:T(8,128)(2,1)} fusion(bf16[192,256]{1,0:T(8,128)(2,1)S(1)} %get-tuple-element.29, bf16[192,4096]{1,0:T(8,128)(2,1)S(1)} %copy-done, bf16[256,4096]{1,0:T(8,128)(2,1)} %collective-permute-done.7), kind=kOutput, calls=%fused_computation.3 | convolution fusion | flops 407896064 | bytes 5865472 | tf_op jit(solution)/shard_map/dot_general | solution.py:186
  96.8 16.3 %all-to-all-done.1 = bf16[4,48,4096]{2,1,0:T(8,128)(2,1)S(1)} async-done(((bf16[4,48,4096]{2,1,0:T(8,128)(2,1)}), bf16[4,48,4096]{2,1,0:T(8,128)(2,1)S(1)}, u32[]{:S(2)}, u32[]{:S(2)}) %all-to-all-start.1) | async-done | bytes 1572896 | tf_op jit(solution)/shard_map/all_to_all | solution.py:183
  113.5 23.8 %all_to_all.26 = bf16[16,48,256]{2,1,0:T(8,128)(2,1)S(1)} all-to-all(bf16[16,48,256]{2,1,0:T(8,128)(2,1)S(1)} %copy.13), channel_id=1, replica_groups=mesh['x'=4,'yl'=2,'z'=8,'yh'=4,'core'=2] {'yl','z'}, dimensions={0} | all-to-all | bytes 786432 | tf_op jit(solution)/shard_map/all_to_all | solution.py:194
  137.4 26.5 %all_to_all.27 = bf16[16,48,256]{2,1,0:T(8,128)(2,1)S(1)} all-to-all(bf16[16,48,256]{2,1,0:T(8,128)(2,1)S(1)} %broadcast_in_dim.34), channel_id=1, replica_groups=mesh['x'=4,'yl'=2,'z'=8,'yh'=4,'core'=2] {'yl','z'}, dimensions={0} | all-to-all | bytes 786432 | tf_op jit(solution)/shard_map/all_to_all | solution.py:196
  163.9 1.3 broadcast_in_dim.35
  165.2 8.3 %all-to-all-start.4 = ((bf16[4,16,48,256]{3,2,1,0:T(8,128)(2,1)}), bf16[4,16,48,256]{3,2,1,0:T(8,128)(2,1)S(1)}, u32[]{:S(2)}, u32[]{:S(2)}) async-start(bf16[4,16,48,256]{3,2,1,0:T(8,128)(2,1)} %broadcast_in_dim.35), calls=%async_computation.5 | async-start | bytes 3145728 | tf_op jit(solution)/shard_map/all_to_all | solution.py:197
  174.1 15.3 %all-to-all-done.4.pieces = bf16[4,16,48,256]{3,2,1,0:T(8,128)(2,1)S(1)} async-done(((bf16[4,16,48,256]{3,2,1,0:T(8,128)(2,1)}), bf16[4,16,48,256]{3,2,1,0:T(8,128)(2,1)S(1)}, u32[]{:S(2)}, u32[]{:S(2)}) %all-to-all-start.4) | async-done | bytes 1572896 | tf_op jit(solution)/shard_map/all_to_all | solution.py:197
  189.4 1.7 shard_map.70
  (30 shorter events, 5.1 us)
Async XLA Ops:
  7.2 20.0 %copy-start.1 = (bf16[64,4096]{1,0:T(8,128)(2,1)S(1)}, bf16[64,4096]{1,0:T(8,128)(2,1)}, u32[]{:S(2)}) copy-start(bf16[64,4096]{1,0:T(8,128)(2,1)} %param.4) | copy-start | bytes 1572868
  9.0 49.8 %collective-permute-start.4 = (bf16[32,4096]{1,0:T(8,128)(2,1)}, bf16[32,4096]{1,0:T(8,128)(2,1)S(1)}, u32[]{:S(2)}, u32[]{:S(2)}) collective-permute-start(bf16[32,4096]{1,0:T(8,128)(2,1)} %get-tuple-element.33), channel_id=1, source_target_pairs={{0,2},{2,4},{4,6},{6,0},{1,3},{3,5},{5,7},{7,1},{8,10},{10,12},{12... | collective-permute-start | bytes 786440 | tf_op jit(solution)/shard_map/ppermute | solution.py:15
  13.5 23.4 %collective-permute-start.1 = (bf16[32,4096]{1,0:T(8,128)(2,1)}, bf16[32,4096]{1,0:T(8,128)(2,1)S(1)}, u32[]{:S(2)}, u32[]{:S(2)}) collective-permute-start(bf16[32,4096]{1,0:T(8,128)(2,1)} %get-tuple-element.33), channel_id=1, source_target_pairs={{0,6},{2,0},{4,2},{6,4},{1,7},{3,1},{5,3},{7,5},{8,14},{10,8},{12,... | collective-permute-start | bytes 786440 | tf_op jit(solution)/shard_map/ppermute | solution.py:15
  17.1 42.5 %collective-permute-start.5 = (bf16[32,4096]{1,0:T(8,128)(2,1)S(1)}, bf16[32,4096]{1,0:T(8,128)(2,1)S(1)}, u32[]{:S(2)}, u32[]{:S(2)}) collective-permute-start(bf16[32,4096]{1,0:T(8,128)(2,1)S(1)} %get-tuple-element.34), channel_id=1, source_target_pairs={{0,6},{2,0},{4,2},{6,4},{1,7},{3,1},{5,3},{7,5},{8,14},{10,8},{12,... | collective-permute-start | bytes 786440 | tf_op jit(solution)/shard_map/ppermute | solution.py:15
  21.9 18.0 %collective-permute-start = (bf16[32,4096]{1,0:T(8,128)(2,1)S(1)}, bf16[32,4096]{1,0:T(8,128)(2,1)S(1)}, u32[]{:S(2)}, u32[]{:S(2)}) collective-permute-start(bf16[32,4096]{1,0:T(8,128)(2,1)S(1)} %get-tuple-element.34), channel_id=1, source_target_pairs={{0,2},{2,4},{4,6},{6,0},{1,3},{3,5},{5,7},{7,1},{8,10},{10,12},{12... | collective-permute-start | bytes 786440 | tf_op jit(solution)/shard_map/ppermute | solution.py:15
  27.1 35.1 %copy-start = (bf16[192,4096]{1,0:T(8,128)(2,1)S(1)}, bf16[192,4096]{1,0:T(8,128)(2,1)}, u32[]{:S(2)}) copy-start(bf16[192,4096]{1,0:T(8,128)(2,1)} %head.5) | copy-start | bytes 4718596
  39.9 12.7 %collective-permute-start.2 = (bf16[32,4096]{1,0:T(8,128)(2,1)S(1)}, bf16[32,4096]{1,0:T(8,128)(2,1)S(1)}, u32[]{:S(2)}, u32[]{:S(2)}) collective-permute-start(bf16[32,4096]{1,0:T(8,128)(2,1)S(1)} %collective-permute-done), channel_id=1, source_target_pairs={{0,2},{2,4},{4,6},{6,0},{1,3},{3,5},{5,7},{7,1},{8,10},{10,12},{12... | collective-permute-start | bytes 786440 | tf_op jit(solution)/shard_map/ppermute | solution.py:15
  47.3 10.8 %collective-permute-start.3 = (bf16[32,4096]{1,0:T(8,128)(2,1)S(1)}, bf16[32,4096]{1,0:T(8,128)(2,1)S(1)}, u32[]{:S(2)}, u32[]{:S(2)}) collective-permute-start(bf16[32,4096]{1,0:T(8,128)(2,1)S(1)} %collective-permute-done.1), channel_id=1, source_target_pairs={{0,6},{2,0},{4,2},{6,4},{1,7},{3,1},{5,3},{7,5},{8,14},{10,8},{12,... | collective-permute-start | bytes 786440 | tf_op jit(solution)/shard_map/ppermute | solution.py:15
  60.3 6.3 %collective-permute-start.6 = (bf16[256,4096]{1,0:T(8,128)(2,1)}, bf16[256,4096]{1,0:T(8,128)(2,1)S(1)}, u32[]{:S(2)}, u32[]{:S(2)}) collective-permute-start(bf16[256,4096]{1,0:T(8,128)(2,1)} %bitcast.11.block.own), channel_id=1, source_target_pairs={{0,1},{1,0},{2,3},{3,2},{4,5},{5,4},{6,7},{7,6},{8,9},{9,8},{10,11... | collective-permute-start | bytes 6291464 | tf_op jit(solution)/shard_map/ppermute | solution.py:15
  86.3 6.8 %collective-permute-start.7 = (bf16[256,4096]{1,0:T(8,128)(2,1)}, bf16[256,4096]{1,0:T(8,128)(2,1)}, u32[]{:S(2)}, u32[]{:S(2)}) collective-permute-start(bf16[256,4096]{1,0:T(8,128)(2,1)} %get-tuple-element.30), channel_id=1, source_target_pairs={{0,1},{1,0},{2,3},{3,2},{4,5},{5,4},{6,7},{7,6},{8,9},{9,8},{10,11... | collective-permute-start | bytes 6291464 | tf_op jit(solution)/shard_map/ppermute | solution.py:15
  88.2 24.8 %all-to-all-start.1 = ((bf16[4,48,4096]{2,1,0:T(8,128)(2,1)}), bf16[4,48,4096]{2,1,0:T(8,128)(2,1)S(1)}, u32[]{:S(2)}, u32[]{:S(2)}) async-start(bf16[4,48,4096]{2,1,0:T(8,128)(2,1)} %bitcast.13), calls=%async_computation.1 | async-start | bytes 3145728 | tf_op jit(solution)/shard_map/all_to_all | solution.py:183
  93.1 98.0 %reduce-scatter.2.cloned.1.call-start = ((), (), s32[]{:S(2)}) async-start(), calls=%async_computation.6 | async-start | bytes 2621440 | tf_op jit(solution)/shard_map/reduce_scatter | solution.py:192
  165.2 24.2 %all-to-all-start.4 = ((bf16[4,16,48,256]{3,2,1,0:T(8,128)(2,1)}), bf16[4,16,48,256]{3,2,1,0:T(8,128)(2,1)S(1)}, u32[]{:S(2)}, u32[]{:S(2)}) async-start(bf16[4,16,48,256]{3,2,1,0:T(8,128)(2,1)} %broadcast_in_dim.35), calls=%async_computation.5 | async-start | bytes 3145728 | tf_op jit(solution)/shard_map/all_to_all | solution.py:197
Sparse Core Ops, SparseCore 0:
  113.2 55.5 reduce-scatter.1

commit v6 on v5

--- a/solution.py
+++ b/solution.py
@@ -186,10 +186,19 @@
     home = lax.dot_general(score, head_weight, rows_v, preferred_element_type=F32).astype(BF16)
     terms = (home.astype(F32) + swap(away).astype(F32)).astype(BF16)
 
-    part, terms = lax.optimization_barrier((part, terms))
     part = jnp.sum(part.astype(F32), axis=0).astype(BF16)
     part = part.reshape(v_dev // n_x, n_yl * n_z, -1).transpose(1, 0, 2)
-    grad_hidden = lax.psum_scatter(terms, "yh", scatter_dimension=0, tiled=True)
+
+    terms = terms.reshape(n_yh, tok, width)
+    block = lambda s: lax.dynamic_index_in_dim(terms, (yh + s) % n_yh, 0, False)
+    half, far = tok // 2, block(2)
+    from_below = shift(far[:half], "yh", 1, n_yh)
+    from_above = shift(far[half:], "yh", -1, n_yh)
+    part, from_below, from_above = lax.optimization_barrier((part, from_below, from_above))
+    zero = jnp.zeros((half, width), F32)
+    up = block(1).astype(F32) + jnp.concatenate([from_below.astype(F32), zero], 0)
+    down = block(-1).astype(F32) + jnp.concatenate([zero, from_above.astype(F32)], 0)
+    came = [shift(up.astype(BF16), "yh", 1, n_yh), shift(down.astype(BF16), "yh", -1, n_yh)]
 
     part = lax.all_to_all(part, ("yl", "z"), 0, 0, tiled=True)
     part = jnp.sum(part.astype(F32), axis=0).astype(BF16)
@@ -204,6 +213,7 @@
         compiler_params=params,
         cost_estimate=pl.CostEstimate(flops=0, bytes_accessed=4 * v_dev * width, transcendentals=0),
     )(part)
+    grad_hidden = (block(0).astype(F32) + sum(v.astype(F32) for v in came)).astype(BF16)
     return token_loss, grad_hidden, grad_weight
 
 

time: 199 us -> 183 us (0.920)
  the two profiles are of different devices: /device:TPU:2 before, /device:TPU:72 now
where the time goes in v6:
time: 183 us; the launch traced here: 182 us
  waiting for transfers between devices  55.7 us (30%)
  starting transfers between devices  55.6 us (30%)
  blocking collectives  36.1 us (20%)
  local copies, waits for them, and re-layouts  16.3 us (9%)
  Pallas kernels  10.6 us (6%)
  other arithmetic  4.61 us (3%)
  matrix products  2.34 us (1%)
    ppermute x12, starting transfers between devices, shift(): lax.ppermute(value, axis, [(i, (i + step) % size) for i in range(size)])  43 us
    ppermute x12, waiting for transfers between devices, shift(): lax.ppermute(value, axis, [(i, (i + step) % size) for i in range(size)])  37.7 us
    all_to_all x1, blocking collectives, per_device(): part = lax.all_to_all(part, ('yl', 'z'), 0, 0, tiled=True)  23 us
    all_to_all x1, blocking collectives, per_device(): stats = lax.all_to_all(stats, VOCAB, 0, 0, tiled=True)  13.1 us
    all_to_all x1, waiting for transfers between devices, per_device(): part = lax.all_to_all(part, 'x', 0, 0, tiled=True)  8.78 us
    all_to_all x1, waiting for transfers between devices, per_device(): lax.all_to_all(jnp.broadcast_to(part, (n_x,) + part.shape), 'x', 0, 0, ti...  5.47 us
    pallas_call x1, Pallas kernels, per_device(): pl.pallas_call(score_kernel, out_shape=(jax.ShapeDtypeStruct((v_dev, widt...  4.96 us
    all_to_all x1, starting transfers between devices, per_device(): lax.all_to_all(jnp.broadcast_to(part, (n_yl * n_z,) + part.shape), ('yl',...  4.69 us
  transfers between devices with their start and end apart: 15, of which 10 were waited for; matrix products, arithmetic and copies ran while one was open for 10% of the time, Pallas kernels for 1%

profile of v6, /device:TPU:72, one launch (start us, length us, event | category | flops | bytes accessed | tf_op | source)
XLA Modules:
  0.0 182.2 jit_solution(16869441532337284181)
XLA Ops:
  0.6 1.8 %fusion.7 = (bf16[32,4096]{1,0:T(8,128)(2,1)}, bf16[32,4096]{1,0:T(8,128)(2,1)S(1)}) fusion(bf16[64,4096]{1,0:T(8,128)(2,1)} %param.4), kind=kLoop, calls=%fused_computation.24 | loop fusion | bytes 1048576 | tf_op jit(solution)/shard_map/slice | solution.py:28
  2.5 5.3 %collective-permute-start.1 = (bf16[32,4096]{1,0:T(8,128)(2,1)}, bf16[32,4096]{1,0:T(8,128)(2,1)S(1)}, u32[]{:S(2)}, u32[]{:S(2)}) collective-permute-start(bf16[32,4096]{1,0:T(8,128)(2,1)} %get-tuple-element.39), channel_id=1, source_target_pairs={{0,6},{2,0},{4,2},{6,4},{1,7},{3,1},{5,3},{7,5},{8,14},{10,8},{12,... | collective-permute-start | bytes 786440 | tf_op jit(solution)/shard_map/ppermute | solution.py:15
  7.7 1.9 %collective-permute-start.4 = (bf16[32,4096]{1,0:T(8,128)(2,1)}, bf16[32,4096]{1,0:T(8,128)(2,1)S(1)}, u32[]{:S(2)}, u32[]{:S(2)}) collective-permute-start(bf16[32,4096]{1,0:T(8,128)(2,1)} %get-tuple-element.39), channel_id=1, source_target_pairs={{0,2},{2,4},{4,6},{6,0},{1,3},{3,5},{5,7},{7,1},{8,10},{10,12},{12... | collective-permute-start | bytes 786440 | tf_op jit(solution)/shard_map/ppermute | solution.py:15
  9.7 5.3 %collective-permute-start = (bf16[32,4096]{1,0:T(8,128)(2,1)S(1)}, bf16[32,4096]{1,0:T(8,128)(2,1)S(1)}, u32[]{:S(2)}, u32[]{:S(2)}) collective-permute-start(bf16[32,4096]{1,0:T(8,128)(2,1)S(1)} %get-tuple-element.40), channel_id=1, source_target_pairs={{0,2},{2,4},{4,6},{6,0},{1,3},{3,5},{5,7},{7,1},{8,10},{10,12},{12... | collective-permute-start | bytes 786440 | tf_op jit(solution)/shard_map/ppermute | solution.py:15
  14.9 2.7 %collective-permute-start.5 = (bf16[32,4096]{1,0:T(8,128)(2,1)S(1)}, bf16[32,4096]{1,0:T(8,128)(2,1)S(1)}, u32[]{:S(2)}, u32[]{:S(2)}) collective-permute-start(bf16[32,4096]{1,0:T(8,128)(2,1)S(1)} %get-tuple-element.40), channel_id=1, source_target_pairs={{0,6},{2,0},{4,2},{6,4},{1,7},{3,1},{5,3},{7,5},{8,14},{10,8},{12,... | collective-permute-start | bytes 786440 | tf_op jit(solution)/shard_map/ppermute | solution.py:15
  19.4 1.5 broadcast_in_dim.28
  21.9 14.8 %collective-permute-done = bf16[32,4096]{1,0:T(8,128)(2,1)S(1)} collective-permute-done((bf16[32,4096]{1,0:T(8,128)(2,1)S(1)}, bf16[32,4096]{1,0:T(8,128)(2,1)S(1)}, u32[]{:S(2)}, u32[]{:S(2)}) %collective-permute-start) | collective-permute-done | bytes 262176 | tf_op jit(solution)/shard_map/ppermute | solution.py:15
  36.7 6.3 %collective-permute-start.2 = (bf16[32,4096]{1,0:T(8,128)(2,1)S(1)}, bf16[32,4096]{1,0:T(8,128)(2,1)S(1)}, u32[]{:S(2)}, u32[]{:S(2)}) collective-permute-start(bf16[32,4096]{1,0:T(8,128)(2,1)S(1)} %collective-permute-done), channel_id=1, source_target_pairs={{0,2},{2,4},{4,6},{6,0},{1,3},{3,5},{5,7},{7,1},{8,10},{10,12},{12... | collective-permute-start | bytes 786440 | tf_op jit(solution)/shard_map/ppermute | solution.py:15
  42.9 1.9 %collective-permute-start.3 = (bf16[32,4096]{1,0:T(8,128)(2,1)S(1)}, bf16[32,4096]{1,0:T(8,128)(2,1)S(1)}, u32[]{:S(2)}, u32[]{:S(2)}) collective-permute-start(bf16[32,4096]{1,0:T(8,128)(2,1)S(1)} %collective-permute-done.1), channel_id=1, source_target_pairs={{0,6},{2,0},{4,2},{6,4},{1,7},{3,1},{5,3},{7,5},{8,14},{10,8},{12,... | collective-permute-start | bytes 786440 | tf_op jit(solution)/shard_map/ppermute | solution.py:15
  46.3 2.0 %collective-permute-done.2 = bf16[32,4096]{1,0:T(8,128)(2,1)S(1)} collective-permute-done((bf16[32,4096]{1,0:T(8,128)(2,1)S(1)}, bf16[32,4096]{1,0:T(8,128)(2,1)S(1)}, u32[]{:S(2)}, u32[]{:S(2)}) %collective-permute-start.2) | collective-permute-done | bytes 262176 | tf_op jit(solution)/shard_map/ppermute | solution.py:15
  48.9 6.5 %collective-permute-done.3 = bf16[32,4096]{1,0:T(8,128)(2,1)S(1)} collective-permute-done((bf16[32,4096]{1,0:T(8,128)(2,1)S(1)}, bf16[32,4096]{1,0:T(8,128)(2,1)S(1)}, u32[]{:S(2)}, u32[]{:S(2)}) %collective-permute-start.3) | collective-permute-done | bytes 262176 | tf_op jit(solution)/shard_map/ppermute | solution.py:15
  57.6 1.9 %collective-permute-start.6 = (bf16[256,4096]{1,0:T(8,128)(2,1)}, bf16[256,4096]{1,0:T(8,128)(2,1)S(1)}, u32[]{:S(2)}, u32[]{:S(2)}) collective-permute-start(bf16[256,4096]{1,0:T(8,128)(2,1)} %bitcast.11.block.own), channel_id=1, source_target_pairs={{0,1},{1,0},{2,3},{3,2},{4,5},{5,4},{6,7},{7,6},{8,9},{9,8},{10,11... | collective-permute-start | bytes 6291464 | tf_op jit(solution)/shard_map/ppermute | solution.py:15
  59.5 2.5 %shard_map.67 = (f32[192,256]{1,0:T(8,128)S(1)}, f32[8,256]{1,0:T(8,128)S(1)}) custom-call(s32[2]{0:T(128)S(1)} %pad_add_fusion.where, bf16[192,4096]{1,0:T(8,128)(2,1)S(1)} %copy-done, bf16[256,4096]{1,0:T(8,128)(2,1)} %bitcast.11.block.own, s32[2,256]{1,0:T(2,128)S(1)} %reshape.43.labels), custom_call_target="tpu_custom_call" | custom-call | flops 402653184 | bytes 3670016 | tf_op jit(solution)/shard_map/pallas_call | solution.py:130
  62.0 1.8 %collective-permute-done.6.block.other = bf16[256,4096]{1,0:T(8,128)(2,1)S(1)} collective-permute-done((bf16[256,4096]{1,0:T(8,128)(2,1)}, bf16[256,4096]{1,0:T(8,128)(2,1)S(1)}, u32[]{:S(2)}, u32[]{:S(2)}) %collective-permute-start.6) | collective-permute-done | bytes 2097184 | tf_op jit(solution)/shard_map/ppermute | solution.py:15
  65.3 13.1 %all_to_all.25.stats = f32[8,8,256]{2,1,0:T(8,128)S(1)} all-to-all(f32[8,8,256]{2,1,0:T(8,128)S(1)} %get-tuple-element.24), channel_id=1, replica_groups=mesh['x'=4,'yl'=2,'z'=8,'yh'=4,'core'=2] {'yh','core'}, dimensions={0} | all-to-all | bytes 131072 | tf_op jit(solution)/shard_map/all_to_all | solution.py:146
  78.4 5.0 %shard_map.69 = (bf16[192,4096]{1,0:T(8,128)(2,1)}, bf16[256,4096]{1,0:T(8,128)(2,1)}, bf16[192,256]{1,0:T(8,128)(2,1)S(1)}, f32[1,256]{1,0:T(1,128)S(1)}) custom-call(s32[2]{0:T(128)S(1)} %pad_add_fusion.where, f32[8,8,256]{2,1,0:T(8,128)S(1)} %all_to_all.25.stats, s32[2,256]{1,0:T(2,128)S(1)} %reshape.43.labels, f32[2,256]{1,0:T(2,128)S(1)} %reshape.45.weights, ...), custom_call_target="tpu_custom_call" | custom-call | flops 1207959552 | bytes 9437184 | tf_op jit(solution)/shard_map/pallas_call | solution.py:151
  83.4 1.9 %collective-permute-start.7 = (bf16[256,4096]{1,0:T(8,128)(2,1)}, bf16[256,4096]{1,0:T(8,128)(2,1)}, u32[]{:S(2)}, u32[]{:S(2)}) collective-permute-start(bf16[256,4096]{1,0:T(8,128)(2,1)} %get-tuple-element.30), channel_id=1, source_target_pairs={{0,1},{1,0},{2,3},{3,2},{4,5},{5,4},{6,7},{7,6},{8,9},{9,8},{10,11... | collective-permute-start | bytes 6291464 | tf_op jit(solution)/shard_map/ppermute | solution.py:15
  85.3 4.3 %all-to-all-start.1 = ((bf16[4,48,4096]{2,1,0:T(8,128)(2,1)}), bf16[4,48,4096]{2,1,0:T(8,128)(2,1)S(1)}, u32[]{:S(2)}, u32[]{:S(2)}) async-start(bf16[4,48,4096]{2,1,0:T(8,128)(2,1)} %bitcast.16), calls=%async_computation.1 | async-start | bytes 3145728 | tf_op jit(solution)/shard_map/all_to_all | solution.py:183
  89.8 2.3 %fusion.2 = bf16[256,4096]{1,0:T(8,128)(2,1)S(1)} fusion(bf16[192,256]{1,0:T(8,128)(2,1)S(1)} %get-tuple-element.29, bf16[192,4096]{1,0:T(8,128)(2,1)S(1)} %copy-done, bf16[256,4096]{1,0:T(8,128)(2,1)} %collective-permute-done.7), kind=kOutput, calls=%fused_computation.3 | convolution fusion | flops 407896064 | bytes 5865472 | tf_op jit(solution)/shard_map/dot_general | solution.py:186
  94.2 2.3 %collective-permute-start.8 = (bf16[32,4096]{1,0:T(8,128)(2,1)}, bf16[32,4096]{1,0:T(8,128)(2,1)S(1)}, u32[]{:S(2)}, u32[]{:S(2)}) collective-permute-start(bf16[32,4096]{1,0:T(8,128)(2,1)} %get-tuple-element.38), channel_id=1, source_target_pairs={{0,2},{2,4},{4,6},{6,0},{1,3},{3,5},{5,7},{7,1},{8,10},{10,12},{12... | collective-permute-start | bytes 786440 | tf_op jit(solution)/shard_map/ppermute | solution.py:15
  96.6 5.6 %collective-permute-start.9 = (bf16[32,4096]{1,0:T(8,128)(2,1)}, bf16[32,4096]{1,0:T(8,128)(2,1)}, u32[]{:S(2)}, u32[]{:S(2)}) collective-permute-start(bf16[32,4096]{1,0:T(8,128)(2,1)} %get-tuple-element.37), channel_id=1, source_target_pairs={{0,6},{2,0},{4,2},{6,4},{1,7},{3,1},{5,3},{7,5},{8,14},{10,8},{12,... | collective-permute-start | bytes 786440 | tf_op jit(solution)/shard_map/ppermute | solution.py:15
  102.2 8.8 %all-to-all-done.1 = bf16[4,48,4096]{2,1,0:T(8,128)(2,1)S(1)} async-done(((bf16[4,48,4096]{2,1,0:T(8,128)(2,1)}), bf16[4,48,4096]{2,1,0:T(8,128)(2,1)S(1)}, u32[]{:S(2)}, u32[]{:S(2)}) %all-to-all-start.1) | async-done | bytes 1572896 | tf_op jit(solution)/shard_map/all_to_all | solution.py:183
  113.4 23.0 %all_to_all.26 = bf16[16,48,256]{2,1,0:T(8,128)(2,1)S(1)} all-to-all(bf16[16,48,256]{2,1,0:T(8,128)(2,1)S(1)} %copy.13), channel_id=1, replica_groups=mesh['x'=4,'yl'=2,'z'=8,'yh'=4,'core'=2] {'yl','z'}, dimensions={0} | all-to-all | bytes 786432 | tf_op jit(solution)/shard_map/all_to_all | solution.py:203
  137.3 4.7 %all-to-all-start.3 = ((bf16[16,48,256]{2,1,0:T(8,128)(2,1)}), bf16[16,48,256]{2,1,0:T(8,128)(2,1)S(1)}, u32[]{:S(2)}, u32[]{:S(2)}) async-start(bf16[16,48,256]{2,1,0:T(8,128)(2,1)} %broadcast_in_dim.35), calls=%async_computation.3 | async-start | bytes 786432 | tf_op jit(solution)/shard_map/all_to_all | solution.py:205
  143.2 2.4 %collective-permute-start.10 = (bf16[64,4096]{1,0:T(8,128)(2,1)S(1)}, bf16[64,4096]{1,0:T(8,128)(2,1)S(1)}, u32[]{:S(2)}, u32[]{:S(2)}) collective-permute-start(bf16[64,4096]{1,0:T(8,128)(2,1)S(1)} %get-tuple-element.35), channel_id=1, source_target_pairs={{0,2},{2,4},{4,6},{6,0},{1,3},{3,5},{5,7},{7,1},{8,10},{10,12},{12... | collective-permute-start | bytes 1572872 | tf_op jit(solution)/shard_map/ppermute | solution.py:15
  145.5 5.6 %collective-permute-start.11 = (bf16[64,4096]{1,0:T(8,128)(2,1)S(1)}, bf16[64,4096]{1,0:T(8,128)(2,1)}, u32[]{:S(2)}, u32[]{:S(2)}) collective-permute-start(bf16[64,4096]{1,0:T(8,128)(2,1)S(1)} %get-tuple-element.36), channel_id=1, source_target_pairs={{0,6},{2,0},{4,2},{6,4},{1,7},{3,1},{5,3},{7,5},{8,14},{10,8},{12,... | collective-permute-start | bytes 1572872 | tf_op jit(solution)/shard_map/ppermute | solution.py:15
  151.1 3.8 %all-to-all-done.3 = bf16[16,48,256]{2,1,0:T(8,128)(2,1)S(1)} async-done(((bf16[16,48,256]{2,1,0:T(8,128)(2,1)}), bf16[16,48,256]{2,1,0:T(8,128)(2,1)S(1)}, u32[]{:S(2)}, u32[]{:S(2)}) %all-to-all-start.3) | async-done | bytes 393248 | tf_op jit(solution)/shard_map/all_to_all | solution.py:205
  156.2 3.6 %all-to-all-start.4 = ((bf16[4,16,48,256]{3,2,1,0:T(8,128)(2,1)}), bf16[4,16,48,256]{3,2,1,0:T(8,128)(2,1)S(1)}, u32[]{:S(2)}, u32[]{:S(2)}) async-start(bf16[4,16,48,256]{3,2,1,0:T(8,128)(2,1)} %broadcast_in_dim.36), calls=%async_computation.4 | async-start | bytes 3145728 | tf_op jit(solution)/shard_map/all_to_all | solution.py:206
  160.3 11.4 %collective-permute-done.10 = bf16[64,4096]{1,0:T(8,128)(2,1)S(1)} collective-permute-done((bf16[64,4096]{1,0:T(8,128)(2,1)S(1)}, bf16[64,4096]{1,0:T(8,128)(2,1)S(1)}, u32[]{:S(2)}, u32[]{:S(2)}) %collective-permute-start.10) | collective-permute-done | bytes 524320 | tf_op jit(solution)/shard_map/ppermute | solution.py:15
  172.8 2.2 %fusion.5 = bf16[64,4096]{1,0:T(8,128)(2,1)} fusion(bf16[64,4096]{1,0:T(8,128)(2,1)} %collective-permute-done.11, bf16[64,4096]{1,0:T(8,128)(2,1)S(1)} %collective-permute-done.10, bf16[4,64,4096]{2,1,0:T(8,128)(2,1)} %bitcast.44, s32[]{:T(128)S(6)} %select_n.76), kind=kLoop, calls=%fused_computation.9 | loop fusion | flops 1572864 | bytes 2097156 | tf_op jit(solution)/shard_map/convert_element_type | solution.py:216
  175.0 5.5 %all-to-all-done.4.pieces = bf16[4,16,48,256]{3,2,1,0:T(8,128)(2,1)S(1)} async-done(((bf16[4,16,48,256]{3,2,1,0:T(8,128)(2,1)}), bf16[4,16,48,256]{3,2,1,0:T(8,128)(2,1)S(1)}, u32[]{:S(2)}, u32[]{:S(2)}) %all-to-all-start.4) | async-done | bytes 1572896 | tf_op jit(solution)/shard_map/all_to_all | solution.py:206
  180.5 1.7 shard_map.70
  (45 shorter events, 18.2 us)
Async XLA Ops:
  0.6 20.3 %copy-start.3 = (bf16[64,4096]{1,0:T(8,128)(2,1)S(1)}, bf16[64,4096]{1,0:T(8,128)(2,1)}, u32[]{:S(2)}) copy-start(bf16[64,4096]{1,0:T(8,128)(2,1)} %param.4) | copy-start | bytes 1572868
  2.5 34.2 %collective-permute-start.1 = (bf16[32,4096]{1,0:T(8,128)(2,1)}, bf16[32,4096]{1,0:T(8,128)(2,1)S(1)}, u32[]{:S(2)}, u32[]{:S(2)}) collective-permute-start(bf16[32,4096]{1,0:T(8,128)(2,1)} %get-tuple-element.39), channel_id=1, source_target_pairs={{0,6},{2,0},{4,2},{6,4},{1,7},{3,1},{5,3},{7,5},{8,14},{10,8},{12,... | collective-permute-start | bytes 786440 | tf_op jit(solution)/shard_map/ppermute | solution.py:15
  7.7 48.4 %collective-permute-start.4 = (bf16[32,4096]{1,0:T(8,128)(2,1)}, bf16[32,4096]{1,0:T(8,128)(2,1)S(1)}, u32[]{:S(2)}, u32[]{:S(2)}) collective-permute-start(bf16[32,4096]{1,0:T(8,128)(2,1)} %get-tuple-element.39), channel_id=1, source_target_pairs={{0,2},{2,4},{4,6},{6,0},{1,3},{3,5},{5,7},{7,1},{8,10},{10,12},{12... | collective-permute-start | bytes 786440 | tf_op jit(solution)/shard_map/ppermute | solution.py:15
  9.7 27.0 %collective-permute-start = (bf16[32,4096]{1,0:T(8,128)(2,1)S(1)}, bf16[32,4096]{1,0:T(8,128)(2,1)S(1)}, u32[]{:S(2)}, u32[]{:S(2)}) collective-permute-start(bf16[32,4096]{1,0:T(8,128)(2,1)S(1)} %get-tuple-element.40), channel_id=1, source_target_pairs={{0,2},{2,4},{4,6},{6,0},{1,3},{3,5},{5,7},{7,1},{8,10},{10,12},{12... | collective-permute-start | bytes 786440 | tf_op jit(solution)/shard_map/ppermute | solution.py:15
  14.9 41.9 %collective-permute-start.5 = (bf16[32,4096]{1,0:T(8,128)(2,1)S(1)}, bf16[32,4096]{1,0:T(8,128)(2,1)S(1)}, u32[]{:S(2)}, u32[]{:S(2)}) collective-permute-start(bf16[32,4096]{1,0:T(8,128)(2,1)S(1)} %get-tuple-element.40), channel_id=1, source_target_pairs={{0,6},{2,0},{4,2},{6,4},{1,7},{3,1},{5,3},{7,5},{8,14},{10,8},{12,... | collective-permute-start | bytes 786440 | tf_op jit(solution)/shard_map/ppermute | solution.py:15
  20.9 38.6 %copy-start = (bf16[192,4096]{1,0:T(8,128)(2,1)S(1)}, bf16[192,4096]{1,0:T(8,128)(2,1)}, u32[]{:S(2)}) copy-start(bf16[192,4096]{1,0:T(8,128)(2,1)} %head.5) | copy-start | bytes 4718596
  36.7 11.6 %collective-permute-start.2 = (bf16[32,4096]{1,0:T(8,128)(2,1)S(1)}, bf16[32,4096]{1,0:T(8,128)(2,1)S(1)}, u32[]{:S(2)}, u32[]{:S(2)}) collective-permute-start(bf16[32,4096]{1,0:T(8,128)(2,1)S(1)} %collective-permute-done), channel_id=1, source_target_pairs={{0,2},{2,4},{4,6},{6,0},{1,3},{3,5},{5,7},{7,1},{8,10},{10,12},{12... | collective-permute-start | bytes 786440 | tf_op jit(solution)/shard_map/ppermute | solution.py:15
  42.9 12.5 %collective-permute-start.3 = (bf16[32,4096]{1,0:T(8,128)(2,1)S(1)}, bf16[32,4096]{1,0:T(8,128)(2,1)S(1)}, u32[]{:S(2)}, u32[]{:S(2)}) collective-permute-start(bf16[32,4096]{1,0:T(8,128)(2,1)S(1)} %collective-permute-done.1), channel_id=1, source_target_pairs={{0,6},{2,0},{4,2},{6,4},{1,7},{3,1},{5,3},{7,5},{8,14},{10,8},{12,... | collective-permute-start | bytes 786440 | tf_op jit(solution)/shard_map/ppermute | solution.py:15
  57.6 6.3 %collective-permute-start.6 = (bf16[256,4096]{1,0:T(8,128)(2,1)}, bf16[256,4096]{1,0:T(8,128)(2,1)S(1)}, u32[]{:S(2)}, u32[]{:S(2)}) collective-permute-start(bf16[256,4096]{1,0:T(8,128)(2,1)} %bitcast.11.block.own), channel_id=1, source_target_pairs={{0,1},{1,0},{2,3},{3,2},{4,5},{5,4},{6,7},{7,6},{8,9},{9,8},{10,11... | collective-permute-start | bytes 6291464 | tf_op jit(solution)/shard_map/ppermute | solution.py:15
  83.4 6.4 %collective-permute-start.7 = (bf16[256,4096]{1,0:T(8,128)(2,1)}, bf16[256,4096]{1,0:T(8,128)(2,1)}, u32[]{:S(2)}, u32[]{:S(2)}) collective-permute-start(bf16[256,4096]{1,0:T(8,128)(2,1)} %get-tuple-element.30), channel_id=1, source_target_pairs={{0,1},{1,0},{2,3},{3,2},{4,5},{5,4},{6,7},{7,6},{8,9},{9,8},{10,11... | collective-permute-start | bytes 6291464 | tf_op jit(solution)/shard_map/ppermute | solution.py:15
  85.3 25.7 %all-to-all-start.1 = ((bf16[4,48,4096]{2,1,0:T(8,128)(2,1)}), bf16[4,48,4096]{2,1,0:T(8,128)(2,1)S(1)}, u32[]{:S(2)}, u32[]{:S(2)}) async-start(bf16[4,48,4096]{2,1,0:T(8,128)(2,1)} %bitcast.16), calls=%async_computation.1 | async-start | bytes 3145728 | tf_op jit(solution)/shard_map/all_to_all | solution.py:183
  92.1 1.3 copy-start.1
  94.2 19.0 %collective-permute-start.8 = (bf16[32,4096]{1,0:T(8,128)(2,1)}, bf16[32,4096]{1,0:T(8,128)(2,1)S(1)}, u32[]{:S(2)}, u32[]{:S(2)}) collective-permute-start(bf16[32,4096]{1,0:T(8,128)(2,1)} %get-tuple-element.38), channel_id=1, source_target_pairs={{0,2},{2,4},{4,6},{6,0},{1,3},{3,5},{5,7},{7,1},{8,10},{10,12},{12... | collective-permute-start | bytes 786440 | tf_op jit(solution)/shard_map/ppermute | solution.py:15
  96.6 16.7 %collective-permute-start.9 = (bf16[32,4096]{1,0:T(8,128)(2,1)}, bf16[32,4096]{1,0:T(8,128)(2,1)}, u32[]{:S(2)}, u32[]{:S(2)}) collective-permute-start(bf16[32,4096]{1,0:T(8,128)(2,1)} %get-tuple-element.37), channel_id=1, source_target_pairs={{0,6},{2,0},{4,2},{6,4},{1,7},{3,1},{5,3},{7,5},{8,14},{10,8},{12,... | collective-permute-start | bytes 786440 | tf_op jit(solution)/shard_map/ppermute | solution.py:15
  112.1 29.9 %copy-start.2 = (bf16[256,4096]{1,0:T(8,128)(2,1)S(1)}, bf16[256,4096]{1,0:T(8,128)(2,1)}, u32[]{:S(2)}) copy-start(bf16[256,4096]{1,0:T(8,128)(2,1)} %copy-done.1) | copy-start | bytes 6291460
  113.3 24.0 %copy-start.4 = (bf16[32,4096]{1,0:T(8,128)(2,1)}, bf16[32,4096]{1,0:T(8,128)(2,1)S(1)}, u32[]{:S(2)}) copy-start(bf16[32,4096]{1,0:T(8,128)(2,1)S(1)} %collective-permute-done.8) | copy-start | bytes 786436
  137.3 17.6 %all-to-all-start.3 = ((bf16[16,48,256]{2,1,0:T(8,128)(2,1)}), bf16[16,48,256]{2,1,0:T(8,128)(2,1)S(1)}, u32[]{:S(2)}, u32[]{:S(2)}) async-start(bf16[16,48,256]{2,1,0:T(8,128)(2,1)} %broadcast_in_dim.35), calls=%async_computation.3 | async-start | bytes 786432 | tf_op jit(solution)/shard_map/all_to_all | solution.py:205
  143.2 28.5 %collective-permute-start.10 = (bf16[64,4096]{1,0:T(8,128)(2,1)S(1)}, bf16[64,4096]{1,0:T(8,128)(2,1)S(1)}, u32[]{:S(2)}, u32[]{:S(2)}) collective-permute-start(bf16[64,4096]{1,0:T(8,128)(2,1)S(1)} %get-tuple-element.35), channel_id=1, source_target_pairs={{0,2},{2,4},{4,6},{6,0},{1,3},{3,5},{5,7},{7,1},{8,10},{10,12},{12... | collective-permute-start | bytes 1572872 | tf_op jit(solution)/shard_map/ppermute | solution.py:15
  145.5 27.3 %collective-permute-start.11 = (bf16[64,4096]{1,0:T(8,128)(2,1)S(1)}, bf16[64,4096]{1,0:T(8,128)(2,1)}, u32[]{:S(2)}, u32[]{:S(2)}) collective-permute-start(bf16[64,4096]{1,0:T(8,128)(2,1)S(1)} %get-tuple-element.36), channel_id=1, source_target_pairs={{0,6},{2,0},{4,2},{6,4},{1,7},{3,1},{5,3},{7,5},{8,14},{10,8},{12,... | collective-permute-start | bytes 1572872 | tf_op jit(solution)/shard_map/ppermute | solution.py:15
  156.2 24.3 %all-to-all-start.4 = ((bf16[4,16,48,256]{3,2,1,0:T(8,128)(2,1)}), bf16[4,16,48,256]{3,2,1,0:T(8,128)(2,1)S(1)}, u32[]{:S(2)}, u32[]{:S(2)}) async-start(bf16[4,16,48,256]{3,2,1,0:T(8,128)(2,1)} %broadcast_in_dim.36), calls=%async_computation.4 | async-start | bytes 3145728 | tf_op jit(solution)/shard_map/all_to_all | solution.py:206

commit v7 on v6

v7 whole, which is shorter than its diff:
```python
import jax
import jax.numpy as jnp
from jax import lax
from jax.experimental import pallas as pl
from jax.experimental.pallas import tpu as pltpu
from jax.sharding import Mesh
from jax.sharding import PartitionSpec as P

F32, BF16 = jnp.float32, jnp.bfloat16
DP = ("x", "yl", "z")
VOCAB = ("yh", "core")


def shift(value, axis, step, size):
    return lax.ppermute(value, axis, [(i, (i + step) % size) for i in range(size)])


def swap(value):
    return shift(value, "core", 1, 2)


def hits(where, labels, shape):
    return lax.broadcasted_iota(jnp.int32, shape, 0) + where[1] == labels


def block_stats(where, head, pieces, labels, logits):
    rows_t = (((1,), (1,)), ((), ()))
    block = jnp.concatenate([piece[...] for piece in pieces], axis=0)
    value = lax.dot_general(head[...], block, rows_t, preferred_element_type=F32)
    logits[...] = value
    top = jnp.max(value, axis=0, keepdims=True)
    total = jnp.sum(jnp.exp(value - top), axis=0, keepdims=True)
    target = jnp.sum(jnp.where(hits(where, labels, value.shape), value, 0.0), axis=0, keepdims=True)
    blank = jnp.zeros_like(top)
    tile = jnp.concatenate([top, total, target] + [blank] * 5, axis=0)
    return jnp.where(where[0] == 0, tile, pltpu.roll(tile, tile.shape[1] // 2, 1))


def near_kernel(where, head, labels, *refs):
    pieces, logits, stats = refs[:6], refs[6:9], refs[9]
    n = logits[0].shape[1]
    for m in range(3):
        lanes = slice(m * n, (m + 1) * n)
        stats[:, lanes] = block_stats(where, head, pieces[2 * m : 2 * m + 2], labels[:, lanes], logits[m])


def far_kernel(where, head, labels, near, *refs):
    pieces, logits, stats = refs[:4], refs[4], refs[5]
    n = logits.shape[1]
    tiles = [near[:, m * n : (m + 1) * n] for m in range(3)]
    tiles.append(block_stats(where, head, pieces, labels[:, 3 * n :], logits))
    for m, tile in enumerate(tiles):
        at = pl.multiple_of(where[2 + m] * 8, 8)
        for shard in range(stats.shape[0]):
            stats[shard, pl.ds(at, 8), :] = tile


def score_kernel(where, stats, labels, weights, *refs):
    all_logits, pieces, head = refs[:4], refs[4:14], refs[14]
    grad, away, score, loss, held, turned = refs[15:]
    n = all_logits[0].shape[1]
    half = n // 2

    @pl.when(pl.program_id(0) == 0)
    def _():
        for m, logits in enumerate(all_logits):
            lanes = slice(m * n, (m + 1) * n)
            part = stats[:, pl.ds(pl.multiple_of(where[2 + m] * 8, 8), 8), :]
            tops = part[:, 0, :]
            top = jnp.max(tops, axis=0, keepdims=True)
            total = jnp.sum(part[:, 1, :] * jnp.exp(tops - top), axis=0, keepdims=True)
            log_total = top + jnp.log(total)
            lost = log_total - jnp.sum(part[:, 2, :], axis=0, keepdims=True)
            both = jnp.concatenate([log_total, lost] + [jnp.zeros_like(top)] * 6, axis=0)
            both = jnp.where(where[0] == 0, both, pltpu.roll(both, half, 1))
            if m == 0:
                loss[...] = both[1:2]
            hit = hits(where, labels[:, lanes], logits.shape).astype(F32)
            value = weights[:, lanes] * (jnp.exp(logits[...] - both[0:1]) - hit)
            held[:, lanes] = value.astype(BF16)
            value = value.T.astype(BF16)
            score[m * half : (m + 1) * half] = value[:half]
            turned[m * half : (m + 1) * half] = value[half:]

    block = jnp.concatenate([piece[...] for piece in pieces], axis=0)
    grad[...] = jnp.dot(held[...], block, preferred_element_type=F32).astype(BF16)
    away[...] = jnp.dot(turned[...], head[...], preferred_element_type=F32).astype(BF16)


def lay_kernel(pieces, out):
    cols = pieces.shape[3]
    for i in range(pieces.shape[1]):
        out[:, i * cols : (i + 1) * cols] = pieces[0, i]


def per_device(hidden, targets, token_weight, head_weight, *, n_x, n_yl, n_z, n_yh):
    yh, core = lax.axis_index("yh"), lax.axis_index("core")
    tok, width = hidden.shape
    v_dev = head_weight.shape[0]
    half, both, n_own, n_shards = tok // 2, 2 * tok, n_yh * tok, 2 * n_yh

    def local_order(value):
        value = value.reshape(n_yh, 2, tok)
        value = lax.dynamic_slice_in_dim(jnp.concatenate([value, value], 0), yh, n_yh, 0)
        value = jnp.where(core == 0, value, value[:, ::-1])
        return jnp.concatenate([value[0], value[3], value[1], value[2]], 0).reshape(1, -1)

    labels, weights = local_order(targets), local_order(token_weight)
    where = jnp.stack([core, (yh * 2 + core) * v_dev] + [(yh + d) % n_yh for d in (0, n_yh - 1, 1, 2)])

    before = shift(hidden, "yh", 1, n_yh)
    after = shift(hidden, "yh", -1, n_yh)
    own_other = swap(hidden)
    before, labels, weights, where = lax.optimization_barrier((before, labels, weights, where))
    low, high, before, after = lax.optimization_barrier((before[:half], after[half:], before, after))
    far_low = shift(low, "yh", 1, n_yh)
    far_high = shift(high, "yh", -1, n_yh)
    near = (hidden, own_other, before, swap(before), after, swap(after))

    smem, vmem = pl.BlockSpec(memory_space=pltpu.SMEM), pl.BlockSpec(memory_space=pltpu.VMEM)
    params = pltpu.CompilerParams(vmem_limit_bytes=32 << 20)
    block_logits = jax.ShapeDtypeStruct((v_dev, both), F32)

    def cost(blocks):
        return pl.CostEstimate(
            flops=2 * v_dev * blocks * both * width,
            bytes_accessed=2 * (v_dev + blocks * both) * width,
            transcendentals=v_dev * blocks * both,
        )

    *near_logits, stats = pl.pallas_call(
        near_kernel,
        out_shape=(block_logits,) * 3 + (jax.ShapeDtypeStruct((8, 3 * both), F32),),
        in_specs=[smem] + [vmem] * 8,
        out_specs=(vmem,) * 4,
        compiler_params=params,
        cost_estimate=cost(3),
    )(where, head_weight, labels, *near)
    far_low, far_high, *near_logits, stats = lax.optimization_barrier((far_low, far_high, *near_logits, stats))
    far = (far_low, far_high, swap(far_low), swap(far_high))
    far_logits, stats = pl.pallas_call(
        far_kernel,
        out_shape=(block_logits, jax.ShapeDtypeStruct((n_shards, 8 * n_yh, both), F32)),
        in_specs=[smem] + [vmem] * 7,
        out_specs=(vmem,) * 2,
        compiler_params=params,
        cost_estimate=cost(1),
    )(where, head_weight, labels, stats, *far)
    stats = lax.all_to_all(stats, VOCAB, 0, 0, tiled=True)

    cols = min(1024, width)
    whole = lambda *shape: pl.BlockSpec(shape, lambda i: (0,) * len(shape))
    wide = lambda rows: pl.BlockSpec((rows, cols), lambda i: (0, i))
    partial, away, score, loss = pl.pallas_call(
        score_kernel,
        out_shape=(
            jax.ShapeDtypeStruct((v_dev, width), BF16),
            jax.ShapeDtypeStruct((n_own, width), BF16),
            jax.ShapeDtypeStruct((n_own, v_dev), BF16),
            jax.ShapeDtypeStruct((1, both), F32),
        ),
        grid=(width // cols,),
        in_specs=[smem, whole(*stats.shape), whole(1, 2 * n_own), whole(1, 2 * n_own)]
        + [whole(v_dev, both)] * 4
        + [wide(tok)] * 6
        + [wide(half)] * 4
        + [wide(v_dev)],
        out_specs=(wide(v_dev), wide(n_own), whole(n_own, v_dev), whole(1, both)),
        scratch_shapes=[pltpu.VMEM((v_dev, 2 * n_own), BF16), pltpu.VMEM((n_own, v_dev), BF16)],
        compiler_params=params,
        cost_estimate=pl.CostEstimate(
            flops=6 * v_dev * n_own * width,
            bytes_accessed=2 * (2 * v_dev + 3 * n_own) * width,
            transcendentals=2 * v_dev * n_own,
        ),
    )(where, stats, labels, weights, *near_logits, far_logits, *near, *far, head_weight)
    token_loss = loss[0, :tok]

    part = partial.reshape(n_x, v_dev // n_x, width)
    part = lax.all_to_all(part, "x", 0, 0, tiled=True)

    home = jnp.dot(score, head_weight, preferred_element_type=F32).astype(BF16)
    terms = (home.astype(F32) + swap(away).astype(F32)).astype(BF16)
    part = jnp.sum(part.astype(F32), axis=0).astype(BF16)
    part = part.reshape(v_dev // n_x, n_yl * n_z, -1).transpose(1, 0, 2)

    mine, up, down, far = (terms[m * tok : (m + 1) * tok] for m in (0, 2, 1, 3))
    from_below = shift(far[:half], "yh", 1, n_yh)
    from_above = shift(far[half:], "yh", -1, n_yh)
    part, from_below, from_above = lax.optimization_barrier((part, from_below, from_above))
    zero = jnp.zeros((half, width), F32)
    up = up.astype(F32) + jnp.concatenate([from_below.astype(F32), zero], 0)
    down = down.astype(F32) + jnp.concatenate([zero, from_above.astype(F32)], 0)
    came = [shift(up.astype(BF16), "yh", 1, n_yh), shift(down.astype(BF16), "yh", -1, n_yh)]

    part = lax.all_to_all(part, ("yl", "z"), 0, 0, tiled=True)
    part = jnp.sum(part.astype(F32), axis=0).astype(BF16)
    part = lax.all_to_all(jnp.broadcast_to(part, (n_yl * n_z,) + part.shape), ("yl", "z"), 0, 0, tiled=True)
    part = lax.all_to_all(jnp.broadcast_to(part, (n_x,) + part.shape), "x", 0, 0, tiled=True)
    grad_weight = pl.pallas_call(
        lay_kernel,
        out_shape=jax.ShapeDtypeStruct((v_dev, width), BF16),
        grid=(n_x,),
        in_specs=[pl.BlockSpec((1,) + part.shape[1:], lambda i: (i, 0, 0, 0))],
        out_specs=pl.BlockSpec((v_dev // n_x, width), lambda i: (i, 0)),
        compiler_params=params,
        cost_estimate=pl.CostEstimate(flops=0, bytes_accessed=4 * v_dev * width, transcendentals=0),
    )(part)
    grad_hidden = (mine.astype(F32) + sum(v.astype(F32) for v in came)).astype(BF16)
    return token_loss, grad_hidden, grad_weight


def fine(mesh_devices, sizes):
    mesh = Mesh(mesh_devices.reshape(sizes), ("x", "yl", "z", "yh", "core"))

    def body(*args):
        return per_device(*args, n_x=sizes[0], n_yl=sizes[1], n_z=sizes[2], n_yh=sizes[3])

    tokens = ("x", "yl", "z", "yh", "core")
    return jax.shard_map(
        body,
        mesh=mesh,
        in_specs=(P(tokens, None), P(DP), P(DP), P(VOCAB, None)),
        out_specs=(P(tokens), P(tokens, None), P(VOCAB, None)),
        check_vma=False,
    )


def solution(mesh):
    return fine(mesh.devices, (4, 2, 8, 4, 2))
```

time: 183 us -> 181 us (0.989)
  waiting for transfers between devices: 55.7 us -> 64.6 us
  local copies, waits for them, and re-layouts: 16.3 us -> 8.41 us
    ppermute x12 -> x14, waiting for transfers between devices: 37.7 us -> 43.6 us  [shift(): lax.ppermute(value, axis, [(i, (i + step) % size) for i in range(size)])]
    dynamic_update_slice x7 -> x0, local copies, waits for them, and re-layouts: 5.11 us -> none  [the longest x6 4.29 us: gather_yh(): out = lax.dynamic_update_slice(out, piece[None, None], (owner, part, 0, 0))]
    all_to_all x1, waiting for transfers between devices: 8.78 us -> 10.8 us  [per_device(): part = lax.all_to_all(part, 'x', 0, 0, tiled=True)]
    ppermute x12 -> x14, starting transfers between devices: 43 us -> 42.4 us  [shift(): lax.ppermute(value, axis, [(i, (i + step) % size) for i in range(size)])]
  transfers between devices with their start and end apart: 15 -> 17, of which waited for: 10 -> 9; matrix products, arithmetic and copies ran while one was open for 10% -> 6% of each run, Pallas kernels for 1% -> 1%
where the time goes in v7:
time: 181 us; the launch traced here: 180 us
  waiting for transfers between devices  64.6 us (36%)
  starting transfers between devices  55.4 us (31%)
  blocking collectives  35 us (19%)
  Pallas kernels  9.39 us (5%)
  local copies, waits for them, and re-layouts  8.41 us (5%)
  other arithmetic  3.98 us (2%)
  matrix products  2.29 us (1%)
    ppermute x14, waiting for transfers between devices, shift(): lax.ppermute(value, axis, [(i, (i + step) % size) for i in range(size)])  43.6 us
    ppermute x14, starting transfers between devices, shift(): lax.ppermute(value, axis, [(i, (i + step) % size) for i in range(size)])  42.4 us
    all_to_all x1, blocking collectives, per_device(): part = lax.all_to_all(part, ('yl', 'z'), 0, 0, tiled=True)  23 us
    all_to_all x1, blocking collectives, per_device(): stats = lax.all_to_all(stats, VOCAB, 0, 0, tiled=True)  12.1 us
    all_to_all x1, waiting for transfers between devices, per_device(): part = lax.all_to_all(part, 'x', 0, 0, tiled=True)  10.8 us
    all_to_all x1, waiting for transfers between devices, per_device(): lax.all_to_all(jnp.broadcast_to(part, (n_x,) + part.shape), 'x', 0, 0, ti...  6.68 us
    all_to_all x1, starting transfers between devices, per_device(): lax.all_to_all(jnp.broadcast_to(part, (n_yl * n_z,) + part.shape), ('yl',...  4.69 us
    pallas_call x1, Pallas kernels, per_device(): pl.pallas_call(score_kernel, out_shape=(jax.ShapeDtypeStruct((v_dev, widt...  4.44 us
  transfers between devices with their start and end apart: 17, of which 9 were waited for; matrix products, arithmetic and copies ran while one was open for 6% of the time, Pallas kernels for 1%

profile of v7, /device:TPU:72, one launch (start us, length us, event | category | flops | bytes accessed | tf_op | source)
XLA Modules:
  0.0 180.2 jit_solution(6642603127427802087)
XLA Ops:
  0.6 1.9 %collective-permute-start.4 = (bf16[64,4096]{1,0:T(8,128)(2,1)}, bf16[64,4096]{1,0:T(8,128)(2,1)S(1)}, u32[]{:S(2)}, u32[]{:S(2)}) collective-permute-start(bf16[64,4096]{1,0:T(8,128)(2,1)} %refs_4_.1), channel_id=1, source_target_pairs={{0,1},{1,0},{2,3},{3,2},{4,5},{5,4},{6,7},{7,6},{8,9},{9,8},{10,11... | collective-permute-start | bytes 1572872 | tf_op jit(solution)/shard_map/ppermute | solution.py:15
  2.6 5.3 %collective-permute-start.1 = (bf16[64,4096]{1,0:T(8,128)(2,1)}, bf16[64,4096]{1,0:T(8,128)(2,1)S(1)}, u32[]{:S(2)}, u32[]{:S(2)}) collective-permute-start(bf16[64,4096]{1,0:T(8,128)(2,1)} %refs_4_.1), channel_id=1, source_target_pairs={{0,6},{2,0},{4,2},{6,4},{1,7},{3,1},{5,3},{7,5},{8,14},{10,8},{12,... | collective-permute-start | bytes 1572872 | tf_op jit(solution)/shard_map/ppermute | solution.py:15
  7.8 1.9 %collective-permute-start = (bf16[64,4096]{1,0:T(8,128)(2,1)}, bf16[64,4096]{1,0:T(8,128)(2,1)S(1)}, u32[]{:S(2)}, u32[]{:S(2)}) collective-permute-start(bf16[64,4096]{1,0:T(8,128)(2,1)} %refs_4_.1), channel_id=1, source_target_pairs={{0,2},{2,4},{4,6},{6,0},{1,3},{3,5},{5,7},{7,1},{8,10},{10,12},{12... | collective-permute-start | bytes 1572872 | tf_op jit(solution)/shard_map/ppermute | solution.py:15
  11.8 25.6 %collective-permute-done.refs_2_.refs_6_ = bf16[64,4096]{1,0:T(8,128)(2,1)S(1)} collective-permute-done((bf16[64,4096]{1,0:T(8,128)(2,1)}, bf16[64,4096]{1,0:T(8,128)(2,1)S(1)}, u32[]{:S(2)}, u32[]{:S(2)}) %collective-permute-start) | collective-permute-done | bytes 524320 | tf_op jit(solution)/shard_map/ppermute | solution.py:15
  37.4 1.9 %collective-permute-start.5 = (bf16[64,4096]{1,0:T(8,128)(2,1)S(1)}, bf16[64,4096]{1,0:T(8,128)(2,1)S(1)}, u32[]{:S(2)}, u32[]{:S(2)}) collective-permute-start(bf16[64,4096]{1,0:T(8,128)(2,1)S(1)} %collective-permute-done.refs_2_.refs_6_), channel_id=1, source_target_pairs={{0,1},{1,0},{2,3},{3,2},{4,5},{5,4},{6,7},{7,6},{8,9},{9,8},{10,11... | collective-permute-start | bytes 1572872 | tf_op jit(solution)/shard_map/ppermute | solution.py:15
  39.3 2.4 %collective-permute-start.6 = (bf16[64,4096]{1,0:T(8,128)(2,1)S(1)}, bf16[64,4096]{1,0:T(8,128)(2,1)S(1)}, u32[]{:S(2)}, u32[]{:S(2)}) collective-permute-start(bf16[64,4096]{1,0:T(8,128)(2,1)S(1)} %collective-permute-done.1.refs_4_.refs_8_), channel_id=1, source_target_pairs={{0,1},{1,0},{2,3},{3,2},{4,5},{5,4},{6,7},{7,6},{8,9},{9,8},{10,11... | collective-permute-start | bytes 1572872 | tf_op jit(solution)/shard_map/ppermute | solution.py:15
  41.7 1.9 %collective-permute-start.2 = (bf16[32,4096]{1,0:T(8,128)(2,1)S(1)}, bf16[32,4096]{1,0:T(8,128)(2,1)S(1)}, u32[]{:S(2)}, u32[]{:S(2)}) collective-permute-start(bf16[32,4096]{1,0:T(8,128)(2,1)S(1)} %slice.59), channel_id=1, source_target_pairs={{0,2},{2,4},{4,6},{6,0},{1,3},{3,5},{5,7},{7,1},{8,10},{10,12},{12... | collective-permute-start | bytes 786440 | tf_op jit(solution)/shard_map/ppermute | solution.py:15
  43.7 6.0 %collective-permute-start.3 = (bf16[32,4096]{1,0:T(8,128)(2,1)S(1)}, bf16[32,4096]{1,0:T(8,128)(2,1)S(1)}, u32[]{:S(2)}, u32[]{:S(2)}) collective-permute-start(bf16[32,4096]{1,0:T(8,128)(2,1)S(1)} %slice.75), channel_id=1, source_target_pairs={{0,6},{2,0},{4,2},{6,4},{1,7},{3,1},{5,3},{7,5},{8,14},{10,8},{12,... | collective-permute-start | bytes 786440 | tf_op jit(solution)/shard_map/ppermute | solution.py:15
  49.7 1.4 copy-done
  52.2 2.0 %shard_map.67 = (f32[192,128]{1,0:T(8,128)S(1)}, f32[192,128]{1,0:T(8,128)S(1)}, f32[192,128]{1,0:T(8,128)S(1)}, f32[8,384]{1,0:T(8,128)S(1)}) custom-call(s32[6]{0:T(128)S(1)} %stack.27.where, bf16[192,4096]{1,0:T(8,128)(2,1)S(1)} %copy-done, s32[1,512]{1,0:T(1,128)S(1)} %reshape.25.labels, bf16[64,4096]{1,0:T(8,128)(2,1)S(1)} %copy-done.2, ...), custom_call_target="tpu_custom_call" | custom-call | flops 603979776 | bytes 4718592 | tf_op jit(solution)/shard_map/pallas_call | solution.py:131
  54.9 4.9 %collective-permute-done.3.refs_1_.refs_11_ = bf16[32,4096]{1,0:T(8,128)(2,1)S(1)} collective-permute-done((bf16[32,4096]{1,0:T(8,128)(2,1)S(1)}, bf16[32,4096]{1,0:T(8,128)(2,1)S(1)}, u32[]{:S(2)}, u32[]{:S(2)}) %collective-permute-start.3) | collective-permute-done | bytes 262176 | tf_op jit(solution)/shard_map/ppermute | solution.py:15
  59.8 1.9 %collective-permute-start.7 = (bf16[32,4096]{1,0:T(8,128)(2,1)S(1)}, bf16[32,4096]{1,0:T(8,128)(2,1)S(1)}, u32[]{:S(2)}, u32[]{:S(2)}) collective-permute-start(bf16[32,4096]{1,0:T(8,128)(2,1)S(1)} %collective-permute-done.2.refs_0_.refs_10_), channel_id=1, source_target_pairs={{0,1},{1,0},{2,3},{3,2},{4,5},{5,4},{6,7},{7,6},{8,9},{9,8},{10,11... | collective-permute-start | bytes 786440 | tf_op jit(solution)/shard_map/ppermute | solution.py:15
  61.7 2.4 %collective-permute-start.8 = (bf16[32,4096]{1,0:T(8,128)(2,1)S(1)}, bf16[32,4096]{1,0:T(8,128)(2,1)S(1)}, u32[]{:S(2)}, u32[]{:S(2)}) collective-permute-start(bf16[32,4096]{1,0:T(8,128)(2,1)S(1)} %collective-permute-done.3.refs_1_.refs_11_), channel_id=1, source_target_pairs={{0,1},{1,0},{2,3},{3,2},{4,5},{5,4},{6,7},{7,6},{8,9},{9,8},{10,11... | collective-permute-start | bytes 786440 | tf_op jit(solution)/shard_map/ppermute | solution.py:15
  66.5 12.1 %all_to_all.25.stats = f32[8,32,128]{2,1,0:T(8,128)S(1)} all-to-all(f32[8,32,128]{2,1,0:T(8,128)S(1)} %get-tuple-element.44), channel_id=1, replica_groups=mesh['x'=4,'yl'=2,'z'=8,'yh'=4,'core'=2] {'yh','core'}, dimensions={0} | all-to-all | bytes 262144 | tf_op jit(solution)/shard_map/all_to_all | solution.py:149
  78.5 4.4 %shard_map.69 = (bf16[192,4096]{1,0:T(8,128)(2,1)}, bf16[256,4096]{1,0:T(8,128)(2,1)}, bf16[256,192]{1,0:T(8,128)(2,1)S(1)}, f32[1,128]{1,0:T(1,128)S(1)}) custom-call(s32[6]{0:T(128)S(1)} %stack.27.where, f32[8,32,128]{2,1,0:T(8,128)S(1)} %all_to_all.25.stats, s32[1,512]{1,0:T(1,128)S(1)} %reshape.25.labels, f32[1,512]{1,0:T(1,128)S(1)} %reshape.27.weights, ...), custom_call_target="tpu_custom_call" | custom-call | flops 1207959552 | bytes 9437184 | tf_op jit(solution)/shard_map/pallas_call | solution.py:154
  83.0 2.0 %collective-permute-start.9 = (bf16[256,4096]{1,0:T(8,128)(2,1)}, bf16[256,4096]{1,0:T(8,128)(2,1)}, u32[]{:S(2)}, u32[]{:S(2)}) collective-permute-start(bf16[256,4096]{1,0:T(8,128)(2,1)} %get-tuple-element.52), channel_id=1, source_target_pairs={{0,1},{1,0},{2,3},{3,2},{4,5},{5,4},{6,7},{7,6},{8,9},{9,8},{10,11... | collective-permute-start | bytes 6291464 | tf_op jit(solution)/shard_map/ppermute | solution.py:15
  85.0 4.3 %all-to-all-start.1 = ((bf16[4,48,4096]{2,1,0:T(8,128)(2,1)}), bf16[4,48,4096]{2,1,0:T(8,128)(2,1)S(1)}, u32[]{:S(2)}, u32[]{:S(2)}) async-start(bf16[4,48,4096]{2,1,0:T(8,128)(2,1)} %bitcast.15), calls=%async_computation.1 | async-start | bytes 3145728 | tf_op jit(solution)/shard_map/all_to_all | solution.py:180
  89.5 2.3 %fusion.2 = bf16[256,4096]{1,0:T(8,128)(2,1)S(1)} fusion(bf16[256,192]{1,0:T(8,128)(2,1)S(1)} %get-tuple-element.51, bf16[192,4096]{1,0:T(8,128)(2,1)S(1)} %copy-done.1, bf16[256,4096]{1,0:T(8,128)(2,1)} %collective-permute-done.9), kind=kOutput, calls=%fused_computation.3 | convolution fusion | flops 407896064 | bytes 5865472 | tf_op jit(solution)/shard_map/dot_general | solution.py:182
  93.2 2.2 %collective-permute-start.11 = (bf16[32,4096]{1,0:T(8,128)(2,1)S(1)}, bf16[32,4096]{1,0:T(8,128)(2,1)S(1)}, u32[]{:S(2)}, u32[]{:S(2)}) collective-permute-start(bf16[32,4096]{1,0:T(8,128)(2,1)S(1)} %get-tuple-element.59), channel_id=1, source_target_pairs={{0,6},{2,0},{4,2},{6,4},{1,7},{3,1},{5,3},{7,5},{8,14},{10,8},{12,... | collective-permute-start | bytes 786440 | tf_op jit(solution)/shard_map/ppermute | solution.py:15
  95.4 4.6 %collective-permute-start.10 = (bf16[32,4096]{1,0:T(8,128)(2,1)S(1)}, bf16[32,4096]{1,0:T(8,128)(2,1)S(1)}, u32[]{:S(2)}, u32[]{:S(2)}) collective-permute-start(bf16[32,4096]{1,0:T(8,128)(2,1)S(1)} %get-tuple-element.60), channel_id=1, source_target_pairs={{0,2},{2,4},{4,6},{6,0},{1,3},{3,5},{5,7},{7,1},{8,10},{10,12},{12... | collective-permute-start | bytes 786440 | tf_op jit(solution)/shard_map/ppermute | solution.py:15
  99.9 10.8 %all-to-all-done.1 = bf16[4,48,4096]{2,1,0:T(8,128)(2,1)S(1)} async-done(((bf16[4,48,4096]{2,1,0:T(8,128)(2,1)}), bf16[4,48,4096]{2,1,0:T(8,128)(2,1)S(1)}, u32[]{:S(2)}, u32[]{:S(2)}) %all-to-all-start.1) | async-done | bytes 1572896 | tf_op jit(solution)/shard_map/all_to_all | solution.py:180
  111.3 23.0 %all_to_all.26 = bf16[16,48,256]{2,1,0:T(8,128)(2,1)S(1)} all-to-all(bf16[16,48,256]{2,1,0:T(8,128)(2,1)S(1)} %copy.7), channel_id=1, replica_groups=mesh['x'=4,'yl'=2,'z'=8,'yh'=4,'core'=2] {'yl','z'}, dimensions={0} | all-to-all | bytes 786432 | tf_op jit(solution)/shard_map/all_to_all | solution.py:196
  135.1 4.7 %all-to-all-start.3 = ((bf16[16,48,256]{2,1,0:T(8,128)(2,1)}), bf16[16,48,256]{2,1,0:T(8,128)(2,1)S(1)}, u32[]{:S(2)}, u32[]{:S(2)}) async-start(bf16[16,48,256]{2,1,0:T(8,128)(2,1)} %broadcast_in_dim.7), calls=%async_computation.3 | async-start | bytes 786432 | tf_op jit(solution)/shard_map/all_to_all | solution.py:198
  139.8 1.3 add_convert_fusion.2
  141.1 3.5 %collective-permute-start.12 = (bf16[64,4096]{1,0:T(8,128)(2,1)S(1)}, bf16[64,4096]{1,0:T(8,128)(2,1)S(1)}, u32[]{:S(2)}, u32[]{:S(2)}) collective-permute-start(bf16[64,4096]{1,0:T(8,128)(2,1)S(1)} %get-tuple-element.57), channel_id=1, source_target_pairs={{0,2},{2,4},{4,6},{6,0},{1,3},{3,5},{5,7},{7,1},{8,10},{10,12},{12... | collective-permute-start | bytes 1572872 | tf_op jit(solution)/shard_map/ppermute | solution.py:15
  144.6 4.5 %collective-permute-start.13 = (bf16[64,4096]{1,0:T(8,128)(2,1)S(1)}, bf16[64,4096]{1,0:T(8,128)(2,1)}, u32[]{:S(2)}, u32[]{:S(2)}) collective-permute-start(bf16[64,4096]{1,0:T(8,128)(2,1)S(1)} %get-tuple-element.58), channel_id=1, source_target_pairs={{0,6},{2,0},{4,2},{6,4},{1,7},{3,1},{5,3},{7,5},{8,14},{10,8},{12,... | collective-permute-start | bytes 1572872 | tf_op jit(solution)/shard_map/ppermute | solution.py:15
  149.1 3.6 %all-to-all-done.3 = bf16[16,48,256]{2,1,0:T(8,128)(2,1)S(1)} async-done(((bf16[16,48,256]{2,1,0:T(8,128)(2,1)}), bf16[16,48,256]{2,1,0:T(8,128)(2,1)S(1)}, u32[]{:S(2)}, u32[]{:S(2)}) %all-to-all-start.3) | async-done | bytes 393248 | tf_op jit(solution)/shard_map/all_to_all | solution.py:198
  154.0 4.0 %all-to-all-start.4 = ((bf16[4,16,48,256]{3,2,1,0:T(8,128)(2,1)}), bf16[4,16,48,256]{3,2,1,0:T(8,128)(2,1)S(1)}, u32[]{:S(2)}, u32[]{:S(2)}) async-start(bf16[4,16,48,256]{3,2,1,0:T(8,128)(2,1)} %broadcast_in_dim.8), calls=%async_computation.4 | async-start | bytes 3145728 | tf_op jit(solution)/shard_map/all_to_all | solution.py:199
  158.5 11.1 %collective-permute-done.12 = bf16[64,4096]{1,0:T(8,128)(2,1)S(1)} collective-permute-done((bf16[64,4096]{1,0:T(8,128)(2,1)S(1)}, bf16[64,4096]{1,0:T(8,128)(2,1)S(1)}, u32[]{:S(2)}, u32[]{:S(2)}) %collective-permute-start.12) | collective-permute-done | bytes 524320 | tf_op jit(solution)/shard_map/ppermute | solution.py:15
  169.6 2.2 %add_convert_fusion = bf16[64,4096]{1,0:T(8,128)(2,1)} fusion(bf16[64,4096]{1,0:T(8,128)(2,1)} %collective-permute-done.13, bf16[64,4096]{1,0:T(8,128)(2,1)S(1)} %collective-permute-done.12, bf16[256,4096]{1,0:T(8,128)(2,1)} %copy-done.4), kind=kLoop, calls=%fused_computation.4 | loop fusion | flops 1572864 | bytes 2097152 | tf_op jit(solution)/shard_map/convert_element_type | solution.py:209
  171.8 6.7 %all-to-all-done.4.pieces = bf16[4,16,48,256]{3,2,1,0:T(8,128)(2,1)S(1)} async-done(((bf16[4,16,48,256]{3,2,1,0:T(8,128)(2,1)}), bf16[4,16,48,256]{3,2,1,0:T(8,128)(2,1)S(1)}, u32[]{:S(2)}, u32[]{:S(2)}) %all-to-all-start.4) | async-done | bytes 1572896 | tf_op jit(solution)/shard_map/all_to_all | solution.py:199
  178.5 1.7 shard_map.70
  (46 shorter events, 10.7 us)
Async XLA Ops:
  0.6 49.1 %collective-permute-start.4 = (bf16[64,4096]{1,0:T(8,128)(2,1)}, bf16[64,4096]{1,0:T(8,128)(2,1)S(1)}, u32[]{:S(2)}, u32[]{:S(2)}) collective-permute-start(bf16[64,4096]{1,0:T(8,128)(2,1)} %refs_4_.1), channel_id=1, source_target_pairs={{0,1},{1,0},{2,3},{3,2},{4,5},{5,4},{6,7},{7,6},{8,9},{9,8},{10,11... | collective-permute-start | bytes 1572872 | tf_op jit(solution)/shard_map/ppermute | solution.py:15
  2.6 34.8 %collective-permute-start.1 = (bf16[64,4096]{1,0:T(8,128)(2,1)}, bf16[64,4096]{1,0:T(8,128)(2,1)S(1)}, u32[]{:S(2)}, u32[]{:S(2)}) collective-permute-start(bf16[64,4096]{1,0:T(8,128)(2,1)} %refs_4_.1), channel_id=1, source_target_pairs={{0,6},{2,0},{4,2},{6,4},{1,7},{3,1},{5,3},{7,5},{8,14},{10,8},{12,... | collective-permute-start | bytes 1572872 | tf_op jit(solution)/shard_map/ppermute | solution.py:15
  7.8 29.5 %collective-permute-start = (bf16[64,4096]{1,0:T(8,128)(2,1)}, bf16[64,4096]{1,0:T(8,128)(2,1)S(1)}, u32[]{:S(2)}, u32[]{:S(2)}) collective-permute-start(bf16[64,4096]{1,0:T(8,128)(2,1)} %refs_4_.1), channel_id=1, source_target_pairs={{0,2},{2,4},{4,6},{6,0},{1,3},{3,5},{5,7},{7,1},{8,10},{10,12},{12... | collective-permute-start | bytes 1572872 | tf_op jit(solution)/shard_map/ppermute | solution.py:15
  37.4 12.3 %collective-permute-start.5 = (bf16[64,4096]{1,0:T(8,128)(2,1)S(1)}, bf16[64,4096]{1,0:T(8,128)(2,1)S(1)}, u32[]{:S(2)}, u32[]{:S(2)}) collective-permute-start(bf16[64,4096]{1,0:T(8,128)(2,1)S(1)} %collective-permute-done.refs_2_.refs_6_), channel_id=1, source_target_pairs={{0,1},{1,0},{2,3},{3,2},{4,5},{5,4},{6,7},{7,6},{8,9},{9,8},{10,11... | collective-permute-start | bytes 1572872 | tf_op jit(solution)/shard_map/ppermute | solution.py:15
  39.3 10.4 %collective-permute-start.6 = (bf16[64,4096]{1,0:T(8,128)(2,1)S(1)}, bf16[64,4096]{1,0:T(8,128)(2,1)S(1)}, u32[]{:S(2)}, u32[]{:S(2)}) collective-permute-start(bf16[64,4096]{1,0:T(8,128)(2,1)S(1)} %collective-permute-done.1.refs_4_.refs_8_), channel_id=1, source_target_pairs={{0,1},{1,0},{2,3},{3,2},{4,5},{5,4},{6,7},{7,6},{8,9},{9,8},{10,11... | collective-permute-start | bytes 1572872 | tf_op jit(solution)/shard_map/ppermute | solution.py:15
  41.7 13.2 %collective-permute-start.2 = (bf16[32,4096]{1,0:T(8,128)(2,1)S(1)}, bf16[32,4096]{1,0:T(8,128)(2,1)S(1)}, u32[]{:S(2)}, u32[]{:S(2)}) collective-permute-start(bf16[32,4096]{1,0:T(8,128)(2,1)S(1)} %slice.59), channel_id=1, source_target_pairs={{0,2},{2,4},{4,6},{6,0},{1,3},{3,5},{5,7},{7,1},{8,10},{10,12},{12... | collective-permute-start | bytes 786440 | tf_op jit(solution)/shard_map/ppermute | solution.py:15
  43.7 16.1 %collective-permute-start.3 = (bf16[32,4096]{1,0:T(8,128)(2,1)S(1)}, bf16[32,4096]{1,0:T(8,128)(2,1)S(1)}, u32[]{:S(2)}, u32[]{:S(2)}) collective-permute-start(bf16[32,4096]{1,0:T(8,128)(2,1)S(1)} %slice.75), channel_id=1, source_target_pairs={{0,6},{2,0},{4,2},{6,4},{1,7},{3,1},{5,3},{7,5},{8,14},{10,8},{12,... | collective-permute-start | bytes 786440 | tf_op jit(solution)/shard_map/ppermute | solution.py:15
  49.7 1.4 copy-start
  51.1 1.0 copy-start.2
  54.2 24.3 %copy-start.3 = (bf16[64,4096]{1,0:T(8,128)(2,1)S(1)}, bf16[64,4096]{1,0:T(8,128)(2,1)}, u32[]{:S(2)}) copy-start(bf16[64,4096]{1,0:T(8,128)(2,1)} %refs_4_.1) | copy-start | bytes 1572868
  59.8 4.3 %collective-permute-start.7 = (bf16[32,4096]{1,0:T(8,128)(2,1)S(1)}, bf16[32,4096]{1,0:T(8,128)(2,1)S(1)}, u32[]{:S(2)}, u32[]{:S(2)}) collective-permute-start(bf16[32,4096]{1,0:T(8,128)(2,1)S(1)} %collective-permute-done.2.refs_0_.refs_10_), channel_id=1, source_target_pairs={{0,1},{1,0},{2,3},{3,2},{4,5},{5,4},{6,7},{7,6},{8,9},{9,8},{10,11... | collective-permute-start | bytes 786440 | tf_op jit(solution)/shard_map/ppermute | solution.py:15
  61.7 3.5 %collective-permute-start.8 = (bf16[32,4096]{1,0:T(8,128)(2,1)S(1)}, bf16[32,4096]{1,0:T(8,128)(2,1)S(1)}, u32[]{:S(2)}, u32[]{:S(2)}) collective-permute-start(bf16[32,4096]{1,0:T(8,128)(2,1)S(1)} %collective-permute-done.3.refs_1_.refs_11_), channel_id=1, source_target_pairs={{0,1},{1,0},{2,3},{3,2},{4,5},{5,4},{6,7},{7,6},{8,9},{9,8},{10,11... | collective-permute-start | bytes 786440 | tf_op jit(solution)/shard_map/ppermute | solution.py:15
  83.0 6.5 %copy-start.1 = (bf16[192,4096]{1,0:T(8,128)(2,1)S(1)}, bf16[192,4096]{1,0:T(8,128)(2,1)}, u32[]{:S(2)}) copy-start(bf16[192,4096]{1,0:T(8,128)(2,1)} %refs_14_.1) | copy-start | bytes 4718596
  83.0 6.5 %collective-permute-start.9 = (bf16[256,4096]{1,0:T(8,128)(2,1)}, bf16[256,4096]{1,0:T(8,128)(2,1)}, u32[]{:S(2)}, u32[]{:S(2)}) collective-permute-start(bf16[256,4096]{1,0:T(8,128)(2,1)} %get-tuple-element.52), channel_id=1, source_target_pairs={{0,1},{1,0},{2,3},{3,2},{4,5},{5,4},{6,7},{7,6},{8,9},{9,8},{10,11... | collective-permute-start | bytes 6291464 | tf_op jit(solution)/shard_map/ppermute | solution.py:15
  85.0 25.7 %all-to-all-start.1 = ((bf16[4,48,4096]{2,1,0:T(8,128)(2,1)}), bf16[4,48,4096]{2,1,0:T(8,128)(2,1)S(1)}, u32[]{:S(2)}, u32[]{:S(2)}) async-start(bf16[4,48,4096]{2,1,0:T(8,128)(2,1)} %bitcast.15), calls=%async_computation.1 | async-start | bytes 3145728 | tf_op jit(solution)/shard_map/all_to_all | solution.py:180
  91.8 1.3 copy-start.4
  93.2 17.9 %collective-permute-start.11 = (bf16[32,4096]{1,0:T(8,128)(2,1)S(1)}, bf16[32,4096]{1,0:T(8,128)(2,1)S(1)}, u32[]{:S(2)}, u32[]{:S(2)}) collective-permute-start(bf16[32,4096]{1,0:T(8,128)(2,1)S(1)} %get-tuple-element.59), channel_id=1, source_target_pairs={{0,6},{2,0},{4,2},{6,4},{1,7},{3,1},{5,3},{7,5},{8,14},{10,8},{12,... | collective-permute-start | bytes 786440 | tf_op jit(solution)/shard_map/ppermute | solution.py:15
  95.4 15.8 %collective-permute-start.10 = (bf16[32,4096]{1,0:T(8,128)(2,1)S(1)}, bf16[32,4096]{1,0:T(8,128)(2,1)S(1)}, u32[]{:S(2)}, u32[]{:S(2)}) collective-permute-start(bf16[32,4096]{1,0:T(8,128)(2,1)S(1)} %get-tuple-element.60), channel_id=1, source_target_pairs={{0,2},{2,4},{4,6},{6,0},{1,3},{3,5},{5,7},{7,1},{8,10},{10,12},{12... | collective-permute-start | bytes 786440 | tf_op jit(solution)/shard_map/ppermute | solution.py:15
  135.1 17.6 %all-to-all-start.3 = ((bf16[16,48,256]{2,1,0:T(8,128)(2,1)}), bf16[16,48,256]{2,1,0:T(8,128)(2,1)S(1)}, u32[]{:S(2)}, u32[]{:S(2)}) async-start(bf16[16,48,256]{2,1,0:T(8,128)(2,1)} %broadcast_in_dim.7), calls=%async_computation.3 | async-start | bytes 786432 | tf_op jit(solution)/shard_map/all_to_all | solution.py:198
  141.1 28.5 %collective-permute-start.12 = (bf16[64,4096]{1,0:T(8,128)(2,1)S(1)}, bf16[64,4096]{1,0:T(8,128)(2,1)S(1)}, u32[]{:S(2)}, u32[]{:S(2)}) collective-permute-start(bf16[64,4096]{1,0:T(8,128)(2,1)S(1)} %get-tuple-element.57), channel_id=1, source_target_pairs={{0,2},{2,4},{4,6},{6,0},{1,3},{3,5},{5,7},{7,1},{8,10},{10,12},{12... | collective-permute-start | bytes 1572872 | tf_op jit(solution)/shard_map/ppermute | solution.py:15
  144.6 25.0 %collective-permute-start.13 = (bf16[64,4096]{1,0:T(8,128)(2,1)S(1)}, bf16[64,4096]{1,0:T(8,128)(2,1)}, u32[]{:S(2)}, u32[]{:S(2)}) collective-permute-start(bf16[64,4096]{1,0:T(8,128)(2,1)S(1)} %get-tuple-element.58), channel_id=1, source_target_pairs={{0,6},{2,0},{4,2},{6,4},{1,7},{3,1},{5,3},{7,5},{8,14},{10,8},{12,... | collective-permute-start | bytes 1572872 | tf_op jit(solution)/shard_map/ppermute | solution.py:15
  154.0 24.5 %all-to-all-start.4 = ((bf16[4,16,48,256]{3,2,1,0:T(8,128)(2,1)}), bf16[4,16,48,256]{3,2,1,0:T(8,128)(2,1)S(1)}, u32[]{:S(2)}, u32[]{:S(2)}) async-start(bf16[4,16,48,256]{3,2,1,0:T(8,128)(2,1)} %broadcast_in_dim.8), calls=%async_computation.4 | async-start | bytes 3145728 | tf_op jit(solution)/shard_map/all_to_all | solution.py:199

commit v8 on v7

--- a/solution.py
+++ b/solution.py
@@ -87,10 +87,20 @@
     away[...] = jnp.dot(turned[...], head[...], preferred_element_type=F32).astype(BF16)
 
 
-def lay_kernel(pieces, out):
-    cols = pieces.shape[3]
-    for i in range(pieces.shape[1]):
-        out[:, i * cols : (i + 1) * cols] = pieces[0, i]
+def sum_kernel(parts, out):
+    cols = out.shape[2]
+    for i in range(out.shape[0]):
+        part = parts[:, :, i * cols : (i + 1) * cols].astype(F32)
+        out[i] = jnp.sum(part, axis=0).astype(BF16)
+
+
+def lay_kernel(where, own, before, after, far_low, far_high, out):
+    n, rows, cols = own.shape
+    for at, pieces in ((6, (own,)), (7, (before,)), (8, (after,)), (9, (far_low, far_high))):
+        row = pl.ds(pl.multiple_of(where[at] * rows, rows), rows)
+        pieces = [(piece, i) for piece in pieces for i in range(piece.shape[0])]
+        for j, (piece, i) in enumerate(pieces):
+            out[row, j * cols : (j + 1) * cols] = piece[i]
 
 
 def per_device(hidden, targets, token_weight, head_weight, *, n_x, n_yl, n_z, n_yh):
@@ -106,7 +116,8 @@
         return jnp.concatenate([value[0], value[3], value[1], value[2]], 0).reshape(1, -1)
 
     labels, weights = local_order(targets), local_order(token_weight)
-    where = jnp.stack([core, (yh * 2 + core) * v_dev] + [(yh + d) % n_yh for d in (0, n_yh - 1, 1, 2)])
+    where = [core, (yh * 2 + core) * v_dev] + [(yh + d) % n_yh for d in (0, n_yh - 1, 1, 2)]
+    where = jnp.stack(where + [(lax.axis_index("x") + d) % n_x for d in (0, n_x - 1, 1, 2)])
 
     before = shift(hidden, "yh", 1, n_yh)
     after = shift(hidden, "yh", -1, n_yh)
@@ -181,8 +192,17 @@
 
     home = jnp.dot(score, head_weight, preferred_element_type=F32).astype(BF16)
     terms = (home.astype(F32) + swap(away).astype(F32)).astype(BF16)
-    part = jnp.sum(part.astype(F32), axis=0).astype(BF16)
-    part = part.reshape(v_dev // n_x, n_yl * n_z, -1).transpose(1, 0, 2)
+    n_rest, rows = n_yl * n_z, v_dev // n_x
+    step = min(4, n_rest)
+    part = pl.pallas_call(
+        sum_kernel,
+        out_shape=jax.ShapeDtypeStruct((n_rest, rows, width // n_rest), BF16),
+        grid=(n_rest // step,),
+        in_specs=[pl.BlockSpec((n_x, rows, step * width // n_rest), lambda i: (0, 0, i))],
+        out_specs=pl.BlockSpec((step, rows, width // n_rest), lambda i: (i, 0, 0)),
+        compiler_params=params,
+        cost_estimate=pl.CostEstimate(flops=v_dev * width, bytes_accessed=3 * v_dev * width, transcendentals=0),
+    )(part)
 
     mine, up, down, far = (terms[m * tok : (m + 1) * tok] for m in (0, 2, 1, 3))
     from_below = shift(far[:half], "yh", 1, n_yh)
@@ -196,16 +216,18 @@
     part = lax.all_to_all(part, ("yl", "z"), 0, 0, tiled=True)
     part = jnp.sum(part.astype(F32), axis=0).astype(BF16)
     part = lax.all_to_all(jnp.broadcast_to(part, (n_yl * n_z,) + part.shape), ("yl", "z"), 0, 0, tiled=True)
-    part = lax.all_to_all(jnp.broadcast_to(part, (n_x,) + part.shape), "x", 0, 0, tiled=True)
+    x_before = shift(part, "x", 1, n_x)
+    x_after = shift(part, "x", -1, n_x)
+    x_low = shift(x_before[: n_rest // 2], "x", 1, n_x)
+    x_high = shift(x_after[n_rest // 2 :], "x", -1, n_x)
     grad_weight = pl.pallas_call(
         lay_kernel,
         out_shape=jax.ShapeDtypeStruct((v_dev, width), BF16),
-        grid=(n_x,),
-        in_specs=[pl.BlockSpec((1,) + part.shape[1:], lambda i: (i, 0, 0, 0))],
-        out_specs=pl.BlockSpec((v_dev // n_x, width), lambda i: (i, 0)),
+        in_specs=[smem] + [vmem] * 5,
+        out_specs=vmem,
         compiler_params=params,
         cost_estimate=pl.CostEstimate(flops=0, bytes_accessed=4 * v_dev * width, transcendentals=0),
-    )(part)
+    )(where, part, x_before, x_after, x_low, x_high)
     grad_hidden = (mine.astype(F32) + sum(v.astype(F32) for v in came)).astype(BF16)
     return token_loss, grad_hidden, grad_weight
 

time: 181 us -> 182 us (level)
  starting transfers between devices: 55.4 us -> 63.5 us
  waiting for transfers between devices: 64.6 us -> 59.3 us
    ppermute x14 -> x18, starting transfers between devices: 42.4 us -> 54.5 us  [shift(): lax.ppermute(value, axis, [(i, (i + step) % size) for i in range(size)])]
    all_to_all x1 -> x0, waiting for transfers between devices: 6.68 us -> none  [per_device(): lax.all_to_all(jnp.broadcast_to(part, (n_x,) + part.shape), 'x', 0, 0, ti...]
    all_to_all x1 -> x0, starting transfers between devices: 4.01 us -> none  [per_device(): lax.all_to_all(jnp.broadcast_to(part, (n_x,) + part.shape), 'x', 0, 0, ti...]
    ppermute x14 -> x18, waiting for transfers between devices: 43.6 us -> 43.2 us  [shift(): lax.ppermute(value, axis, [(i, (i + step) % size) for i in range(size)])]
    unnamed x11 -> x14, local copies, waits for them, and re-layouts: 3.85 us -> 3.6 us
  transfers between devices with their start and end apart: 17 -> 20, of which waited for: 9 -> 9; matrix products, arithmetic and copies ran while one was open for 6% -> 4% of each run, Pallas kernels for 1% -> 1%
where the time goes in v8:
time: 182 us; the launch traced here: 181 us
  starting transfers between devices  63.5 us (35%)
  waiting for transfers between devices  59.3 us (33%)
  blocking collectives  35.2 us (19%)
  Pallas kernels  9.92 us (5%)
  local copies, waits for them, and re-layouts  6.82 us (4%)
  other arithmetic  3.29 us (2%)
  matrix products  2.29 us (1%)
    ppermute x18, starting transfers between devices, shift(): lax.ppermute(value, axis, [(i, (i + step) % size) for i in range(size)])  54.5 us
    ppermute x18, waiting for transfers between devices, shift(): lax.ppermute(value, axis, [(i, (i + step) % size) for i in range(size)])  43.2 us
    all_to_all x1, blocking collectives, per_device(): part = lax.all_to_all(part, ('yl', 'z'), 0, 0, tiled=True)  23.1 us
    all_to_all x1, waiting for transfers between devices, per_device(): part = lax.all_to_all(part, 'x', 0, 0, tiled=True)  12.1 us
    all_to_all x1, blocking collectives, per_device(): stats = lax.all_to_all(stats, VOCAB, 0, 0, tiled=True)  12 us
    all_to_all x1, starting transfers between devices, per_device(): lax.all_to_all(jnp.broadcast_to(part, (n_yl * n_z,) + part.shape), ('yl',...  4.69 us
    pallas_call x1, Pallas kernels, per_device(): pl.pallas_call(score_kernel, out_shape=(jax.ShapeDtypeStruct((v_dev, widt...  4.46 us
    all_to_all x1, starting transfers between devices, per_device(): part = lax.all_to_all(part, 'x', 0, 0, tiled=True)  4.31 us
  transfers between devices with their start and end apart: 20, of which 9 were waited for; matrix products, arithmetic and copies ran while one was open for 4% of the time, Pallas kernels for 1%

profile of v8, /device:TPU:72, one launch (start us, length us, event | category | flops | bytes accessed | tf_op | source)
XLA Modules:
  0.0 181.4 jit_solution(3412073888949279255)
XLA Ops:
  0.6 1.9 %collective-permute-start.4 = (bf16[64,4096]{1,0:T(8,128)(2,1)}, bf16[64,4096]{1,0:T(8,128)(2,1)S(1)}, u32[]{:S(2)}, u32[]{:S(2)}) collective-permute-start(bf16[64,4096]{1,0:T(8,128)(2,1)} %refs_4_.1), channel_id=1, source_target_pairs={{0,1},{1,0},{2,3},{3,2},{4,5},{5,4},{6,7},{7,6},{8,9},{9,8},{10,11... | collective-permute-start | bytes 1572872 | tf_op jit(solution)/shard_map/ppermute | solution.py:15
  2.6 5.3 %collective-permute-start.1 = (bf16[64,4096]{1,0:T(8,128)(2,1)}, bf16[64,4096]{1,0:T(8,128)(2,1)S(1)}, u32[]{:S(2)}, u32[]{:S(2)}) collective-permute-start(bf16[64,4096]{1,0:T(8,128)(2,1)} %refs_4_.1), channel_id=1, source_target_pairs={{0,6},{2,0},{4,2},{6,4},{1,7},{3,1},{5,3},{7,5},{8,14},{10,8},{12,... | collective-permute-start | bytes 1572872 | tf_op jit(solution)/shard_map/ppermute | solution.py:15
  7.8 1.9 %collective-permute-start = (bf16[64,4096]{1,0:T(8,128)(2,1)}, bf16[64,4096]{1,0:T(8,128)(2,1)S(1)}, u32[]{:S(2)}, u32[]{:S(2)}) collective-permute-start(bf16[64,4096]{1,0:T(8,128)(2,1)} %refs_4_.1), channel_id=1, source_target_pairs={{0,2},{2,4},{4,6},{6,0},{1,3},{3,5},{5,7},{7,1},{8,10},{10,12},{12... | collective-permute-start | bytes 1572872 | tf_op jit(solution)/shard_map/ppermute | solution.py:15
  11.8 25.5 %collective-permute-done.refs_2_.refs_6_ = bf16[64,4096]{1,0:T(8,128)(2,1)S(1)} collective-permute-done((bf16[64,4096]{1,0:T(8,128)(2,1)}, bf16[64,4096]{1,0:T(8,128)(2,1)S(1)}, u32[]{:S(2)}, u32[]{:S(2)}) %collective-permute-start) | collective-permute-done | bytes 524320 | tf_op jit(solution)/shard_map/ppermute | solution.py:15
  37.4 1.9 %collective-permute-start.5 = (bf16[64,4096]{1,0:T(8,128)(2,1)S(1)}, bf16[64,4096]{1,0:T(8,128)(2,1)S(1)}, u32[]{:S(2)}, u32[]{:S(2)}) collective-permute-start(bf16[64,4096]{1,0:T(8,128)(2,1)S(1)} %collective-permute-done.refs_2_.refs_6_), channel_id=1, source_target_pairs={{0,1},{1,0},{2,3},{3,2},{4,5},{5,4},{6,7},{7,6},{8,9},{9,8},{10,11... | collective-permute-start | bytes 1572872 | tf_op jit(solution)/shard_map/ppermute | solution.py:15
  39.3 2.4 %collective-permute-start.6 = (bf16[64,4096]{1,0:T(8,128)(2,1)S(1)}, bf16[64,4096]{1,0:T(8,128)(2,1)S(1)}, u32[]{:S(2)}, u32[]{:S(2)}) collective-permute-start(bf16[64,4096]{1,0:T(8,128)(2,1)S(1)} %collective-permute-done.1.refs_4_.refs_8_), channel_id=1, source_target_pairs={{0,1},{1,0},{2,3},{3,2},{4,5},{5,4},{6,7},{7,6},{8,9},{9,8},{10,11... | collective-permute-start | bytes 1572872 | tf_op jit(solution)/shard_map/ppermute | solution.py:15
  41.7 1.9 %collective-permute-start.2 = (bf16[32,4096]{1,0:T(8,128)(2,1)S(1)}, bf16[32,4096]{1,0:T(8,128)(2,1)S(1)}, u32[]{:S(2)}, u32[]{:S(2)}) collective-permute-start(bf16[32,4096]{1,0:T(8,128)(2,1)S(1)} %slice.65), channel_id=1, source_target_pairs={{0,2},{2,4},{4,6},{6,0},{1,3},{3,5},{5,7},{7,1},{8,10},{10,12},{12... | collective-permute-start | bytes 786440 | tf_op jit(solution)/shard_map/ppermute | solution.py:15
  43.7 6.0 %collective-permute-start.3 = (bf16[32,4096]{1,0:T(8,128)(2,1)S(1)}, bf16[32,4096]{1,0:T(8,128)(2,1)S(1)}, u32[]{:S(2)}, u32[]{:S(2)}) collective-permute-start(bf16[32,4096]{1,0:T(8,128)(2,1)S(1)} %slice.83), channel_id=1, source_target_pairs={{0,6},{2,0},{4,2},{6,4},{1,7},{3,1},{5,3},{7,5},{8,14},{10,8},{12,... | collective-permute-start | bytes 786440 | tf_op jit(solution)/shard_map/ppermute | solution.py:15
  52.2 2.0 %shard_map.67 = (f32[192,128]{1,0:T(8,128)S(1)}, f32[192,128]{1,0:T(8,128)S(1)}, f32[192,128]{1,0:T(8,128)S(1)}, f32[8,384]{1,0:T(8,128)S(1)}) custom-call(s32[10]{0:T(128)S(1)} %stack.43.where, bf16[192,4096]{1,0:T(8,128)(2,1)S(1)} %copy-done, s32[1,512]{1,0:T(1,128)S(1)} %reshape.22.labels, bf16[64,4096]{1,0:T(8,128)(2,1)S(1)} %copy-done.2, ...), custom_call_target="tpu_custom_call" | custom-call | flops 603979776 | bytes 4718592 | tf_op jit(solution)/shard_map/pallas_call | solution.py:142
  54.9 4.9 %collective-permute-done.3.refs_1_.refs_11_ = bf16[32,4096]{1,0:T(8,128)(2,1)S(1)} collective-permute-done((bf16[32,4096]{1,0:T(8,128)(2,1)S(1)}, bf16[32,4096]{1,0:T(8,128)(2,1)S(1)}, u32[]{:S(2)}, u32[]{:S(2)}) %collective-permute-start.3) | collective-permute-done | bytes 262176 | tf_op jit(solution)/shard_map/ppermute | solution.py:15
  59.8 1.9 %collective-permute-start.7 = (bf16[32,4096]{1,0:T(8,128)(2,1)S(1)}, bf16[32,4096]{1,0:T(8,128)(2,1)S(1)}, u32[]{:S(2)}, u32[]{:S(2)}) collective-permute-start(bf16[32,4096]{1,0:T(8,128)(2,1)S(1)} %collective-permute-done.2.refs_0_.refs_10_), channel_id=1, source_target_pairs={{0,1},{1,0},{2,3},{3,2},{4,5},{5,4},{6,7},{7,6},{8,9},{9,8},{10,11... | collective-permute-start | bytes 786440 | tf_op jit(solution)/shard_map/ppermute | solution.py:15
  61.7 2.4 %collective-permute-start.8 = (bf16[32,4096]{1,0:T(8,128)(2,1)S(1)}, bf16[32,4096]{1,0:T(8,128)(2,1)S(1)}, u32[]{:S(2)}, u32[]{:S(2)}) collective-permute-start(bf16[32,4096]{1,0:T(8,128)(2,1)S(1)} %collective-permute-done.3.refs_1_.refs_11_), channel_id=1, source_target_pairs={{0,1},{1,0},{2,3},{3,2},{4,5},{5,4},{6,7},{7,6},{8,9},{9,8},{10,11... | collective-permute-start | bytes 786440 | tf_op jit(solution)/shard_map/ppermute | solution.py:15
  66.5 12.0 %all_to_all.20.stats = f32[8,32,128]{2,1,0:T(8,128)S(1)} all-to-all(f32[8,32,128]{2,1,0:T(8,128)S(1)} %get-tuple-element.44), channel_id=1, replica_groups=mesh['x'=4,'yl'=2,'z'=8,'yh'=4,'core'=2] {'yh','core'}, dimensions={0} | all-to-all | bytes 262144 | tf_op jit(solution)/shard_map/all_to_all | solution.py:160
  78.5 4.5 %shard_map.69 = (bf16[192,4096]{1,0:T(8,128)(2,1)S(1)}, bf16[256,4096]{1,0:T(8,128)(2,1)}, bf16[256,192]{1,0:T(8,128)(2,1)S(1)}, f32[1,128]{1,0:T(1,128)S(1)}) custom-call(s32[10]{0:T(128)S(1)} %stack.43.where, f32[8,32,128]{2,1,0:T(8,128)S(1)} %all_to_all.20.stats, s32[1,512]{1,0:T(1,128)S(1)} %reshape.22.labels, f32[1,512]{1,0:T(1,128)S(1)} %reshape.24.weights, ...), custom_call_target="tpu_custom_call" | custom-call | flops 1207959552 | bytes 9437184 | tf_op jit(solution)/shard_map/pallas_call | solution.py:165
  84.1 2.0 %collective-permute-start.9 = (bf16[256,4096]{1,0:T(8,128)(2,1)}, bf16[256,4096]{1,0:T(8,128)(2,1)}, u32[]{:S(2)}, u32[]{:S(2)}) collective-permute-start(bf16[256,4096]{1,0:T(8,128)(2,1)} %get-tuple-element.52), channel_id=1, source_target_pairs={{0,1},{1,0},{2,3},{3,2},{4,5},{5,4},{6,7},{7,6},{8,9},{9,8},{10,11... | collective-permute-start | bytes 6291464 | tf_op jit(solution)/shard_map/ppermute | solution.py:15
  86.2 4.3 %all-to-all-start.1 = ((bf16[4,48,4096]{2,1,0:T(8,128)(2,1)}), bf16[4,48,4096]{2,1,0:T(8,128)(2,1)S(1)}, u32[]{:S(2)}, u32[]{:S(2)}) async-start(bf16[4,48,4096]{2,1,0:T(8,128)(2,1)} %bitcast.31), calls=%async_computation.1 | async-start | bytes 3145728 | tf_op jit(solution)/shard_map/all_to_all | solution.py:191
  90.7 2.3 %fusion.2 = bf16[256,4096]{1,0:T(8,128)(2,1)S(1)} fusion(bf16[256,192]{1,0:T(8,128)(2,1)S(1)} %get-tuple-element.51, bf16[192,4096]{1,0:T(8,128)(2,1)S(1)} %copy-done.1, bf16[256,4096]{1,0:T(8,128)(2,1)} %collective-permute-done.9), kind=kOutput, calls=%fused_computation.3 | convolution fusion | flops 407896064 | bytes 5865472 | tf_op jit(solution)/shard_map/dot_general | solution.py:193
  93.0 2.2 %collective-permute-start.11 = (bf16[32,4096]{1,0:T(8,128)(2,1)S(1)}, bf16[32,4096]{1,0:T(8,128)(2,1)S(1)}, u32[]{:S(2)}, u32[]{:S(2)}) collective-permute-start(bf16[32,4096]{1,0:T(8,128)(2,1)S(1)} %get-tuple-element.59), channel_id=1, source_target_pairs={{0,6},{2,0},{4,2},{6,4},{1,7},{3,1},{5,3},{7,5},{8,14},{10,8},{12,... | collective-permute-start | bytes 786440 | tf_op jit(solution)/shard_map/ppermute | solution.py:15
  95.2 4.6 %collective-permute-start.10 = (bf16[32,4096]{1,0:T(8,128)(2,1)S(1)}, bf16[32,4096]{1,0:T(8,128)(2,1)S(1)}, u32[]{:S(2)}, u32[]{:S(2)}) collective-permute-start(bf16[32,4096]{1,0:T(8,128)(2,1)S(1)} %get-tuple-element.60), channel_id=1, source_target_pairs={{0,2},{2,4},{4,6},{6,0},{1,3},{3,5},{5,7},{7,1},{8,10},{10,12},{12... | collective-permute-start | bytes 786440 | tf_op jit(solution)/shard_map/ppermute | solution.py:15
  99.8 12.1 %all-to-all-done.1.parts = bf16[4,48,4096]{2,1,0:T(8,128)(2,1)S(1)} async-done(((bf16[4,48,4096]{2,1,0:T(8,128)(2,1)}), bf16[4,48,4096]{2,1,0:T(8,128)(2,1)S(1)}, u32[]{:S(2)}, u32[]{:S(2)}) %all-to-all-start.1) | async-done | bytes 1572896 | tf_op jit(solution)/shard_map/all_to_all | solution.py:191
  112.3 23.1 %all_to_all.21 = bf16[16,48,256]{2,1,0:T(8,128)(2,1)S(1)} all-to-all(bf16[16,48,256]{2,1,0:T(8,128)(2,1)S(1)} %shard_map.70), channel_id=1, replica_groups=mesh['x'=4,'yl'=2,'z'=8,'yh'=4,'core'=2] {'yl','z'}, dimensions={0} | all-to-all | bytes 786432 | tf_op jit(solution)/shard_map/all_to_all | solution.py:216
  136.3 4.7 %all-to-all-start.3 = ((bf16[16,48,256]{2,1,0:T(8,128)(2,1)}), bf16[16,48,256]{2,1,0:T(8,128)(2,1)S(1)}, u32[]{:S(2)}, u32[]{:S(2)}) async-start(bf16[16,48,256]{2,1,0:T(8,128)(2,1)} %broadcast_in_dim.4), calls=%async_computation.3 | async-start | bytes 786432 | tf_op jit(solution)/shard_map/all_to_all | solution.py:218
  141.9 2.4 %collective-permute-start.12 = (bf16[64,4096]{1,0:T(8,128)(2,1)}, bf16[64,4096]{1,0:T(8,128)(2,1)}, u32[]{:S(2)}, u32[]{:S(2)}) collective-permute-start(bf16[64,4096]{1,0:T(8,128)(2,1)} %get-tuple-element.57), channel_id=1, source_target_pairs={{0,2},{2,4},{4,6},{6,0},{1,3},{3,5},{5,7},{7,1},{8,10},{10,12},{12... | collective-permute-start | bytes 1572872 | tf_op jit(solution)/shard_map/ppermute | solution.py:15
  144.3 5.5 %collective-permute-start.13 = (bf16[64,4096]{1,0:T(8,128)(2,1)S(1)}, bf16[64,4096]{1,0:T(8,128)(2,1)}, u32[]{:S(2)}, u32[]{:S(2)}) collective-permute-start(bf16[64,4096]{1,0:T(8,128)(2,1)S(1)} %get-tuple-element.58), channel_id=1, source_target_pairs={{0,6},{2,0},{4,2},{6,4},{1,7},{3,1},{5,3},{7,5},{8,14},{10,8},{12,... | collective-permute-start | bytes 1572872 | tf_op jit(solution)/shard_map/ppermute | solution.py:15
  149.9 4.0 %all-to-all-done.3.own = bf16[16,48,256]{2,1,0:T(8,128)(2,1)S(1)} async-done(((bf16[16,48,256]{2,1,0:T(8,128)(2,1)}), bf16[16,48,256]{2,1,0:T(8,128)(2,1)S(1)}, u32[]{:S(2)}, u32[]{:S(2)}) %all-to-all-start.3) | async-done | bytes 393248 | tf_op jit(solution)/shard_map/all_to_all | solution.py:218
  153.9 3.1 %collective-permute-start.15 = (bf16[16,48,256]{2,1,0:T(8,128)(2,1)S(1)}, bf16[16,48,256]{2,1,0:T(8,128)(2,1)S(1)}, u32[]{:S(2)}, u32[]{:S(2)}) collective-permute-start(bf16[16,48,256]{2,1,0:T(8,128)(2,1)S(1)} %all-to-all-done.3.own), channel_id=1, source_target_pairs={{0,384},{128,0},{256,128},{384,256},{1,385},{129,1},{257,129},{385... | collective-permute-start | bytes 1179656 | tf_op jit(solution)/shard_map/ppermute | solution.py:15
  157.0 2.8 %collective-permute-start.14 = (bf16[16,48,256]{2,1,0:T(8,128)(2,1)S(1)}, bf16[16,48,256]{2,1,0:T(8,128)(2,1)S(1)}, u32[]{:S(2)}, u32[]{:S(2)}) collective-permute-start(bf16[16,48,256]{2,1,0:T(8,128)(2,1)S(1)} %all-to-all-done.3.own), channel_id=1, source_target_pairs={{0,128},{128,256},{256,384},{384,0},{1,129},{129,257},{257,385},{3... | collective-permute-start | bytes 1179656 | tf_op jit(solution)/shard_map/ppermute | solution.py:15
  160.3 6.2 %collective-permute-done.15.after = bf16[16,48,256]{2,1,0:T(8,128)(2,1)S(1)} collective-permute-done((bf16[16,48,256]{2,1,0:T(8,128)(2,1)S(1)}, bf16[16,48,256]{2,1,0:T(8,128)(2,1)S(1)}, u32[]{:S(2)}, u32[]{:S(2)}) %collective-permute-start.15) | collective-permute-done | bytes 393248 | tf_op jit(solution)/shard_map/ppermute | solution.py:15
  166.5 4.3 %collective-permute-start.17 = (bf16[8,48,256]{2,1,0:T(8,128)(2,1)S(1)}, bf16[8,48,256]{2,1,0:T(8,128)(2,1)S(1)}, u32[]{:S(2)}, u32[]{:S(2)}) collective-permute-start(bf16[8,48,256]{2,1,0:T(8,128)(2,1)S(1)} %slice.90), channel_id=1, source_target_pairs={{0,384},{128,0},{256,128},{384,256},{1,385},{129,1},{257,129},{385... | collective-permute-start | bytes 589832 | tf_op jit(solution)/shard_map/ppermute | solution.py:15
  170.8 1.9 %collective-permute-start.16 = (bf16[8,48,256]{2,1,0:T(8,128)(2,1)S(1)}, bf16[8,48,256]{2,1,0:T(8,128)(2,1)S(1)}, u32[]{:S(2)}, u32[]{:S(2)}) collective-permute-start(bf16[8,48,256]{2,1,0:T(8,128)(2,1)S(1)} %slice.89), channel_id=1, source_target_pairs={{0,128},{128,256},{256,384},{384,0},{1,129},{129,257},{257,385},{3... | collective-permute-start | bytes 589832 | tf_op jit(solution)/shard_map/ppermute | solution.py:15
  172.7 2.2 %add_convert_fusion = bf16[64,4096]{1,0:T(8,128)(2,1)} fusion(bf16[64,4096]{1,0:T(8,128)(2,1)} %collective-permute-done.13, bf16[64,4096]{1,0:T(8,128)(2,1)} %collective-permute-done.12, bf16[256,4096]{1,0:T(8,128)(2,1)S(1)} %copy-done.6), kind=kLoop, calls=%fused_computation.4 | loop fusion | flops 1572864 | bytes 2097152 | tf_op jit(solution)/shard_map/convert_element_type | solution.py:231
  174.9 4.6 %collective-permute-done.16.far_low = bf16[8,48,256]{2,1,0:T(8,128)(2,1)S(1)} collective-permute-done((bf16[8,48,256]{2,1,0:T(8,128)(2,1)S(1)}, bf16[8,48,256]{2,1,0:T(8,128)(2,1)S(1)}, u32[]{:S(2)}, u32[]{:S(2)}) %collective-permute-start.16) | collective-permute-done | bytes 196640 | tf_op jit(solution)/shard_map/ppermute | solution.py:15
  (55 shorter events, 13.3 us)
Async XLA Ops:
  0.6 49.1 %collective-permute-start.4 = (bf16[64,4096]{1,0:T(8,128)(2,1)}, bf16[64,4096]{1,0:T(8,128)(2,1)S(1)}, u32[]{:S(2)}, u32[]{:S(2)}) collective-permute-start(bf16[64,4096]{1,0:T(8,128)(2,1)} %refs_4_.1), channel_id=1, source_target_pairs={{0,1},{1,0},{2,3},{3,2},{4,5},{5,4},{6,7},{7,6},{8,9},{9,8},{10,11... | collective-permute-start | bytes 1572872 | tf_op jit(solution)/shard_map/ppermute | solution.py:15
  2.6 34.8 %collective-permute-start.1 = (bf16[64,4096]{1,0:T(8,128)(2,1)}, bf16[64,4096]{1,0:T(8,128)(2,1)S(1)}, u32[]{:S(2)}, u32[]{:S(2)}) collective-permute-start(bf16[64,4096]{1,0:T(8,128)(2,1)} %refs_4_.1), channel_id=1, source_target_pairs={{0,6},{2,0},{4,2},{6,4},{1,7},{3,1},{5,3},{7,5},{8,14},{10,8},{12,... | collective-permute-start | bytes 1572872 | tf_op jit(solution)/shard_map/ppermute | solution.py:15
  7.8 29.5 %collective-permute-start = (bf16[64,4096]{1,0:T(8,128)(2,1)}, bf16[64,4096]{1,0:T(8,128)(2,1)S(1)}, u32[]{:S(2)}, u32[]{:S(2)}) collective-permute-start(bf16[64,4096]{1,0:T(8,128)(2,1)} %refs_4_.1), channel_id=1, source_target_pairs={{0,2},{2,4},{4,6},{6,0},{1,3},{3,5},{5,7},{7,1},{8,10},{10,12},{12... | collective-permute-start | bytes 1572872 | tf_op jit(solution)/shard_map/ppermute | solution.py:15
  37.4 12.3 %collective-permute-start.5 = (bf16[64,4096]{1,0:T(8,128)(2,1)S(1)}, bf16[64,4096]{1,0:T(8,128)(2,1)S(1)}, u32[]{:S(2)}, u32[]{:S(2)}) collective-permute-start(bf16[64,4096]{1,0:T(8,128)(2,1)S(1)} %collective-permute-done.refs_2_.refs_6_), channel_id=1, source_target_pairs={{0,1},{1,0},{2,3},{3,2},{4,5},{5,4},{6,7},{7,6},{8,9},{9,8},{10,11... | collective-permute-start | bytes 1572872 | tf_op jit(solution)/shard_map/ppermute | solution.py:15
  39.3 10.4 %collective-permute-start.6 = (bf16[64,4096]{1,0:T(8,128)(2,1)S(1)}, bf16[64,4096]{1,0:T(8,128)(2,1)S(1)}, u32[]{:S(2)}, u32[]{:S(2)}) collective-permute-start(bf16[64,4096]{1,0:T(8,128)(2,1)S(1)} %collective-permute-done.1.refs_4_.refs_8_), channel_id=1, source_target_pairs={{0,1},{1,0},{2,3},{3,2},{4,5},{5,4},{6,7},{7,6},{8,9},{9,8},{10,11... | collective-permute-start | bytes 1572872 | tf_op jit(solution)/shard_map/ppermute | solution.py:15
  41.7 13.2 %collective-permute-start.2 = (bf16[32,4096]{1,0:T(8,128)(2,1)S(1)}, bf16[32,4096]{1,0:T(8,128)(2,1)S(1)}, u32[]{:S(2)}, u32[]{:S(2)}) collective-permute-start(bf16[32,4096]{1,0:T(8,128)(2,1)S(1)} %slice.65), channel_id=1, source_target_pairs={{0,2},{2,4},{4,6},{6,0},{1,3},{3,5},{5,7},{7,1},{8,10},{10,12},{12... | collective-permute-start | bytes 786440 | tf_op jit(solution)/shard_map/ppermute | solution.py:15
  43.7 16.1 %collective-permute-start.3 = (bf16[32,4096]{1,0:T(8,128)(2,1)S(1)}, bf16[32,4096]{1,0:T(8,128)(2,1)S(1)}, u32[]{:S(2)}, u32[]{:S(2)}) collective-permute-start(bf16[32,4096]{1,0:T(8,128)(2,1)S(1)} %slice.83), channel_id=1, source_target_pairs={{0,6},{2,0},{4,2},{6,4},{1,7},{3,1},{5,3},{7,5},{8,14},{10,8},{12,... | collective-permute-start | bytes 786440 | tf_op jit(solution)/shard_map/ppermute | solution.py:15
  49.7 1.4 copy-start
  51.1 1.0 copy-start.2
  54.2 24.3 %copy-start.3 = (bf16[64,4096]{1,0:T(8,128)(2,1)S(1)}, bf16[64,4096]{1,0:T(8,128)(2,1)}, u32[]{:S(2)}) copy-start(bf16[64,4096]{1,0:T(8,128)(2,1)} %refs_4_.1) | copy-start | bytes 1572868
  59.8 4.3 %collective-permute-start.7 = (bf16[32,4096]{1,0:T(8,128)(2,1)S(1)}, bf16[32,4096]{1,0:T(8,128)(2,1)S(1)}, u32[]{:S(2)}, u32[]{:S(2)}) collective-permute-start(bf16[32,4096]{1,0:T(8,128)(2,1)S(1)} %collective-permute-done.2.refs_0_.refs_10_), channel_id=1, source_target_pairs={{0,1},{1,0},{2,3},{3,2},{4,5},{5,4},{6,7},{7,6},{8,9},{9,8},{10,11... | collective-permute-start | bytes 786440 | tf_op jit(solution)/shard_map/ppermute | solution.py:15
  61.7 3.5 %collective-permute-start.8 = (bf16[32,4096]{1,0:T(8,128)(2,1)S(1)}, bf16[32,4096]{1,0:T(8,128)(2,1)S(1)}, u32[]{:S(2)}, u32[]{:S(2)}) collective-permute-start(bf16[32,4096]{1,0:T(8,128)(2,1)S(1)} %collective-permute-done.3.refs_1_.refs_11_), channel_id=1, source_target_pairs={{0,1},{1,0},{2,3},{3,2},{4,5},{5,4},{6,7},{7,6},{8,9},{9,8},{10,11... | collective-permute-start | bytes 786440 | tf_op jit(solution)/shard_map/ppermute | solution.py:15
  83.0 1.1 copy-start.4
  84.1 6.5 %copy-start.1 = (bf16[192,4096]{1,0:T(8,128)(2,1)S(1)}, bf16[192,4096]{1,0:T(8,128)(2,1)}, u32[]{:S(2)}) copy-start(bf16[192,4096]{1,0:T(8,128)(2,1)} %refs_14_.1) | copy-start | bytes 4718596
  84.1 6.5 %collective-permute-start.9 = (bf16[256,4096]{1,0:T(8,128)(2,1)}, bf16[256,4096]{1,0:T(8,128)(2,1)}, u32[]{:S(2)}, u32[]{:S(2)}) collective-permute-start(bf16[256,4096]{1,0:T(8,128)(2,1)} %get-tuple-element.52), channel_id=1, source_target_pairs={{0,1},{1,0},{2,3},{3,2},{4,5},{5,4},{6,7},{7,6},{8,9},{9,8},{10,11... | collective-permute-start | bytes 6291464 | tf_op jit(solution)/shard_map/ppermute | solution.py:15
  86.2 25.7 %all-to-all-start.1 = ((bf16[4,48,4096]{2,1,0:T(8,128)(2,1)}), bf16[4,48,4096]{2,1,0:T(8,128)(2,1)S(1)}, u32[]{:S(2)}, u32[]{:S(2)}) async-start(bf16[4,48,4096]{2,1,0:T(8,128)(2,1)} %bitcast.31), calls=%async_computation.1 | async-start | bytes 3145728 | tf_op jit(solution)/shard_map/all_to_all | solution.py:191
  93.0 2.3 %copy-start.5 = (bf16[256,4096]{1,0:T(8,128)(2,1)}, bf16[256,4096]{1,0:T(8,128)(2,1)S(1)}, u32[]{:S(2)}) copy-start(bf16[256,4096]{1,0:T(8,128)(2,1)S(1)} %fusion.2) | copy-start | bytes 6291460
  93.0 19.3 %collective-permute-start.11 = (bf16[32,4096]{1,0:T(8,128)(2,1)S(1)}, bf16[32,4096]{1,0:T(8,128)(2,1)S(1)}, u32[]{:S(2)}, u32[]{:S(2)}) collective-permute-start(bf16[32,4096]{1,0:T(8,128)(2,1)S(1)} %get-tuple-element.59), channel_id=1, source_target_pairs={{0,6},{2,0},{4,2},{6,4},{1,7},{3,1},{5,3},{7,5},{8,14},{10,8},{12,... | collective-permute-start | bytes 786440 | tf_op jit(solution)/shard_map/ppermute | solution.py:15
  95.2 17.1 %collective-permute-start.10 = (bf16[32,4096]{1,0:T(8,128)(2,1)S(1)}, bf16[32,4096]{1,0:T(8,128)(2,1)S(1)}, u32[]{:S(2)}, u32[]{:S(2)}) collective-permute-start(bf16[32,4096]{1,0:T(8,128)(2,1)S(1)} %get-tuple-element.60), channel_id=1, source_target_pairs={{0,2},{2,4},{4,6},{6,0},{1,3},{3,5},{5,7},{7,1},{8,10},{10,12},{12... | collective-permute-start | bytes 786440 | tf_op jit(solution)/shard_map/ppermute | solution.py:15
  112.3 28.7 %copy-start.6 = (bf16[256,4096]{1,0:T(8,128)(2,1)S(1)}, bf16[256,4096]{1,0:T(8,128)(2,1)}, u32[]{:S(2)}) copy-start(bf16[256,4096]{1,0:T(8,128)(2,1)} %copy-done.5) | copy-start | bytes 6291460
  136.3 17.6 %all-to-all-start.3 = ((bf16[16,48,256]{2,1,0:T(8,128)(2,1)}), bf16[16,48,256]{2,1,0:T(8,128)(2,1)S(1)}, u32[]{:S(2)}, u32[]{:S(2)}) async-start(bf16[16,48,256]{2,1,0:T(8,128)(2,1)} %broadcast_in_dim.4), calls=%async_computation.3 | async-start | bytes 786432 | tf_op jit(solution)/shard_map/all_to_all | solution.py:218
  141.9 30.8 %collective-permute-start.12 = (bf16[64,4096]{1,0:T(8,128)(2,1)}, bf16[64,4096]{1,0:T(8,128)(2,1)}, u32[]{:S(2)}, u32[]{:S(2)}) collective-permute-start(bf16[64,4096]{1,0:T(8,128)(2,1)} %get-tuple-element.57), channel_id=1, source_target_pairs={{0,2},{2,4},{4,6},{6,0},{1,3},{3,5},{5,7},{7,1},{8,10},{10,12},{12... | collective-permute-start | bytes 1572872 | tf_op jit(solution)/shard_map/ppermute | solution.py:15
  144.3 28.4 %collective-permute-start.13 = (bf16[64,4096]{1,0:T(8,128)(2,1)S(1)}, bf16[64,4096]{1,0:T(8,128)(2,1)}, u32[]{:S(2)}, u32[]{:S(2)}) collective-permute-start(bf16[64,4096]{1,0:T(8,128)(2,1)S(1)} %get-tuple-element.58), channel_id=1, source_target_pairs={{0,6},{2,0},{4,2},{6,4},{1,7},{3,1},{5,3},{7,5},{8,14},{10,8},{12,... | collective-permute-start | bytes 1572872 | tf_op jit(solution)/shard_map/ppermute | solution.py:15
  153.9 12.5 %collective-permute-start.15 = (bf16[16,48,256]{2,1,0:T(8,128)(2,1)S(1)}, bf16[16,48,256]{2,1,0:T(8,128)(2,1)S(1)}, u32[]{:S(2)}, u32[]{:S(2)}) collective-permute-start(bf16[16,48,256]{2,1,0:T(8,128)(2,1)S(1)} %all-to-all-done.3.own), channel_id=1, source_target_pairs={{0,384},{128,0},{256,128},{384,256},{1,385},{129,1},{257,129},{385... | collective-permute-start | bytes 1179656 | tf_op jit(solution)/shard_map/ppermute | solution.py:15
  157.0 13.8 %collective-permute-start.14 = (bf16[16,48,256]{2,1,0:T(8,128)(2,1)S(1)}, bf16[16,48,256]{2,1,0:T(8,128)(2,1)S(1)}, u32[]{:S(2)}, u32[]{:S(2)}) collective-permute-start(bf16[16,48,256]{2,1,0:T(8,128)(2,1)S(1)} %all-to-all-done.3.own), channel_id=1, source_target_pairs={{0,128},{128,256},{256,384},{384,0},{1,129},{129,257},{257,385},{3... | collective-permute-start | bytes 1179656 | tf_op jit(solution)/shard_map/ppermute | solution.py:15
  166.5 8.5 %collective-permute-start.17 = (bf16[8,48,256]{2,1,0:T(8,128)(2,1)S(1)}, bf16[8,48,256]{2,1,0:T(8,128)(2,1)S(1)}, u32[]{:S(2)}, u32[]{:S(2)}) collective-permute-start(bf16[8,48,256]{2,1,0:T(8,128)(2,1)S(1)} %slice.90), channel_id=1, source_target_pairs={{0,384},{128,0},{256,128},{384,256},{1,385},{129,1},{257,129},{385... | collective-permute-start | bytes 589832 | tf_op jit(solution)/shard_map/ppermute | solution.py:15
  170.8 8.8 %collective-permute-start.16 = (bf16[8,48,256]{2,1,0:T(8,128)(2,1)S(1)}, bf16[8,48,256]{2,1,0:T(8,128)(2,1)S(1)}, u32[]{:S(2)}, u32[]{:S(2)}) collective-permute-start(bf16[8,48,256]{2,1,0:T(8,128)(2,1)S(1)} %slice.89), channel_id=1, source_target_pairs={{0,128},{128,256},{256,384},{384,0},{1,129},{129,257},{257,385},{3... | collective-permute-start | bytes 589832 | tf_op jit(solution)/shard_map/ppermute | solution.py:15

commit v9 on v8

--- a/solution.py
+++ b/solution.py
@@ -36,20 +36,16 @@
     return jnp.where(where[0] == 0, tile, pltpu.roll(tile, tile.shape[1] // 2, 1))
 
 
-def near_kernel(where, head, labels, *refs):
-    pieces, logits, stats = refs[:6], refs[6:9], refs[9]
+def stage_kernel(head, own, head_out, own_out):
+    head_out[...] = head[...]
+    own_out[...] = own[...]
+
+
+def logits_kernel(where, head, labels, *refs):
+    pieces, logits, stats = refs[:10], refs[10:14], refs[14]
     n = logits[0].shape[1]
-    for m in range(3):
-        lanes = slice(m * n, (m + 1) * n)
-        stats[:, lanes] = block_stats(where, head, pieces[2 * m : 2 * m + 2], labels[:, lanes], logits[m])
-
-
-def far_kernel(where, head, labels, near, *refs):
-    pieces, logits, stats = refs[:4], refs[4], refs[5]
-    n = logits.shape[1]
-    tiles = [near[:, m * n : (m + 1) * n] for m in range(3)]
-    tiles.append(block_stats(where, head, pieces, labels[:, 3 * n :], logits))
-    for m, tile in enumerate(tiles):
+    for m, chosen in enumerate((pieces[:2], pieces[2:4], pieces[4:6], pieces[6:])):
+        tile = block_stats(where, head, chosen, labels[:, m * n : (m + 1) * n], logits[m])
         at = pl.multiple_of(where[2 + m] * 8, 8)
         for shard in range(stats.shape[0]):
             stats[shard, pl.ds(at, 8), :] = tile
@@ -119,44 +115,40 @@
     where = [core, (yh * 2 + core) * v_dev] + [(yh + d) % n_yh for d in (0, n_yh - 1, 1, 2)]
     where = jnp.stack(where + [(lax.axis_index("x") + d) % n_x for d in (0, n_x - 1, 1, 2)])
 
+    smem, vmem = pl.BlockSpec(memory_space=pltpu.SMEM), pl.BlockSpec(memory_space=pltpu.VMEM)
+    params = pltpu.CompilerParams(vmem_limit_bytes=16 << 20)
+    head_near, own_near = pl.pallas_call(
+        stage_kernel,
+        out_shape=(jax.ShapeDtypeStruct(head_weight.shape, BF16), jax.ShapeDtypeStruct(hidden.shape, BF16)),
+        in_specs=[vmem] * 2,
+        out_specs=(vmem,) * 2,
+        compiler_params=params,
+    )(head_weight, hidden)
+
     before = shift(hidden, "yh", 1, n_yh)
     after = shift(hidden, "yh", -1, n_yh)
-    own_other = swap(hidden)
-    before, labels, weights, where = lax.optimization_barrier((before, labels, weights, where))
-    low, high, before, after = lax.optimization_barrier((before[:half], after[half:], before, after))
-    far_low = shift(low, "yh", 1, n_yh)
-    far_high = shift(high, "yh", -1, n_yh)
-    near = (hidden, own_other, before, swap(before), after, swap(after))
-
-    smem, vmem = pl.BlockSpec(memory_space=pltpu.SMEM), pl.BlockSpec(memory_space=pltpu.VMEM)
-    params = pltpu.CompilerParams(vmem_limit_bytes=32 << 20)
+    before, labels, weights, where, head_near, own_near = lax.optimization_barrier(
+        (before, labels, weights, where, head_near, own_near)
+    )
+    far_low = shift(before[:half], "yh", 1, n_yh)
+    far_high = shift(after[half:], "yh", -1, n_yh)
+    near = (own_near, swap(hidden), before, swap(before), after, swap(after))
+    far = (far_low, far_high, swap(far_low), swap(far_high))
+
     block_logits = jax.ShapeDtypeStruct((v_dev, both), F32)
 
-    def cost(blocks):
-        return pl.CostEstimate(
-            flops=2 * v_dev * blocks * both * width,
-            bytes_accessed=2 * (v_dev + blocks * both) * width,
-            transcendentals=v_dev * blocks * both,
-        )
-
-    *near_logits, stats = pl.pallas_call(
-        near_kernel,
-        out_shape=(block_logits,) * 3 + (jax.ShapeDtypeStruct((8, 3 * both), F32),),
-        in_specs=[smem] + [vmem] * 8,
-        out_specs=(vmem,) * 4,
-        compiler_params=params,
-        cost_estimate=cost(3),
-    )(where, head_weight, labels, *near)
-    far_low, far_high, *near_logits, stats = lax.optimization_barrier((far_low, far_high, *near_logits, stats))
-    far = (far_low, far_high, swap(far_low), swap(far_high))
-    far_logits, stats = pl.pallas_call(
-        far_kernel,
-        out_shape=(block_logits, jax.ShapeDtypeStruct((n_shards, 8 * n_yh, both), F32)),
-        in_specs=[smem] + [vmem] * 7,
-        out_specs=(vmem,) * 2,
-        compiler_params=params,
-        cost_estimate=cost(1),
-    )(where, head_weight, labels, stats, *far)
+    *logits, stats = pl.pallas_call(
+        logits_kernel,
+        out_shape=(block_logits,) * 4 + (jax.ShapeDtypeStruct((n_shards, 8 * n_yh, both), F32),),
+        in_specs=[smem] + [vmem] * 12,
+        out_specs=(vmem,) * 5,
+        compiler_params=params,
+        cost_estimate=pl.CostEstimate(
+            flops=4 * v_dev * n_own * width,
+            bytes_accessed=2 * (v_dev + 2 * n_own) * width,
+            transcendentals=2 * v_dev * n_own,
+        ),
+    )(where, head_near, labels, *near, *far)
     stats = lax.all_to_all(stats, VOCAB, 0, 0, tiled=True)
 
     cols = min(1024, width)
@@ -184,13 +176,13 @@
             bytes_accessed=2 * (2 * v_dev + 3 * n_own) * width,
             transcendentals=2 * v_dev * n_own,
         ),
-    )(where, stats, labels, weights, *near_logits, far_logits, *near, *far, head_weight)
+    )(where, stats, labels, weights, *logits, *near, *far, head_near)
     token_loss = loss[0, :tok]
 
     part = partial.reshape(n_x, v_dev // n_x, width)
     part = lax.all_to_all(part, "x", 0, 0, tiled=True)
 
-    home = jnp.dot(score, head_weight, preferred_element_type=F32).astype(BF16)
+    home = jnp.dot(score, head_near, preferred_element_type=F32).astype(BF16)
     terms = (home.astype(F32) + swap(away).astype(F32)).astype(BF16)
     n_rest, rows = n_yl * n_z, v_dev // n_x
     step = min(4, n_rest)

time: 182 us -> 180 us (0.989)
  waiting for transfers between devices: 59.3 us -> 40.6 us
  starting transfers between devices: 63.5 us -> 72.8 us
  blocking collectives: 35.2 us -> 40.8 us
  local copies, waits for them, and re-layouts: 6.82 us -> 8.64 us
    ppermute x18, waiting for transfers between devices: 43.2 us -> 24.5 us  [shift(): lax.ppermute(value, axis, [(i, (i + step) % size) for i in range(size)])]
    ppermute x18, starting transfers between devices: 54.5 us -> 63.8 us  [shift(): lax.ppermute(value, axis, [(i, (i + step) % size) for i in range(size)])]
    all_to_all x1, blocking collectives: 12 us -> 17.7 us  [per_device(): stats = lax.all_to_all(stats, VOCAB, 0, 0, tiled=True)]
    unnamed x14, local copies, waits for them, and re-layouts: 3.6 us -> 5.43 us
  transfers between devices with their start and end apart: 20 -> 20, of which waited for: 9 -> 9; matrix products, arithmetic and copies ran while one was open for 4% -> 4% of each run, Pallas kernels for 1% -> 0%
where the time goes in v9:
time: 180 us; the launch traced here: 179 us
  starting transfers between devices  72.8 us (40%)
  blocking collectives  40.8 us (23%)
  waiting for transfers between devices  40.6 us (23%)
  Pallas kernels  9.23 us (5%)
  local copies, waits for them, and re-layouts  8.64 us (5%)
  other arithmetic  3.29 us (2%)
  matrix products  2.29 us (1%)
    ppermute x18, starting transfers between devices, shift(): lax.ppermute(value, axis, [(i, (i + step) % size) for i in range(size)])  63.8 us
    ppermute x18, waiting for transfers between devices, shift(): lax.ppermute(value, axis, [(i, (i + step) % size) for i in range(size)])  24.5 us
    all_to_all x1, blocking collectives, per_device(): part = lax.all_to_all(part, ('yl', 'z'), 0, 0, tiled=True)  23.1 us
    all_to_all x1, blocking collectives, per_device(): stats = lax.all_to_all(stats, VOCAB, 0, 0, tiled=True)  17.7 us
    all_to_all x1, waiting for transfers between devices, per_device(): part = lax.all_to_all(part, 'x', 0, 0, tiled=True)  12.1 us
    unnamed x14, local copies, waits for them, and re-layouts  5.43 us
    all_to_all x1, starting transfers between devices, per_device(): lax.all_to_all(jnp.broadcast_to(part, (n_yl * n_z,) + part.shape), ('yl',...  4.69 us
    pallas_call x1, Pallas kernels, per_device(): pl.pallas_call(score_kernel, out_shape=(jax.ShapeDtypeStruct((v_dev, widt...  4.47 us
  transfers between devices with their start and end apart: 20, of which 9 were waited for; matrix products, arithmetic and copies ran while one was open for 4% of the time, Pallas kernels for 0%

profile of v9, /device:TPU:72, one launch (start us, length us, event | category | flops | bytes accessed | tf_op | source)
XLA Modules:
  0.0 178.7 jit_solution(10079761578597183110)
XLA Ops:
  0.6 4.5 %collective-permute-start = (bf16[64,4096]{1,0:T(8,128)(2,1)}, bf16[64,4096]{1,0:T(8,128)(2,1)S(1)}, u32[]{:S(2)}, u32[]{:S(2)}) collective-permute-start(bf16[64,4096]{1,0:T(8,128)(2,1)} %own.1), channel_id=1, source_target_pairs={{0,2},{2,4},{4,6},{6,0},{1,3},{3,5},{5,7},{7,1},{8,10},{10,12},{12... | collective-permute-start | bytes 1572872 | tf_op jit(solution)/shard_map/ppermute | solution.py:15
  5.1 3.5 %collective-permute-start.3 = (bf16[64,4096]{1,0:T(8,128)(2,1)}, bf16[64,4096]{1,0:T(8,128)(2,1)S(1)}, u32[]{:S(2)}, u32[]{:S(2)}) collective-permute-start(bf16[64,4096]{1,0:T(8,128)(2,1)} %own.1), channel_id=1, source_target_pairs={{0,6},{2,0},{4,2},{6,4},{1,7},{3,1},{5,3},{7,5},{8,14},{10,8},{12,... | collective-permute-start | bytes 1572872 | tf_op jit(solution)/shard_map/ppermute | solution.py:15
  8.6 1.9 %collective-permute-start.1 = (bf16[64,4096]{1,0:T(8,128)(2,1)}, bf16[64,4096]{1,0:T(8,128)(2,1)S(1)}, u32[]{:S(2)}, u32[]{:S(2)}) collective-permute-start(bf16[64,4096]{1,0:T(8,128)(2,1)} %own.1), channel_id=1, source_target_pairs={{0,1},{1,0},{2,3},{3,2},{4,5},{5,4},{6,7},{7,6},{8,9},{9,8},{10,11... | collective-permute-start | bytes 1572872 | tf_op jit(solution)/shard_map/ppermute | solution.py:15
  16.0 7.7 %collective-permute-done.3.refs_4_.refs_8_ = bf16[64,4096]{1,0:T(8,128)(2,1)S(1)} collective-permute-done((bf16[64,4096]{1,0:T(8,128)(2,1)}, bf16[64,4096]{1,0:T(8,128)(2,1)S(1)}, u32[]{:S(2)}, u32[]{:S(2)}) %collective-permute-start.3) | collective-permute-done | bytes 524320 | tf_op jit(solution)/shard_map/ppermute | solution.py:15
  23.7 4.5 %collective-permute-start.6 = (bf16[32,4096]{1,0:T(8,128)(2,1)S(1)}, bf16[32,4096]{1,0:T(8,128)(2,1)S(1)}, u32[]{:S(2)}, u32[]{:S(2)}) collective-permute-start(bf16[32,4096]{1,0:T(8,128)(2,1)S(1)} %slice.83), channel_id=1, source_target_pairs={{0,6},{2,0},{4,2},{6,4},{1,7},{3,1},{5,3},{7,5},{8,14},{10,8},{12,... | collective-permute-start | bytes 786440 | tf_op jit(solution)/shard_map/ppermute | solution.py:15
  29.8 10.9 %collective-permute-start.5 = (bf16[32,4096]{1,0:T(8,128)(2,1)S(1)}, bf16[32,4096]{1,0:T(8,128)(2,1)S(1)}, u32[]{:S(2)}, u32[]{:S(2)}) collective-permute-start(bf16[32,4096]{1,0:T(8,128)(2,1)S(1)} %slice.65), channel_id=1, source_target_pairs={{0,2},{2,4},{4,6},{6,0},{1,3},{3,5},{5,7},{7,1},{8,10},{10,12},{12... | collective-permute-start | bytes 786440 | tf_op jit(solution)/shard_map/ppermute | solution.py:15
  40.7 1.9 %collective-permute-start.4 = (bf16[64,4096]{1,0:T(8,128)(2,1)S(1)}, bf16[64,4096]{1,0:T(8,128)(2,1)S(1)}, u32[]{:S(2)}, u32[]{:S(2)}) collective-permute-start(bf16[64,4096]{1,0:T(8,128)(2,1)S(1)} %collective-permute-done.3.refs_4_.refs_8_), channel_id=1, source_target_pairs={{0,1},{1,0},{2,3},{3,2},{4,5},{5,4},{6,7},{7,6},{8,9},{9,8},{10,11... | collective-permute-start | bytes 1572872 | tf_op jit(solution)/shard_map/ppermute | solution.py:15
  42.6 2.4 %collective-permute-start.2 = (bf16[64,4096]{1,0:T(8,128)(2,1)S(1)}, bf16[64,4096]{1,0:T(8,128)(2,1)S(1)}, u32[]{:S(2)}, u32[]{:S(2)}) collective-permute-start(bf16[64,4096]{1,0:T(8,128)(2,1)S(1)} %collective-permute-done.refs_2_.refs_6_), channel_id=1, source_target_pairs={{0,1},{1,0},{2,3},{3,2},{4,5},{5,4},{6,7},{7,6},{8,9},{9,8},{10,11... | collective-permute-start | bytes 1572872 | tf_op jit(solution)/shard_map/ppermute | solution.py:15
  45.0 3.3 %collective-permute-done.6.refs_7_.refs_11_ = bf16[32,4096]{1,0:T(8,128)(2,1)S(1)} collective-permute-done((bf16[32,4096]{1,0:T(8,128)(2,1)S(1)}, bf16[32,4096]{1,0:T(8,128)(2,1)S(1)}, u32[]{:S(2)}, u32[]{:S(2)}) %collective-permute-start.6) | collective-permute-done | bytes 262176 | tf_op jit(solution)/shard_map/ppermute | solution.py:15
  48.3 1.9 %collective-permute-start.8 = (bf16[32,4096]{1,0:T(8,128)(2,1)S(1)}, bf16[32,4096]{1,0:T(8,128)(2,1)S(1)}, u32[]{:S(2)}, u32[]{:S(2)}) collective-permute-start(bf16[32,4096]{1,0:T(8,128)(2,1)S(1)} %collective-permute-done.6.refs_7_.refs_11_), channel_id=1, source_target_pairs={{0,1},{1,0},{2,3},{3,2},{4,5},{5,4},{6,7},{7,6},{8,9},{9,8},{10,11... | collective-permute-start | bytes 786440 | tf_op jit(solution)/shard_map/ppermute | solution.py:15
  50.2 2.4 %collective-permute-start.7 = (bf16[32,4096]{1,0:T(8,128)(2,1)S(1)}, bf16[32,4096]{1,0:T(8,128)(2,1)S(1)}, u32[]{:S(2)}, u32[]{:S(2)}) collective-permute-start(bf16[32,4096]{1,0:T(8,128)(2,1)S(1)} %collective-permute-done.5.refs_6_.refs_10_), channel_id=1, source_target_pairs={{0,1},{1,0},{2,3},{3,2},{4,5},{5,4},{6,7},{7,6},{8,9},{9,8},{10,11... | collective-permute-start | bytes 786440 | tf_op jit(solution)/shard_map/ppermute | solution.py:15
  54.8 2.4 %shard_map.68 = (f32[192,128]{1,0:T(8,128)S(1)}, f32[192,128]{1,0:T(8,128)S(1)}, f32[192,128]{1,0:T(8,128)S(1)}, f32[192,128]{1,0:T(8,128)S(1)}, f32[8,32,128]{2,1,0:T(8,128)S(1)}) custom-call(s32[10]{0:T(128)S(1)} %stack.43.where, bf16[192,4096]{1,0:T(8,128)(2,1)S(1)} %get-tuple-element.26.head.refs_14_, s32[1,512]{1,0:T(1,128)S(1)} %reshape.22.labels, ...), custom_call_target="tpu_custom_call" | custom-call | flops 805306368 | bytes 5767168 | tf_op jit(solution)/shard_map/pallas_call | solution.py:140
  57.3 17.7 %all_to_all.20.stats = f32[8,32,128]{2,1,0:T(8,128)S(1)} all-to-all(f32[8,32,128]{2,1,0:T(8,128)S(1)} %get-tuple-element.30), channel_id=1, replica_groups=mesh['x'=4,'yl'=2,'z'=8,'yh'=4,'core'=2] {'yh','core'}, dimensions={0} | all-to-all | bytes 262144 | tf_op jit(solution)/shard_map/all_to_all | solution.py:152
  74.9 4.5 %shard_map.69 = (bf16[192,4096]{1,0:T(8,128)(2,1)S(1)}, bf16[256,4096]{1,0:T(8,128)(2,1)}, bf16[256,192]{1,0:T(8,128)(2,1)S(1)}, f32[1,128]{1,0:T(1,128)S(1)}) custom-call(s32[10]{0:T(128)S(1)} %stack.43.where, f32[8,32,128]{2,1,0:T(8,128)S(1)} %all_to_all.20.stats, s32[1,512]{1,0:T(1,128)S(1)} %reshape.22.labels, f32[1,512]{1,0:T(1,128)S(1)} %reshape.24.weights, ...), custom_call_target="tpu_custom_call" | custom-call | flops 1207959552 | bytes 9437184 | tf_op jit(solution)/shard_map/pallas_call | solution.py:157
  80.5 1.9 %collective-permute-start.9 = (bf16[256,4096]{1,0:T(8,128)(2,1)}, bf16[256,4096]{1,0:T(8,128)(2,1)}, u32[]{:S(2)}, u32[]{:S(2)}) collective-permute-start(bf16[256,4096]{1,0:T(8,128)(2,1)} %get-tuple-element.38), channel_id=1, source_target_pairs={{0,1},{1,0},{2,3},{3,2},{4,5},{5,4},{6,7},{7,6},{8,9},{9,8},{10,11... | collective-permute-start | bytes 6291464 | tf_op jit(solution)/shard_map/ppermute | solution.py:15
  82.5 4.3 %all-to-all-start.1 = ((bf16[4,48,4096]{2,1,0:T(8,128)(2,1)}), bf16[4,48,4096]{2,1,0:T(8,128)(2,1)S(1)}, u32[]{:S(2)}, u32[]{:S(2)}) async-start(bf16[4,48,4096]{2,1,0:T(8,128)(2,1)} %bitcast.31), calls=%async_computation.1 | async-start | bytes 3145728 | tf_op jit(solution)/shard_map/all_to_all | solution.py:183
  86.9 2.3 %fusion.2 = bf16[256,4096]{1,0:T(8,128)(2,1)S(1)} fusion(bf16[256,192]{1,0:T(8,128)(2,1)S(1)} %get-tuple-element.37, bf16[192,4096]{1,0:T(8,128)(2,1)S(1)} %get-tuple-element.26.head.refs_14_, bf16[256,4096]{1,0:T(8,128)(2,1)} %collective-permute-done.9), kind=kOutput, calls=%fused_computation.3 | convolution fusion | flops 407896064 | bytes 5865472 | tf_op jit(solution)/shard_map/dot_general | solution.py:185
  89.3 2.5 %collective-permute-start.11 = (bf16[32,4096]{1,0:T(8,128)(2,1)S(1)}, bf16[32,4096]{1,0:T(8,128)(2,1)S(1)}, u32[]{:S(2)}, u32[]{:S(2)}) collective-permute-start(bf16[32,4096]{1,0:T(8,128)(2,1)S(1)} %get-tuple-element.45), channel_id=1, source_target_pairs={{0,6},{2,0},{4,2},{6,4},{1,7},{3,1},{5,3},{7,5},{8,14},{10,8},{12,... | collective-permute-start | bytes 786440 | tf_op jit(solution)/shard_map/ppermute | solution.py:15
  91.8 4.3 %collective-permute-start.10 = (bf16[32,4096]{1,0:T(8,128)(2,1)S(1)}, bf16[32,4096]{1,0:T(8,128)(2,1)S(1)}, u32[]{:S(2)}, u32[]{:S(2)}) collective-permute-start(bf16[32,4096]{1,0:T(8,128)(2,1)S(1)} %get-tuple-element.46), channel_id=1, source_target_pairs={{0,2},{2,4},{4,6},{6,0},{1,3},{3,5},{5,7},{7,1},{8,10},{10,12},{12... | collective-permute-start | bytes 786440 | tf_op jit(solution)/shard_map/ppermute | solution.py:15
  96.1 12.1 %all-to-all-done.1.parts = bf16[4,48,4096]{2,1,0:T(8,128)(2,1)S(1)} async-done(((bf16[4,48,4096]{2,1,0:T(8,128)(2,1)}), bf16[4,48,4096]{2,1,0:T(8,128)(2,1)S(1)}, u32[]{:S(2)}, u32[]{:S(2)}) %all-to-all-start.1) | async-done | bytes 1572896 | tf_op jit(solution)/shard_map/all_to_all | solution.py:183
  108.6 23.1 %all_to_all.21 = bf16[16,48,256]{2,1,0:T(8,128)(2,1)S(1)} all-to-all(bf16[16,48,256]{2,1,0:T(8,128)(2,1)S(1)} %shard_map.70), channel_id=1, replica_groups=mesh['x'=4,'yl'=2,'z'=8,'yh'=4,'core'=2] {'yl','z'}, dimensions={0} | all-to-all | bytes 786432 | tf_op jit(solution)/shard_map/all_to_all | solution.py:208
  132.5 4.7 %all-to-all-start.3 = ((bf16[16,48,256]{2,1,0:T(8,128)(2,1)}), bf16[16,48,256]{2,1,0:T(8,128)(2,1)S(1)}, u32[]{:S(2)}, u32[]{:S(2)}) async-start(bf16[16,48,256]{2,1,0:T(8,128)(2,1)} %broadcast_in_dim.4), calls=%async_computation.3 | async-start | bytes 786432 | tf_op jit(solution)/shard_map/all_to_all | solution.py:210
  138.2 3.6 %collective-permute-start.12 = (bf16[64,4096]{1,0:T(8,128)(2,1)}, bf16[64,4096]{1,0:T(8,128)(2,1)}, u32[]{:S(2)}, u32[]{:S(2)}) collective-permute-start(bf16[64,4096]{1,0:T(8,128)(2,1)} %get-tuple-element.43), channel_id=1, source_target_pairs={{0,2},{2,4},{4,6},{6,0},{1,3},{3,5},{5,7},{7,1},{8,10},{10,12},{12... | collective-permute-start | bytes 1572872 | tf_op jit(solution)/shard_map/ppermute | solution.py:15
  141.8 4.3 %collective-permute-start.13 = (bf16[64,4096]{1,0:T(8,128)(2,1)S(1)}, bf16[64,4096]{1,0:T(8,128)(2,1)}, u32[]{:S(2)}, u32[]{:S(2)}) collective-permute-start(bf16[64,4096]{1,0:T(8,128)(2,1)S(1)} %get-tuple-element.44), channel_id=1, source_target_pairs={{0,6},{2,0},{4,2},{6,4},{1,7},{3,1},{5,3},{7,5},{8,14},{10,8},{12,... | collective-permute-start | bytes 1572872 | tf_op jit(solution)/shard_map/ppermute | solution.py:15
  146.1 4.0 %all-to-all-done.3.own = bf16[16,48,256]{2,1,0:T(8,128)(2,1)S(1)} async-done(((bf16[16,48,256]{2,1,0:T(8,128)(2,1)}), bf16[16,48,256]{2,1,0:T(8,128)(2,1)S(1)}, u32[]{:S(2)}, u32[]{:S(2)}) %all-to-all-start.3) | async-done | bytes 393248 | tf_op jit(solution)/shard_map/all_to_all | solution.py:210
  150.2 4.1 %collective-permute-start.15 = (bf16[16,48,256]{2,1,0:T(8,128)(2,1)S(1)}, bf16[16,48,256]{2,1,0:T(8,128)(2,1)S(1)}, u32[]{:S(2)}, u32[]{:S(2)}) collective-permute-start(bf16[16,48,256]{2,1,0:T(8,128)(2,1)S(1)} %all-to-all-done.3.own), channel_id=1, source_target_pairs={{0,384},{128,0},{256,128},{384,256},{1,385},{129,1},{257,129},{385... | collective-permute-start | bytes 1179656 | tf_op jit(solution)/shard_map/ppermute | solution.py:15
  154.3 1.9 %collective-permute-start.14 = (bf16[16,48,256]{2,1,0:T(8,128)(2,1)S(1)}, bf16[16,48,256]{2,1,0:T(8,128)(2,1)S(1)}, u32[]{:S(2)}, u32[]{:S(2)}) collective-permute-start(bf16[16,48,256]{2,1,0:T(8,128)(2,1)S(1)} %all-to-all-done.3.own), channel_id=1, source_target_pairs={{0,128},{128,256},{256,384},{384,0},{1,129},{129,257},{257,385},{3... | collective-permute-start | bytes 1179656 | tf_op jit(solution)/shard_map/ppermute | solution.py:15
  156.7 6.0 %collective-permute-done.15.after = bf16[16,48,256]{2,1,0:T(8,128)(2,1)S(1)} collective-permute-done((bf16[16,48,256]{2,1,0:T(8,128)(2,1)S(1)}, bf16[16,48,256]{2,1,0:T(8,128)(2,1)S(1)}, u32[]{:S(2)}, u32[]{:S(2)}) %collective-permute-start.15) | collective-permute-done | bytes 393248 | tf_op jit(solution)/shard_map/ppermute | solution.py:15
  162.7 5.3 %collective-permute-start.17 = (bf16[8,48,256]{2,1,0:T(8,128)(2,1)S(1)}, bf16[8,48,256]{2,1,0:T(8,128)(2,1)S(1)}, u32[]{:S(2)}, u32[]{:S(2)}) collective-permute-start(bf16[8,48,256]{2,1,0:T(8,128)(2,1)S(1)} %slice.90), channel_id=1, source_target_pairs={{0,384},{128,0},{256,128},{384,256},{1,385},{129,1},{257,129},{385... | collective-permute-start | bytes 589832 | tf_op jit(solution)/shard_map/ppermute | solution.py:15
  168.1 1.9 %collective-permute-start.16 = (bf16[8,48,256]{2,1,0:T(8,128)(2,1)S(1)}, bf16[8,48,256]{2,1,0:T(8,128)(2,1)S(1)}, u32[]{:S(2)}, u32[]{:S(2)}) collective-permute-start(bf16[8,48,256]{2,1,0:T(8,128)(2,1)S(1)} %slice.89), channel_id=1, source_target_pairs={{0,128},{128,256},{256,384},{384,0},{1,129},{129,257},{257,385},{3... | collective-permute-start | bytes 589832 | tf_op jit(solution)/shard_map/ppermute | solution.py:15
  170.0 2.2 %add_convert_fusion = bf16[64,4096]{1,0:T(8,128)(2,1)} fusion(bf16[64,4096]{1,0:T(8,128)(2,1)} %collective-permute-done.13, bf16[64,4096]{1,0:T(8,128)(2,1)} %collective-permute-done.12, bf16[256,4096]{1,0:T(8,128)(2,1)S(1)} %copy-done.6), kind=kLoop, calls=%fused_computation.4 | loop fusion | flops 1572864 | bytes 2097152 | tf_op jit(solution)/shard_map/convert_element_type | solution.py:223
  172.2 4.6 %collective-permute-done.16.far_low = bf16[8,48,256]{2,1,0:T(8,128)(2,1)S(1)} collective-permute-done((bf16[8,48,256]{2,1,0:T(8,128)(2,1)S(1)}, bf16[8,48,256]{2,1,0:T(8,128)(2,1)S(1)}, u32[]{:S(2)}, u32[]{:S(2)}) %collective-permute-start.16) | collective-permute-done | bytes 196640 | tf_op jit(solution)/shard_map/ppermute | solution.py:15
  (55 shorter events, 14.9 us)
Async XLA Ops:
  0.6 29.1 %collective-permute-start = (bf16[64,4096]{1,0:T(8,128)(2,1)}, bf16[64,4096]{1,0:T(8,128)(2,1)S(1)}, u32[]{:S(2)}, u32[]{:S(2)}) collective-permute-start(bf16[64,4096]{1,0:T(8,128)(2,1)} %own.1), channel_id=1, source_target_pairs={{0,2},{2,4},{4,6},{6,0},{1,3},{3,5},{5,7},{7,1},{8,10},{10,12},{12... | collective-permute-start | bytes 1572872 | tf_op jit(solution)/shard_map/ppermute | solution.py:15
  5.1 18.5 %collective-permute-start.3 = (bf16[64,4096]{1,0:T(8,128)(2,1)}, bf16[64,4096]{1,0:T(8,128)(2,1)S(1)}, u32[]{:S(2)}, u32[]{:S(2)}) collective-permute-start(bf16[64,4096]{1,0:T(8,128)(2,1)} %own.1), channel_id=1, source_target_pairs={{0,6},{2,0},{4,2},{6,4},{1,7},{3,1},{5,3},{7,5},{8,14},{10,8},{12,... | collective-permute-start | bytes 1572872 | tf_op jit(solution)/shard_map/ppermute | solution.py:15
  8.6 44.0 %collective-permute-start.1 = (bf16[64,4096]{1,0:T(8,128)(2,1)}, bf16[64,4096]{1,0:T(8,128)(2,1)S(1)}, u32[]{:S(2)}, u32[]{:S(2)}) collective-permute-start(bf16[64,4096]{1,0:T(8,128)(2,1)} %own.1), channel_id=1, source_target_pairs={{0,1},{1,0},{2,3},{3,2},{4,5},{5,4},{6,7},{7,6},{8,9},{9,8},{10,11... | collective-permute-start | bytes 1572872 | tf_op jit(solution)/shard_map/ppermute | solution.py:15
  12.5 1.4 copy-start.3
  13.9 1.0 copy-start.4
  15.1 0.8 copy-start
  23.7 24.6 %collective-permute-start.6 = (bf16[32,4096]{1,0:T(8,128)(2,1)S(1)}, bf16[32,4096]{1,0:T(8,128)(2,1)S(1)}, u32[]{:S(2)}, u32[]{:S(2)}) collective-permute-start(bf16[32,4096]{1,0:T(8,128)(2,1)S(1)} %slice.83), channel_id=1, source_target_pairs={{0,6},{2,0},{4,2},{6,4},{1,7},{3,1},{5,3},{7,5},{8,14},{10,8},{12,... | collective-permute-start | bytes 786440 | tf_op jit(solution)/shard_map/ppermute | solution.py:15
  29.8 20.5 %collective-permute-start.5 = (bf16[32,4096]{1,0:T(8,128)(2,1)S(1)}, bf16[32,4096]{1,0:T(8,128)(2,1)S(1)}, u32[]{:S(2)}, u32[]{:S(2)}) collective-permute-start(bf16[32,4096]{1,0:T(8,128)(2,1)S(1)} %slice.65), channel_id=1, source_target_pairs={{0,2},{2,4},{4,6},{6,0},{1,3},{3,5},{5,7},{7,1},{8,10},{10,12},{12... | collective-permute-start | bytes 786440 | tf_op jit(solution)/shard_map/ppermute | solution.py:15
  40.7 12.0 %collective-permute-start.4 = (bf16[64,4096]{1,0:T(8,128)(2,1)S(1)}, bf16[64,4096]{1,0:T(8,128)(2,1)S(1)}, u32[]{:S(2)}, u32[]{:S(2)}) collective-permute-start(bf16[64,4096]{1,0:T(8,128)(2,1)S(1)} %collective-permute-done.3.refs_4_.refs_8_), channel_id=1, source_target_pairs={{0,1},{1,0},{2,3},{3,2},{4,5},{5,4},{6,7},{7,6},{8,9},{9,8},{10,11... | collective-permute-start | bytes 1572872 | tf_op jit(solution)/shard_map/ppermute | solution.py:15
  42.6 11.2 %collective-permute-start.2 = (bf16[64,4096]{1,0:T(8,128)(2,1)S(1)}, bf16[64,4096]{1,0:T(8,128)(2,1)S(1)}, u32[]{:S(2)}, u32[]{:S(2)}) collective-permute-start(bf16[64,4096]{1,0:T(8,128)(2,1)S(1)} %collective-permute-done.refs_2_.refs_6_), channel_id=1, source_target_pairs={{0,1},{1,0},{2,3},{3,2},{4,5},{5,4},{6,7},{7,6},{8,9},{9,8},{10,11... | collective-permute-start | bytes 1572872 | tf_op jit(solution)/shard_map/ppermute | solution.py:15
  48.3 4.4 %collective-permute-start.8 = (bf16[32,4096]{1,0:T(8,128)(2,1)S(1)}, bf16[32,4096]{1,0:T(8,128)(2,1)S(1)}, u32[]{:S(2)}, u32[]{:S(2)}) collective-permute-start(bf16[32,4096]{1,0:T(8,128)(2,1)S(1)} %collective-permute-done.6.refs_7_.refs_11_), channel_id=1, source_target_pairs={{0,1},{1,0},{2,3},{3,2},{4,5},{5,4},{6,7},{7,6},{8,9},{9,8},{10,11... | collective-permute-start | bytes 786440 | tf_op jit(solution)/shard_map/ppermute | solution.py:15
  50.2 3.6 %collective-permute-start.7 = (bf16[32,4096]{1,0:T(8,128)(2,1)S(1)}, bf16[32,4096]{1,0:T(8,128)(2,1)S(1)}, u32[]{:S(2)}, u32[]{:S(2)}) collective-permute-start(bf16[32,4096]{1,0:T(8,128)(2,1)S(1)} %collective-permute-done.5.refs_6_.refs_10_), channel_id=1, source_target_pairs={{0,1},{1,0},{2,3},{3,2},{4,5},{5,4},{6,7},{7,6},{8,9},{9,8},{10,11... | collective-permute-start | bytes 786440 | tf_op jit(solution)/shard_map/ppermute | solution.py:15
  53.8 1.0 copy-start.1
  79.4 1.1 copy-start.2
  80.5 6.4 %collective-permute-start.9 = (bf16[256,4096]{1,0:T(8,128)(2,1)}, bf16[256,4096]{1,0:T(8,128)(2,1)}, u32[]{:S(2)}, u32[]{:S(2)}) collective-permute-start(bf16[256,4096]{1,0:T(8,128)(2,1)} %get-tuple-element.38), channel_id=1, source_target_pairs={{0,1},{1,0},{2,3},{3,2},{4,5},{5,4},{6,7},{7,6},{8,9},{9,8},{10,11... | collective-permute-start | bytes 6291464 | tf_op jit(solution)/shard_map/ppermute | solution.py:15
  82.5 25.7 %all-to-all-start.1 = ((bf16[4,48,4096]{2,1,0:T(8,128)(2,1)}), bf16[4,48,4096]{2,1,0:T(8,128)(2,1)S(1)}, u32[]{:S(2)}, u32[]{:S(2)}) async-start(bf16[4,48,4096]{2,1,0:T(8,128)(2,1)} %bitcast.31), calls=%async_computation.1 | async-start | bytes 3145728 | tf_op jit(solution)/shard_map/all_to_all | solution.py:183
  89.2 2.5 %copy-start.5 = (bf16[256,4096]{1,0:T(8,128)(2,1)}, bf16[256,4096]{1,0:T(8,128)(2,1)S(1)}, u32[]{:S(2)}) copy-start(bf16[256,4096]{1,0:T(8,128)(2,1)S(1)} %fusion.2) | copy-start | bytes 6291460
  89.3 19.3 %collective-permute-start.11 = (bf16[32,4096]{1,0:T(8,128)(2,1)S(1)}, bf16[32,4096]{1,0:T(8,128)(2,1)S(1)}, u32[]{:S(2)}, u32[]{:S(2)}) collective-permute-start(bf16[32,4096]{1,0:T(8,128)(2,1)S(1)} %get-tuple-element.45), channel_id=1, source_target_pairs={{0,6},{2,0},{4,2},{6,4},{1,7},{3,1},{5,3},{7,5},{8,14},{10,8},{12,... | collective-permute-start | bytes 786440 | tf_op jit(solution)/shard_map/ppermute | solution.py:15
  91.8 16.8 %collective-permute-start.10 = (bf16[32,4096]{1,0:T(8,128)(2,1)S(1)}, bf16[32,4096]{1,0:T(8,128)(2,1)S(1)}, u32[]{:S(2)}, u32[]{:S(2)}) collective-permute-start(bf16[32,4096]{1,0:T(8,128)(2,1)S(1)} %get-tuple-element.46), channel_id=1, source_target_pairs={{0,2},{2,4},{4,6},{6,0},{1,3},{3,5},{5,7},{7,1},{8,10},{10,12},{12... | collective-permute-start | bytes 786440 | tf_op jit(solution)/shard_map/ppermute | solution.py:15
  108.5 28.7 %copy-start.6 = (bf16[256,4096]{1,0:T(8,128)(2,1)S(1)}, bf16[256,4096]{1,0:T(8,128)(2,1)}, u32[]{:S(2)}) copy-start(bf16[256,4096]{1,0:T(8,128)(2,1)} %copy-done.5) | copy-start | bytes 6291460
  132.5 17.6 %all-to-all-start.3 = ((bf16[16,48,256]{2,1,0:T(8,128)(2,1)}), bf16[16,48,256]{2,1,0:T(8,128)(2,1)S(1)}, u32[]{:S(2)}, u32[]{:S(2)}) async-start(bf16[16,48,256]{2,1,0:T(8,128)(2,1)} %broadcast_in_dim.4), calls=%async_computation.3 | async-start | bytes 786432 | tf_op jit(solution)/shard_map/all_to_all | solution.py:210
  138.2 31.8 %collective-permute-start.12 = (bf16[64,4096]{1,0:T(8,128)(2,1)}, bf16[64,4096]{1,0:T(8,128)(2,1)}, u32[]{:S(2)}, u32[]{:S(2)}) collective-permute-start(bf16[64,4096]{1,0:T(8,128)(2,1)} %get-tuple-element.43), channel_id=1, source_target_pairs={{0,2},{2,4},{4,6},{6,0},{1,3},{3,5},{5,7},{7,1},{8,10},{10,12},{12... | collective-permute-start | bytes 1572872 | tf_op jit(solution)/shard_map/ppermute | solution.py:15
  141.8 28.2 %collective-permute-start.13 = (bf16[64,4096]{1,0:T(8,128)(2,1)S(1)}, bf16[64,4096]{1,0:T(8,128)(2,1)}, u32[]{:S(2)}, u32[]{:S(2)}) collective-permute-start(bf16[64,4096]{1,0:T(8,128)(2,1)S(1)} %get-tuple-element.44), channel_id=1, source_target_pairs={{0,6},{2,0},{4,2},{6,4},{1,7},{3,1},{5,3},{7,5},{8,14},{10,8},{12,... | collective-permute-start | bytes 1572872 | tf_op jit(solution)/shard_map/ppermute | solution.py:15
  150.2 12.5 %collective-permute-start.15 = (bf16[16,48,256]{2,1,0:T(8,128)(2,1)S(1)}, bf16[16,48,256]{2,1,0:T(8,128)(2,1)S(1)}, u32[]{:S(2)}, u32[]{:S(2)}) collective-permute-start(bf16[16,48,256]{2,1,0:T(8,128)(2,1)S(1)} %all-to-all-done.3.own), channel_id=1, source_target_pairs={{0,384},{128,0},{256,128},{384,256},{1,385},{129,1},{257,129},{385... | collective-permute-start | bytes 1179656 | tf_op jit(solution)/shard_map/ppermute | solution.py:15
  154.3 13.8 %collective-permute-start.14 = (bf16[16,48,256]{2,1,0:T(8,128)(2,1)S(1)}, bf16[16,48,256]{2,1,0:T(8,128)(2,1)S(1)}, u32[]{:S(2)}, u32[]{:S(2)}) collective-permute-start(bf16[16,48,256]{2,1,0:T(8,128)(2,1)S(1)} %all-to-all-done.3.own), channel_id=1, source_target_pairs={{0,128},{128,256},{256,384},{384,0},{1,129},{129,257},{257,385},{3... | collective-permute-start | bytes 1179656 | tf_op jit(solution)/shard_map/ppermute | solution.py:15
  162.7 9.5 %collective-permute-start.17 = (bf16[8,48,256]{2,1,0:T(8,128)(2,1)S(1)}, bf16[8,48,256]{2,1,0:T(8,128)(2,1)S(1)}, u32[]{:S(2)}, u32[]{:S(2)}) collective-permute-start(bf16[8,48,256]{2,1,0:T(8,128)(2,1)S(1)} %slice.90), channel_id=1, source_target_pairs={{0,384},{128,0},{256,128},{384,256},{1,385},{129,1},{257,129},{385... | collective-permute-start | bytes 589832 | tf_op jit(solution)/shard_map/ppermute | solution.py:15
  168.1 8.8 %collective-permute-start.16 = (bf16[8,48,256]{2,1,0:T(8,128)(2,1)S(1)}, bf16[8,48,256]{2,1,0:T(8,128)(2,1)S(1)}, u32[]{:S(2)}, u32[]{:S(2)}) collective-permute-start(bf16[8,48,256]{2,1,0:T(8,128)(2,1)S(1)} %slice.89), channel_id=1, source_target_pairs={{0,128},{128,256},{256,384},{384,0},{1,129},{129,257},{257,385},{3... | collective-permute-start | bytes 589832 | tf_op jit(solution)/shard_map/ppermute | solution.py:15

commit v10 on v9

--- a/solution.py
+++ b/solution.py
@@ -32,7 +32,7 @@
     total = jnp.sum(jnp.exp(value - top), axis=0, keepdims=True)
     target = jnp.sum(jnp.where(hits(where, labels, value.shape), value, 0.0), axis=0, keepdims=True)
     blank = jnp.zeros_like(top)
-    tile = jnp.concatenate([top, total, target] + [blank] * 5, axis=0)
+    tile = jnp.concatenate([top, total, target, blank] * 2, axis=0)
     return jnp.where(where[0] == 0, tile, pltpu.roll(tile, tile.shape[1] // 2, 1))
 
 
@@ -41,46 +41,66 @@
     own_out[...] = own[...]
 
 
+def pick(where, tiles, place):
+    chosen = tiles[0]
+    for m in range(1, 4):
+        chosen = jnp.where(where[2 + m] == place, tiles[m], chosen)
+    return chosen
+
+
 def logits_kernel(where, head, labels, *refs):
     pieces, logits, stats = refs[:10], refs[10:14], refs[14]
     n = logits[0].shape[1]
+    tiles = []
     for m, chosen in enumerate((pieces[:2], pieces[2:4], pieces[4:6], pieces[6:])):
-        tile = block_stats(where, head, chosen, labels[:, m * n : (m + 1) * n], logits[m])
-        at = pl.multiple_of(where[2 + m] * 8, 8)
+        tiles.append(block_stats(where, head, chosen, labels[:, m * n : (m + 1) * n], logits[m]))
+    upper = lax.broadcasted_iota(jnp.int32, (8, n), 0) < 4
+    for pair in range(2):
+        line = jnp.where(upper, pick(where, tiles, 2 * pair), pick(where, tiles, 2 * pair + 1))
         for shard in range(stats.shape[0]):
-            stats[shard, pl.ds(at, 8), :] = tile
+            stats[shard, 8 * pair : 8 * pair + 8, :] = line
 
 
 def score_kernel(where, stats, labels, weights, *refs):
     all_logits, pieces, head = refs[:4], refs[4:14], refs[14]
-    grad, away, score, loss, held, turned = refs[15:]
+    grad, away, score, loss, held, turned, near, sent = refs[15:]
     n = all_logits[0].shape[1]
     half = n // 2
 
-    @pl.when(pl.program_id(0) == 0)
-    def _():
-        for m, logits in enumerate(all_logits):
-            lanes = slice(m * n, (m + 1) * n)
-            part = stats[:, pl.ds(pl.multiple_of(where[2 + m] * 8, 8), 8), :]
-            tops = part[:, 0, :]
-            top = jnp.max(tops, axis=0, keepdims=True)
-            total = jnp.sum(part[:, 1, :] * jnp.exp(tops - top), axis=0, keepdims=True)
-            log_total = top + jnp.log(total)
-            lost = log_total - jnp.sum(part[:, 2, :], axis=0, keepdims=True)
-            both = jnp.concatenate([log_total, lost] + [jnp.zeros_like(top)] * 6, axis=0)
-            both = jnp.where(where[0] == 0, both, pltpu.roll(both, half, 1))
-            if m == 0:
-                loss[...] = both[1:2]
-            hit = hits(where, labels[:, lanes], logits.shape).astype(F32)
-            value = weights[:, lanes] * (jnp.exp(logits[...] - both[0:1]) - hit)
-            held[:, lanes] = value.astype(BF16)
-            value = value.T.astype(BF16)
-            score[m * half : (m + 1) * half] = value[:half]
-            turned[m * half : (m + 1) * half] = value[half:]
-
-    block = jnp.concatenate([piece[...] for piece in pieces], axis=0)
-    grad[...] = jnp.dot(held[...], block, preferred_element_type=F32).astype(BF16)
-    away[...] = jnp.dot(turned[...], head[...], preferred_element_type=F32).astype(BF16)
+    merged = []
+    for place in range(4):
+        tops = stats[:, 4 * place, :]
+        top = jnp.max(tops, axis=0, keepdims=True)
+        total = jnp.sum(stats[:, 4 * place + 1, :] * jnp.exp(tops - top), axis=0, keepdims=True)
+        log_total = top + jnp.log(total)
+        lost = log_total - jnp.sum(stats[:, 4 * place + 2, :], axis=0, keepdims=True)
+        merged.append(jnp.concatenate([log_total, lost] + [jnp.zeros_like(top)] * 6, axis=0))
+    for m, logits in enumerate(all_logits):
+        lanes = slice(m * n, (m + 1) * n)
+        both = merged[0]
+        for place in range(1, 4):
+            both = jnp.where(where[2 + m] == place, merged[place], both)
+        both = jnp.where(where[0] == 0, both, pltpu.roll(both, half, 1))
+        if m == 0:
+            loss[...] = both[1:2]
+        hit = hits(where, labels[:, lanes], logits.shape).astype(F32)
+        value = weights[:, lanes] * (jnp.exp(logits[...] - both[0:1]) - hit)
+        held[:, lanes] = value.astype(BF16)
+        value = value.T.astype(BF16)
+        score[m * half : (m + 1) * half] = value[:half]
+        turned[m * half : (m + 1) * half] = value[half:]
+
+    cols = head.shape[1] // 4
+    copies = []
+    for i in range(4):
+        span = slice(i * cols, (i + 1) * cols)
+        block = jnp.concatenate([piece[:, span] for piece in pieces], axis=0)
+        near[:, span] = jnp.dot(held[...], block, preferred_element_type=F32).astype(BF16)
+        copies.append(pltpu.make_async_copy(near.at[:, span], grad.at[:, span], sent.at[i]))
+        copies[-1].start()
+        away[:, span] = jnp.dot(turned[...], head[:, span], preferred_element_type=F32).astype(BF16)
+    for copy in copies:
+        copy.wait()
 
 
 def sum_kernel(parts, out):
@@ -139,7 +159,7 @@
 
     *logits, stats = pl.pallas_call(
         logits_kernel,
-        out_shape=(block_logits,) * 4 + (jax.ShapeDtypeStruct((n_shards, 8 * n_yh, both), F32),),
+        out_shape=(block_logits,) * 4 + (jax.ShapeDtypeStruct((n_shards, 4 * n_yh, both), F32),),
         in_specs=[smem] + [vmem] * 12,
         out_specs=(vmem,) * 5,
         compiler_params=params,
@@ -151,9 +171,6 @@
     )(where, head_near, labels, *near, *far)
     stats = lax.all_to_all(stats, VOCAB, 0, 0, tiled=True)
 
-    cols = min(1024, width)
-    whole = lambda *shape: pl.BlockSpec(shape, lambda i: (0,) * len(shape))
-    wide = lambda rows: pl.BlockSpec((rows, cols), lambda i: (0, i))
     partial, away, score, loss = pl.pallas_call(
         score_kernel,
         out_shape=(
@@ -162,15 +179,15 @@
             jax.ShapeDtypeStruct((n_own, v_dev), BF16),
             jax.ShapeDtypeStruct((1, both), F32),
         ),
-        grid=(width // cols,),
-        in_specs=[smem, whole(*stats.shape), whole(1, 2 * n_own), whole(1, 2 * n_own)]
-        + [whole(v_dev, both)] * 4
-        + [wide(tok)] * 6
-        + [wide(half)] * 4
-        + [wide(v_dev)],
-        out_specs=(wide(v_dev), wide(n_own), whole(n_own, v_dev), whole(1, both)),
-        scratch_shapes=[pltpu.VMEM((v_dev, 2 * n_own), BF16), pltpu.VMEM((n_own, v_dev), BF16)],
-        compiler_params=params,
+        in_specs=[smem] + [vmem] * 18,
+        out_specs=(pl.BlockSpec(memory_space=pl.ANY),) + (vmem,) * 3,
+        scratch_shapes=[
+            pltpu.VMEM((v_dev, 2 * n_own), BF16),
+            pltpu.VMEM((n_own, v_dev), BF16),
+            pltpu.VMEM((v_dev, width), BF16),
+            pltpu.SemaphoreType.DMA((4,)),
+        ],
+        compiler_params=pltpu.CompilerParams(vmem_limit_bytes=48 << 20),
         cost_estimate=pl.CostEstimate(
             flops=6 * v_dev * n_own * width,
             bytes_accessed=2 * (2 * v_dev + 3 * n_own) * width,

time: 180 us -> 180 us (level)
  waiting for transfers between devices: 40.6 us -> 38.8 us
    unnamed x14 -> x18, local copies, waits for them, and re-layouts: 5.43 us -> 4.3 us
  transfers between devices with their start and end apart: 20 -> 20, of which waited for: 9 -> 10; matrix products, arithmetic and copies ran while one was open for 4% -> 5% of each run, Pallas kernels for 0% -> 0%
where the time goes in v10:
time: 180 us; the launch traced here: 179 us
  starting transfers between devices  74 us (41%)
  blocking collectives  40.2 us (22%)
  waiting for transfers between devices  38.8 us (22%)
  Pallas kernels  9.89 us (5%)
  local copies, waits for them, and re-layouts  8.29 us (5%)
  other arithmetic  4.23 us (2%)
  matrix products  2.29 us (1%)
    ppermute x18, starting transfers between devices, shift(): lax.ppermute(value, axis, [(i, (i + step) % size) for i in range(size)])  65 us
    ppermute x18, waiting for transfers between devices, shift(): lax.ppermute(value, axis, [(i, (i + step) % size) for i in range(size)])  24.4 us
    all_to_all x1, blocking collectives, per_device(): part = lax.all_to_all(part, ('yl', 'z'), 0, 0, tiled=True)  23.6 us
    all_to_all x1, blocking collectives, per_device(): stats = lax.all_to_all(stats, VOCAB, 0, 0, tiled=True)  16.6 us
    all_to_all x1, waiting for transfers between devices, per_device(): part = lax.all_to_all(part, 'x', 0, 0, tiled=True)  11.3 us
    pallas_call x1, Pallas kernels, per_device(): pl.pallas_call(score_kernel, out_shape=(jax.ShapeDtypeStruct((v_dev, widt...  5.12 us
    all_to_all x1, starting transfers between devices, per_device(): lax.all_to_all(jnp.broadcast_to(part, (n_yl * n_z,) + part.shape), ('yl',...  4.69 us
    all_to_all x1, starting transfers between devices, per_device(): part = lax.all_to_all(part, 'x', 0, 0, tiled=True)  4.3 us
  transfers between devices with their start and end apart: 20, of which 10 were waited for; matrix products, arithmetic and copies ran while one was open for 5% of the time, Pallas kernels for 0%

profile of v10, /device:TPU:72, one launch (start us, length us, event | category | flops | bytes accessed | tf_op | source)
XLA Modules:
  0.0 178.8 jit_solution(4041892690735800003)
XLA Ops:
  0.6 4.5 %collective-permute-start = (bf16[64,4096]{1,0:T(8,128)(2,1)}, bf16[64,4096]{1,0:T(8,128)(2,1)S(1)}, u32[]{:S(2)}, u32[]{:S(2)}) collective-permute-start(bf16[64,4096]{1,0:T(8,128)(2,1)} %own.1), channel_id=1, source_target_pairs={{0,2},{2,4},{4,6},{6,0},{1,3},{3,5},{5,7},{7,1},{8,10},{10,12},{12... | collective-permute-start | bytes 1572872 | tf_op jit(solution)/shard_map/ppermute | solution.py:15
  5.1 3.5 %collective-permute-start.3 = (bf16[64,4096]{1,0:T(8,128)(2,1)}, bf16[64,4096]{1,0:T(8,128)(2,1)S(1)}, u32[]{:S(2)}, u32[]{:S(2)}) collective-permute-start(bf16[64,4096]{1,0:T(8,128)(2,1)} %own.1), channel_id=1, source_target_pairs={{0,6},{2,0},{4,2},{6,4},{1,7},{3,1},{5,3},{7,5},{8,14},{10,8},{12,... | collective-permute-start | bytes 1572872 | tf_op jit(solution)/shard_map/ppermute | solution.py:15
  8.6 1.9 %collective-permute-start.1 = (bf16[64,4096]{1,0:T(8,128)(2,1)}, bf16[64,4096]{1,0:T(8,128)(2,1)S(1)}, u32[]{:S(2)}, u32[]{:S(2)}) collective-permute-start(bf16[64,4096]{1,0:T(8,128)(2,1)} %own.1), channel_id=1, source_target_pairs={{0,1},{1,0},{2,3},{3,2},{4,5},{5,4},{6,7},{7,6},{8,9},{9,8},{10,11... | collective-permute-start | bytes 1572872 | tf_op jit(solution)/shard_map/ppermute | solution.py:15
  16.0 7.7 %collective-permute-done.3.refs_4_.refs_8_ = bf16[64,4096]{1,0:T(8,128)(2,1)S(1)} collective-permute-done((bf16[64,4096]{1,0:T(8,128)(2,1)}, bf16[64,4096]{1,0:T(8,128)(2,1)S(1)}, u32[]{:S(2)}, u32[]{:S(2)}) %collective-permute-start.3) | collective-permute-done | bytes 524320 | tf_op jit(solution)/shard_map/ppermute | solution.py:15
  23.7 4.5 %collective-permute-start.6 = (bf16[32,4096]{1,0:T(8,128)(2,1)S(1)}, bf16[32,4096]{1,0:T(8,128)(2,1)S(1)}, u32[]{:S(2)}, u32[]{:S(2)}) collective-permute-start(bf16[32,4096]{1,0:T(8,128)(2,1)S(1)} %slice.83), channel_id=1, source_target_pairs={{0,6},{2,0},{4,2},{6,4},{1,7},{3,1},{5,3},{7,5},{8,14},{10,8},{12,... | collective-permute-start | bytes 786440 | tf_op jit(solution)/shard_map/ppermute | solution.py:15
  29.8 11.0 %collective-permute-start.5 = (bf16[32,4096]{1,0:T(8,128)(2,1)S(1)}, bf16[32,4096]{1,0:T(8,128)(2,1)S(1)}, u32[]{:S(2)}, u32[]{:S(2)}) collective-permute-start(bf16[32,4096]{1,0:T(8,128)(2,1)S(1)} %slice.65), channel_id=1, source_target_pairs={{0,2},{2,4},{4,6},{6,0},{1,3},{3,5},{5,7},{7,1},{8,10},{10,12},{12... | collective-permute-start | bytes 786440 | tf_op jit(solution)/shard_map/ppermute | solution.py:15
  40.8 1.9 %collective-permute-start.4 = (bf16[64,4096]{1,0:T(8,128)(2,1)S(1)}, bf16[64,4096]{1,0:T(8,128)(2,1)S(1)}, u32[]{:S(2)}, u32[]{:S(2)}) collective-permute-start(bf16[64,4096]{1,0:T(8,128)(2,1)S(1)} %collective-permute-done.3.refs_4_.refs_8_), channel_id=1, source_target_pairs={{0,1},{1,0},{2,3},{3,2},{4,5},{5,4},{6,7},{7,6},{8,9},{9,8},{10,11... | collective-permute-start | bytes 1572872 | tf_op jit(solution)/shard_map/ppermute | solution.py:15
  42.7 2.4 %collective-permute-start.2 = (bf16[64,4096]{1,0:T(8,128)(2,1)S(1)}, bf16[64,4096]{1,0:T(8,128)(2,1)S(1)}, u32[]{:S(2)}, u32[]{:S(2)}) collective-permute-start(bf16[64,4096]{1,0:T(8,128)(2,1)S(1)} %collective-permute-done.refs_2_.refs_6_), channel_id=1, source_target_pairs={{0,1},{1,0},{2,3},{3,2},{4,5},{5,4},{6,7},{7,6},{8,9},{9,8},{10,11... | collective-permute-start | bytes 1572872 | tf_op jit(solution)/shard_map/ppermute | solution.py:15
  45.1 3.1 %collective-permute-done.6.refs_7_.refs_11_ = bf16[32,4096]{1,0:T(8,128)(2,1)S(1)} collective-permute-done((bf16[32,4096]{1,0:T(8,128)(2,1)S(1)}, bf16[32,4096]{1,0:T(8,128)(2,1)S(1)}, u32[]{:S(2)}, u32[]{:S(2)}) %collective-permute-start.6) | collective-permute-done | bytes 262176 | tf_op jit(solution)/shard_map/ppermute | solution.py:15
  48.3 1.9 %collective-permute-start.8 = (bf16[32,4096]{1,0:T(8,128)(2,1)S(1)}, bf16[32,4096]{1,0:T(8,128)(2,1)S(1)}, u32[]{:S(2)}, u32[]{:S(2)}) collective-permute-start(bf16[32,4096]{1,0:T(8,128)(2,1)S(1)} %collective-permute-done.6.refs_7_.refs_11_), channel_id=1, source_target_pairs={{0,1},{1,0},{2,3},{3,2},{4,5},{5,4},{6,7},{7,6},{8,9},{9,8},{10,11... | collective-permute-start | bytes 786440 | tf_op jit(solution)/shard_map/ppermute | solution.py:15
  50.2 2.4 %collective-permute-start.7 = (bf16[32,4096]{1,0:T(8,128)(2,1)S(1)}, bf16[32,4096]{1,0:T(8,128)(2,1)S(1)}, u32[]{:S(2)}, u32[]{:S(2)}) collective-permute-start(bf16[32,4096]{1,0:T(8,128)(2,1)S(1)} %collective-permute-done.5.refs_6_.refs_10_), channel_id=1, source_target_pairs={{0,1},{1,0},{2,3},{3,2},{4,5},{5,4},{6,7},{7,6},{8,9},{9,8},{10,11... | collective-permute-start | bytes 786440 | tf_op jit(solution)/shard_map/ppermute | solution.py:15
  54.8 2.5 %shard_map.68 = (f32[192,128]{1,0:T(8,128)S(1)}, f32[192,128]{1,0:T(8,128)S(1)}, f32[192,128]{1,0:T(8,128)S(1)}, f32[192,128]{1,0:T(8,128)S(1)}, f32[8,16,128]{2,1,0:T(8,128)S(1)}) custom-call(s32[10]{0:T(128)S(1)} %stack.43.where, bf16[192,4096]{1,0:T(8,128)(2,1)S(1)} %get-tuple-element.26.head.refs_14_, s32[1,512]{1,0:T(1,128)S(1)} %reshape.22.labels, ...), custom_call_target="tpu_custom_call" | custom-call | flops 805306368 | bytes 5767168 | tf_op jit(solution)/shard_map/pallas_call | solution.py:160
  57.3 16.6 %all_to_all.20.stats = f32[8,16,128]{2,1,0:T(8,128)S(1)} all-to-all(f32[8,16,128]{2,1,0:T(8,128)S(1)} %get-tuple-element.30), channel_id=1, replica_groups=mesh['x'=4,'yl'=2,'z'=8,'yh'=4,'core'=2] {'yh','core'}, dimensions={0} | all-to-all | bytes 131072 | tf_op jit(solution)/shard_map/all_to_all | solution.py:172
  73.9 5.1 %shard_map.69 = (bf16[192,4096]{1,0:T(8,128)(2,1)}, bf16[256,4096]{1,0:T(8,128)(2,1)}, bf16[256,192]{1,0:T(8,128)(2,1)S(1)}, f32[1,128]{1,0:T(1,128)S(1)}) custom-call(s32[10]{0:T(128)S(1)} %stack.43.where, f32[8,16,128]{2,1,0:T(8,128)S(1)} %all_to_all.20.stats, s32[1,512]{1,0:T(1,128)S(1)} %reshape.22.labels, f32[1,512]{1,0:T(1,128)S(1)} %reshape.24.weights, ...), custom_call_target="tpu_custom_call" | custom-call | flops 1207959552 | bytes 9437184 | tf_op jit(solution)/shard_map/pallas_call | solution.py:174
  79.0 2.1 %collective-permute-start.9 = (bf16[256,4096]{1,0:T(8,128)(2,1)}, bf16[256,4096]{1,0:T(8,128)(2,1)}, u32[]{:S(2)}, u32[]{:S(2)}) collective-permute-start(bf16[256,4096]{1,0:T(8,128)(2,1)} %get-tuple-element.38), channel_id=1, source_target_pairs={{0,1},{1,0},{2,3},{3,2},{4,5},{5,4},{6,7},{7,6},{8,9},{9,8},{10,11... | collective-permute-start | bytes 6291464 | tf_op jit(solution)/shard_map/ppermute | solution.py:15
  81.1 4.3 %all-to-all-start.1 = ((bf16[4,48,4096]{2,1,0:T(8,128)(2,1)}), bf16[4,48,4096]{2,1,0:T(8,128)(2,1)S(1)}, u32[]{:S(2)}, u32[]{:S(2)}) async-start(bf16[4,48,4096]{2,1,0:T(8,128)(2,1)} %bitcast.31), calls=%async_computation.1 | async-start | bytes 3145728 | tf_op jit(solution)/shard_map/all_to_all | solution.py:200
  85.6 2.3 %fusion.2 = bf16[256,4096]{1,0:T(8,128)(2,1)S(1)} fusion(bf16[256,192]{1,0:T(8,128)(2,1)S(1)} %get-tuple-element.37, bf16[192,4096]{1,0:T(8,128)(2,1)S(1)} %copy-done.1, bf16[256,4096]{1,0:T(8,128)(2,1)} %collective-permute-done.9), kind=kOutput, calls=%fused_computation.3 | convolution fusion | flops 407896064 | bytes 5865472 | tf_op jit(solution)/shard_map/dot_general | solution.py:202
  88.7 2.5 %collective-permute-start.11 = (bf16[32,4096]{1,0:T(8,128)(2,1)}, bf16[32,4096]{1,0:T(8,128)(2,1)S(1)}, u32[]{:S(2)}, u32[]{:S(2)}) collective-permute-start(bf16[32,4096]{1,0:T(8,128)(2,1)} %get-tuple-element.45), channel_id=1, source_target_pairs={{0,6},{2,0},{4,2},{6,4},{1,7},{3,1},{5,3},{7,5},{8,14},{10,8},{12,... | collective-permute-start | bytes 786440 | tf_op jit(solution)/shard_map/ppermute | solution.py:15
  91.2 4.3 %collective-permute-start.10 = (bf16[32,4096]{1,0:T(8,128)(2,1)S(1)}, bf16[32,4096]{1,0:T(8,128)(2,1)}, u32[]{:S(2)}, u32[]{:S(2)}) collective-permute-start(bf16[32,4096]{1,0:T(8,128)(2,1)S(1)} %get-tuple-element.46), channel_id=1, source_target_pairs={{0,2},{2,4},{4,6},{6,0},{1,3},{3,5},{5,7},{7,1},{8,10},{10,12},{12... | collective-permute-start | bytes 786440 | tf_op jit(solution)/shard_map/ppermute | solution.py:15
  95.4 11.3 %all-to-all-done.1.parts = bf16[4,48,4096]{2,1,0:T(8,128)(2,1)S(1)} async-done(((bf16[4,48,4096]{2,1,0:T(8,128)(2,1)}), bf16[4,48,4096]{2,1,0:T(8,128)(2,1)S(1)}, u32[]{:S(2)}, u32[]{:S(2)}) %all-to-all-start.1) | async-done | bytes 1572896 | tf_op jit(solution)/shard_map/all_to_all | solution.py:200
  107.5 23.6 %all_to_all.21 = bf16[16,48,256]{2,1,0:T(8,128)(2,1)S(1)} all-to-all(bf16[16,48,256]{2,1,0:T(8,128)(2,1)S(1)} %shard_map.70), channel_id=1, replica_groups=mesh['x'=4,'yl'=2,'z'=8,'yh'=4,'core'=2] {'yl','z'}, dimensions={0} | all-to-all | bytes 786432 | tf_op jit(solution)/shard_map/all_to_all | solution.py:225
  132.0 4.7 %all-to-all-start.3 = ((bf16[16,48,256]{2,1,0:T(8,128)(2,1)}), bf16[16,48,256]{2,1,0:T(8,128)(2,1)S(1)}, u32[]{:S(2)}, u32[]{:S(2)}) async-start(bf16[16,48,256]{2,1,0:T(8,128)(2,1)} %broadcast_in_dim.4), calls=%async_computation.3 | async-start | bytes 786432 | tf_op jit(solution)/shard_map/all_to_all | solution.py:227
  138.5 3.4 %collective-permute-start.12 = (bf16[64,4096]{1,0:T(8,128)(2,1)}, bf16[64,4096]{1,0:T(8,128)(2,1)}, u32[]{:S(2)}, u32[]{:S(2)}) collective-permute-start(bf16[64,4096]{1,0:T(8,128)(2,1)} %get-tuple-element.43), channel_id=1, source_target_pairs={{0,2},{2,4},{4,6},{6,0},{1,3},{3,5},{5,7},{7,1},{8,10},{10,12},{12... | collective-permute-start | bytes 1572872 | tf_op jit(solution)/shard_map/ppermute | solution.py:15
  142.0 4.5 %collective-permute-start.13 = (bf16[64,4096]{1,0:T(8,128)(2,1)S(1)}, bf16[64,4096]{1,0:T(8,128)(2,1)}, u32[]{:S(2)}, u32[]{:S(2)}) collective-permute-start(bf16[64,4096]{1,0:T(8,128)(2,1)S(1)} %get-tuple-element.44), channel_id=1, source_target_pairs={{0,6},{2,0},{4,2},{6,4},{1,7},{3,1},{5,3},{7,5},{8,14},{10,8},{12,... | collective-permute-start | bytes 1572872 | tf_op jit(solution)/shard_map/ppermute | solution.py:15
  146.5 3.1 %all-to-all-done.3.own = bf16[16,48,256]{2,1,0:T(8,128)(2,1)S(1)} async-done(((bf16[16,48,256]{2,1,0:T(8,128)(2,1)}), bf16[16,48,256]{2,1,0:T(8,128)(2,1)S(1)}, u32[]{:S(2)}, u32[]{:S(2)}) %all-to-all-start.3) | async-done | bytes 393248 | tf_op jit(solution)/shard_map/all_to_all | solution.py:227
  149.6 4.8 %collective-permute-start.15 = (bf16[16,48,256]{2,1,0:T(8,128)(2,1)S(1)}, bf16[16,48,256]{2,1,0:T(8,128)(2,1)S(1)}, u32[]{:S(2)}, u32[]{:S(2)}) collective-permute-start(bf16[16,48,256]{2,1,0:T(8,128)(2,1)S(1)} %all-to-all-done.3.own), channel_id=1, source_target_pairs={{0,384},{128,0},{256,128},{384,256},{1,385},{129,1},{257,129},{385... | collective-permute-start | bytes 1179656 | tf_op jit(solution)/shard_map/ppermute | solution.py:15
  154.4 1.9 %collective-permute-start.14 = (bf16[16,48,256]{2,1,0:T(8,128)(2,1)S(1)}, bf16[16,48,256]{2,1,0:T(8,128)(2,1)S(1)}, u32[]{:S(2)}, u32[]{:S(2)}) collective-permute-start(bf16[16,48,256]{2,1,0:T(8,128)(2,1)S(1)} %all-to-all-done.3.own), channel_id=1, source_target_pairs={{0,128},{128,256},{256,384},{384,0},{1,129},{129,257},{257,385},{3... | collective-permute-start | bytes 1179656 | tf_op jit(solution)/shard_map/ppermute | solution.py:15
  156.8 5.7 %collective-permute-done.15.after = bf16[16,48,256]{2,1,0:T(8,128)(2,1)S(1)} collective-permute-done((bf16[16,48,256]{2,1,0:T(8,128)(2,1)S(1)}, bf16[16,48,256]{2,1,0:T(8,128)(2,1)S(1)}, u32[]{:S(2)}, u32[]{:S(2)}) %collective-permute-start.15) | collective-permute-done | bytes 393248 | tf_op jit(solution)/shard_map/ppermute | solution.py:15
  162.5 5.6 %collective-permute-start.17 = (bf16[8,48,256]{2,1,0:T(8,128)(2,1)S(1)}, bf16[8,48,256]{2,1,0:T(8,128)(2,1)S(1)}, u32[]{:S(2)}, u32[]{:S(2)}) collective-permute-start(bf16[8,48,256]{2,1,0:T(8,128)(2,1)S(1)} %slice.90), channel_id=1, source_target_pairs={{0,384},{128,0},{256,128},{384,256},{1,385},{129,1},{257,129},{385... | collective-permute-start | bytes 589832 | tf_op jit(solution)/shard_map/ppermute | solution.py:15
  168.2 1.9 %collective-permute-start.16 = (bf16[8,48,256]{2,1,0:T(8,128)(2,1)S(1)}, bf16[8,48,256]{2,1,0:T(8,128)(2,1)S(1)}, u32[]{:S(2)}, u32[]{:S(2)}) collective-permute-start(bf16[8,48,256]{2,1,0:T(8,128)(2,1)S(1)} %slice.89), channel_id=1, source_target_pairs={{0,128},{128,256},{256,384},{384,0},{1,129},{129,257},{257,385},{3... | collective-permute-start | bytes 589832 | tf_op jit(solution)/shard_map/ppermute | solution.py:15
  170.1 2.2 %add_convert_fusion = bf16[64,4096]{1,0:T(8,128)(2,1)} fusion(bf16[64,4096]{1,0:T(8,128)(2,1)} %collective-permute-done.13, bf16[64,4096]{1,0:T(8,128)(2,1)} %collective-permute-done.12, bf16[256,4096]{1,0:T(8,128)(2,1)S(1)} %copy-done.8), kind=kLoop, calls=%fused_computation.4 | loop fusion | flops 1572864 | bytes 2097152 | tf_op jit(solution)/shard_map/convert_element_type | solution.py:240
  172.3 4.6 %collective-permute-done.16.far_low = bf16[8,48,256]{2,1,0:T(8,128)(2,1)S(1)} collective-permute-done((bf16[8,48,256]{2,1,0:T(8,128)(2,1)S(1)}, bf16[8,48,256]{2,1,0:T(8,128)(2,1)S(1)}, u32[]{:S(2)}, u32[]{:S(2)}) %collective-permute-start.16) | collective-permute-done | bytes 196640 | tf_op jit(solution)/shard_map/ppermute | solution.py:15
  (59 shorter events, 15.8 us)
Async XLA Ops:
  0.6 29.1 %collective-permute-start = (bf16[64,4096]{1,0:T(8,128)(2,1)}, bf16[64,4096]{1,0:T(8,128)(2,1)S(1)}, u32[]{:S(2)}, u32[]{:S(2)}) collective-permute-start(bf16[64,4096]{1,0:T(8,128)(2,1)} %own.1), channel_id=1, source_target_pairs={{0,2},{2,4},{4,6},{6,0},{1,3},{3,5},{5,7},{7,1},{8,10},{10,12},{12... | collective-permute-start | bytes 1572872 | tf_op jit(solution)/shard_map/ppermute | solution.py:15
  5.1 18.5 %collective-permute-start.3 = (bf16[64,4096]{1,0:T(8,128)(2,1)}, bf16[64,4096]{1,0:T(8,128)(2,1)S(1)}, u32[]{:S(2)}, u32[]{:S(2)}) collective-permute-start(bf16[64,4096]{1,0:T(8,128)(2,1)} %own.1), channel_id=1, source_target_pairs={{0,6},{2,0},{4,2},{6,4},{1,7},{3,1},{5,3},{7,5},{8,14},{10,8},{12,... | collective-permute-start | bytes 1572872 | tf_op jit(solution)/shard_map/ppermute | solution.py:15
  8.6 44.0 %collective-permute-start.1 = (bf16[64,4096]{1,0:T(8,128)(2,1)}, bf16[64,4096]{1,0:T(8,128)(2,1)S(1)}, u32[]{:S(2)}, u32[]{:S(2)}) collective-permute-start(bf16[64,4096]{1,0:T(8,128)(2,1)} %own.1), channel_id=1, source_target_pairs={{0,1},{1,0},{2,3},{3,2},{4,5},{5,4},{6,7},{7,6},{8,9},{9,8},{10,11... | collective-permute-start | bytes 1572872 | tf_op jit(solution)/shard_map/ppermute | solution.py:15
  12.5 1.4 copy-start.5
  13.9 1.0 copy-start.6
  15.1 0.8 copy-start.2
  15.9 41.4 %copy-start = (bf16[192,4096]{1,0:T(8,128)(2,1)}, bf16[192,4096]{1,0:T(8,128)(2,1)S(1)}, u32[]{:S(2)}) copy-start(bf16[192,4096]{1,0:T(8,128)(2,1)S(1)} %get-tuple-element.26.head.refs_14_) | copy-start | bytes 4718596
  23.7 24.6 %collective-permute-start.6 = (bf16[32,4096]{1,0:T(8,128)(2,1)S(1)}, bf16[32,4096]{1,0:T(8,128)(2,1)S(1)}, u32[]{:S(2)}, u32[]{:S(2)}) collective-permute-start(bf16[32,4096]{1,0:T(8,128)(2,1)S(1)} %slice.83), channel_id=1, source_target_pairs={{0,6},{2,0},{4,2},{6,4},{1,7},{3,1},{5,3},{7,5},{8,14},{10,8},{12,... | collective-permute-start | bytes 786440 | tf_op jit(solution)/shard_map/ppermute | solution.py:15
  29.7 44.2 %copy-start.4 = (bf16[64,4096]{1,0:T(8,128)(2,1)S(1)}, bf16[64,4096]{1,0:T(8,128)(2,1)}, u32[]{:S(2)}) copy-start(bf16[64,4096]{1,0:T(8,128)(2,1)} %copy-done.2) | copy-start | bytes 1572868
  29.8 20.4 %collective-permute-start.5 = (bf16[32,4096]{1,0:T(8,128)(2,1)S(1)}, bf16[32,4096]{1,0:T(8,128)(2,1)S(1)}, u32[]{:S(2)}, u32[]{:S(2)}) collective-permute-start(bf16[32,4096]{1,0:T(8,128)(2,1)S(1)} %slice.65), channel_id=1, source_target_pairs={{0,2},{2,4},{4,6},{6,0},{1,3},{3,5},{5,7},{7,1},{8,10},{10,12},{12... | collective-permute-start | bytes 786440 | tf_op jit(solution)/shard_map/ppermute | solution.py:15
  40.8 11.9 %collective-permute-start.4 = (bf16[64,4096]{1,0:T(8,128)(2,1)S(1)}, bf16[64,4096]{1,0:T(8,128)(2,1)S(1)}, u32[]{:S(2)}, u32[]{:S(2)}) collective-permute-start(bf16[64,4096]{1,0:T(8,128)(2,1)S(1)} %collective-permute-done.3.refs_4_.refs_8_), channel_id=1, source_target_pairs={{0,1},{1,0},{2,3},{3,2},{4,5},{5,4},{6,7},{7,6},{8,9},{9,8},{10,11... | collective-permute-start | bytes 1572872 | tf_op jit(solution)/shard_map/ppermute | solution.py:15
  42.7 11.0 %collective-permute-start.2 = (bf16[64,4096]{1,0:T(8,128)(2,1)S(1)}, bf16[64,4096]{1,0:T(8,128)(2,1)S(1)}, u32[]{:S(2)}, u32[]{:S(2)}) collective-permute-start(bf16[64,4096]{1,0:T(8,128)(2,1)S(1)} %collective-permute-done.refs_2_.refs_6_), channel_id=1, source_target_pairs={{0,1},{1,0},{2,3},{3,2},{4,5},{5,4},{6,7},{7,6},{8,9},{9,8},{10,11... | collective-permute-start | bytes 1572872 | tf_op jit(solution)/shard_map/ppermute | solution.py:15
  48.3 4.4 %collective-permute-start.8 = (bf16[32,4096]{1,0:T(8,128)(2,1)S(1)}, bf16[32,4096]{1,0:T(8,128)(2,1)S(1)}, u32[]{:S(2)}, u32[]{:S(2)}) collective-permute-start(bf16[32,4096]{1,0:T(8,128)(2,1)S(1)} %collective-permute-done.6.refs_7_.refs_11_), channel_id=1, source_target_pairs={{0,1},{1,0},{2,3},{3,2},{4,5},{5,4},{6,7},{7,6},{8,9},{9,8},{10,11... | collective-permute-start | bytes 786440 | tf_op jit(solution)/shard_map/ppermute | solution.py:15
  50.2 3.6 %collective-permute-start.7 = (bf16[32,4096]{1,0:T(8,128)(2,1)S(1)}, bf16[32,4096]{1,0:T(8,128)(2,1)S(1)}, u32[]{:S(2)}, u32[]{:S(2)}) collective-permute-start(bf16[32,4096]{1,0:T(8,128)(2,1)S(1)} %collective-permute-done.5.refs_6_.refs_10_), channel_id=1, source_target_pairs={{0,1},{1,0},{2,3},{3,2},{4,5},{5,4},{6,7},{7,6},{8,9},{9,8},{10,11... | collective-permute-start | bytes 786440 | tf_op jit(solution)/shard_map/ppermute | solution.py:15
  53.8 1.0 copy-start.3
  79.0 6.5 %copy-start.1 = (bf16[192,4096]{1,0:T(8,128)(2,1)S(1)}, bf16[192,4096]{1,0:T(8,128)(2,1)}, u32[]{:S(2)}) copy-start(bf16[192,4096]{1,0:T(8,128)(2,1)} %copy-done) | copy-start | bytes 4718596
  79.0 6.5 %collective-permute-start.9 = (bf16[256,4096]{1,0:T(8,128)(2,1)}, bf16[256,4096]{1,0:T(8,128)(2,1)}, u32[]{:S(2)}, u32[]{:S(2)}) collective-permute-start(bf16[256,4096]{1,0:T(8,128)(2,1)} %get-tuple-element.38), channel_id=1, source_target_pairs={{0,1},{1,0},{2,3},{3,2},{4,5},{5,4},{6,7},{7,6},{8,9},{9,8},{10,11... | collective-permute-start | bytes 6291464 | tf_op jit(solution)/shard_map/ppermute | solution.py:15
  81.1 25.7 %all-to-all-start.1 = ((bf16[4,48,4096]{2,1,0:T(8,128)(2,1)}), bf16[4,48,4096]{2,1,0:T(8,128)(2,1)S(1)}, u32[]{:S(2)}, u32[]{:S(2)}) async-start(bf16[4,48,4096]{2,1,0:T(8,128)(2,1)} %bitcast.31), calls=%async_computation.1 | async-start | bytes 3145728 | tf_op jit(solution)/shard_map/all_to_all | solution.py:200
  87.9 3.3 %copy-start.7 = (bf16[256,4096]{1,0:T(8,128)(2,1)}, bf16[256,4096]{1,0:T(8,128)(2,1)S(1)}, u32[]{:S(2)}) copy-start(bf16[256,4096]{1,0:T(8,128)(2,1)S(1)} %fusion.2) | copy-start | bytes 6291460
  88.7 18.5 %collective-permute-start.11 = (bf16[32,4096]{1,0:T(8,128)(2,1)}, bf16[32,4096]{1,0:T(8,128)(2,1)S(1)}, u32[]{:S(2)}, u32[]{:S(2)}) collective-permute-start(bf16[32,4096]{1,0:T(8,128)(2,1)} %get-tuple-element.45), channel_id=1, source_target_pairs={{0,6},{2,0},{4,2},{6,4},{1,7},{3,1},{5,3},{7,5},{8,14},{10,8},{12,... | collective-permute-start | bytes 786440 | tf_op jit(solution)/shard_map/ppermute | solution.py:15
  91.2 16.4 %collective-permute-start.10 = (bf16[32,4096]{1,0:T(8,128)(2,1)S(1)}, bf16[32,4096]{1,0:T(8,128)(2,1)}, u32[]{:S(2)}, u32[]{:S(2)}) collective-permute-start(bf16[32,4096]{1,0:T(8,128)(2,1)S(1)} %get-tuple-element.46), channel_id=1, source_target_pairs={{0,2},{2,4},{4,6},{6,0},{1,3},{3,5},{5,7},{7,1},{8,10},{10,12},{12... | collective-permute-start | bytes 786440 | tf_op jit(solution)/shard_map/ppermute | solution.py:15
  107.2 29.5 %copy-start.8 = (bf16[256,4096]{1,0:T(8,128)(2,1)S(1)}, bf16[256,4096]{1,0:T(8,128)(2,1)}, u32[]{:S(2)}) copy-start(bf16[256,4096]{1,0:T(8,128)(2,1)} %copy-done.7) | copy-start | bytes 6291460
  132.0 17.6 %all-to-all-start.3 = ((bf16[16,48,256]{2,1,0:T(8,128)(2,1)}), bf16[16,48,256]{2,1,0:T(8,128)(2,1)S(1)}, u32[]{:S(2)}, u32[]{:S(2)}) async-start(bf16[16,48,256]{2,1,0:T(8,128)(2,1)} %broadcast_in_dim.4), calls=%async_computation.3 | async-start | bytes 786432 | tf_op jit(solution)/shard_map/all_to_all | solution.py:227
  138.5 31.6 %collective-permute-start.12 = (bf16[64,4096]{1,0:T(8,128)(2,1)}, bf16[64,4096]{1,0:T(8,128)(2,1)}, u32[]{:S(2)}, u32[]{:S(2)}) collective-permute-start(bf16[64,4096]{1,0:T(8,128)(2,1)} %get-tuple-element.43), channel_id=1, source_target_pairs={{0,2},{2,4},{4,6},{6,0},{1,3},{3,5},{5,7},{7,1},{8,10},{10,12},{12... | collective-permute-start | bytes 1572872 | tf_op jit(solution)/shard_map/ppermute | solution.py:15
  142.0 28.2 %collective-permute-start.13 = (bf16[64,4096]{1,0:T(8,128)(2,1)S(1)}, bf16[64,4096]{1,0:T(8,128)(2,1)}, u32[]{:S(2)}, u32[]{:S(2)}) collective-permute-start(bf16[64,4096]{1,0:T(8,128)(2,1)S(1)} %get-tuple-element.44), channel_id=1, source_target_pairs={{0,6},{2,0},{4,2},{6,4},{1,7},{3,1},{5,3},{7,5},{8,14},{10,8},{12,... | collective-permute-start | bytes 1572872 | tf_op jit(solution)/shard_map/ppermute | solution.py:15
  149.6 12.9 %collective-permute-start.15 = (bf16[16,48,256]{2,1,0:T(8,128)(2,1)S(1)}, bf16[16,48,256]{2,1,0:T(8,128)(2,1)S(1)}, u32[]{:S(2)}, u32[]{:S(2)}) collective-permute-start(bf16[16,48,256]{2,1,0:T(8,128)(2,1)S(1)} %all-to-all-done.3.own), channel_id=1, source_target_pairs={{0,384},{128,0},{256,128},{384,256},{1,385},{129,1},{257,129},{385... | collective-permute-start | bytes 1179656 | tf_op jit(solution)/shard_map/ppermute | solution.py:15
  154.4 13.8 %collective-permute-start.14 = (bf16[16,48,256]{2,1,0:T(8,128)(2,1)S(1)}, bf16[16,48,256]{2,1,0:T(8,128)(2,1)S(1)}, u32[]{:S(2)}, u32[]{:S(2)}) collective-permute-start(bf16[16,48,256]{2,1,0:T(8,128)(2,1)S(1)} %all-to-all-done.3.own), channel_id=1, source_target_pairs={{0,128},{128,256},{256,384},{384,0},{1,129},{129,257},{257,385},{3... | collective-permute-start | bytes 1179656 | tf_op jit(solution)/shard_map/ppermute | solution.py:15
  162.5 9.8 %collective-permute-start.17 = (bf16[8,48,256]{2,1,0:T(8,128)(2,1)S(1)}, bf16[8,48,256]{2,1,0:T(8,128)(2,1)S(1)}, u32[]{:S(2)}, u32[]{:S(2)}) collective-permute-start(bf16[8,48,256]{2,1,0:T(8,128)(2,1)S(1)} %slice.90), channel_id=1, source_target_pairs={{0,384},{128,0},{256,128},{384,256},{1,385},{129,1},{257,129},{385... | collective-permute-start | bytes 589832 | tf_op jit(solution)/shard_map/ppermute | solution.py:15
  168.2 8.8 %collective-permute-start.16 = (bf16[8,48,256]{2,1,0:T(8,128)(2,1)S(1)}, bf16[8,48,256]{2,1,0:T(8,128)(2,1)S(1)}, u32[]{:S(2)}, u32[]{:S(2)}) collective-permute-start(bf16[8,48,256]{2,1,0:T(8,128)(2,1)S(1)} %slice.89), channel_id=1, source_target_pairs={{0,128},{128,256},{256,384},{384,0},{1,129},{129,257},{257,385},{3... | collective-permute-start | bytes 589832 | tf_op jit(solution)/shard_map/ppermute | solution.py:15

commit v11 on v10

--- a/solution.py
+++ b/solution.py
@@ -217,14 +217,17 @@
     from_below = shift(far[:half], "yh", 1, n_yh)
     from_above = shift(far[half:], "yh", -1, n_yh)
     part, from_below, from_above = lax.optimization_barrier((part, from_below, from_above))
-    zero = jnp.zeros((half, width), F32)
-    up = up.astype(F32) + jnp.concatenate([from_below.astype(F32), zero], 0)
-    down = down.astype(F32) + jnp.concatenate([zero, from_above.astype(F32)], 0)
-    came = [shift(up.astype(BF16), "yh", 1, n_yh), shift(down.astype(BF16), "yh", -1, n_yh)]
+    up_high = shift(up[half:], "yh", 1, n_yh)
+    down_low = shift(down[:half], "yh", -1, n_yh)
+    up_low = (up[:half].astype(F32) + from_below.astype(F32)).astype(BF16)
+    down_high = (down[half:].astype(F32) + from_above.astype(F32)).astype(BF16)
+    up_low, down_high = shift(up_low, "yh", 1, n_yh), shift(down_high, "yh", -1, n_yh)
 
     part = lax.all_to_all(part, ("yl", "z"), 0, 0, tiled=True)
+    part, up_high, down_low = lax.optimization_barrier((part, up_high, down_low))
     part = jnp.sum(part.astype(F32), axis=0).astype(BF16)
     part = lax.all_to_all(jnp.broadcast_to(part, (n_yl * n_z,) + part.shape), ("yl", "z"), 0, 0, tiled=True)
+    part, up_low, down_high = lax.optimization_barrier((part, up_low, down_high))
     x_before = shift(part, "x", 1, n_x)
     x_after = shift(part, "x", -1, n_x)
     x_low = shift(x_before[: n_rest // 2], "x", 1, n_x)
@@ -237,6 +240,7 @@
         compiler_params=params,
         cost_estimate=pl.CostEstimate(flops=0, bytes_accessed=4 * v_dev * width, transcendentals=0),
     )(where, part, x_before, x_after, x_low, x_high)
+    came = jnp.concatenate([up_low, up_high], 0), jnp.concatenate([down_low, down_high], 0)
     grad_hidden = (mine.astype(F32) + sum(v.astype(F32) for v in came)).astype(BF16)
     return token_loss, grad_hidden, grad_weight
 

time: 180 us -> 201 us (1.12)
  the two profiles are of different devices: /device:TPU:72 before, /device:TPU:8 now
where the time goes in v11:
time: 201 us; the launch traced here: 200 us
  starting transfers between devices  94.7 us (47%)
  waiting for transfers between devices  62.4 us (31%)
  blocking collectives  16.9 us (8%)
  Pallas kernels  11 us (5%)
  local copies, waits for them, and re-layouts  8.48 us (4%)
  other arithmetic  3.26 us (2%)
  matrix products  2.29 us (1%)
    ppermute x20, starting transfers between devices, shift(): lax.ppermute(value, axis, [(i, (i + step) % size) for i in range(size)])  70.1 us
    ppermute x20, waiting for transfers between devices, shift(): lax.ppermute(value, axis, [(i, (i + step) % size) for i in range(size)])  51.2 us
    all_to_all x1, blocking collectives, per_device(): stats = lax.all_to_all(stats, VOCAB, 0, 0, tiled=True)  16.9 us
    all_to_all x1, starting transfers between devices, per_device(): part = lax.all_to_all(part, ('yl', 'z'), 0, 0, tiled=True)  11.9 us
    all_to_all x1, waiting for transfers between devices, per_device(): part = lax.all_to_all(part, 'x', 0, 0, tiled=True)  11.3 us
    all_to_all x1, starting transfers between devices, per_device(): lax.all_to_all(jnp.broadcast_to(part, (n_yl * n_z,) + part.shape), ('yl',...  8.3 us
    pallas_call x1, Pallas kernels, per_device(): pl.pallas_call(score_kernel, out_shape=(jax.ShapeDtypeStruct((v_dev, widt...  5.11 us
    all_to_all x1, starting transfers between devices, per_device(): part = lax.all_to_all(part, 'x', 0, 0, tiled=True)  4.42 us
  transfers between devices with their start and end apart: 23, of which 12 were waited for; matrix products, arithmetic and copies ran while one was open for 4% of the time, Pallas kernels for 1%

profile of v11, /device:TPU:8, one launch (start us, length us, event | category | flops | bytes accessed | tf_op | source)
XLA Modules:
  0.0 200.2 jit_solution(7713284766655217721)
XLA Ops:
  0.6 4.5 %collective-permute-start = (bf16[64,4096]{1,0:T(8,128)(2,1)}, bf16[64,4096]{1,0:T(8,128)(2,1)S(1)}, u32[]{:S(2)}, u32[]{:S(2)}) collective-permute-start(bf16[64,4096]{1,0:T(8,128)(2,1)} %own.1), channel_id=1, source_target_pairs={{0,2},{2,4},{4,6},{6,0},{1,3},{3,5},{5,7},{7,1},{8,10},{10,12},{12... | collective-permute-start | bytes 1572872 | tf_op jit(solution)/shard_map/ppermute | solution.py:15
  5.1 3.5 %collective-permute-start.3 = (bf16[64,4096]{1,0:T(8,128)(2,1)}, bf16[64,4096]{1,0:T(8,128)(2,1)S(1)}, u32[]{:S(2)}, u32[]{:S(2)}) collective-permute-start(bf16[64,4096]{1,0:T(8,128)(2,1)} %own.1), channel_id=1, source_target_pairs={{0,6},{2,0},{4,2},{6,4},{1,7},{3,1},{5,3},{7,5},{8,14},{10,8},{12,... | collective-permute-start | bytes 1572872 | tf_op jit(solution)/shard_map/ppermute | solution.py:15
  8.6 1.9 collective-permute-start.1
  16.0 7.7 %collective-permute-done.3.refs_4_.refs_8_ = bf16[64,4096]{1,0:T(8,128)(2,1)S(1)} collective-permute-done((bf16[64,4096]{1,0:T(8,128)(2,1)}, bf16[64,4096]{1,0:T(8,128)(2,1)S(1)}, u32[]{:S(2)}, u32[]{:S(2)}) %collective-permute-start.3) | collective-permute-done | bytes 524320 | tf_op jit(solution)/shard_map/ppermute | solution.py:15
  23.7 4.5 %collective-permute-start.6 = (bf16[32,4096]{1,0:T(8,128)(2,1)S(1)}, bf16[32,4096]{1,0:T(8,128)(2,1)S(1)}, u32[]{:S(2)}, u32[]{:S(2)}) collective-permute-start(bf16[32,4096]{1,0:T(8,128)(2,1)S(1)} %slice.97), channel_id=1, source_target_pairs={{0,6},{2,0},{4,2},{6,4},{1,7},{3,1},{5,3},{7,5},{8,14},{10,8},{12,... | collective-permute-start | bytes 786440 | tf_op jit(solution)/shard_map/ppermute | solution.py:15
  29.8 11.0 %collective-permute-start.5 = (bf16[32,4096]{1,0:T(8,128)(2,1)S(1)}, bf16[32,4096]{1,0:T(8,128)(2,1)S(1)}, u32[]{:S(2)}, u32[]{:S(2)}) collective-permute-start(bf16[32,4096]{1,0:T(8,128)(2,1)S(1)} %slice.77), channel_id=1, source_target_pairs={{0,2},{2,4},{4,6},{6,0},{1,3},{3,5},{5,7},{7,1},{8,10},{10,12},{12... | collective-permute-start | bytes 786440 | tf_op jit(solution)/shard_map/ppermute | solution.py:15
  42.7 2.4 %collective-permute-start.2 = (bf16[64,4096]{1,0:T(8,128)(2,1)S(1)}, bf16[64,4096]{1,0:T(8,128)(2,1)S(1)}, u32[]{:S(2)}, u32[]{:S(2)}) collective-permute-start(bf16[64,4096]{1,0:T(8,128)(2,1)S(1)} %collective-permute-done.refs_2_.refs_6_), channel_id=1, source_target_pairs={{0,1},{1,0},{2,3},{3,2},{4,5},{5,4},{6,7},{7,6},{8,9},{9,8},{10,11... | collective-permute-start | bytes 1572872 | tf_op jit(solution)/shard_map/ppermute | solution.py:15
  47.1 2.8 %collective-permute-done.5.refs_6_.refs_10_ = bf16[32,4096]{1,0:T(8,128)(2,1)S(1)} collective-permute-done((bf16[32,4096]{1,0:T(8,128)(2,1)S(1)}, bf16[32,4096]{1,0:T(8,128)(2,1)S(1)}, u32[]{:S(2)}, u32[]{:S(2)}) %collective-permute-start.5) | collective-permute-done | bytes 262176 | tf_op jit(solution)/shard_map/ppermute | solution.py:15
  54.4 2.5 %shard_map.68 = (f32[192,128]{1,0:T(8,128)S(1)}, f32[192,128]{1,0:T(8,128)S(1)}, f32[192,128]{1,0:T(8,128)S(1)}, f32[192,128]{1,0:T(8,128)S(1)}, f32[8,16,128]{2,1,0:T(8,128)S(1)}) custom-call(s32[10]{0:T(128)S(1)} %stack.43.where, bf16[192,4096]{1,0:T(8,128)(2,1)S(1)} %get-tuple-element.32.head.refs_14_, s32[1,512]{1,0:T(1,128)S(1)} %reshape.22.labels, ...), custom_call_target="tpu_custom_call" | custom-call | flops 805306368 | bytes 5767168 | tf_op jit(solution)/shard_map/pallas_call | solution.py:160
  56.8 16.9 %all_to_all.20.stats = f32[8,16,128]{2,1,0:T(8,128)S(1)} all-to-all(f32[8,16,128]{2,1,0:T(8,128)S(1)} %get-tuple-element.36), channel_id=1, replica_groups=mesh['x'=4,'yl'=2,'z'=8,'yh'=4,'core'=2] {'yh','core'}, dimensions={0} | all-to-all | bytes 131072 | tf_op jit(solution)/shard_map/all_to_all | solution.py:172
  73.8 5.1 %shard_map.69 = (bf16[192,4096]{1,0:T(8,128)(2,1)}, bf16[256,4096]{1,0:T(8,128)(2,1)}, bf16[256,192]{1,0:T(8,128)(2,1)S(1)}, f32[1,128]{1,0:T(1,128)S(1)}) custom-call(s32[10]{0:T(128)S(1)} %stack.43.where, f32[8,16,128]{2,1,0:T(8,128)S(1)} %all_to_all.20.stats, s32[1,512]{1,0:T(1,128)S(1)} %reshape.22.labels, f32[1,512]{1,0:T(1,128)S(1)} %reshape.24.weights, ...), custom_call_target="tpu_custom_call" | custom-call | flops 1207959552 | bytes 9437184 | tf_op jit(solution)/shard_map/pallas_call | solution.py:174
  78.9 2.1 %collective-permute-start.9 = (bf16[256,4096]{1,0:T(8,128)(2,1)}, bf16[256,4096]{1,0:T(8,128)(2,1)}, u32[]{:S(2)}, u32[]{:S(2)}) collective-permute-start(bf16[256,4096]{1,0:T(8,128)(2,1)} %get-tuple-element.44), channel_id=1, source_target_pairs={{0,1},{1,0},{2,3},{3,2},{4,5},{5,4},{6,7},{7,6},{8,9},{9,8},{10,11... | collective-permute-start | bytes 6291464 | tf_op jit(solution)/shard_map/ppermute | solution.py:15
  81.0 4.4 %all-to-all-start.1 = ((bf16[4,48,4096]{2,1,0:T(8,128)(2,1)}), bf16[4,48,4096]{2,1,0:T(8,128)(2,1)S(1)}, u32[]{:S(2)}, u32[]{:S(2)}) async-start(bf16[4,48,4096]{2,1,0:T(8,128)(2,1)} %bitcast.31), calls=%async_computation.1 | async-start | bytes 3145728 | tf_op jit(solution)/shard_map/all_to_all | solution.py:200
  85.5 2.3 %fusion.2 = bf16[256,4096]{1,0:T(8,128)(2,1)S(1)} fusion(bf16[256,192]{1,0:T(8,128)(2,1)S(1)} %get-tuple-element.43, bf16[192,4096]{1,0:T(8,128)(2,1)S(1)} %copy-done.1, bf16[256,4096]{1,0:T(8,128)(2,1)} %collective-permute-done.9), kind=kOutput, calls=%fused_computation.3 | convolution fusion | flops 407896064 | bytes 5865472 | tf_op jit(solution)/shard_map/dot_general | solution.py:202
  88.8 2.5 %collective-permute-start.11 = (bf16[32,4096]{1,0:T(8,128)(2,1)}, bf16[32,4096]{1,0:T(8,128)(2,1)S(1)}, u32[]{:S(2)}, u32[]{:S(2)}) collective-permute-start(bf16[32,4096]{1,0:T(8,128)(2,1)} %get-tuple-element.59), channel_id=1, source_target_pairs={{0,6},{2,0},{4,2},{6,4},{1,7},{3,1},{5,3},{7,5},{8,14},{10,8},{12,... | collective-permute-start | bytes 786440 | tf_op jit(solution)/shard_map/ppermute | solution.py:15
  91.2 4.3 %collective-permute-start.10 = (bf16[32,4096]{1,0:T(8,128)(2,1)S(1)}, bf16[32,4096]{1,0:T(8,128)(2,1)}, u32[]{:S(2)}, u32[]{:S(2)}) collective-permute-start(bf16[32,4096]{1,0:T(8,128)(2,1)S(1)} %get-tuple-element.60), channel_id=1, source_target_pairs={{0,2},{2,4},{4,6},{6,0},{1,3},{3,5},{5,7},{7,1},{8,10},{10,12},{12... | collective-permute-start | bytes 786440 | tf_op jit(solution)/shard_map/ppermute | solution.py:15
  95.5 11.3 %all-to-all-done.1.parts = bf16[4,48,4096]{2,1,0:T(8,128)(2,1)S(1)} async-done(((bf16[4,48,4096]{2,1,0:T(8,128)(2,1)}), bf16[4,48,4096]{2,1,0:T(8,128)(2,1)S(1)}, u32[]{:S(2)}, u32[]{:S(2)}) %all-to-all-start.1) | async-done | bytes 1572896 | tf_op jit(solution)/shard_map/all_to_all | solution.py:200
  108.3 11.9 %all-to-all-start.2 = ((bf16[16,48,256]{2,1,0:T(8,128)(2,1)}), bf16[16,48,256]{2,1,0:T(8,128)(2,1)S(1)}, u32[]{:S(2)}, u32[]{:S(2)}) async-start(bf16[16,48,256]{2,1,0:T(8,128)(2,1)} %shard_map.70), calls=%async_computation.2 | async-start | bytes 786432 | tf_op jit(solution)/shard_map/all_to_all | solution.py:226
  120.3 2.5 %collective-permute-start.13 = (bf16[32,4096]{1,0:T(8,128)(2,1)}, bf16[32,4096]{1,0:T(8,128)(2,1)S(1)}, u32[]{:S(2)}, u32[]{:S(2)}) collective-permute-start(bf16[32,4096]{1,0:T(8,128)(2,1)} %get-tuple-element.57), channel_id=1, source_target_pairs={{0,6},{2,0},{4,2},{6,4},{1,7},{3,1},{5,3},{7,5},{8,14},{10,8},{12,... | collective-permute-start | bytes 786440 | tf_op jit(solution)/shard_map/ppermute | solution.py:15
  122.7 4.3 %collective-permute-start.12 = (bf16[32,4096]{1,0:T(8,128)(2,1)}, bf16[32,4096]{1,0:T(8,128)(2,1)S(1)}, u32[]{:S(2)}, u32[]{:S(2)}) collective-permute-start(bf16[32,4096]{1,0:T(8,128)(2,1)} %get-tuple-element.58), channel_id=1, source_target_pairs={{0,2},{2,4},{4,6},{6,0},{1,3},{3,5},{5,7},{7,1},{8,10},{10,12},{12... | collective-permute-start | bytes 786440 | tf_op jit(solution)/shard_map/ppermute | solution.py:15
  127.0 9.9 %collective-permute-done.13 = bf16[32,4096]{1,0:T(8,128)(2,1)S(1)} collective-permute-done((bf16[32,4096]{1,0:T(8,128)(2,1)}, bf16[32,4096]{1,0:T(8,128)(2,1)S(1)}, u32[]{:S(2)}, u32[]{:S(2)}) %collective-permute-start.13) | collective-permute-done | bytes 262176 | tf_op jit(solution)/shard_map/ppermute | solution.py:15
  137.0 2.2 %collective-permute-done.12 = bf16[32,4096]{1,0:T(8,128)(2,1)S(1)} collective-permute-done((bf16[32,4096]{1,0:T(8,128)(2,1)}, bf16[32,4096]{1,0:T(8,128)(2,1)S(1)}, u32[]{:S(2)}, u32[]{:S(2)}) %collective-permute-start.12) | collective-permute-done | bytes 262176 | tf_op jit(solution)/shard_map/ppermute | solution.py:15
  140.0 8.3 %all-to-all-start.3 = ((bf16[16,48,256]{2,1,0:T(8,128)(2,1)}), bf16[16,48,256]{2,1,0:T(8,128)(2,1)S(1)}, u32[]{:S(2)}, u32[]{:S(2)}) async-start(bf16[16,48,256]{2,1,0:T(8,128)(2,1)} %broadcast_in_dim.3), calls=%async_computation.3 | async-start | bytes 786432 | tf_op jit(solution)/shard_map/all_to_all | solution.py:229
  149.4 4.3 %collective-permute-start.15 = (bf16[32,4096]{1,0:T(8,128)(2,1)S(1)}, bf16[32,4096]{1,0:T(8,128)(2,1)S(1)}, u32[]{:S(2)}, u32[]{:S(2)}) collective-permute-start(bf16[32,4096]{1,0:T(8,128)(2,1)S(1)} %get-tuple-element.55), channel_id=1, source_target_pairs={{0,6},{2,0},{4,2},{6,4},{1,7},{3,1},{5,3},{7,5},{8,14},{10,8},{12,... | collective-permute-start | bytes 786440 | tf_op jit(solution)/shard_map/ppermute | solution.py:15
  153.7 2.5 %collective-permute-start.14 = (bf16[32,4096]{1,0:T(8,128)(2,1)S(1)}, bf16[32,4096]{1,0:T(8,128)(2,1)}, u32[]{:S(2)}, u32[]{:S(2)}) collective-permute-start(bf16[32,4096]{1,0:T(8,128)(2,1)S(1)} %get-tuple-element.56), channel_id=1, source_target_pairs={{0,2},{2,4},{4,6},{6,0},{1,3},{3,5},{5,7},{7,1},{8,10},{10,12},{12... | collective-permute-start | bytes 786440 | tf_op jit(solution)/shard_map/ppermute | solution.py:15
  156.2 9.4 %collective-permute-done.15 = bf16[32,4096]{1,0:T(8,128)(2,1)S(1)} collective-permute-done((bf16[32,4096]{1,0:T(8,128)(2,1)S(1)}, bf16[32,4096]{1,0:T(8,128)(2,1)S(1)}, u32[]{:S(2)}, u32[]{:S(2)}) %collective-permute-start.15) | collective-permute-done | bytes 262176 | tf_op jit(solution)/shard_map/ppermute | solution.py:15
  165.6 5.1 %collective-permute-done.14 = bf16[32,4096]{1,0:T(8,128)(2,1)} collective-permute-done((bf16[32,4096]{1,0:T(8,128)(2,1)S(1)}, bf16[32,4096]{1,0:T(8,128)(2,1)}, u32[]{:S(2)}, u32[]{:S(2)}) %collective-permute-start.14) | collective-permute-done | bytes 262176 | tf_op jit(solution)/shard_map/ppermute | solution.py:15
  170.6 4.8 %collective-permute-start.17 = (bf16[16,48,256]{2,1,0:T(8,128)(2,1)S(1)}, bf16[16,48,256]{2,1,0:T(8,128)(2,1)S(1)}, u32[]{:S(2)}, u32[]{:S(2)}) collective-permute-start(bf16[16,48,256]{2,1,0:T(8,128)(2,1)S(1)} %all-to-all-done.3.own), channel_id=1, source_target_pairs={{0,384},{128,0},{256,128},{384,256},{1,385},{129,1},{257,129},{385... | collective-permute-start | bytes 1179656 | tf_op jit(solution)/shard_map/ppermute | solution.py:15
  177.8 6.1 %collective-permute-done.17.after = bf16[16,48,256]{2,1,0:T(8,128)(2,1)S(1)} collective-permute-done((bf16[16,48,256]{2,1,0:T(8,128)(2,1)S(1)}, bf16[16,48,256]{2,1,0:T(8,128)(2,1)S(1)}, u32[]{:S(2)}, u32[]{:S(2)}) %collective-permute-start.17) | collective-permute-done | bytes 393248 | tf_op jit(solution)/shard_map/ppermute | solution.py:15
  184.0 5.6 %collective-permute-start.19 = (bf16[8,48,256]{2,1,0:T(8,128)(2,1)S(1)}, bf16[8,48,256]{2,1,0:T(8,128)(2,1)S(1)}, u32[]{:S(2)}, u32[]{:S(2)}) collective-permute-start(bf16[8,48,256]{2,1,0:T(8,128)(2,1)S(1)} %slice.106), channel_id=1, source_target_pairs={{0,384},{128,0},{256,128},{384,256},{1,385},{129,1},{257,129},{385... | collective-permute-start | bytes 589832 | tf_op jit(solution)/shard_map/ppermute | solution.py:15
  191.5 2.0 %add_convert_fusion = bf16[64,4096]{1,0:T(8,128)(2,1)} fusion(bf16[256,4096]{1,0:T(8,128)(2,1)S(1)} %copy-done.8, bf16[32,4096]{1,0:T(8,128)(2,1)} %copy-done.9, bf16[32,4096]{1,0:T(8,128)(2,1)} %collective-permute-done.14, bf16[32,4096]{1,0:T(8,128)(2,1)S(1)} %collective-permute-done.15, bf16[32,4096]{1,0:T(8,128)(2,1)S(1)} %collective-permute-done.13), kind=kLoop, calls=%fused_computation.4 | loop fusion | flops 3145728 | bytes 2097152 | tf_op jit(solution)/shard_map/convert_element_type | solution.py:244
  193.5 4.9 %collective-permute-done.18.far_low = bf16[8,48,256]{2,1,0:T(8,128)(2,1)S(1)} collective-permute-done((bf16[8,48,256]{2,1,0:T(8,128)(2,1)S(1)}, bf16[8,48,256]{2,1,0:T(8,128)(2,1)S(1)}, u32[]{:S(2)}, u32[]{:S(2)}) %collective-permute-start.18) | collective-permute-done | bytes 196640 | tf_op jit(solution)/shard_map/ppermute | solution.py:15
  (66 shorter events, 25.9 us)
Async XLA Ops:
  0.6 29.1 %collective-permute-start = (bf16[64,4096]{1,0:T(8,128)(2,1)}, bf16[64,4096]{1,0:T(8,128)(2,1)S(1)}, u32[]{:S(2)}, u32[]{:S(2)}) collective-permute-start(bf16[64,4096]{1,0:T(8,128)(2,1)} %own.1), channel_id=1, source_target_pairs={{0,2},{2,4},{4,6},{6,0},{1,3},{3,5},{5,7},{7,1},{8,10},{10,12},{12... | collective-permute-start | bytes 1572872 | tf_op jit(solution)/shard_map/ppermute | solution.py:15
  5.1 18.5 %collective-permute-start.3 = (bf16[64,4096]{1,0:T(8,128)(2,1)}, bf16[64,4096]{1,0:T(8,128)(2,1)S(1)}, u32[]{:S(2)}, u32[]{:S(2)}) collective-permute-start(bf16[64,4096]{1,0:T(8,128)(2,1)} %own.1), channel_id=1, source_target_pairs={{0,6},{2,0},{4,2},{6,4},{1,7},{3,1},{5,3},{7,5},{8,14},{10,8},{12,... | collective-permute-start | bytes 1572872 | tf_op jit(solution)/shard_map/ppermute | solution.py:15
  8.6 43.2 %collective-permute-start.1 = (bf16[64,4096]{1,0:T(8,128)(2,1)}, bf16[64,4096]{1,0:T(8,128)(2,1)S(1)}, u32[]{:S(2)}, u32[]{:S(2)}) collective-permute-start(bf16[64,4096]{1,0:T(8,128)(2,1)} %own.1), channel_id=1, source_target_pairs={{0,1},{1,0},{2,3},{3,2},{4,5},{5,4},{6,7},{7,6},{8,9},{9,8},{10,11... | collective-permute-start | bytes 1572872 | tf_op jit(solution)/shard_map/ppermute | solution.py:15
  12.5 1.4 copy-start.5
  13.9 1.0 copy-start.6
  15.9 41.0 %copy-start = (bf16[192,4096]{1,0:T(8,128)(2,1)}, bf16[192,4096]{1,0:T(8,128)(2,1)S(1)}, u32[]{:S(2)}) copy-start(bf16[192,4096]{1,0:T(8,128)(2,1)S(1)} %get-tuple-element.32.head.refs_14_) | copy-start | bytes 4718596
  23.7 21.5 %collective-permute-start.6 = (bf16[32,4096]{1,0:T(8,128)(2,1)S(1)}, bf16[32,4096]{1,0:T(8,128)(2,1)S(1)}, u32[]{:S(2)}, u32[]{:S(2)}) collective-permute-start(bf16[32,4096]{1,0:T(8,128)(2,1)S(1)} %slice.97), channel_id=1, source_target_pairs={{0,6},{2,0},{4,2},{6,4},{1,7},{3,1},{5,3},{7,5},{8,14},{10,8},{12,... | collective-permute-start | bytes 786440 | tf_op jit(solution)/shard_map/ppermute | solution.py:15
  29.7 44.0 %copy-start.4 = (bf16[64,4096]{1,0:T(8,128)(2,1)S(1)}, bf16[64,4096]{1,0:T(8,128)(2,1)}, u32[]{:S(2)}) copy-start(bf16[64,4096]{1,0:T(8,128)(2,1)} %copy-done.2) | copy-start | bytes 1572868
  29.8 20.1 %collective-permute-start.5 = (bf16[32,4096]{1,0:T(8,128)(2,1)S(1)}, bf16[32,4096]{1,0:T(8,128)(2,1)S(1)}, u32[]{:S(2)}, u32[]{:S(2)}) collective-permute-start(bf16[32,4096]{1,0:T(8,128)(2,1)S(1)} %slice.77), channel_id=1, source_target_pairs={{0,2},{2,4},{4,6},{6,0},{1,3},{3,5},{5,7},{7,1},{8,10},{10,12},{12... | collective-permute-start | bytes 786440 | tf_op jit(solution)/shard_map/ppermute | solution.py:15
  40.8 11.0 %collective-permute-start.4 = (bf16[64,4096]{1,0:T(8,128)(2,1)S(1)}, bf16[64,4096]{1,0:T(8,128)(2,1)S(1)}, u32[]{:S(2)}, u32[]{:S(2)}) collective-permute-start(bf16[64,4096]{1,0:T(8,128)(2,1)S(1)} %collective-permute-done.3.refs_4_.refs_8_), channel_id=1, source_target_pairs={{0,1},{1,0},{2,3},{3,2},{4,5},{5,4},{6,7},{7,6},{8,9},{9,8},{10,11... | collective-permute-start | bytes 1572872 | tf_op jit(solution)/shard_map/ppermute | solution.py:15
  42.7 10.6 %collective-permute-start.2 = (bf16[64,4096]{1,0:T(8,128)(2,1)S(1)}, bf16[64,4096]{1,0:T(8,128)(2,1)S(1)}, u32[]{:S(2)}, u32[]{:S(2)}) collective-permute-start(bf16[64,4096]{1,0:T(8,128)(2,1)S(1)} %collective-permute-done.refs_2_.refs_6_), channel_id=1, source_target_pairs={{0,1},{1,0},{2,3},{3,2},{4,5},{5,4},{6,7},{7,6},{8,9},{9,8},{10,11... | collective-permute-start | bytes 1572872 | tf_op jit(solution)/shard_map/ppermute | solution.py:15
  45.2 6.7 %collective-permute-start.8 = (bf16[32,4096]{1,0:T(8,128)(2,1)S(1)}, bf16[32,4096]{1,0:T(8,128)(2,1)S(1)}, u32[]{:S(2)}, u32[]{:S(2)}) collective-permute-start(bf16[32,4096]{1,0:T(8,128)(2,1)S(1)} %collective-permute-done.6.refs_7_.refs_11_), channel_id=1, source_target_pairs={{0,1},{1,0},{2,3},{3,2},{4,5},{5,4},{6,7},{7,6},{8,9},{9,8},{10,11... | collective-permute-start | bytes 786440 | tf_op jit(solution)/shard_map/ppermute | solution.py:15
  49.9 3.4 %collective-permute-start.7 = (bf16[32,4096]{1,0:T(8,128)(2,1)S(1)}, bf16[32,4096]{1,0:T(8,128)(2,1)S(1)}, u32[]{:S(2)}, u32[]{:S(2)}) collective-permute-start(bf16[32,4096]{1,0:T(8,128)(2,1)S(1)} %collective-permute-done.5.refs_6_.refs_10_), channel_id=1, source_target_pairs={{0,1},{1,0},{2,3},{3,2},{4,5},{5,4},{6,7},{7,6},{8,9},{9,8},{10,11... | collective-permute-start | bytes 786440 | tf_op jit(solution)/shard_map/ppermute | solution.py:15
  53.3 1.0 copy-start.3
  78.9 6.5 %copy-start.1 = (bf16[192,4096]{1,0:T(8,128)(2,1)S(1)}, bf16[192,4096]{1,0:T(8,128)(2,1)}, u32[]{:S(2)}) copy-start(bf16[192,4096]{1,0:T(8,128)(2,1)} %copy-done) | copy-start | bytes 4718596
  78.9 6.5 %collective-permute-start.9 = (bf16[256,4096]{1,0:T(8,128)(2,1)}, bf16[256,4096]{1,0:T(8,128)(2,1)}, u32[]{:S(2)}, u32[]{:S(2)}) collective-permute-start(bf16[256,4096]{1,0:T(8,128)(2,1)} %get-tuple-element.44), channel_id=1, source_target_pairs={{0,1},{1,0},{2,3},{3,2},{4,5},{5,4},{6,7},{7,6},{8,9},{9,8},{10,11... | collective-permute-start | bytes 6291464 | tf_op jit(solution)/shard_map/ppermute | solution.py:15
  81.0 25.8 %all-to-all-start.1 = ((bf16[4,48,4096]{2,1,0:T(8,128)(2,1)}), bf16[4,48,4096]{2,1,0:T(8,128)(2,1)S(1)}, u32[]{:S(2)}, u32[]{:S(2)}) async-start(bf16[4,48,4096]{2,1,0:T(8,128)(2,1)} %bitcast.31), calls=%async_computation.1 | async-start | bytes 3145728 | tf_op jit(solution)/shard_map/all_to_all | solution.py:200
  87.8 3.5 %copy-start.7 = (bf16[256,4096]{1,0:T(8,128)(2,1)}, bf16[256,4096]{1,0:T(8,128)(2,1)S(1)}, u32[]{:S(2)}) copy-start(bf16[256,4096]{1,0:T(8,128)(2,1)S(1)} %fusion.2) | copy-start | bytes 6291460
  88.8 19.6 %collective-permute-start.11 = (bf16[32,4096]{1,0:T(8,128)(2,1)}, bf16[32,4096]{1,0:T(8,128)(2,1)S(1)}, u32[]{:S(2)}, u32[]{:S(2)}) collective-permute-start(bf16[32,4096]{1,0:T(8,128)(2,1)} %get-tuple-element.59), channel_id=1, source_target_pairs={{0,6},{2,0},{4,2},{6,4},{1,7},{3,1},{5,3},{7,5},{8,14},{10,8},{12,... | collective-permute-start | bytes 786440 | tf_op jit(solution)/shard_map/ppermute | solution.py:15
  91.2 17.1 %collective-permute-start.10 = (bf16[32,4096]{1,0:T(8,128)(2,1)S(1)}, bf16[32,4096]{1,0:T(8,128)(2,1)}, u32[]{:S(2)}, u32[]{:S(2)}) collective-permute-start(bf16[32,4096]{1,0:T(8,128)(2,1)S(1)} %get-tuple-element.60), channel_id=1, source_target_pairs={{0,2},{2,4},{4,6},{6,0},{1,3},{3,5},{5,7},{7,1},{8,10},{10,12},{12... | collective-permute-start | bytes 786440 | tf_op jit(solution)/shard_map/ppermute | solution.py:15
  108.3 40.0 %copy-start.8 = (bf16[256,4096]{1,0:T(8,128)(2,1)S(1)}, bf16[256,4096]{1,0:T(8,128)(2,1)}, u32[]{:S(2)}) copy-start(bf16[256,4096]{1,0:T(8,128)(2,1)} %copy-done.7) | copy-start | bytes 6291460
  108.3 30.8 %all-to-all-start.2 = ((bf16[16,48,256]{2,1,0:T(8,128)(2,1)}), bf16[16,48,256]{2,1,0:T(8,128)(2,1)S(1)}, u32[]{:S(2)}, u32[]{:S(2)}) async-start(bf16[16,48,256]{2,1,0:T(8,128)(2,1)} %shard_map.70), calls=%async_computation.2 | async-start | bytes 786432 | tf_op jit(solution)/shard_map/all_to_all | solution.py:226
  120.3 16.7 %collective-permute-start.13 = (bf16[32,4096]{1,0:T(8,128)(2,1)}, bf16[32,4096]{1,0:T(8,128)(2,1)S(1)}, u32[]{:S(2)}, u32[]{:S(2)}) collective-permute-start(bf16[32,4096]{1,0:T(8,128)(2,1)} %get-tuple-element.57), channel_id=1, source_target_pairs={{0,6},{2,0},{4,2},{6,4},{1,7},{3,1},{5,3},{7,5},{8,14},{10,8},{12,... | collective-permute-start | bytes 786440 | tf_op jit(solution)/shard_map/ppermute | solution.py:15
  122.7 16.4 %collective-permute-start.12 = (bf16[32,4096]{1,0:T(8,128)(2,1)}, bf16[32,4096]{1,0:T(8,128)(2,1)S(1)}, u32[]{:S(2)}, u32[]{:S(2)}) collective-permute-start(bf16[32,4096]{1,0:T(8,128)(2,1)} %get-tuple-element.58), channel_id=1, source_target_pairs={{0,2},{2,4},{4,6},{6,0},{1,3},{3,5},{5,7},{7,1},{8,10},{10,12},{12... | collective-permute-start | bytes 786440 | tf_op jit(solution)/shard_map/ppermute | solution.py:15
  139.2 0.8 copy-start.9
  140.0 30.6 %all-to-all-start.3 = ((bf16[16,48,256]{2,1,0:T(8,128)(2,1)}), bf16[16,48,256]{2,1,0:T(8,128)(2,1)S(1)}, u32[]{:S(2)}, u32[]{:S(2)}) async-start(bf16[16,48,256]{2,1,0:T(8,128)(2,1)} %broadcast_in_dim.3), calls=%async_computation.3 | async-start | bytes 786432 | tf_op jit(solution)/shard_map/all_to_all | solution.py:229
  149.4 16.2 %collective-permute-start.15 = (bf16[32,4096]{1,0:T(8,128)(2,1)S(1)}, bf16[32,4096]{1,0:T(8,128)(2,1)S(1)}, u32[]{:S(2)}, u32[]{:S(2)}) collective-permute-start(bf16[32,4096]{1,0:T(8,128)(2,1)S(1)} %get-tuple-element.55), channel_id=1, source_target_pairs={{0,6},{2,0},{4,2},{6,4},{1,7},{3,1},{5,3},{7,5},{8,14},{10,8},{12,... | collective-permute-start | bytes 786440 | tf_op jit(solution)/shard_map/ppermute | solution.py:15
  153.7 16.9 %collective-permute-start.14 = (bf16[32,4096]{1,0:T(8,128)(2,1)S(1)}, bf16[32,4096]{1,0:T(8,128)(2,1)}, u32[]{:S(2)}, u32[]{:S(2)}) collective-permute-start(bf16[32,4096]{1,0:T(8,128)(2,1)S(1)} %get-tuple-element.56), channel_id=1, source_target_pairs={{0,2},{2,4},{4,6},{6,0},{1,3},{3,5},{5,7},{7,1},{8,10},{10,12},{12... | collective-permute-start | bytes 786440 | tf_op jit(solution)/shard_map/ppermute | solution.py:15
  170.6 13.3 %collective-permute-start.17 = (bf16[16,48,256]{2,1,0:T(8,128)(2,1)S(1)}, bf16[16,48,256]{2,1,0:T(8,128)(2,1)S(1)}, u32[]{:S(2)}, u32[]{:S(2)}) collective-permute-start(bf16[16,48,256]{2,1,0:T(8,128)(2,1)S(1)} %all-to-all-done.3.own), channel_id=1, source_target_pairs={{0,384},{128,0},{256,128},{384,256},{1,385},{129,1},{257,129},{385... | collective-permute-start | bytes 1179656 | tf_op jit(solution)/shard_map/ppermute | solution.py:15
  175.4 14.2 %collective-permute-start.16 = (bf16[16,48,256]{2,1,0:T(8,128)(2,1)S(1)}, bf16[16,48,256]{2,1,0:T(8,128)(2,1)S(1)}, u32[]{:S(2)}, u32[]{:S(2)}) collective-permute-start(bf16[16,48,256]{2,1,0:T(8,128)(2,1)S(1)} %all-to-all-done.3.own), channel_id=1, source_target_pairs={{0,128},{128,256},{256,384},{384,0},{1,129},{129,257},{257,385},{3... | collective-permute-start | bytes 1179656 | tf_op jit(solution)/shard_map/ppermute | solution.py:15
  184.0 9.6 %collective-permute-start.19 = (bf16[8,48,256]{2,1,0:T(8,128)(2,1)S(1)}, bf16[8,48,256]{2,1,0:T(8,128)(2,1)S(1)}, u32[]{:S(2)}, u32[]{:S(2)}) collective-permute-start(bf16[8,48,256]{2,1,0:T(8,128)(2,1)S(1)} %slice.106), channel_id=1, source_target_pairs={{0,384},{128,0},{256,128},{384,256},{1,385},{129,1},{257,129},{385... | collective-permute-start | bytes 589832 | tf_op jit(solution)/shard_map/ppermute | solution.py:15
  189.6 8.8 %collective-permute-start.18 = (bf16[8,48,256]{2,1,0:T(8,128)(2,1)S(1)}, bf16[8,48,256]{2,1,0:T(8,128)(2,1)S(1)}, u32[]{:S(2)}, u32[]{:S(2)}) collective-permute-start(bf16[8,48,256]{2,1,0:T(8,128)(2,1)S(1)} %slice.105), channel_id=1, source_target_pairs={{0,128},{128,256},{256,384},{384,0},{1,129},{129,257},{257,385},{3... | collective-permute-start | bytes 589832 | tf_op jit(solution)/shard_map/ppermute | solution.py:15
  (1 other events, 0.8 us)

commit v12 on v10

--- a/solution.py
+++ b/solution.py
@@ -110,13 +110,10 @@
         out[i] = jnp.sum(part, axis=0).astype(BF16)
 
 
-def lay_kernel(where, own, before, after, far_low, far_high, out):
-    n, rows, cols = own.shape
-    for at, pieces in ((6, (own,)), (7, (before,)), (8, (after,)), (9, (far_low, far_high))):
-        row = pl.ds(pl.multiple_of(where[at] * rows, rows), rows)
-        pieces = [(piece, i) for piece in pieces for i in range(piece.shape[0])]
-        for j, (piece, i) in enumerate(pieces):
-            out[row, j * cols : (j + 1) * cols] = piece[i]
+def lay_kernel(pieces, out):
+    cols = pieces.shape[3]
+    for i in range(pieces.shape[1]):
+        out[:, i * cols : (i + 1) * cols] = pieces[0, i]
 
 
 def per_device(hidden, targets, token_weight, head_weight, *, n_x, n_yl, n_z, n_yh):
@@ -133,7 +130,7 @@
 
     labels, weights = local_order(targets), local_order(token_weight)
     where = [core, (yh * 2 + core) * v_dev] + [(yh + d) % n_yh for d in (0, n_yh - 1, 1, 2)]
-    where = jnp.stack(where + [(lax.axis_index("x") + d) % n_x for d in (0, n_x - 1, 1, 2)])
+    where = jnp.stack(where)
 
     smem, vmem = pl.BlockSpec(memory_space=pltpu.SMEM), pl.BlockSpec(memory_space=pltpu.VMEM)
     params = pltpu.CompilerParams(vmem_limit_bytes=16 << 20)
@@ -224,19 +221,17 @@
 
     part = lax.all_to_all(part, ("yl", "z"), 0, 0, tiled=True)
     part = jnp.sum(part.astype(F32), axis=0).astype(BF16)
-    part = lax.all_to_all(jnp.broadcast_to(part, (n_yl * n_z,) + part.shape), ("yl", "z"), 0, 0, tiled=True)
-    x_before = shift(part, "x", 1, n_x)
-    x_after = shift(part, "x", -1, n_x)
-    x_low = shift(x_before[: n_rest // 2], "x", 1, n_x)
-    x_high = shift(x_after[n_rest // 2 :], "x", -1, n_x)
+    part = lax.all_to_all(jnp.broadcast_to(part, (n_x * n_rest,) + part.shape), DP, 0, 0, tiled=True)
+    part = part.reshape((n_x, n_rest) + part.shape[1:])
     grad_weight = pl.pallas_call(
         lay_kernel,
         out_shape=jax.ShapeDtypeStruct((v_dev, width), BF16),
-        in_specs=[smem] + [vmem] * 5,
-        out_specs=vmem,
+        grid=(n_x,),
+        in_specs=[pl.BlockSpec((1,) + part.shape[1:], lambda i: (i, 0, 0, 0))],
+        out_specs=pl.BlockSpec((rows, width), lambda i: (i, 0)),
         compiler_params=params,
         cost_estimate=pl.CostEstimate(flops=0, bytes_accessed=4 * v_dev * width, transcendentals=0),
-    )(where, part, x_before, x_after, x_low, x_high)
+    )(part)
     grad_hidden = (mine.astype(F32) + sum(v.astype(F32) for v in came)).astype(BF16)
     return token_loss, grad_hidden, grad_weight
 

time: 180 us -> 187 us (1.039)
  the two profiles are of different devices: /device:TPU:72 before, /device:TPU:30 now
where the time goes in v12:
time: 187 us; the launch traced here: 185 us
  waiting for transfers between devices  68.2 us (36%)
  starting transfers between devices  55.7 us (30%)
  blocking collectives  37 us (20%)
  Pallas kernels  9.78 us (5%)
  local copies, waits for them, and re-layouts  7.96 us (4%)
  other arithmetic  3.55 us (2%)
  matrix products  2.32 us (1%)
    ppermute x14, waiting for transfers between devices, shift(): lax.ppermute(value, axis, [(i, (i + step) % size) for i in range(size)])  59.2 us
    ppermute x14, starting transfers between devices, shift(): lax.ppermute(value, axis, [(i, (i + step) % size) for i in range(size)])  41.6 us
    all_to_all x1, blocking collectives, per_device(): part = lax.all_to_all(part, ('yl', 'z'), 0, 0, tiled=True)  23.2 us
    all_to_all x1, blocking collectives, per_device(): stats = lax.all_to_all(stats, VOCAB, 0, 0, tiled=True)  13.9 us
    all_to_all x1, starting transfers between devices, per_device(): lax.all_to_all(jnp.broadcast_to(part, (n_x * n_rest,) + part.shape), DP,...  9.23 us
    all_to_all x1, waiting for transfers between devices, per_device(): part = lax.all_to_all(part, 'x', 0, 0, tiled=True)  8.95 us
    pallas_call x1, Pallas kernels, per_device(): pl.pallas_call(score_kernel, out_shape=(jax.ShapeDtypeStruct((v_dev, widt...  5.12 us
    all_to_all x1, starting transfers between devices, per_device(): part = lax.all_to_all(part, 'x', 0, 0, tiled=True)  4.78 us
  transfers between devices with their start and end apart: 16, of which 8 were waited for; matrix products, arithmetic and copies ran while one was open for 4% of the time, Pallas kernels for 0%

profile of v12, /device:TPU:30, one launch (start us, length us, event | category | flops | bytes accessed | tf_op | source)
XLA Modules:
  0.0 185.5 jit_solution(18180982817096206182)
XLA Ops:
  0.6 4.8 %collective-permute-start = (bf16[64,4096]{1,0:T(8,128)(2,1)}, bf16[64,4096]{1,0:T(8,128)(2,1)S(1)}, u32[]{:S(2)}, u32[]{:S(2)}) collective-permute-start(bf16[64,4096]{1,0:T(8,128)(2,1)} %own.1), channel_id=1, source_target_pairs={{0,2},{2,4},{4,6},{6,0},{1,3},{3,5},{5,7},{7,1},{8,10},{10,12},{12... | collective-permute-start | bytes 1572872 | tf_op jit(solution)/shard_map/ppermute | solution.py:15
  5.4 1.9 %collective-permute-start.3 = (bf16[64,4096]{1,0:T(8,128)(2,1)}, bf16[64,4096]{1,0:T(8,128)(2,1)S(1)}, u32[]{:S(2)}, u32[]{:S(2)}) collective-permute-start(bf16[64,4096]{1,0:T(8,128)(2,1)} %own.1), channel_id=1, source_target_pairs={{0,6},{2,0},{4,2},{6,4},{1,7},{3,1},{5,3},{7,5},{8,14},{10,8},{12,... | collective-permute-start | bytes 1572872 | tf_op jit(solution)/shard_map/ppermute | solution.py:15
  7.4 1.9 %collective-permute-start.1 = (bf16[64,4096]{1,0:T(8,128)(2,1)}, bf16[64,4096]{1,0:T(8,128)(2,1)S(1)}, u32[]{:S(2)}, u32[]{:S(2)}) collective-permute-start(bf16[64,4096]{1,0:T(8,128)(2,1)} %own.1), channel_id=1, source_target_pairs={{0,1},{1,0},{2,3},{3,2},{4,5},{5,4},{6,7},{7,6},{8,9},{9,8},{10,11... | collective-permute-start | bytes 1572872 | tf_op jit(solution)/shard_map/ppermute | solution.py:15
  11.3 1.4 copy-done.5
  14.7 19.4 %collective-permute-done.3.refs_4_.refs_8_ = bf16[64,4096]{1,0:T(8,128)(2,1)S(1)} collective-permute-done((bf16[64,4096]{1,0:T(8,128)(2,1)}, bf16[64,4096]{1,0:T(8,128)(2,1)S(1)}, u32[]{:S(2)}, u32[]{:S(2)}) %collective-permute-start.3) | collective-permute-done | bytes 524320 | tf_op jit(solution)/shard_map/ppermute | solution.py:15
  34.2 1.9 %collective-permute-start.6 = (bf16[32,4096]{1,0:T(8,128)(2,1)S(1)}, bf16[32,4096]{1,0:T(8,128)(2,1)S(1)}, u32[]{:S(2)}, u32[]{:S(2)}) collective-permute-start(bf16[32,4096]{1,0:T(8,128)(2,1)S(1)} %slice.75), channel_id=1, source_target_pairs={{0,6},{2,0},{4,2},{6,4},{1,7},{3,1},{5,3},{7,5},{8,14},{10,8},{12,... | collective-permute-start | bytes 786440 | tf_op jit(solution)/shard_map/ppermute | solution.py:15
  36.2 6.2 %collective-permute-start.5 = (bf16[32,4096]{1,0:T(8,128)(2,1)S(1)}, bf16[32,4096]{1,0:T(8,128)(2,1)S(1)}, u32[]{:S(2)}, u32[]{:S(2)}) collective-permute-start(bf16[32,4096]{1,0:T(8,128)(2,1)S(1)} %slice.59), channel_id=1, source_target_pairs={{0,2},{2,4},{4,6},{6,0},{1,3},{3,5},{5,7},{7,1},{8,10},{10,12},{12... | collective-permute-start | bytes 786440 | tf_op jit(solution)/shard_map/ppermute | solution.py:15
  42.3 1.9 %collective-permute-start.4 = (bf16[64,4096]{1,0:T(8,128)(2,1)S(1)}, bf16[64,4096]{1,0:T(8,128)(2,1)S(1)}, u32[]{:S(2)}, u32[]{:S(2)}) collective-permute-start(bf16[64,4096]{1,0:T(8,128)(2,1)S(1)} %collective-permute-done.3.refs_4_.refs_8_), channel_id=1, source_target_pairs={{0,1},{1,0},{2,3},{3,2},{4,5},{5,4},{6,7},{7,6},{8,9},{9,8},{10,11... | collective-permute-start | bytes 1572872 | tf_op jit(solution)/shard_map/ppermute | solution.py:15
  44.3 2.4 %collective-permute-start.2 = (bf16[64,4096]{1,0:T(8,128)(2,1)S(1)}, bf16[64,4096]{1,0:T(8,128)(2,1)S(1)}, u32[]{:S(2)}, u32[]{:S(2)}) collective-permute-start(bf16[64,4096]{1,0:T(8,128)(2,1)S(1)} %collective-permute-done.refs_2_.refs_6_), channel_id=1, source_target_pairs={{0,1},{1,0},{2,3},{3,2},{4,5},{5,4},{6,7},{7,6},{8,9},{9,8},{10,11... | collective-permute-start | bytes 1572872 | tf_op jit(solution)/shard_map/ppermute | solution.py:15
  46.7 2.0 %collective-permute-done.6.refs_7_.refs_11_ = bf16[32,4096]{1,0:T(8,128)(2,1)S(1)} collective-permute-done((bf16[32,4096]{1,0:T(8,128)(2,1)S(1)}, bf16[32,4096]{1,0:T(8,128)(2,1)S(1)}, u32[]{:S(2)}, u32[]{:S(2)}) %collective-permute-start.6) | collective-permute-done | bytes 262176 | tf_op jit(solution)/shard_map/ppermute | solution.py:15
  48.7 1.9 %collective-permute-start.8 = (bf16[32,4096]{1,0:T(8,128)(2,1)S(1)}, bf16[32,4096]{1,0:T(8,128)(2,1)S(1)}, u32[]{:S(2)}, u32[]{:S(2)}) collective-permute-start(bf16[32,4096]{1,0:T(8,128)(2,1)S(1)} %collective-permute-done.6.refs_7_.refs_11_), channel_id=1, source_target_pairs={{0,1},{1,0},{2,3},{3,2},{4,5},{5,4},{6,7},{7,6},{8,9},{9,8},{10,11... | collective-permute-start | bytes 786440 | tf_op jit(solution)/shard_map/ppermute | solution.py:15
  51.2 1.9 %collective-permute-start.7 = (bf16[32,4096]{1,0:T(8,128)(2,1)S(1)}, bf16[32,4096]{1,0:T(8,128)(2,1)S(1)}, u32[]{:S(2)}, u32[]{:S(2)}) collective-permute-start(bf16[32,4096]{1,0:T(8,128)(2,1)S(1)} %collective-permute-done.5.refs_6_.refs_10_), channel_id=1, source_target_pairs={{0,1},{1,0},{2,3},{3,2},{4,5},{5,4},{6,7},{7,6},{8,9},{9,8},{10,11... | collective-permute-start | bytes 786440 | tf_op jit(solution)/shard_map/ppermute | solution.py:15
  53.2 1.5 collective-permute-done.7.refs_8_.refs_12_
  55.7 2.5 %shard_map.68 = (f32[192,128]{1,0:T(8,128)S(1)}, f32[192,128]{1,0:T(8,128)S(1)}, f32[192,128]{1,0:T(8,128)S(1)}, f32[192,128]{1,0:T(8,128)S(1)}, f32[8,16,128]{2,1,0:T(8,128)S(1)}) custom-call(s32[6]{0:T(128)S(1)} %stack.27.where, bf16[192,4096]{1,0:T(8,128)(2,1)S(1)} %get-tuple-element.26.head.refs_14_, s32[1,512]{1,0:T(1,128)S(1)} %reshape.25.labels, ...), custom_call_target="tpu_custom_call" | custom-call | flops 805306368 | bytes 5767168 | tf_op jit(solution)/shard_map/pallas_call | solution.py:157
  58.2 13.9 %all_to_all.20.stats = f32[8,16,128]{2,1,0:T(8,128)S(1)} all-to-all(f32[8,16,128]{2,1,0:T(8,128)S(1)} %get-tuple-element.30), channel_id=1, replica_groups=mesh['x'=4,'yl'=2,'z'=8,'yh'=4,'core'=2] {'yh','core'}, dimensions={0} | all-to-all | bytes 131072 | tf_op jit(solution)/shard_map/all_to_all | solution.py:169
  72.0 5.1 %shard_map.69 = (bf16[192,4096]{1,0:T(8,128)(2,1)}, bf16[256,4096]{1,0:T(8,128)(2,1)}, bf16[256,192]{1,0:T(8,128)(2,1)S(1)}, f32[1,128]{1,0:T(1,128)S(1)}) custom-call(s32[6]{0:T(128)S(1)} %stack.27.where, f32[8,16,128]{2,1,0:T(8,128)S(1)} %all_to_all.20.stats, s32[1,512]{1,0:T(1,128)S(1)} %reshape.25.labels, f32[1,512]{1,0:T(1,128)S(1)} %reshape.27.weights, ...), custom_call_target="tpu_custom_call" | custom-call | flops 1207959552 | bytes 9437184 | tf_op jit(solution)/shard_map/pallas_call | solution.py:171
  77.2 2.1 %collective-permute-start.9 = (bf16[256,4096]{1,0:T(8,128)(2,1)}, bf16[256,4096]{1,0:T(8,128)(2,1)}, u32[]{:S(2)}, u32[]{:S(2)}) collective-permute-start(bf16[256,4096]{1,0:T(8,128)(2,1)} %get-tuple-element.38), channel_id=1, source_target_pairs={{0,1},{1,0},{2,3},{3,2},{4,5},{5,4},{6,7},{7,6},{8,9},{9,8},{10,11... | collective-permute-start | bytes 6291464 | tf_op jit(solution)/shard_map/ppermute | solution.py:15
  79.2 4.8 %all-to-all-start.1 = ((bf16[4,48,4096]{2,1,0:T(8,128)(2,1)}), bf16[4,48,4096]{2,1,0:T(8,128)(2,1)S(1)}, u32[]{:S(2)}, u32[]{:S(2)}) async-start(bf16[4,48,4096]{2,1,0:T(8,128)(2,1)} %bitcast.29), calls=%async_computation.1 | async-start | bytes 3145728 | tf_op jit(solution)/shard_map/all_to_all | solution.py:197
  84.0 2.3 %fusion.2 = bf16[256,4096]{1,0:T(8,128)(2,1)S(1)} fusion(bf16[256,192]{1,0:T(8,128)(2,1)S(1)} %get-tuple-element.37, bf16[192,4096]{1,0:T(8,128)(2,1)S(1)} %copy-done.1, bf16[256,4096]{1,0:T(8,128)(2,1)} %collective-permute-done.9), kind=kOutput, calls=%fused_computation.3 | convolution fusion | flops 407896064 | bytes 5865472 | tf_op jit(solution)/shard_map/dot_general | solution.py:199
  86.4 4.1 %collective-permute-start.11 = (bf16[32,4096]{1,0:T(8,128)(2,1)S(1)}, bf16[32,4096]{1,0:T(8,128)(2,1)S(1)}, u32[]{:S(2)}, u32[]{:S(2)}) collective-permute-start(bf16[32,4096]{1,0:T(8,128)(2,1)S(1)} %get-tuple-element.45), channel_id=1, source_target_pairs={{0,6},{2,0},{4,2},{6,4},{1,7},{3,1},{5,3},{7,5},{8,14},{10,8},{12,... | collective-permute-start | bytes 786440 | tf_op jit(solution)/shard_map/ppermute | solution.py:15
  90.5 3.8 %collective-permute-start.10 = (bf16[32,4096]{1,0:T(8,128)(2,1)S(1)}, bf16[32,4096]{1,0:T(8,128)(2,1)S(1)}, u32[]{:S(2)}, u32[]{:S(2)}) collective-permute-start(bf16[32,4096]{1,0:T(8,128)(2,1)S(1)} %get-tuple-element.46), channel_id=1, source_target_pairs={{0,2},{2,4},{4,6},{6,0},{1,3},{3,5},{5,7},{7,1},{8,10},{10,12},{12... | collective-permute-start | bytes 786440 | tf_op jit(solution)/shard_map/ppermute | solution.py:15
  94.4 8.9 %all-to-all-done.1.parts = bf16[4,48,4096]{2,1,0:T(8,128)(2,1)S(1)} async-done(((bf16[4,48,4096]{2,1,0:T(8,128)(2,1)}), bf16[4,48,4096]{2,1,0:T(8,128)(2,1)S(1)}, u32[]{:S(2)}, u32[]{:S(2)}) %all-to-all-start.1) | async-done | bytes 1572896 | tf_op jit(solution)/shard_map/all_to_all | solution.py:197
  103.7 2.0 %collective-permute-done.10 = bf16[32,4096]{1,0:T(8,128)(2,1)S(1)} collective-permute-done((bf16[32,4096]{1,0:T(8,128)(2,1)S(1)}, bf16[32,4096]{1,0:T(8,128)(2,1)S(1)}, u32[]{:S(2)}, u32[]{:S(2)}) %collective-permute-start.10) | collective-permute-done | bytes 262176 | tf_op jit(solution)/shard_map/ppermute | solution.py:15
  105.7 23.2 %all_to_all.21 = bf16[16,48,256]{2,1,0:T(8,128)(2,1)S(1)} all-to-all(bf16[16,48,256]{2,1,0:T(8,128)(2,1)S(1)} %shard_map.70), channel_id=1, replica_groups=mesh['x'=4,'yl'=2,'z'=8,'yh'=4,'core'=2] {'yl','z'}, dimensions={0} | all-to-all | bytes 786432 | tf_op jit(solution)/shard_map/all_to_all | solution.py:222
  130.2 9.2 %all-to-all-start.3 = ((bf16[64,48,256]{2,1,0:T(8,128)(2,1)}), bf16[64,48,256]{2,1,0:T(8,128)(2,1)S(1)}, u32[]{:S(2)}, u32[]{:S(2)}) async-start(bf16[64,48,256]{2,1,0:T(8,128)(2,1)} %broadcast_in_dim.4), calls=%async_computation.3 | async-start | bytes 3145728 | tf_op jit(solution)/shard_map/all_to_all | solution.py:224
  139.5 1.4 add_convert_fusion.2
  140.8 4.7 %collective-permute-start.12 = (bf16[64,4096]{1,0:T(8,128)(2,1)S(1)}, bf16[64,4096]{1,0:T(8,128)(2,1)S(1)}, u32[]{:S(2)}, u32[]{:S(2)}) collective-permute-start(bf16[64,4096]{1,0:T(8,128)(2,1)S(1)} %get-tuple-element.43), channel_id=1, source_target_pairs={{0,2},{2,4},{4,6},{6,0},{1,3},{3,5},{5,7},{7,1},{8,10},{10,12},{12... | collective-permute-start | bytes 1572872 | tf_op jit(solution)/shard_map/ppermute | solution.py:15
  145.5 2.0 %collective-permute-start.13 = (bf16[64,4096]{1,0:T(8,128)(2,1)S(1)}, bf16[64,4096]{1,0:T(8,128)(2,1)S(1)}, u32[]{:S(2)}, u32[]{:S(2)}) collective-permute-start(bf16[64,4096]{1,0:T(8,128)(2,1)S(1)} %get-tuple-element.44), channel_id=1, source_target_pairs={{0,6},{2,0},{4,2},{6,4},{1,7},{3,1},{5,3},{7,5},{8,14},{10,8},{12,... | collective-permute-start | bytes 1572872 | tf_op jit(solution)/shard_map/ppermute | solution.py:15
  148.1 8.9 %collective-permute-done.12 = bf16[64,4096]{1,0:T(8,128)(2,1)S(1)} collective-permute-done((bf16[64,4096]{1,0:T(8,128)(2,1)S(1)}, bf16[64,4096]{1,0:T(8,128)(2,1)S(1)}, u32[]{:S(2)}, u32[]{:S(2)}) %collective-permute-start.12) | collective-permute-done | bytes 524320 | tf_op jit(solution)/shard_map/ppermute | solution.py:15
  157.0 24.8 %collective-permute-done.13 = bf16[64,4096]{1,0:T(8,128)(2,1)S(1)} collective-permute-done((bf16[64,4096]{1,0:T(8,128)(2,1)S(1)}, bf16[64,4096]{1,0:T(8,128)(2,1)S(1)}, u32[]{:S(2)}, u32[]{:S(2)}) %collective-permute-start.13) | collective-permute-done | bytes 524320 | tf_op jit(solution)/shard_map/ppermute | solution.py:15
  181.8 2.0 %add_convert_fusion = bf16[64,4096]{1,0:T(8,128)(2,1)} fusion(bf16[64,4096]{1,0:T(8,128)(2,1)S(1)} %collective-permute-done.13, bf16[64,4096]{1,0:T(8,128)(2,1)S(1)} %collective-permute-done.12, bf16[256,4096]{1,0:T(8,128)(2,1)} %copy-done.7), kind=kLoop, calls=%fused_computation.4 | loop fusion | flops 1572864 | bytes 2097152 | tf_op jit(solution)/shard_map/convert_element_type | solution.py:235
  183.8 1.7 shard_map.71
  (47 shorter events, 7.9 us)
Async XLA Ops:
  0.6 35.5 %collective-permute-start = (bf16[64,4096]{1,0:T(8,128)(2,1)}, bf16[64,4096]{1,0:T(8,128)(2,1)S(1)}, u32[]{:S(2)}, u32[]{:S(2)}) collective-permute-start(bf16[64,4096]{1,0:T(8,128)(2,1)} %own.1), channel_id=1, source_target_pairs={{0,2},{2,4},{4,6},{6,0},{1,3},{3,5},{5,7},{7,1},{8,10},{10,12},{12... | collective-permute-start | bytes 1572872 | tf_op jit(solution)/shard_map/ppermute | solution.py:15
  5.4 28.7 %collective-permute-start.3 = (bf16[64,4096]{1,0:T(8,128)(2,1)}, bf16[64,4096]{1,0:T(8,128)(2,1)S(1)}, u32[]{:S(2)}, u32[]{:S(2)}) collective-permute-start(bf16[64,4096]{1,0:T(8,128)(2,1)} %own.1), channel_id=1, source_target_pairs={{0,6},{2,0},{4,2},{6,4},{1,7},{3,1},{5,3},{7,5},{8,14},{10,8},{12,... | collective-permute-start | bytes 1572872 | tf_op jit(solution)/shard_map/ppermute | solution.py:15
  7.4 45.8 %collective-permute-start.1 = (bf16[64,4096]{1,0:T(8,128)(2,1)}, bf16[64,4096]{1,0:T(8,128)(2,1)S(1)}, u32[]{:S(2)}, u32[]{:S(2)}) collective-permute-start(bf16[64,4096]{1,0:T(8,128)(2,1)} %own.1), channel_id=1, source_target_pairs={{0,1},{1,0},{2,3},{3,2},{4,5},{5,4},{6,7},{7,6},{8,9},{9,8},{10,11... | collective-permute-start | bytes 1572872 | tf_op jit(solution)/shard_map/ppermute | solution.py:15
  11.3 1.4 copy-start.5
  12.7 1.0 copy-start.6
  13.8 0.8 copy-start.2
  14.6 43.5 %copy-start = (bf16[192,4096]{1,0:T(8,128)(2,1)}, bf16[192,4096]{1,0:T(8,128)(2,1)S(1)}, u32[]{:S(2)}) copy-start(bf16[192,4096]{1,0:T(8,128)(2,1)S(1)} %get-tuple-element.26.head.refs_14_) | copy-start | bytes 4718596
  34.2 14.5 %collective-permute-start.6 = (bf16[32,4096]{1,0:T(8,128)(2,1)S(1)}, bf16[32,4096]{1,0:T(8,128)(2,1)S(1)}, u32[]{:S(2)}, u32[]{:S(2)}) collective-permute-start(bf16[32,4096]{1,0:T(8,128)(2,1)S(1)} %slice.75), channel_id=1, source_target_pairs={{0,6},{2,0},{4,2},{6,4},{1,7},{3,1},{5,3},{7,5},{8,14},{10,8},{12,... | collective-permute-start | bytes 786440 | tf_op jit(solution)/shard_map/ppermute | solution.py:15
  36.1 35.9 %copy-start.4 = (bf16[64,4096]{1,0:T(8,128)(2,1)S(1)}, bf16[64,4096]{1,0:T(8,128)(2,1)}, u32[]{:S(2)}) copy-start(bf16[64,4096]{1,0:T(8,128)(2,1)} %copy-done.2) | copy-start | bytes 1572868
  36.2 15.1 %collective-permute-start.5 = (bf16[32,4096]{1,0:T(8,128)(2,1)S(1)}, bf16[32,4096]{1,0:T(8,128)(2,1)S(1)}, u32[]{:S(2)}, u32[]{:S(2)}) collective-permute-start(bf16[32,4096]{1,0:T(8,128)(2,1)S(1)} %slice.59), channel_id=1, source_target_pairs={{0,2},{2,4},{4,6},{6,0},{1,3},{3,5},{5,7},{7,1},{8,10},{10,12},{12... | collective-permute-start | bytes 786440 | tf_op jit(solution)/shard_map/ppermute | solution.py:15
  42.3 10.8 %collective-permute-start.4 = (bf16[64,4096]{1,0:T(8,128)(2,1)S(1)}, bf16[64,4096]{1,0:T(8,128)(2,1)S(1)}, u32[]{:S(2)}, u32[]{:S(2)}) collective-permute-start(bf16[64,4096]{1,0:T(8,128)(2,1)S(1)} %collective-permute-done.3.refs_4_.refs_8_), channel_id=1, source_target_pairs={{0,1},{1,0},{2,3},{3,2},{4,5},{5,4},{6,7},{7,6},{8,9},{9,8},{10,11... | collective-permute-start | bytes 1572872 | tf_op jit(solution)/shard_map/ppermute | solution.py:15
  44.3 10.4 %collective-permute-start.2 = (bf16[64,4096]{1,0:T(8,128)(2,1)S(1)}, bf16[64,4096]{1,0:T(8,128)(2,1)S(1)}, u32[]{:S(2)}, u32[]{:S(2)}) collective-permute-start(bf16[64,4096]{1,0:T(8,128)(2,1)S(1)} %collective-permute-done.refs_2_.refs_6_), channel_id=1, source_target_pairs={{0,1},{1,0},{2,3},{3,2},{4,5},{5,4},{6,7},{7,6},{8,9},{9,8},{10,11... | collective-permute-start | bytes 1572872 | tf_op jit(solution)/shard_map/ppermute | solution.py:15
  48.7 4.5 %collective-permute-start.8 = (bf16[32,4096]{1,0:T(8,128)(2,1)S(1)}, bf16[32,4096]{1,0:T(8,128)(2,1)S(1)}, u32[]{:S(2)}, u32[]{:S(2)}) collective-permute-start(bf16[32,4096]{1,0:T(8,128)(2,1)S(1)} %collective-permute-done.6.refs_7_.refs_11_), channel_id=1, source_target_pairs={{0,1},{1,0},{2,3},{3,2},{4,5},{5,4},{6,7},{7,6},{8,9},{9,8},{10,11... | collective-permute-start | bytes 786440 | tf_op jit(solution)/shard_map/ppermute | solution.py:15
  51.2 3.4 %collective-permute-start.7 = (bf16[32,4096]{1,0:T(8,128)(2,1)S(1)}, bf16[32,4096]{1,0:T(8,128)(2,1)S(1)}, u32[]{:S(2)}, u32[]{:S(2)}) collective-permute-start(bf16[32,4096]{1,0:T(8,128)(2,1)S(1)} %collective-permute-done.5.refs_6_.refs_10_), channel_id=1, source_target_pairs={{0,1},{1,0},{2,3},{3,2},{4,5},{5,4},{6,7},{7,6},{8,9},{9,8},{10,11... | collective-permute-start | bytes 786440 | tf_op jit(solution)/shard_map/ppermute | solution.py:15
  54.7 1.0 copy-start.3
  77.2 6.9 %copy-start.1 = (bf16[192,4096]{1,0:T(8,128)(2,1)S(1)}, bf16[192,4096]{1,0:T(8,128)(2,1)}, u32[]{:S(2)}) copy-start(bf16[192,4096]{1,0:T(8,128)(2,1)} %copy-done) | copy-start | bytes 4718596
  77.2 6.8 %collective-permute-start.9 = (bf16[256,4096]{1,0:T(8,128)(2,1)}, bf16[256,4096]{1,0:T(8,128)(2,1)}, u32[]{:S(2)}, u32[]{:S(2)}) collective-permute-start(bf16[256,4096]{1,0:T(8,128)(2,1)} %get-tuple-element.38), channel_id=1, source_target_pairs={{0,1},{1,0},{2,3},{3,2},{4,5},{5,4},{6,7},{7,6},{8,9},{9,8},{10,11... | collective-permute-start | bytes 6291464 | tf_op jit(solution)/shard_map/ppermute | solution.py:15
  79.2 24.1 %all-to-all-start.1 = ((bf16[4,48,4096]{2,1,0:T(8,128)(2,1)}), bf16[4,48,4096]{2,1,0:T(8,128)(2,1)S(1)}, u32[]{:S(2)}, u32[]{:S(2)}) async-start(bf16[4,48,4096]{2,1,0:T(8,128)(2,1)} %bitcast.29), calls=%async_computation.1 | async-start | bytes 3145728 | tf_op jit(solution)/shard_map/all_to_all | solution.py:197
  86.4 4.2 %copy-start.7 = (bf16[256,4096]{1,0:T(8,128)(2,1)}, bf16[256,4096]{1,0:T(8,128)(2,1)S(1)}, u32[]{:S(2)}) copy-start(bf16[256,4096]{1,0:T(8,128)(2,1)S(1)} %fusion.2) | copy-start | bytes 6291460
  86.4 17.3 %collective-permute-start.11 = (bf16[32,4096]{1,0:T(8,128)(2,1)S(1)}, bf16[32,4096]{1,0:T(8,128)(2,1)S(1)}, u32[]{:S(2)}, u32[]{:S(2)}) collective-permute-start(bf16[32,4096]{1,0:T(8,128)(2,1)S(1)} %get-tuple-element.45), channel_id=1, source_target_pairs={{0,6},{2,0},{4,2},{6,4},{1,7},{3,1},{5,3},{7,5},{8,14},{10,8},{12,... | collective-permute-start | bytes 786440 | tf_op jit(solution)/shard_map/ppermute | solution.py:15
  90.5 15.2 %collective-permute-start.10 = (bf16[32,4096]{1,0:T(8,128)(2,1)S(1)}, bf16[32,4096]{1,0:T(8,128)(2,1)S(1)}, u32[]{:S(2)}, u32[]{:S(2)}) collective-permute-start(bf16[32,4096]{1,0:T(8,128)(2,1)S(1)} %get-tuple-element.46), channel_id=1, source_target_pairs={{0,2},{2,4},{4,6},{6,0},{1,3},{3,5},{5,7},{7,1},{8,10},{10,12},{12... | collective-permute-start | bytes 786440 | tf_op jit(solution)/shard_map/ppermute | solution.py:15
  130.2 53.6 %all-to-all-start.3 = ((bf16[64,48,256]{2,1,0:T(8,128)(2,1)}), bf16[64,48,256]{2,1,0:T(8,128)(2,1)S(1)}, u32[]{:S(2)}, u32[]{:S(2)}) async-start(bf16[64,48,256]{2,1,0:T(8,128)(2,1)} %broadcast_in_dim.4), calls=%async_computation.3 | async-start | bytes 3145728 | tf_op jit(solution)/shard_map/all_to_all | solution.py:224
  140.8 16.2 %collective-permute-start.12 = (bf16[64,4096]{1,0:T(8,128)(2,1)S(1)}, bf16[64,4096]{1,0:T(8,128)(2,1)S(1)}, u32[]{:S(2)}, u32[]{:S(2)}) collective-permute-start(bf16[64,4096]{1,0:T(8,128)(2,1)S(1)} %get-tuple-element.43), channel_id=1, source_target_pairs={{0,2},{2,4},{4,6},{6,0},{1,3},{3,5},{5,7},{7,1},{8,10},{10,12},{12... | collective-permute-start | bytes 1572872 | tf_op jit(solution)/shard_map/ppermute | solution.py:15
  145.5 36.2 %collective-permute-start.13 = (bf16[64,4096]{1,0:T(8,128)(2,1)S(1)}, bf16[64,4096]{1,0:T(8,128)(2,1)S(1)}, u32[]{:S(2)}, u32[]{:S(2)}) collective-permute-start(bf16[64,4096]{1,0:T(8,128)(2,1)S(1)} %get-tuple-element.44), channel_id=1, source_target_pairs={{0,6},{2,0},{4,2},{6,4},{1,7},{3,1},{5,3},{7,5},{8,14},{10,8},{12,... | collective-permute-start | bytes 1572872 | tf_op jit(solution)/shard_map/ppermute | solution.py:15

commit v13 on v12

--- a/solution.py
+++ b/solution.py
@@ -221,8 +221,8 @@
 
     part = lax.all_to_all(part, ("yl", "z"), 0, 0, tiled=True)
     part = jnp.sum(part.astype(F32), axis=0).astype(BF16)
-    part = lax.all_to_all(jnp.broadcast_to(part, (n_x * n_rest,) + part.shape), DP, 0, 0, tiled=True)
-    part = part.reshape((n_x, n_rest) + part.shape[1:])
+    part = lax.all_to_all(jnp.broadcast_to(part, (n_rest,) + part.shape), ("yl", "z"), 0, 0, tiled=True)
+    part = lax.all_to_all(jnp.broadcast_to(part, (n_x,) + part.shape), "x", 0, 0, tiled=True)
     grad_weight = pl.pallas_call(
         lay_kernel,
         out_shape=jax.ShapeDtypeStruct((v_dev, width), BF16),

time: 187 us -> 178 us (0.952)
  the two profiles are of different devices: /device:TPU:30 before, /device:TPU:72 now
where the time goes in v13:
time: 178 us; the launch traced here: 177 us
  starting transfers between devices  64.2 us (36%)
  waiting for transfers between devices  47.2 us (27%)
  blocking collectives  39.7 us (22%)
  Pallas kernels  9.76 us (5%)
  local copies, waits for them, and re-layouts  8.74 us (5%)
  other arithmetic  3.71 us (2%)
  matrix products  2.32 us (1%)
    ppermute x14, starting transfers between devices, shift(): lax.ppermute(value, axis, [(i, (i + step) % size) for i in range(size)])  50.8 us
    ppermute x14, waiting for transfers between devices, shift(): lax.ppermute(value, axis, [(i, (i + step) % size) for i in range(size)])  24.4 us
    all_to_all x1, blocking collectives, per_device(): part = lax.all_to_all(part, ('yl', 'z'), 0, 0, tiled=True)  23.1 us
    all_to_all x1, blocking collectives, per_device(): stats = lax.all_to_all(stats, VOCAB, 0, 0, tiled=True)  16.6 us
    all_to_all x1, waiting for transfers between devices, per_device(): part = lax.all_to_all(part, 'x', 0, 0, tiled=True)  12.1 us
    all_to_all x1, waiting for transfers between devices, per_device(): lax.all_to_all(jnp.broadcast_to(part, (n_x,) + part.shape), 'x', 0, 0, ti...  7.08 us
    pallas_call x1, Pallas kernels, per_device(): pl.pallas_call(score_kernel, out_shape=(jax.ShapeDtypeStruct((v_dev, widt...  5.11 us
    all_to_all x1, starting transfers between devices, per_device(): lax.all_to_all(jnp.broadcast_to(part, (n_rest,) + part.shape), ('yl', 'z'...  4.69 us
  transfers between devices with their start and end apart: 17, of which 9 were waited for; matrix products, arithmetic and copies ran while one was open for 5% of the time, Pallas kernels for 0%

profile of v13, /device:TPU:72, one launch (start us, length us, event | category | flops | bytes accessed | tf_op | source)
XLA Modules:
  0.0 176.6 jit_solution(11283721961235290007)
XLA Ops:
  0.6 4.5 %collective-permute-start = (bf16[64,4096]{1,0:T(8,128)(2,1)}, bf16[64,4096]{1,0:T(8,128)(2,1)S(1)}, u32[]{:S(2)}, u32[]{:S(2)}) collective-permute-start(bf16[64,4096]{1,0:T(8,128)(2,1)} %own.1), channel_id=1, source_target_pairs={{0,2},{2,4},{4,6},{6,0},{1,3},{3,5},{5,7},{7,1},{8,10},{10,12},{12... | collective-permute-start | bytes 1572872 | tf_op jit(solution)/shard_map/ppermute | solution.py:15
  5.1 3.5 %collective-permute-start.3 = (bf16[64,4096]{1,0:T(8,128)(2,1)}, bf16[64,4096]{1,0:T(8,128)(2,1)S(1)}, u32[]{:S(2)}, u32[]{:S(2)}) collective-permute-start(bf16[64,4096]{1,0:T(8,128)(2,1)} %own.1), channel_id=1, source_target_pairs={{0,6},{2,0},{4,2},{6,4},{1,7},{3,1},{5,3},{7,5},{8,14},{10,8},{12,... | collective-permute-start | bytes 1572872 | tf_op jit(solution)/shard_map/ppermute | solution.py:15
  8.6 1.9 %collective-permute-start.1 = (bf16[64,4096]{1,0:T(8,128)(2,1)}, bf16[64,4096]{1,0:T(8,128)(2,1)S(1)}, u32[]{:S(2)}, u32[]{:S(2)}) collective-permute-start(bf16[64,4096]{1,0:T(8,128)(2,1)} %own.1), channel_id=1, source_target_pairs={{0,1},{1,0},{2,3},{3,2},{4,5},{5,4},{6,7},{7,6},{8,9},{9,8},{10,11... | collective-permute-start | bytes 1572872 | tf_op jit(solution)/shard_map/ppermute | solution.py:15
  12.5 1.4 copy-done.5
  15.9 7.7 %collective-permute-done.3.refs_4_.refs_8_ = bf16[64,4096]{1,0:T(8,128)(2,1)S(1)} collective-permute-done((bf16[64,4096]{1,0:T(8,128)(2,1)}, bf16[64,4096]{1,0:T(8,128)(2,1)S(1)}, u32[]{:S(2)}, u32[]{:S(2)}) %collective-permute-start.3) | collective-permute-done | bytes 524320 | tf_op jit(solution)/shard_map/ppermute | solution.py:15
  23.7 4.5 %collective-permute-start.6 = (bf16[32,4096]{1,0:T(8,128)(2,1)S(1)}, bf16[32,4096]{1,0:T(8,128)(2,1)S(1)}, u32[]{:S(2)}, u32[]{:S(2)}) collective-permute-start(bf16[32,4096]{1,0:T(8,128)(2,1)S(1)} %slice.75), channel_id=1, source_target_pairs={{0,6},{2,0},{4,2},{6,4},{1,7},{3,1},{5,3},{7,5},{8,14},{10,8},{12,... | collective-permute-start | bytes 786440 | tf_op jit(solution)/shard_map/ppermute | solution.py:15
  28.2 1.5 collective-permute-done.refs_2_.refs_6_
  29.8 11.0 %collective-permute-start.5 = (bf16[32,4096]{1,0:T(8,128)(2,1)S(1)}, bf16[32,4096]{1,0:T(8,128)(2,1)S(1)}, u32[]{:S(2)}, u32[]{:S(2)}) collective-permute-start(bf16[32,4096]{1,0:T(8,128)(2,1)S(1)} %slice.59), channel_id=1, source_target_pairs={{0,2},{2,4},{4,6},{6,0},{1,3},{3,5},{5,7},{7,1},{8,10},{10,12},{12... | collective-permute-start | bytes 786440 | tf_op jit(solution)/shard_map/ppermute | solution.py:15
  40.8 1.9 %collective-permute-start.4 = (bf16[64,4096]{1,0:T(8,128)(2,1)S(1)}, bf16[64,4096]{1,0:T(8,128)(2,1)S(1)}, u32[]{:S(2)}, u32[]{:S(2)}) collective-permute-start(bf16[64,4096]{1,0:T(8,128)(2,1)S(1)} %collective-permute-done.3.refs_4_.refs_8_), channel_id=1, source_target_pairs={{0,1},{1,0},{2,3},{3,2},{4,5},{5,4},{6,7},{7,6},{8,9},{9,8},{10,11... | collective-permute-start | bytes 1572872 | tf_op jit(solution)/shard_map/ppermute | solution.py:15
  42.7 2.4 %collective-permute-start.2 = (bf16[64,4096]{1,0:T(8,128)(2,1)S(1)}, bf16[64,4096]{1,0:T(8,128)(2,1)S(1)}, u32[]{:S(2)}, u32[]{:S(2)}) collective-permute-start(bf16[64,4096]{1,0:T(8,128)(2,1)S(1)} %collective-permute-done.refs_2_.refs_6_), channel_id=1, source_target_pairs={{0,1},{1,0},{2,3},{3,2},{4,5},{5,4},{6,7},{7,6},{8,9},{9,8},{10,11... | collective-permute-start | bytes 1572872 | tf_op jit(solution)/shard_map/ppermute | solution.py:15
  45.1 3.1 %collective-permute-done.6.refs_7_.refs_11_ = bf16[32,4096]{1,0:T(8,128)(2,1)S(1)} collective-permute-done((bf16[32,4096]{1,0:T(8,128)(2,1)S(1)}, bf16[32,4096]{1,0:T(8,128)(2,1)S(1)}, u32[]{:S(2)}, u32[]{:S(2)}) %collective-permute-start.6) | collective-permute-done | bytes 262176 | tf_op jit(solution)/shard_map/ppermute | solution.py:15
  48.3 1.9 %collective-permute-start.8 = (bf16[32,4096]{1,0:T(8,128)(2,1)S(1)}, bf16[32,4096]{1,0:T(8,128)(2,1)S(1)}, u32[]{:S(2)}, u32[]{:S(2)}) collective-permute-start(bf16[32,4096]{1,0:T(8,128)(2,1)S(1)} %collective-permute-done.6.refs_7_.refs_11_), channel_id=1, source_target_pairs={{0,1},{1,0},{2,3},{3,2},{4,5},{5,4},{6,7},{7,6},{8,9},{9,8},{10,11... | collective-permute-start | bytes 786440 | tf_op jit(solution)/shard_map/ppermute | solution.py:15
  50.2 2.4 %collective-permute-start.7 = (bf16[32,4096]{1,0:T(8,128)(2,1)S(1)}, bf16[32,4096]{1,0:T(8,128)(2,1)S(1)}, u32[]{:S(2)}, u32[]{:S(2)}) collective-permute-start(bf16[32,4096]{1,0:T(8,128)(2,1)S(1)} %collective-permute-done.5.refs_6_.refs_10_), channel_id=1, source_target_pairs={{0,1},{1,0},{2,3},{3,2},{4,5},{5,4},{6,7},{7,6},{8,9},{9,8},{10,11... | collective-permute-start | bytes 786440 | tf_op jit(solution)/shard_map/ppermute | solution.py:15
  54.8 2.5 %shard_map.68 = (f32[192,128]{1,0:T(8,128)S(1)}, f32[192,128]{1,0:T(8,128)S(1)}, f32[192,128]{1,0:T(8,128)S(1)}, f32[192,128]{1,0:T(8,128)S(1)}, f32[8,16,128]{2,1,0:T(8,128)S(1)}) custom-call(s32[6]{0:T(128)S(1)} %stack.27.where, bf16[192,4096]{1,0:T(8,128)(2,1)S(1)} %get-tuple-element.26.head.refs_14_, s32[1,512]{1,0:T(1,128)S(1)} %reshape.22.labels, ...), custom_call_target="tpu_custom_call" | custom-call | flops 805306368 | bytes 5767168 | tf_op jit(solution)/shard_map/pallas_call | solution.py:157
  57.3 16.6 %all_to_all.25.stats = f32[8,16,128]{2,1,0:T(8,128)S(1)} all-to-all(f32[8,16,128]{2,1,0:T(8,128)S(1)} %get-tuple-element.30), channel_id=1, replica_groups=mesh['x'=4,'yl'=2,'z'=8,'yh'=4,'core'=2] {'yh','core'}, dimensions={0} | all-to-all | bytes 131072 | tf_op jit(solution)/shard_map/all_to_all | solution.py:169
  73.9 5.1 %shard_map.69 = (bf16[192,4096]{1,0:T(8,128)(2,1)}, bf16[256,4096]{1,0:T(8,128)(2,1)}, bf16[256,192]{1,0:T(8,128)(2,1)S(1)}, f32[1,128]{1,0:T(1,128)S(1)}) custom-call(s32[6]{0:T(128)S(1)} %stack.27.where, f32[8,16,128]{2,1,0:T(8,128)S(1)} %all_to_all.25.stats, s32[1,512]{1,0:T(1,128)S(1)} %reshape.22.labels, f32[1,512]{1,0:T(1,128)S(1)} %reshape.24.weights, ...), custom_call_target="tpu_custom_call" | custom-call | flops 1207959552 | bytes 9437184 | tf_op jit(solution)/shard_map/pallas_call | solution.py:171
  79.0 2.1 %collective-permute-start.9 = (bf16[256,4096]{1,0:T(8,128)(2,1)}, bf16[256,4096]{1,0:T(8,128)(2,1)}, u32[]{:S(2)}, u32[]{:S(2)}) collective-permute-start(bf16[256,4096]{1,0:T(8,128)(2,1)} %get-tuple-element.38), channel_id=1, source_target_pairs={{0,1},{1,0},{2,3},{3,2},{4,5},{5,4},{6,7},{7,6},{8,9},{9,8},{10,11... | collective-permute-start | bytes 6291464 | tf_op jit(solution)/shard_map/ppermute | solution.py:15
  81.1 4.3 %all-to-all-start.1 = ((bf16[4,48,4096]{2,1,0:T(8,128)(2,1)}), bf16[4,48,4096]{2,1,0:T(8,128)(2,1)S(1)}, u32[]{:S(2)}, u32[]{:S(2)}) async-start(bf16[4,48,4096]{2,1,0:T(8,128)(2,1)} %bitcast.27), calls=%async_computation.1 | async-start | bytes 3145728 | tf_op jit(solution)/shard_map/all_to_all | solution.py:197
  85.6 2.3 %fusion.2 = bf16[256,4096]{1,0:T(8,128)(2,1)S(1)} fusion(bf16[256,192]{1,0:T(8,128)(2,1)S(1)} %get-tuple-element.37, bf16[192,4096]{1,0:T(8,128)(2,1)S(1)} %copy-done.1, bf16[256,4096]{1,0:T(8,128)(2,1)} %collective-permute-done.9), kind=kOutput, calls=%fused_computation.3 | convolution fusion | flops 407896064 | bytes 5865472 | tf_op jit(solution)/shard_map/dot_general | solution.py:199
  87.9 2.5 %collective-permute-start.11 = (bf16[32,4096]{1,0:T(8,128)(2,1)S(1)}, bf16[32,4096]{1,0:T(8,128)(2,1)S(1)}, u32[]{:S(2)}, u32[]{:S(2)}) collective-permute-start(bf16[32,4096]{1,0:T(8,128)(2,1)S(1)} %get-tuple-element.45), channel_id=1, source_target_pairs={{0,6},{2,0},{4,2},{6,4},{1,7},{3,1},{5,3},{7,5},{8,14},{10,8},{12,... | collective-permute-start | bytes 786440 | tf_op jit(solution)/shard_map/ppermute | solution.py:15
  90.4 4.3 %collective-permute-start.10 = (bf16[32,4096]{1,0:T(8,128)(2,1)S(1)}, bf16[32,4096]{1,0:T(8,128)(2,1)S(1)}, u32[]{:S(2)}, u32[]{:S(2)}) collective-permute-start(bf16[32,4096]{1,0:T(8,128)(2,1)S(1)} %get-tuple-element.46), channel_id=1, source_target_pairs={{0,2},{2,4},{4,6},{6,0},{1,3},{3,5},{5,7},{7,1},{8,10},{10,12},{12... | collective-permute-start | bytes 786440 | tf_op jit(solution)/shard_map/ppermute | solution.py:15
  94.7 12.1 %all-to-all-done.1.parts = bf16[4,48,4096]{2,1,0:T(8,128)(2,1)S(1)} async-done(((bf16[4,48,4096]{2,1,0:T(8,128)(2,1)}), bf16[4,48,4096]{2,1,0:T(8,128)(2,1)S(1)}, u32[]{:S(2)}, u32[]{:S(2)}) %all-to-all-start.1) | async-done | bytes 1572896 | tf_op jit(solution)/shard_map/all_to_all | solution.py:197
  107.2 23.1 %all_to_all.26 = bf16[16,48,256]{2,1,0:T(8,128)(2,1)S(1)} all-to-all(bf16[16,48,256]{2,1,0:T(8,128)(2,1)S(1)} %shard_map.70), channel_id=1, replica_groups=mesh['x'=4,'yl'=2,'z'=8,'yh'=4,'core'=2] {'yl','z'}, dimensions={0} | all-to-all | bytes 786432 | tf_op jit(solution)/shard_map/all_to_all | solution.py:222
  131.1 4.7 %all-to-all-start.3 = ((bf16[16,48,256]{2,1,0:T(8,128)(2,1)}), bf16[16,48,256]{2,1,0:T(8,128)(2,1)S(1)}, u32[]{:S(2)}, u32[]{:S(2)}) async-start(bf16[16,48,256]{2,1,0:T(8,128)(2,1)} %broadcast_in_dim.7), calls=%async_computation.3 | async-start | bytes 786432 | tf_op jit(solution)/shard_map/all_to_all | solution.py:224
  137.2 3.4 %collective-permute-start.12 = (bf16[64,4096]{1,0:T(8,128)(2,1)S(1)}, bf16[64,4096]{1,0:T(8,128)(2,1)S(1)}, u32[]{:S(2)}, u32[]{:S(2)}) collective-permute-start(bf16[64,4096]{1,0:T(8,128)(2,1)S(1)} %get-tuple-element.43), channel_id=1, source_target_pairs={{0,2},{2,4},{4,6},{6,0},{1,3},{3,5},{5,7},{7,1},{8,10},{10,12},{12... | collective-permute-start | bytes 1572872 | tf_op jit(solution)/shard_map/ppermute | solution.py:15
  140.6 4.5 %collective-permute-start.13 = (bf16[64,4096]{1,0:T(8,128)(2,1)S(1)}, bf16[64,4096]{1,0:T(8,128)(2,1)}, u32[]{:S(2)}, u32[]{:S(2)}) collective-permute-start(bf16[64,4096]{1,0:T(8,128)(2,1)S(1)} %get-tuple-element.44), channel_id=1, source_target_pairs={{0,6},{2,0},{4,2},{6,4},{1,7},{3,1},{5,3},{7,5},{8,14},{10,8},{12,... | collective-permute-start | bytes 1572872 | tf_op jit(solution)/shard_map/ppermute | solution.py:15
  145.1 3.6 %all-to-all-done.3 = bf16[16,48,256]{2,1,0:T(8,128)(2,1)S(1)} async-done(((bf16[16,48,256]{2,1,0:T(8,128)(2,1)}), bf16[16,48,256]{2,1,0:T(8,128)(2,1)S(1)}, u32[]{:S(2)}, u32[]{:S(2)}) %all-to-all-start.3) | async-done | bytes 393248 | tf_op jit(solution)/shard_map/all_to_all | solution.py:224
  150.0 4.4 %all-to-all-start.4 = ((bf16[4,16,48,256]{3,2,1,0:T(8,128)(2,1)}), bf16[4,16,48,256]{3,2,1,0:T(8,128)(2,1)S(1)}, u32[]{:S(2)}, u32[]{:S(2)}) async-start(bf16[4,16,48,256]{3,2,1,0:T(8,128)(2,1)} %broadcast_in_dim.8), calls=%async_computation.4 | async-start | bytes 3145728 | tf_op jit(solution)/shard_map/all_to_all | solution.py:225
  155.0 10.7 %collective-permute-done.12 = bf16[64,4096]{1,0:T(8,128)(2,1)S(1)} collective-permute-done((bf16[64,4096]{1,0:T(8,128)(2,1)S(1)}, bf16[64,4096]{1,0:T(8,128)(2,1)S(1)}, u32[]{:S(2)}, u32[]{:S(2)}) %collective-permute-start.12) | collective-permute-done | bytes 524320 | tf_op jit(solution)/shard_map/ppermute | solution.py:15
  165.7 2.2 %add_convert_fusion = bf16[64,4096]{1,0:T(8,128)(2,1)} fusion(bf16[64,4096]{1,0:T(8,128)(2,1)} %collective-permute-done.13, bf16[64,4096]{1,0:T(8,128)(2,1)S(1)} %collective-permute-done.12, bf16[256,4096]{1,0:T(8,128)(2,1)} %copy-done.7), kind=kLoop, calls=%fused_computation.4 | loop fusion | flops 1572864 | bytes 2097152 | tf_op jit(solution)/shard_map/convert_element_type | solution.py:235
  167.9 7.1 %all-to-all-done.4.pieces = bf16[4,16,48,256]{3,2,1,0:T(8,128)(2,1)S(1)} async-done(((bf16[4,16,48,256]{3,2,1,0:T(8,128)(2,1)}), bf16[4,16,48,256]{3,2,1,0:T(8,128)(2,1)S(1)}, u32[]{:S(2)}, u32[]{:S(2)}) %all-to-all-start.4) | async-done | bytes 1572896 | tf_op jit(solution)/shard_map/all_to_all | solution.py:225
  175.0 1.7 shard_map.71
  (50 shorter events, 10.7 us)
Async XLA Ops:
  0.6 29.1 %collective-permute-start = (bf16[64,4096]{1,0:T(8,128)(2,1)}, bf16[64,4096]{1,0:T(8,128)(2,1)S(1)}, u32[]{:S(2)}, u32[]{:S(2)}) collective-permute-start(bf16[64,4096]{1,0:T(8,128)(2,1)} %own.1), channel_id=1, source_target_pairs={{0,2},{2,4},{4,6},{6,0},{1,3},{3,5},{5,7},{7,1},{8,10},{10,12},{12... | collective-permute-start | bytes 1572872 | tf_op jit(solution)/shard_map/ppermute | solution.py:15
  5.1 18.5 %collective-permute-start.3 = (bf16[64,4096]{1,0:T(8,128)(2,1)}, bf16[64,4096]{1,0:T(8,128)(2,1)S(1)}, u32[]{:S(2)}, u32[]{:S(2)}) collective-permute-start(bf16[64,4096]{1,0:T(8,128)(2,1)} %own.1), channel_id=1, source_target_pairs={{0,6},{2,0},{4,2},{6,4},{1,7},{3,1},{5,3},{7,5},{8,14},{10,8},{12,... | collective-permute-start | bytes 1572872 | tf_op jit(solution)/shard_map/ppermute | solution.py:15
  8.6 44.0 %collective-permute-start.1 = (bf16[64,4096]{1,0:T(8,128)(2,1)}, bf16[64,4096]{1,0:T(8,128)(2,1)S(1)}, u32[]{:S(2)}, u32[]{:S(2)}) collective-permute-start(bf16[64,4096]{1,0:T(8,128)(2,1)} %own.1), channel_id=1, source_target_pairs={{0,1},{1,0},{2,3},{3,2},{4,5},{5,4},{6,7},{7,6},{8,9},{9,8},{10,11... | collective-permute-start | bytes 1572872 | tf_op jit(solution)/shard_map/ppermute | solution.py:15
  12.5 1.4 copy-start.5
  13.9 1.0 copy-start.6
  15.1 0.8 copy-start.2
  15.9 41.4 %copy-start = (bf16[192,4096]{1,0:T(8,128)(2,1)}, bf16[192,4096]{1,0:T(8,128)(2,1)S(1)}, u32[]{:S(2)}) copy-start(bf16[192,4096]{1,0:T(8,128)(2,1)S(1)} %get-tuple-element.26.head.refs_14_) | copy-start | bytes 4718596
  23.7 24.6 %collective-permute-start.6 = (bf16[32,4096]{1,0:T(8,128)(2,1)S(1)}, bf16[32,4096]{1,0:T(8,128)(2,1)S(1)}, u32[]{:S(2)}, u32[]{:S(2)}) collective-permute-start(bf16[32,4096]{1,0:T(8,128)(2,1)S(1)} %slice.75), channel_id=1, source_target_pairs={{0,6},{2,0},{4,2},{6,4},{1,7},{3,1},{5,3},{7,5},{8,14},{10,8},{12,... | collective-permute-start | bytes 786440 | tf_op jit(solution)/shard_map/ppermute | solution.py:15
  29.7 44.2 %copy-start.4 = (bf16[64,4096]{1,0:T(8,128)(2,1)S(1)}, bf16[64,4096]{1,0:T(8,128)(2,1)}, u32[]{:S(2)}) copy-start(bf16[64,4096]{1,0:T(8,128)(2,1)} %copy-done.2) | copy-start | bytes 1572868
  29.8 20.4 %collective-permute-start.5 = (bf16[32,4096]{1,0:T(8,128)(2,1)S(1)}, bf16[32,4096]{1,0:T(8,128)(2,1)S(1)}, u32[]{:S(2)}, u32[]{:S(2)}) collective-permute-start(bf16[32,4096]{1,0:T(8,128)(2,1)S(1)} %slice.59), channel_id=1, source_target_pairs={{0,2},{2,4},{4,6},{6,0},{1,3},{3,5},{5,7},{7,1},{8,10},{10,12},{12... | collective-permute-start | bytes 786440 | tf_op jit(solution)/shard_map/ppermute | solution.py:15
  40.8 11.9 %collective-permute-start.4 = (bf16[64,4096]{1,0:T(8,128)(2,1)S(1)}, bf16[64,4096]{1,0:T(8,128)(2,1)S(1)}, u32[]{:S(2)}, u32[]{:S(2)}) collective-permute-start(bf16[64,4096]{1,0:T(8,128)(2,1)S(1)} %collective-permute-done.3.refs_4_.refs_8_), channel_id=1, source_target_pairs={{0,1},{1,0},{2,3},{3,2},{4,5},{5,4},{6,7},{7,6},{8,9},{9,8},{10,11... | collective-permute-start | bytes 1572872 | tf_op jit(solution)/shard_map/ppermute | solution.py:15
  42.7 11.0 %collective-permute-start.2 = (bf16[64,4096]{1,0:T(8,128)(2,1)S(1)}, bf16[64,4096]{1,0:T(8,128)(2,1)S(1)}, u32[]{:S(2)}, u32[]{:S(2)}) collective-permute-start(bf16[64,4096]{1,0:T(8,128)(2,1)S(1)} %collective-permute-done.refs_2_.refs_6_), channel_id=1, source_target_pairs={{0,1},{1,0},{2,3},{3,2},{4,5},{5,4},{6,7},{7,6},{8,9},{9,8},{10,11... | collective-permute-start | bytes 1572872 | tf_op jit(solution)/shard_map/ppermute | solution.py:15
  48.3 4.4 %collective-permute-start.8 = (bf16[32,4096]{1,0:T(8,128)(2,1)S(1)}, bf16[32,4096]{1,0:T(8,128)(2,1)S(1)}, u32[]{:S(2)}, u32[]{:S(2)}) collective-permute-start(bf16[32,4096]{1,0:T(8,128)(2,1)S(1)} %collective-permute-done.6.refs_7_.refs_11_), channel_id=1, source_target_pairs={{0,1},{1,0},{2,3},{3,2},{4,5},{5,4},{6,7},{7,6},{8,9},{9,8},{10,11... | collective-permute-start | bytes 786440 | tf_op jit(solution)/shard_map/ppermute | solution.py:15
  50.2 3.6 %collective-permute-start.7 = (bf16[32,4096]{1,0:T(8,128)(2,1)S(1)}, bf16[32,4096]{1,0:T(8,128)(2,1)S(1)}, u32[]{:S(2)}, u32[]{:S(2)}) collective-permute-start(bf16[32,4096]{1,0:T(8,128)(2,1)S(1)} %collective-permute-done.5.refs_6_.refs_10_), channel_id=1, source_target_pairs={{0,1},{1,0},{2,3},{3,2},{4,5},{5,4},{6,7},{7,6},{8,9},{9,8},{10,11... | collective-permute-start | bytes 786440 | tf_op jit(solution)/shard_map/ppermute | solution.py:15
  53.8 1.0 copy-start.3
  79.0 6.5 %copy-start.1 = (bf16[192,4096]{1,0:T(8,128)(2,1)S(1)}, bf16[192,4096]{1,0:T(8,128)(2,1)}, u32[]{:S(2)}) copy-start(bf16[192,4096]{1,0:T(8,128)(2,1)} %copy-done) | copy-start | bytes 4718596
  79.0 6.5 %collective-permute-start.9 = (bf16[256,4096]{1,0:T(8,128)(2,1)}, bf16[256,4096]{1,0:T(8,128)(2,1)}, u32[]{:S(2)}, u32[]{:S(2)}) collective-permute-start(bf16[256,4096]{1,0:T(8,128)(2,1)} %get-tuple-element.38), channel_id=1, source_target_pairs={{0,1},{1,0},{2,3},{3,2},{4,5},{5,4},{6,7},{7,6},{8,9},{9,8},{10,11... | collective-permute-start | bytes 6291464 | tf_op jit(solution)/shard_map/ppermute | solution.py:15
  81.1 25.7 %all-to-all-start.1 = ((bf16[4,48,4096]{2,1,0:T(8,128)(2,1)}), bf16[4,48,4096]{2,1,0:T(8,128)(2,1)S(1)}, u32[]{:S(2)}, u32[]{:S(2)}) async-start(bf16[4,48,4096]{2,1,0:T(8,128)(2,1)} %bitcast.27), calls=%async_computation.1 | async-start | bytes 3145728 | tf_op jit(solution)/shard_map/all_to_all | solution.py:197
  87.9 2.5 %copy-start.7 = (bf16[256,4096]{1,0:T(8,128)(2,1)}, bf16[256,4096]{1,0:T(8,128)(2,1)S(1)}, u32[]{:S(2)}) copy-start(bf16[256,4096]{1,0:T(8,128)(2,1)S(1)} %fusion.2) | copy-start | bytes 6291460
  87.9 19.2 %collective-permute-start.11 = (bf16[32,4096]{1,0:T(8,128)(2,1)S(1)}, bf16[32,4096]{1,0:T(8,128)(2,1)S(1)}, u32[]{:S(2)}, u32[]{:S(2)}) collective-permute-start(bf16[32,4096]{1,0:T(8,128)(2,1)S(1)} %get-tuple-element.45), channel_id=1, source_target_pairs={{0,6},{2,0},{4,2},{6,4},{1,7},{3,1},{5,3},{7,5},{8,14},{10,8},{12,... | collective-permute-start | bytes 786440 | tf_op jit(solution)/shard_map/ppermute | solution.py:15
  90.4 16.8 %collective-permute-start.10 = (bf16[32,4096]{1,0:T(8,128)(2,1)S(1)}, bf16[32,4096]{1,0:T(8,128)(2,1)S(1)}, u32[]{:S(2)}, u32[]{:S(2)}) collective-permute-start(bf16[32,4096]{1,0:T(8,128)(2,1)S(1)} %get-tuple-element.46), channel_id=1, source_target_pairs={{0,2},{2,4},{4,6},{6,0},{1,3},{3,5},{5,7},{7,1},{8,10},{10,12},{12... | collective-permute-start | bytes 786440 | tf_op jit(solution)/shard_map/ppermute | solution.py:15
  131.1 17.6 %all-to-all-start.3 = ((bf16[16,48,256]{2,1,0:T(8,128)(2,1)}), bf16[16,48,256]{2,1,0:T(8,128)(2,1)S(1)}, u32[]{:S(2)}, u32[]{:S(2)}) async-start(bf16[16,48,256]{2,1,0:T(8,128)(2,1)} %broadcast_in_dim.7), calls=%async_computation.3 | async-start | bytes 786432 | tf_op jit(solution)/shard_map/all_to_all | solution.py:224
  137.2 28.5 %collective-permute-start.12 = (bf16[64,4096]{1,0:T(8,128)(2,1)S(1)}, bf16[64,4096]{1,0:T(8,128)(2,1)S(1)}, u32[]{:S(2)}, u32[]{:S(2)}) collective-permute-start(bf16[64,4096]{1,0:T(8,128)(2,1)S(1)} %get-tuple-element.43), channel_id=1, source_target_pairs={{0,2},{2,4},{4,6},{6,0},{1,3},{3,5},{5,7},{7,1},{8,10},{10,12},{12... | collective-permute-start | bytes 1572872 | tf_op jit(solution)/shard_map/ppermute | solution.py:15
  140.6 25.1 %collective-permute-start.13 = (bf16[64,4096]{1,0:T(8,128)(2,1)S(1)}, bf16[64,4096]{1,0:T(8,128)(2,1)}, u32[]{:S(2)}, u32[]{:S(2)}) collective-permute-start(bf16[64,4096]{1,0:T(8,128)(2,1)S(1)} %get-tuple-element.44), channel_id=1, source_target_pairs={{0,6},{2,0},{4,2},{6,4},{1,7},{3,1},{5,3},{7,5},{8,14},{10,8},{12,... | collective-permute-start | bytes 1572872 | tf_op jit(solution)/shard_map/ppermute | solution.py:15
  150.0 25.0 %all-to-all-start.4 = ((bf16[4,16,48,256]{3,2,1,0:T(8,128)(2,1)}), bf16[4,16,48,256]{3,2,1,0:T(8,128)(2,1)S(1)}, u32[]{:S(2)}, u32[]{:S(2)}) async-start(bf16[4,16,48,256]{3,2,1,0:T(8,128)(2,1)} %broadcast_in_dim.8), calls=%async_computation.4 | async-start | bytes 3145728 | tf_op jit(solution)/shard_map/all_to_all | solution.py:225
